TPU v7x, 32 devices: a whole 2x2x4 slice. The times are simulated.
32 devices in a mesh: groups: 2 (over x), tp: 4 (over y, core), seq: 4 (over z).
Axes of the slice: x: 2, y: 2, z: 4, core: 2. Of those that a mesh axis runs over, the one named last changes fastest.
Arguments:
- hidden_in: bfloat16 [6144, 4608], P(('groups', 'seq', 'tp')), parts along dimension 0, may hold values from -6 to 6
- pre_gain: float32 [4608], replicated, may hold values from 0.1 to 1.9
- post_gain: float32 [4608], replicated, may hold values from 0.1 to 1.9
- w_query: bfloat16 [4608, 1024], P(None, 'tp')
- w_key: bfloat16 [4608, 512], P(None, 'tp')
- w_value: bfloat16 [4608, 512], P(None, 'tp'), may hold values from -0.09375 to 0.09375
- w_out: bfloat16 [1024, 4608], P('tp'), may hold values from -0.1875 to 0.1875
- block_of: int32 [8], replicated, may hold values from 0 to 7, each once
Outputs:
- hidden_out: bfloat16 [6144, 4608], P(('groups', 'seq', 'tp')), parts along dimension 0
There are 2 independent parts, one for each index of `groups`. A program takes and returns all parts, laid end to end along the dimension named above; an argument that names none is the same for every part. Nothing has to cross between parts.
Inputs may be any that keep to these rules, and one draw needn't show every extreme that they name: block_of is a permutation: storage block b (rows b * 384 onward) holds the prompt's positions from block_of[b] * 384 onward.
All inputs are finite; a program needn't handle non-finite values.
Results may differ from a plain program's by a relative error of at most 0.012.
Values may be sent and summed in bfloat16 or wider, within the bound.
No kernel may reach another device: no remote copies, remote signals or barrier semaphores. Data moves between devices by JAX's collectives and lax.ppermute only.
A program may use at most 64 MiB of HBM per device.

v0:
```python
import functools
import math

import jax
import jax.numpy as jnp
from jax import lax
from jax.experimental import pallas as pl
from jax.experimental.pallas import tpu as pltpu
from jax.sharding import PartitionSpec as P

HD = 128
ATT_SCALAR = 144
EPS = 1e-6
MIB = 1024 * 1024
HIDDEN = -1e30
ONES = 16
COST = pl.CostEstimate(flops=1, bytes_accessed=1, transcendentals=0)

ANY = pl.BlockSpec(memory_space=pl.ANY)
HBM = pl.BlockSpec(memory_space=pltpu.HBM)
VMEM = pl.BlockSpec(memory_space=pltpu.VMEM)
SMEM = pl.BlockSpec(memory_space=pltpu.SMEM)


class Came:
    def __init__(self, array):
        self.array, self.shape = array, array.shape


def call(kernel, name, mib, in_specs, outs, scratch, *args, aliases=None):
    in_specs, pinned = list(in_specs), []
    for at, arg in enumerate(args):
        if isinstance(arg, Came):
            arg, in_specs[at] = arg.array, ANY
        elif in_specs[at] is not SMEM:
            arg = pltpu.with_memory_space_constraint(arg, in_specs[at].memory_space)
        pinned.append(arg)
    return pl.pallas_call(
        kernel,
        in_specs=in_specs,
        out_specs=[spec for _, _, spec in outs],
        out_shape=[spec.memory_space(shape, dtype) for shape, dtype, spec in outs],
        scratch_shapes=scratch,
        input_output_aliases=aliases or {},
        compiler_params=pltpu.CompilerParams(vmem_limit_bytes=mib * MIB),
        cost_estimate=COST,
        name=name,
    )(*pinned)


class Copies:
    def __init__(self, semaphores):
        self.semaphores, self.used = semaphores, 0

    def start(self, source, target):
        copy = pltpu.make_async_copy(source, target, self.semaphores.at[self.used])
        self.used += 1
        copy.start()
        return copy


def norm_kernel(cuts, pieces, hidden, gain, *refs):
    parts, (gains, rows, staged, semaphores) = refs[: len(cuts)], refs[len(cuts) :]
    copies = Copies(semaphores)
    count, width = hidden.shape
    step = count // pieces
    spans = [pl.ds(at * step, step) for at in range(pieces)]
    ins = [copies.start(hidden.at[span], rows.at[span]) for span in spans]
    copies.start(gain, gains).wait()
    scale = gains[...].reshape(1, width)
    outs = []
    for at, span in enumerate(spans):
        ins[at].wait()
        x = rows[span, :].astype(jnp.float32)
        square = x * x
        folded = square[:, :128]
        for lane in range(128, width, 128):
            folded = folded + square[:, lane : lane + 128]
        mean = jnp.sum(folded, axis=1, keepdims=True) / width
        staged[span, :] = (x * lax.rsqrt(mean + EPS) * scale).astype(jnp.bfloat16)
        begin = 0
        for cut, part in zip(cuts, parts):
            if begin <= at * step < begin + cut:
                inside = pl.ds(at * step - begin, step)
                outs.append(copies.start(staged.at[span], part.at[inside]))
            begin += cut
    for copy in outs:
        copy.wait()


def norm(hidden, gain, cuts, pieces=3):
    rows, width = hidden.shape
    bf16 = jnp.bfloat16
    return call(
        functools.partial(norm_kernel, cuts, pieces),
        "norm_rows",
        8,
        [HBM, HBM],
        [((cut, width), bf16, HBM) for cut in cuts],
        [
            pltpu.VMEM((width,), jnp.float32),
            pltpu.VMEM((rows, width), bf16),
            pltpu.VMEM((rows, width), bf16),
            pltpu.SemaphoreType.DMA((1 + 2 * pieces,)),
        ],
        hidden,
        gain,
    )


def rotate_into(product, angles, q, kv):
    cos, sin = angles[:, :HD], angles[:, HD:]
    queries = product.shape[1] - 2 * HD

    def rotated(at):
        y = product[:, at : at + HD]
        return y * cos + pltpu.roll(y, HD // 2, 1) * sin

    factor = ATT_SCALAR ** (-0.5) * math.log2(math.e)
    kv[:, :HD] = rotated(queries).astype(jnp.bfloat16)
    kv[:, HD:] = product[:, queries + HD :].astype(jnp.bfloat16)
    for head in range(queries // HD):
        q[head] = (rotated(head * HD) * factor).astype(jnp.bfloat16)


def qkv_kernel(count, first, chunks, trig, wq, wk, wv, *refs):
    parts = refs[:count]
    q, kv, weights, rows, angles, semaphores = refs[count:]
    copies, waits = Copies(semaphores), []
    depth = weights.shape[0] // chunks
    for chunk in range(chunks):
        span, put, column, here = pl.ds(chunk * depth, depth), 0, 0, []
        for part in parts:
            target = rows.at[pl.ds(put, part.shape[0]), span]
            here.append(copies.start(part.at[:, span], target))
            put += part.shape[0]
        for weight in (wq, wk, wv):
            target = weights.at[span, pl.ds(column, weight.shape[1])]
            here.append(copies.start(weight.at[span], target))
            column += weight.shape[1]
        waits.append(here)
    late = copies.start(trig.at[pl.ds(first, put)], angles)
    product = None
    for chunk, here in enumerate(waits):
        for copy in here:
            copy.wait()
        span = pl.ds(chunk * depth, depth)
        term = jnp.dot(rows[:, span], weights[span, :], preferred_element_type=jnp.float32)
        product = term if product is None else product + term
    late.wait()
    rotate_into(product, angles, q, kv)


def qkv(parts, weights, trig, first, chunks=6):
    total, width = sum(part.shape[0] for part in parts), parts[0].shape[1]
    columns = sum(weight.shape[1] for weight in weights)
    heads, bf16 = columns // HD - 2, jnp.bfloat16
    return call(
        functools.partial(qkv_kernel, len(parts), first, chunks),
        "qkv",
        14,
        [HBM] * (4 + len(parts)),
        [((heads, total, HD), bf16, VMEM), ((total, 2 * HD), bf16, VMEM)],
        [
            pltpu.VMEM((width, columns), bf16),
            pltpu.VMEM((total, width), bf16),
            pltpu.VMEM((total, 2 * HD), jnp.float32),
            pltpu.SemaphoreType.DMA((1 + (len(parts) + 3) * chunks,)),
        ],
        trig,
        *weights,
        *parts,
    )


class Step:
    def __init__(self, q, group, slots, same=None, merged=False):
        self.q, self.group, self.slots = q, group, slots
        self.same, self.merged = same, merged


class Chunk:
    def __init__(self, at, runs, share):
        self.at, self.runs, self.share = at, runs, share

    def places(self, core, axis, first, size):
        shape = (size, 1) if axis == 0 else (1, size)
        index = first + lax.broadcasted_iota(jnp.int32, shape, axis)
        result, begin = index, 0
        for which, offset, rows in self.runs:
            base = (core if which == 0 else 1 - core) * self.share + offset - begin
            inside = (index >= begin) & (index < begin + rows)
            result = jnp.where(inside, index + base, result)
            begin += rows
        return result


def attention_kernel(plan, q_chunks, k_chunks, group_parts, fresh, final, table, *refs):
    refs = list(refs)
    take = lambda n: [refs.pop(0) for _ in range(n)]
    count = len(q_chunks)
    qs = take(count)
    kv_parts = [take(n) for n in group_parts]
    take(2 * (count - len(fresh)))
    outs = take(len(final))
    states = [take(2) for _ in range(count)]
    kvs, staged = take(len(group_parts)), take(len(final))
    (semaphores,) = refs
    copies = Copies(semaphores)
    core = table[0]
    waits = {}
    for group, (parts, kv) in enumerate(zip(kv_parts, kvs)):
        each = kv.shape[0] // len(parts)
        waits[group] = [
            copies.start(part, kv.at[pl.ds(slot * each, each)])
            for slot, part in enumerate(parts)
        ]

    def ready(group):
        for copy in waits.pop(group, []):
            copy.wait()

    def attend(q, keys_values, begin, visible=None, bias=None):
        q_ref, (peak, acc) = qs[q], states[q]
        heads = q_ref.shape[0]
        keys = keys_values[:, :HD]
        values = keys_values[:, HD:].T
        values = jnp.concatenate([values, jnp.ones((ONES, keys.shape[0]), values.dtype)], axis=0)
        tiles, tile = acc.shape[0], acc.shape[2] // heads
        scores, tops, weights = [], [], []
        for at in range(tiles):
            q_tile = q_ref[:, at * tile : (at + 1) * tile, :].reshape(heads * tile, HD)
            score = lax.dot_general(
                keys, q_tile, (((1,), (1,)), ((), ())), preferred_element_type=jnp.float32
            )
            if visible is not None:
                seen = jnp.concatenate([visible(at * tile, tile)] * heads, axis=1)
                score = jnp.where(seen, score, HIDDEN)
            if bias is not None:
                score = score + bias
            scores.append(score)
        for at in range(tiles):
            top = jnp.max(scores[at], axis=0, keepdims=True)
            if not begin:
                top = jnp.maximum(peak[at, 0:1, :], top)
            tops.append(top)
            weights.append(jnp.exp2((scores[at] - top).astype(jnp.bfloat16)))
        for at in range(tiles):
            summed = jnp.dot(values, weights[at], preferred_element_type=jnp.float32)
            if not begin:
                summed = summed + acc[at] * jnp.exp2(peak[at, 0:1, :] - tops[at])
            acc[at] = summed
            peak[at] = jnp.broadcast_to(tops[at], peak.shape[1:])

    begun = set(range(count)) - set(fresh)
    for step in plan:
        q, group, kv = step.q, step.group, kvs[step.group]
        q_chunk, k_chunk = q_chunks[q], k_chunks[group]
        if step.same is not None:
            keys_at = k_chunk.places(core, 0, 0, kv.shape[1])
            visible = lambda first, tile: keys_at <= q_chunk.places(core, 1, first, tile)
            own = kv_parts[group][0]
            attend(q, own[step.same], q not in begun, visible=visible)
            begun.add(q)
        start = table[q_chunk.at]
        slots = step.slots
        if not slots:
            continue
        ready(group)
        if step.merged:
            shown = [table[k_chunk.at + slot] < start for slot in slots]

            @pl.when(functools.reduce(jnp.logical_or, shown))
            def _():
                rows = kv.shape[1]
                bias = [
                    jnp.where(see, 0.0, HIDDEN) * jnp.ones((rows, 1), jnp.float32)
                    for see in shown
                ]
                keys_values = kv[slots[0] : slots[-1] + 1].reshape(len(slots) * rows, 2 * HD)
                attend(q, keys_values, False, bias=jnp.concatenate(bias, axis=0))

        else:

            def one(slot, carry):
                @pl.when(table[k_chunk.at + slot] < start)
                def _():
                    attend(q, kv[slot], False)

                return carry

            lax.fori_loop(slots[0], slots[-1] + 1, one, 0)

    for group in list(waits):
        ready(group)
    stores = []
    for out, stage, order in zip(outs, staged, final):
        put = 0
        for q in order:
            acc, heads = states[q][1], qs[q].shape[0]
            tile = acc.shape[2] // heads
            for at in range(acc.shape[0]):
                rows = acc[at, :HD, :] / acc[at, HD : HD + 1, :]
                rows = rows.T.astype(jnp.bfloat16)
                for head in range(heads):
                    stage[put : put + tile, head * HD : (head + 1) * HD] = rows[
                        head * tile : (head + 1) * tile
                    ]
                put += tile
        stores.append(copies.start(stage, out))
    for copy in stores:
        copy.wait()


def attention(plan, table, qs, q_chunks, groups, k_chunks, state, final=()):
    fresh = [at for at, held in enumerate(state) if held is None]
    shapes = []
    for q in qs:
        heads, rows, _ = q.shape
        tile = min(rows, 128)
        shapes += [(rows // tile, deep, heads * tile) for deep in (8, HD + ONES)]
    width = qs[0].shape[0] * HD
    sums = [sum(qs[q].shape[1] for q in order) for order in final]
    outs = [((rows, width), jnp.bfloat16, HBM) for rows in sums]
    scratch = []
    for parts in groups:
        slots = sum(part.shape[0] for part in parts)
        scratch.append(pltpu.VMEM((slots,) + parts[0].shape[1:], jnp.bfloat16))
    scratch += [pltpu.VMEM((rows, width), jnp.bfloat16) for rows in sums]
    parts = [part for parts in groups for part in parts]
    sizes = [len(parts) for parts in groups]
    inputs, aliases = [table, *qs, *parts], {}
    for at, pair in enumerate(state):
        for half, array in enumerate(pair or ()):
            aliases[len(inputs)] = len(outs) + 2 * at + half
            inputs.append(array)
    results = call(
        functools.partial(attention_kernel, plan, q_chunks, k_chunks, sizes, fresh, final),
        "attention",
        10,
        [SMEM] + [VMEM] * (len(inputs) - 1),
        outs + [(shape, jnp.float32, VMEM) for shape in shapes],
        scratch + [pltpu.SemaphoreType.DMA((len(parts) + len(outs),))],
        *inputs,
        aliases=aliases,
    )
    if final:
        return results[: len(final)]
    return [tuple(results[2 * at : 2 * at + 2]) for at in range(len(qs))]


def cut_kernel(sizes, at, table, weights, *refs):
    outs, (held, semaphores) = refs[: len(sizes)], refs[len(sizes) :]
    copies = Copies(semaphores)
    half = sum(sizes)
    first = pl.multiple_of(table[at] * half, half)
    ins, put = [], 0
    for size in sizes:
        target = held.at[pl.ds(put, size)]
        ins.append((copies.start(weights.at[pl.ds(first + put, size)], target), target))
        put += size
    stores = []
    for (copy, piece), out in zip(ins, outs):
        copy.wait()
        stores.append(copies.start(piece, out))
    for copy in stores:
        copy.wait()


def cut(table, at, weights, sizes):
    depth, width = weights.shape
    return call(
        functools.partial(cut_kernel, sizes, at),
        "cut_weights",
        4,
        [SMEM, HBM],
        [((size, width), weights.dtype, HBM) for size in sizes],
        [
            pltpu.VMEM((depth // 2, width), weights.dtype),
            pltpu.SemaphoreType.DMA((2 * len(sizes),)),
        ],
        table,
        weights,
    )


def near_kernel(chunks, left_hbm, weights_hbm, out, left, weights, semaphores):
    copies = Copies(semaphores)
    step = out.shape[1] // chunks
    first = copies.start(left_hbm, left)
    lanes = [pl.ds(chunk * step, step) for chunk in range(chunks)]
    waits = [copies.start(weights_hbm.at[:, at], weights.at[:, at]) for at in lanes]
    first.wait()
    for at, copy in zip(lanes, waits):
        copy.wait()
        out[:, at] = jnp.dot(left[...], weights[:, at], preferred_element_type=jnp.float32)


def output_near(left, weights, chunks=6):
    (rows, columns), width = left.shape, weights.shape[1]
    return call(
        functools.partial(near_kernel, chunks),
        "output_near",
        8,
        [HBM] * 2,
        [((rows, width), jnp.float32, VMEM)],
        [
            pltpu.VMEM(left.shape, left.dtype),
            pltpu.VMEM(weights.shape, weights.dtype),
            pltpu.SemaphoreType.DMA((1 + chunks,)),
        ],
        left,
        weights,
    )[0]


def send_kernel(at, chunks, table, left_hbm, near, *refs):
    count = len(refs) - 5
    pieces, (out, weights, left, staged, semaphores) = refs[:count], refs[count:]
    copies = Copies(semaphores)
    depth, width = weights.shape
    step = width // chunks
    first = copies.start(left_hbm, left)
    waits, put = [], 0
    for index, piece in enumerate(pieces):
        half = table[at] if index < count // 2 else 1 - table[at]
        row = pl.multiple_of(half * (depth // 2) + put % (depth // 2), 16)
        waits.append(copies.start(piece, weights.at[pl.ds(row, piece.shape[0])]))
        put += piece.shape[0]
    for copy in waits:
        copy.wait()
    first.wait()
    half = left.shape[0] // 2
    stores = []
    for chunk in range(chunks):
        span = pl.ds(chunk * step, step)
        staged[:, span] = (
            near[half:, span]
            + jnp.dot(left[half:, :], weights[:, span], preferred_element_type=jnp.float32)
        ).astype(jnp.bfloat16)
        stores.append(copies.start(staged.at[:, span], out.at[:, span]))
    for copy in stores:
        copy.wait()


def output_send(table, at, left, near, pieces, chunks=6):
    (rows, width), columns = near.shape, left.shape[1]
    half, bf16 = (rows // 2, width), jnp.bfloat16
    return call(
        functools.partial(send_kernel, at, chunks),
        "output_send",
        8,
        [SMEM, HBM, VMEM] + [HBM] * len(pieces),
        [(half, bf16, HBM), ((columns, width), bf16, VMEM)],
        [
            pltpu.VMEM(left.shape, bf16),
            pltpu.VMEM(half, bf16),
            pltpu.SemaphoreType.DMA((1 + len(pieces) + chunks,)),
        ],
        table,
        left,
        near,
        *pieces,
    )


def keep_kernel(chunks, left_hbm, hidden, near, weights, out, held, left, semaphores):
    copies = Copies(semaphores)
    first, late = copies.start(left_hbm, left), copies.start(hidden, held)
    first.wait()
    half, step = left.shape[0] // 2, out.shape[1] // chunks
    for chunk in range(chunks):
        span = pl.ds(chunk * step, step)
        out[:, span] = near[:half, span] + jnp.dot(
            left[:half, :], weights[:, span], preferred_element_type=jnp.float32
        )
    late.wait()


def output_keep(left, hidden, near, weights, chunks=6):
    rows, width = near.shape
    return call(
        functools.partial(keep_kernel, chunks),
        "output_keep",
        4,
        [HBM, HBM, VMEM, VMEM],
        [((rows // 2, width), jnp.float32, VMEM), (hidden.shape, hidden.dtype, VMEM)],
        [pltpu.VMEM(left.shape, jnp.bfloat16), pltpu.SemaphoreType.DMA((2,))],
        left,
        hidden,
        near,
        weights,
    )


def final_kernel(chunks, received, hidden, kept, gain, out, other, staged, gains, semaphores):
    copies = Copies(semaphores)
    width = hidden.shape[1]
    step = width // chunks
    lanes = [pl.ds(chunk * step, step) for chunk in range(chunks)]
    waits = [copies.start(received.at[:, span], other.at[:, span]) for span in lanes]
    late = copies.start(gain, gains)
    square = jnp.zeros((hidden.shape[0], 128), jnp.float32)
    for span, copy in zip(lanes, waits):
        copy.wait()
        total = kept[:, span] + other[:, span].astype(jnp.float32)
        for lane in range(0, step, 128):
            part = total[:, lane : lane + 128]
            square = square + part * part
    mean = jnp.sum(square, axis=1, keepdims=True) / width
    scale = lax.rsqrt(mean + EPS)
    late.wait()
    row = gains[...].reshape(1, width)
    stores = []
    for chunk, span in enumerate(lanes):
        total = kept[:, span] + other[:, span].astype(jnp.float32)
        normed = total * scale * row[:, chunk * step : (chunk + 1) * step]
        staged[:, span] = (hidden[:, span].astype(jnp.float32) + normed).astype(jnp.bfloat16)
        stores.append(copies.start(staged.at[:, span], out.at[:, span]))
    for store in stores:
        store.wait()


def output(received, hidden, kept, gain, chunks=6):
    rows, width = hidden.shape
    bf16 = jnp.bfloat16
    return call(
        functools.partial(final_kernel, chunks),
        "output_norm",
        8,
        [HBM, VMEM, VMEM, HBM],
        [((rows, width), bf16, HBM)],
        [
            pltpu.VMEM((rows, width), bf16),
            pltpu.VMEM((rows, width), bf16),
            pltpu.VMEM((width,), jnp.float32),
            pltpu.SemaphoreType.DMA((1 + 2 * chunks,)),
        ],
        received,
        hidden,
        kept,
        gain,
    )[0]


def rotary_table(positions):
    half = HD // 2
    frequency = jnp.power(
        jnp.float32(10000.0), -jnp.arange(half, dtype=jnp.float32) * (2.0 / HD)
    )
    angles = positions.astype(jnp.float32)[:, None] * frequency[None, :]
    cos, sin = jnp.cos(angles), jnp.sin(angles)
    return jnp.concatenate([cos, cos, -sin, sin], axis=1)


def lookup(block_of, index):
    ids = jnp.arange(block_of.shape[0], dtype=jnp.int32)
    return jnp.sum(jnp.where(index[..., None] == ids, block_of, 0), axis=-1)


def flipped(array, axis, bit):
    size = lax.axis_size(axis)
    return lax.ppermute(array, axis, [(i, i ^ bit) for i in range(size)])


def along_line(array):
    size = lax.axis_size("seq")
    parts = [array[None]]
    for by in range(1, size):
        part = lax.ppermute(array, "seq", [(i, (i + by) % size) for i in range(size)])
        parts.append(Came(part[None]))
    return parts


def came(parts):
    return [part.array for part in parts if isinstance(part, Came)]


def after(array, *others):
    return lax.optimization_barrier((array, *others))[0]


def two_chips(hidden, pre_gain, post_gain, wq, wk, wv, w_out, block_of):
    rows = hidden.shape[0]
    block_rows = 2 * rows
    lines, tp = lax.axis_size("seq"), lax.axis_index("tp")
    seq, group = lax.axis_index("seq"), lax.axis_index("groups")
    chip, core = tp // 2, tp % 2

    line = (seq - jnp.arange(lines, dtype=jnp.int32)) % lines
    near_starts = lookup(block_of, 2 * line + chip) * block_rows
    far_starts = lookup(block_of, 2 * line + 1 - chip) * block_rows
    table = jnp.concatenate([jnp.stack([core, group]).astype(jnp.int32), near_starts, far_starts])
    group_at, near_at, far_at = 1, 2, 2 + lines
    run = jnp.arange(rows, dtype=jnp.int32)
    place = jnp.concatenate([core * rows + run, (1 - core) * rows + run])
    trig = rotary_table(jnp.concatenate([near_starts[0] + place, far_starts[0] + place]))
    runs = [(0, 0, rows), (1, 0, rows)]
    near_chunk, far_chunk = Chunk(near_at, runs, rows), Chunk(far_at, runs, rows)
    others, everyone = list(range(1, lines)), list(range(lines))

    own = norm(hidden, pre_gain, [rows])[0]
    away = flipped(own, "tp", 2)
    partner = flipped(own, "tp", 1)

    weights = (wq, wk, wv)
    q_near, kv_near = qkv([own, Came(partner)], weights, trig, 0)
    near = along_line(kv_near)
    half = w_out.shape[0] // 2
    w_cut = cut(table, group_at, after(w_out, kv_near), [half // 4, half * 3 // 8, half * 3 // 8])
    q_near = after(q_near, *w_cut)
    (near_state,) = attention(
        [Step(0, 0, others, same=0)], table, [q_near], [near_chunk], [near], [near_chunk], [None]
    )

    away = after(away, *near_state)
    q_far, kv_far = qkv([Came(away), Came(flipped(away, "tp", 1))], weights, trig, block_rows)
    far = along_line(kv_far)

    fetched = lambda piece, *others: flipped(after(piece, *others), "tp", 2)
    swap = lambda array: flipped(array, "groups", 1)
    w_far = [fetched(piece, away) for piece in w_cut[:2]]
    w_far[0] = after(w_far[0], kv_far)
    near_state, far_state = attention(
        [Step(1, 1, [], same=0), Step(1, 0, everyone), Step(0, 1, [0])],
        table,
        [q_near, q_far],
        [near_chunk, far_chunk],
        [near, far[:1]],
        [near_chunk, far_chunk],
        [near_state, None],
    )
    w_other = [swap(w_far[0])]
    w_far[1] = after(w_far[1], *far_state, *came(far)[:2], w_other[0])
    w_far.append(fetched(w_cut[2], w_far[1]))
    attended, gone = attention(
        [Step(1, 0, others), Step(0, 0, others)],
        table,
        [q_near, q_far],
        [near_chunk, far_chunk],
        [far],
        [far_chunk],
        [near_state, far_state],
        final=[[0], [1]],
    )
    gone = flipped(gone, "tp", 2)
    near_sum = output_near(attended, w_out)
    w_far[2] = after(w_far[2], attended)
    w_other += [swap(piece) for piece in w_far[1:]]
    pieces = [Came(piece) for piece in w_far + w_other]
    sent, w_laid = output_send(table, group_at, Came(gone), near_sum, pieces)
    received = flipped(sent, "tp", 1)
    kept, held = output_keep(Came(gone), hidden, near_sum, w_laid)
    return output(Came(received), held, kept, post_gain)


def any_count(hidden, pre_gain, post_gain, wq, wk, wv, w_out, block_of):
    rows = hidden.shape[0]
    lines = lax.axis_size("seq")
    line = (lax.axis_index("seq") - jnp.arange(lines, dtype=jnp.int32)) % lines
    block = (2 * line[:, None] + jnp.arange(2, dtype=jnp.int32)).reshape(-1)
    block_rows = rows * lax.axis_size("tp") // 2
    starts = lookup(block_of, block) * block_rows
    table = jnp.concatenate([jnp.zeros(2, jnp.int32), starts])
    normed = norm(hidden, pre_gain, [rows], 1)[0]
    normed = lax.all_gather(normed, "tp", axis=0, tiled=True)
    place = jnp.arange(block_rows, dtype=jnp.int32)
    trig = rotary_table((starts[:2, None] + place).reshape(-1))
    qs, keys_values, weights = [], [], (wq, wk, wv)
    for at in range(2):
        first = at * block_rows
        q, kv = qkv([normed[first : first + block_rows]], weights, trig, first)
        qs.append(q)
        keys_values.append(kv)
    kv = lax.all_gather(jnp.stack(keys_values), "seq")[line].reshape(-1, block_rows, 2 * HD)
    rest = list(range(2, 2 * lines))
    runs = [(0, 0, block_rows)]
    attended = attention(
        [Step(0, 0, [1], same=0), Step(1, 0, [0], same=1), Step(0, 0, rest), Step(1, 0, rest)],
        table,
        qs,
        [Chunk(2, runs, 0), Chunk(3, runs, 0)],
        [[kv]],
        [Chunk(2, runs, 0)],
        [None, None],
        final=[[0, 1]],
    )[0]
    partial = jnp.dot(attended, w_out, preferred_element_type=jnp.float32)
    summed = lax.psum_scatter(
        partial.astype(jnp.bfloat16), "tp", scatter_dimension=0, tiled=True
    ).astype(jnp.float32)
    mean = jnp.mean(summed * summed, axis=-1, keepdims=True)
    projected = summed * lax.rsqrt(mean + EPS) * post_gain
    return (hidden.astype(jnp.float32) + projected).astype(jnp.bfloat16)


def solution(mesh):
    return jax.shard_map(
        two_chips if mesh.shape["tp"] == 4 else any_count,
        mesh=mesh,
        in_specs=(
            P(("groups", "seq", "tp"), None),
            P(),
            P(),
            P(None, "tp"),
            P(None, "tp"),
            P(None, "tp"),
            P("tp", None),
            P(),
        ),
        out_specs=P(("groups", "seq", "tp"), None),
        check_vma=False,
    )
```

profile of v0, /device:TPU:0, one launch (start us, length us, event | category | flops | bytes accessed | tf_op | source)
XLA Modules:
  0.0 107.5 jit_solution(17592232309511996020)
XLA Ops:
  0.0 3.1 %norm_rows.1.refs_0_ = bf16[192,4608]{1,0:T(8,128)(2,1)} custom-call(bf16[192,4608]{1,0:T(8,128)(2,1)} %hidden.3, f32[4608]{0:T(1024)} %gain.2), custom_call_target="tpu_custom_call" | custom-call | flops 1 | bytes 1 | tf_op jit(solution)/shard_map/norm_rows/pallas_call | solution.py:38
  3.7 2.6 %collective-permute-start.1 = (bf16[192,4608]{1,0:T(8,128)(2,1)}, bf16[192,4608]{1,0:T(8,128)(2,1)S(1)}, u32[]{:S(2)}, u32[]{:S(2)}) collective-permute-start(bf16[192,4608]{1,0:T(8,128)(2,1)} %norm_rows.1.refs_0_), channel_id=1, source_target_pairs={{0,8},{4,12},{8,0},{12,4},{1,9},{5,13},{9,1},{13,5},{2,10},{6,14},... | collective-permute-start | bytes 5308424 | tf_op jit(solution)/shard_map/ppermute | solution.py:563
  6.7 1.4 %multiply_cosine_fusion = (f32[768,64]{1,0:T(8,128)S(1)}, f32[768,64]{1,0:T(8,128)S(1)}, f32[768,64]{1,0:T(8,128)S(1)}) fusion(f32[768]{0:T(1024)S(1)} %add_convert_fusion, f32[64]{0:T(128)S(1)} %multiply_power_fusion), kind=kLoop, calls=%fused_computation.2 | loop fusion | flops 98304 | bytes 593152 | tf_op jit(solution)/shard_map/cos | solution.py:552
  9.4 4.4 %qkv.2 = (bf16[2,384,128]{2,1,0:T(8,128)(2,1)S(1)}, bf16[384,256]{1,0:T(8,128)(2,1)S(1)}) custom-call(f32[768,256]{1,0:T(8,128)} %pad_maximum_fusion.trig, bf16[4608,256]{1,0:T(8,128)(2,1)} %wq.3, bf16[4608,128]{1,0:T(8,128)(2,1)} %wk.3, bf16[4608,128]{1,0:T(8,128)(2,1)} %wv.3, bf16[192,4608]{1,0:T(8,128)(2,1)} %norm_rows.1.refs_0_, ...), custom_call_target="tpu_custom_call" | custom-call | flops 1 | bytes 1 | tf_op jit(solution)/shard_map/qkv/pallas_call | solution.py:38
  13.8 1.6 %collective-permute-start.2 = (bf16[384,256]{1,0:T(8,128)(2,1)S(1)}, bf16[384,256]{1,0:T(8,128)(2,1)S(1)}, u32[]{:S(2)}, u32[]{:S(2)}) collective-permute-start(bf16[384,256]{1,0:T(8,128)(2,1)S(1)} %get-tuple-element.34), channel_id=1, source_target_pairs={{0,1},{1,2},{2,3},{3,0},{4,5},{5,6},{6,7},{7,4},{8,9},{9,10},{10,1... | collective-permute-start | bytes 589832 | tf_op jit(solution)/shard_map/ppermute | solution.py:570
  15.4 2.6 %collective-permute-start.3 = (bf16[384,256]{1,0:T(8,128)(2,1)S(1)}, bf16[384,256]{1,0:T(8,128)(2,1)S(1)}, u32[]{:S(2)}, u32[]{:S(2)}) collective-permute-start(bf16[384,256]{1,0:T(8,128)(2,1)S(1)} %get-tuple-element.34), channel_id=1, source_target_pairs={{0,2},{1,3},{2,0},{3,1},{4,6},{5,7},{6,4},{7,5},{8,10},{9,11},{10,... | collective-permute-start | bytes 589832 | tf_op jit(solution)/shard_map/ppermute | solution.py:570
  18.0 1.3 %collective-permute-start.4 = (bf16[384,256]{1,0:T(8,128)(2,1)S(1)}, bf16[384,256]{1,0:T(8,128)(2,1)S(1)}, u32[]{:S(2)}, u32[]{:S(2)}) collective-permute-start(bf16[384,256]{1,0:T(8,128)(2,1)S(1)} %get-tuple-element.34), channel_id=1, source_target_pairs={{0,3},{1,0},{2,1},{3,2},{4,7},{5,4},{6,5},{7,6},{8,11},{9,8},{10,9... | collective-permute-start | bytes 589832 | tf_op jit(solution)/shard_map/ppermute | solution.py:570
  19.5 2.6 %cut_weights.1 = (bf16[32,4608]{1,0:T(8,128)(2,1)}, bf16[48,4608]{1,0:T(8,128)(2,1)}, bf16[48,4608]{1,0:T(8,128)(2,1)}) custom-call(s32[10]{0:T(128)S(1)} %pad_add_fusion.1.table, bf16[256,4608]{1,0:T(8,128)(2,1)} %weights_hbm.1), custom_call_target="tpu_custom_call" | custom-call | flops 1 | bytes 1 | tf_op jit(solution)/shard_map/cut_weights/pallas_call | solution.py:38
  22.1 1.5 %collective-permute-done.2 = bf16[384,256]{1,0:T(8,128)(2,1)S(1)} collective-permute-done((bf16[384,256]{1,0:T(8,128)(2,1)S(1)}, bf16[384,256]{1,0:T(8,128)(2,1)S(1)}, u32[]{:S(2)}, u32[]{:S(2)}) %collective-permute-start.2) | collective-permute-done | bytes 196640 | tf_op jit(solution)/shard_map/ppermute | solution.py:570
  23.5 7.7 %collective-permute-done.3 = bf16[384,256]{1,0:T(8,128)(2,1)S(1)} collective-permute-done((bf16[384,256]{1,0:T(8,128)(2,1)S(1)}, bf16[384,256]{1,0:T(8,128)(2,1)S(1)}, u32[]{:S(2)}, u32[]{:S(2)}) %collective-permute-start.3) | collective-permute-done | bytes 196640 | tf_op jit(solution)/shard_map/ppermute | solution.py:570
  31.3 3.0 %attention.3 = (f32[3,8,256]{2,1,0:T(8,128)S(1)}, f32[3,144,256]{2,1,0:T(8,128)S(1)}) custom-call(s32[10]{0:T(128)S(1)} %pad_add_fusion.1.table, bf16[2,384,128]{2,1,0:T(8,128)(2,1)S(1)} %get-tuple-element.39.refs_0_, bf16[1,384,256]{2,1,0:T(8,128)(2,1)S(1)} %bitcast.14, bf16[1,384,256]{2,1,0:T(8,128)(2,1)S(1)} %bitcast.16, ...), custom_call_target="tpu_custom_call" | custom-call | flops 1 | bytes 1 | tf_op jit(solution)/shard_map/attention/pallas_call | solution.py:38
  34.2 11.4 %collective-permute-done.1.refs_0_ = bf16[192,4608]{1,0:T(8,128)(2,1)S(1)} collective-permute-done((bf16[192,4608]{1,0:T(8,128)(2,1)}, bf16[192,4608]{1,0:T(8,128)(2,1)S(1)}, u32[]{:S(2)}, u32[]{:S(2)}) %collective-permute-start.1) | collective-permute-done | bytes 1769504 | tf_op jit(solution)/shard_map/ppermute | solution.py:563
  45.7 1.8 %collective-permute-start.10 = (bf16[32,4608]{1,0:T(8,128)(2,1)}, bf16[32,4608]{1,0:T(8,128)(2,1)S(1)}, u32[]{:S(2)}, u32[]{:S(2)}) collective-permute-start(bf16[32,4608]{1,0:T(8,128)(2,1)} %get-tuple-element.51), channel_id=1, source_target_pairs={{0,8},{4,12},{8,0},{12,4},{1,9},{5,13},{9,1},{13,5},{2,10},{6,14},... | collective-permute-start | bytes 884744 | tf_op jit(solution)/shard_map/ppermute | solution.py:563
  47.7 1.7 %collective-permute-done.5.refs_1_ = bf16[192,4608]{1,0:T(8,128)(2,1)S(1)} collective-permute-done((bf16[192,4608]{1,0:T(8,128)(2,1)S(1)}, bf16[192,4608]{1,0:T(8,128)(2,1)S(1)}, u32[]{:S(2)}, u32[]{:S(2)}) %collective-permute-start.5) | collective-permute-done | bytes 1769504 | tf_op jit(solution)/shard_map/ppermute | solution.py:563
  49.4 4.1 %qkv.3 = (bf16[2,384,128]{2,1,0:T(8,128)(2,1)S(1)}, bf16[384,256]{1,0:T(8,128)(2,1)S(1)}) custom-call(f32[768,256]{1,0:T(8,128)} %pad_maximum_fusion.trig, bf16[4608,256]{1,0:T(8,128)(2,1)} %wq.3, bf16[4608,128]{1,0:T(8,128)(2,1)} %wk.3, bf16[4608,128]{1,0:T(8,128)(2,1)} %wv.3, bf16[192,4608]{1,0:T(8,128)(2,1)S(1)} %collective-permute-done.1.refs_0_, ...), custom_call_target="tpu_custom_call" | custom-call | flops 1 | bytes 1 | tf_op jit(solution)/shard_map/qkv/pallas_call | solution.py:38
  53.5 2.2 %collective-permute-done.10.refs_0_ = bf16[32,4608]{1,0:T(8,128)(2,1)S(1)} collective-permute-done((bf16[32,4608]{1,0:T(8,128)(2,1)}, bf16[32,4608]{1,0:T(8,128)(2,1)S(1)}, u32[]{:S(2)}, u32[]{:S(2)}) %collective-permute-start.10) | collective-permute-done | bytes 294944 | tf_op jit(solution)/shard_map/ppermute | solution.py:563
  55.7 1.7 %collective-permute-start.12 = (bf16[32,4608]{1,0:T(8,128)(2,1)S(1)}, bf16[32,4608]{1,0:T(8,128)(2,1)S(1)}, u32[]{:S(2)}, u32[]{:S(2)}) collective-permute-start(bf16[32,4608]{1,0:T(8,128)(2,1)S(1)} %collective-permute-done.10.refs_0_), channel_id=1, source_target_pairs={{0,16},{16,0},{1,17},{17,1},{2,18},{18,2},{3,19},{19,3},{4,20},{20... | collective-permute-start | bytes 884744 | tf_op jit(solution)/shard_map/ppermute | solution.py:563
  57.4 1.6 %collective-permute-start.6 = (bf16[384,256]{1,0:T(8,128)(2,1)S(1)}, bf16[384,256]{1,0:T(8,128)(2,1)S(1)}, u32[]{:S(2)}, u32[]{:S(2)}) collective-permute-start(bf16[384,256]{1,0:T(8,128)(2,1)S(1)} %get-tuple-element.44), channel_id=1, source_target_pairs={{0,1},{1,2},{2,3},{3,0},{4,5},{5,6},{6,7},{7,4},{8,9},{9,10},{10,1... | collective-permute-start | bytes 589832 | tf_op jit(solution)/shard_map/ppermute | solution.py:570
  59.0 2.6 %collective-permute-start.7 = (bf16[384,256]{1,0:T(8,128)(2,1)S(1)}, bf16[384,256]{1,0:T(8,128)(2,1)S(1)}, u32[]{:S(2)}, u32[]{:S(2)}) collective-permute-start(bf16[384,256]{1,0:T(8,128)(2,1)S(1)} %get-tuple-element.44), channel_id=1, source_target_pairs={{0,2},{1,3},{2,0},{3,1},{4,6},{5,7},{6,4},{7,5},{8,10},{9,11},{10,... | collective-permute-start | bytes 589832 | tf_op jit(solution)/shard_map/ppermute | solution.py:570
  61.6 4.6 %attention.4 = (f32[3,8,256]{2,1,0:T(8,128)S(1)}, f32[3,144,256]{2,1,0:T(8,128)S(1)}, f32[3,8,256]{2,1,0:T(8,128)S(1)}, f32[3,144,256]{2,1,0:T(8,128)S(1)}) custom-call(s32[10]{0:T(128)S(1)} %pad_add_fusion.1.table, bf16[2,384,128]{2,1,0:T(8,128)(2,1)S(1)} %get-tuple-element.39.refs_0_, ...), custom_call_target="tpu_custom_call", output_to_operand_aliasing={{0}: (8, {}), {1}: (9, {})} | custom-call | flops 1 | bytes 1 | tf_op jit(solution)/shard_map/attention/pallas_call | solution.py:38
  67.1 6.4 %collective-permute-done.7 = bf16[384,256]{1,0:T(8,128)(2,1)S(1)} collective-permute-done((bf16[384,256]{1,0:T(8,128)(2,1)S(1)}, bf16[384,256]{1,0:T(8,128)(2,1)S(1)}, u32[]{:S(2)}, u32[]{:S(2)}) %collective-permute-start.7) | collective-permute-done | bytes 196640 | tf_op jit(solution)/shard_map/ppermute | solution.py:570
  73.6 1.5 %collective-permute-start.13 = (bf16[48,4608]{1,0:T(8,128)(2,1)S(1)}, bf16[48,4608]{1,0:T(8,128)(2,1)S(1)}, u32[]{:S(2)}, u32[]{:S(2)}) collective-permute-start(bf16[48,4608]{1,0:T(8,128)(2,1)S(1)} %copy-done.1), channel_id=1, source_target_pairs={{0,8},{4,12},{8,0},{12,4},{1,9},{5,13},{9,1},{13,5},{2,10},{6,14},... | collective-permute-start | bytes 1327112 | tf_op jit(solution)/shard_map/ppermute | solution.py:563
  75.1 1.6 %collective-permute-start.8 = (bf16[384,256]{1,0:T(8,128)(2,1)S(1)}, bf16[384,256]{1,0:T(8,128)(2,1)S(1)}, u32[]{:S(2)}, u32[]{:S(2)}) collective-permute-start(bf16[384,256]{1,0:T(8,128)(2,1)S(1)} %get-tuple-element.44), channel_id=1, source_target_pairs={{0,3},{1,0},{2,1},{3,2},{4,7},{5,4},{6,5},{7,6},{8,11},{9,8},{10,9... | collective-permute-start | bytes 589832 | tf_op jit(solution)/shard_map/ppermute | solution.py:570
  77.3 4.4 %collective-permute-done.8 = bf16[384,256]{1,0:T(8,128)(2,1)S(1)} collective-permute-done((bf16[384,256]{1,0:T(8,128)(2,1)S(1)}, bf16[384,256]{1,0:T(8,128)(2,1)S(1)}, u32[]{:S(2)}, u32[]{:S(2)}) %collective-permute-start.8) | collective-permute-done | bytes 196640 | tf_op jit(solution)/shard_map/ppermute | solution.py:570
  81.6 4.6 %attention.5 = (bf16[384,256]{1,0:T(8,128)(2,1)}, bf16[384,256]{1,0:T(8,128)(2,1)}, f32[3,8,256]{2,1,0:T(8,128)S(1)}, f32[3,144,256]{2,1,0:T(8,128)S(1)}, f32[3,...) custom-call(s32[10]{0:T(128)S(1)} %pad_add_fusion.1.table, ...), custom_call_target="tpu_custom_call", output_to_operand_aliasing={{2}: (7, {}), {3}: (8, {}), {4}: (9, {}), {5}: (10, {})} | custom-call | flops 1 | bytes 1 | tf_op jit(solution)/shard_map/attention/pallas_call | solution.py:38
  87.7 3.4 %output_near.1.near = f32[384,4608]{1,0:T(8,128)S(1)} custom-call(bf16[384,256]{1,0:T(8,128)(2,1)} %get-tuple-element.50.left_hbm, bf16[256,4608]{1,0:T(8,128)(2,1)} %weights_hbm.1), custom_call_target="tpu_custom_call" | custom-call | flops 1 | bytes 1 | tf_op jit(solution)/shard_map/output_near/pallas_call | solution.py:38
  91.1 1.7 %collective-permute-done.9.left_hbm = bf16[384,256]{1,0:T(8,128)(2,1)S(1)} collective-permute-done((bf16[384,256]{1,0:T(8,128)(2,1)}, bf16[384,256]{1,0:T(8,128)(2,1)S(1)}, u32[]{:S(2)}, u32[]{:S(2)}) %collective-permute-start.9) | collective-permute-done | bytes 196640 | tf_op jit(solution)/shard_map/ppermute | solution.py:563
  92.7 4.5 %collective-permute-done.15.refs_5_ = bf16[48,4608]{1,0:T(8,128)(2,1)S(1)} collective-permute-done((bf16[48,4608]{1,0:T(8,128)(2,1)S(1)}, bf16[48,4608]{1,0:T(8,128)(2,1)S(1)}, u32[]{:S(2)}, u32[]{:S(2)}) %collective-permute-start.15) | collective-permute-done | bytes 442400 | tf_op jit(solution)/shard_map/ppermute | solution.py:563
  97.2 3.5 %output_send.1 = (bf16[192,4608]{1,0:T(8,128)(2,1)}, bf16[256,4608]{1,0:T(8,128)(2,1)S(1)}) custom-call(s32[10]{0:T(128)S(1)} %pad_add_fusion.1.table, bf16[384,256]{1,0:T(8,128)(2,1)S(1)} %collective-permute-done.9.left_hbm, f32[384,4608]{1,0:T(8,128)S(1)} %output_near.1.near, bf16[32,4608]{1,0:T(8,128)(2,1)S(1)} %collective-permute-done.10.refs_0_, ...), custom_call_target="tpu_custom_call" | custom-call | flops 1 | bytes 1 | tf_op jit(solution)/shard_map/output_send/pallas_call | solution.py:38
  100.9 1.7 %output_keep.1 = (f32[192,4608]{1,0:T(8,128)S(1)}, bf16[192,4608]{1,0:T(8,128)(2,1)S(1)}) custom-call(bf16[384,256]{1,0:T(8,128)(2,1)S(1)} %collective-permute-done.9.left_hbm, bf16[192,4608]{1,0:T(8,128)(2,1)} %hidden.3, f32[384,4608]{1,0:T(8,128)S(1)} %output_near.1.near, bf16[256,4608]{1,0:T(8,128)(2,1)S(1)} %get-tuple-element.58.weights), custom_call_target="tpu_custom_call" | custom-call | flops 1 | bytes 1 | tf_op jit(solution)/shard_map/output_keep/pallas_call | solution.py:38
  102.6 2.1 %collective-permute-done.16.received = bf16[192,4608]{1,0:T(8,128)(2,1)S(1)} collective-permute-done((bf16[192,4608]{1,0:T(8,128)(2,1)}, bf16[192,4608]{1,0:T(8,128)(2,1)S(1)}, u32[]{:S(2)}, u32[]{:S(2)}) %collective-permute-start.16) | collective-permute-done | bytes 1769504 | tf_op jit(solution)/shard_map/ppermute | solution.py:563
  104.8 2.6 %output_norm.1 = bf16[192,4608]{1,0:T(8,128)(2,1)} custom-call(bf16[192,4608]{1,0:T(8,128)(2,1)S(1)} %collective-permute-done.16.received, bf16[192,4608]{1,0:T(8,128)(2,1)S(1)} %get-tuple-element.59.hidden, f32[192,4608]{1,0:T(8,128)S(1)} %get-tuple-element.60.kept, f32[4608]{0:T(1024)} %gain.3), custom_call_target="tpu_custom_call" | custom-call | flops 1 | bytes 1 | tf_op jit(solution)/shard_map/output_norm/pallas_call | solution.py:38
  (28 shorter events, 5.5 us)
Async XLA Ops:
  0.0 6.3 %copy-start = (s32[8]{0:T(128)S(1)}, s32[8]{0:T(128)}, u32[]{:S(2)}) copy-start(s32[8]{0:T(128)} %param.15) | copy-start | bytes 100
  3.1 6.2 %collective-permute-start = (bf16[192,4608]{1,0:T(8,128)(2,1)}, bf16[192,4608]{1,0:T(8,128)(2,1)}, u32[]{:S(2)}, u32[]{:S(2)}) collective-permute-start(bf16[192,4608]{1,0:T(8,128)(2,1)} %norm_rows.1.refs_0_), channel_id=1, source_target_pairs={{0,4},{4,0},{8,12},{12,8},{1,5},{5,1},{9,13},{13,9},{2,6},{6,2},{1... | collective-permute-start | bytes 5308424 | tf_op jit(solution)/shard_map/ppermute | solution.py:563
  3.7 42.0 %collective-permute-start.1 = (bf16[192,4608]{1,0:T(8,128)(2,1)}, bf16[192,4608]{1,0:T(8,128)(2,1)S(1)}, u32[]{:S(2)}, u32[]{:S(2)}) collective-permute-start(bf16[192,4608]{1,0:T(8,128)(2,1)} %norm_rows.1.refs_0_), channel_id=1, source_target_pairs={{0,8},{4,12},{8,0},{12,4},{1,9},{5,13},{9,1},{13,5},{2,10},{6,14},... | collective-permute-start | bytes 5308424 | tf_op jit(solution)/shard_map/ppermute | solution.py:563
  13.8 9.7 %collective-permute-start.2 = (bf16[384,256]{1,0:T(8,128)(2,1)S(1)}, bf16[384,256]{1,0:T(8,128)(2,1)S(1)}, u32[]{:S(2)}, u32[]{:S(2)}) collective-permute-start(bf16[384,256]{1,0:T(8,128)(2,1)S(1)} %get-tuple-element.34), channel_id=1, source_target_pairs={{0,1},{1,2},{2,3},{3,0},{4,5},{5,6},{6,7},{7,4},{8,9},{9,10},{10,1... | collective-permute-start | bytes 589832 | tf_op jit(solution)/shard_map/ppermute | solution.py:570
  15.4 15.8 %collective-permute-start.3 = (bf16[384,256]{1,0:T(8,128)(2,1)S(1)}, bf16[384,256]{1,0:T(8,128)(2,1)S(1)}, u32[]{:S(2)}, u32[]{:S(2)}) collective-permute-start(bf16[384,256]{1,0:T(8,128)(2,1)S(1)} %get-tuple-element.34), channel_id=1, source_target_pairs={{0,2},{1,3},{2,0},{3,1},{4,6},{5,7},{6,4},{7,5},{8,10},{9,11},{10,... | collective-permute-start | bytes 589832 | tf_op jit(solution)/shard_map/ppermute | solution.py:570
  18.0 13.2 %collective-permute-start.4 = (bf16[384,256]{1,0:T(8,128)(2,1)S(1)}, bf16[384,256]{1,0:T(8,128)(2,1)S(1)}, u32[]{:S(2)}, u32[]{:S(2)}) collective-permute-start(bf16[384,256]{1,0:T(8,128)(2,1)S(1)} %get-tuple-element.34), channel_id=1, source_target_pairs={{0,3},{1,0},{2,1},{3,2},{4,7},{5,4},{6,5},{7,6},{8,11},{9,8},{10,9... | collective-permute-start | bytes 589832 | tf_op jit(solution)/shard_map/ppermute | solution.py:570
  45.7 3.7 %collective-permute-start.5 = (bf16[192,4608]{1,0:T(8,128)(2,1)S(1)}, bf16[192,4608]{1,0:T(8,128)(2,1)S(1)}, u32[]{:S(2)}, u32[]{:S(2)}) collective-permute-start(bf16[192,4608]{1,0:T(8,128)(2,1)S(1)} %collective-permute-done.1.refs_0_), channel_id=1, source_target_pairs={{0,4},{4,0},{8,12},{12,8},{1,5},{5,1},{9,13},{13,9},{2,6},{6,2},{1... | collective-permute-start | bytes 5308424 | tf_op jit(solution)/shard_map/ppermute | solution.py:563
  45.7 10.0 %collective-permute-start.10 = (bf16[32,4608]{1,0:T(8,128)(2,1)}, bf16[32,4608]{1,0:T(8,128)(2,1)S(1)}, u32[]{:S(2)}, u32[]{:S(2)}) collective-permute-start(bf16[32,4608]{1,0:T(8,128)(2,1)} %get-tuple-element.51), channel_id=1, source_target_pairs={{0,8},{4,12},{8,0},{12,4},{1,9},{5,13},{9,1},{13,5},{2,10},{6,14},... | collective-permute-start | bytes 884744 | tf_op jit(solution)/shard_map/ppermute | solution.py:563
  47.4 18.8 %collective-permute-start.11 = (bf16[48,4608]{1,0:T(8,128)(2,1)}, bf16[48,4608]{1,0:T(8,128)(2,1)S(1)}, u32[]{:S(2)}, u32[]{:S(2)}) collective-permute-start(bf16[48,4608]{1,0:T(8,128)(2,1)} %get-tuple-element.53), channel_id=1, source_target_pairs={{0,8},{4,12},{8,0},{12,4},{1,9},{5,13},{9,1},{13,5},{2,10},{6,14},... | collective-permute-start | bytes 1327112 | tf_op jit(solution)/shard_map/ppermute | solution.py:563
  53.5 20.1 %copy-start.1 = (bf16[48,4608]{1,0:T(8,128)(2,1)S(1)}, bf16[48,4608]{1,0:T(8,128)(2,1)}, u32[]{:S(2)}) copy-start(bf16[48,4608]{1,0:T(8,128)(2,1)} %get-tuple-element.55) | copy-start | bytes 1327108
  55.7 17.9 %collective-permute-start.12 = (bf16[32,4608]{1,0:T(8,128)(2,1)S(1)}, bf16[32,4608]{1,0:T(8,128)(2,1)S(1)}, u32[]{:S(2)}, u32[]{:S(2)}) collective-permute-start(bf16[32,4608]{1,0:T(8,128)(2,1)S(1)} %collective-permute-done.10.refs_0_), channel_id=1, source_target_pairs={{0,16},{16,0},{1,17},{17,1},{2,18},{18,2},{3,19},{19,3},{4,20},{20... | collective-permute-start | bytes 884744 | tf_op jit(solution)/shard_map/ppermute | solution.py:563
  57.4 9.7 %collective-permute-start.6 = (bf16[384,256]{1,0:T(8,128)(2,1)S(1)}, bf16[384,256]{1,0:T(8,128)(2,1)S(1)}, u32[]{:S(2)}, u32[]{:S(2)}) collective-permute-start(bf16[384,256]{1,0:T(8,128)(2,1)S(1)} %get-tuple-element.44), channel_id=1, source_target_pairs={{0,1},{1,2},{2,3},{3,0},{4,5},{5,6},{6,7},{7,4},{8,9},{9,10},{10,1... | collective-permute-start | bytes 589832 | tf_op jit(solution)/shard_map/ppermute | solution.py:570
  59.0 14.6 %collective-permute-start.7 = (bf16[384,256]{1,0:T(8,128)(2,1)S(1)}, bf16[384,256]{1,0:T(8,128)(2,1)S(1)}, u32[]{:S(2)}, u32[]{:S(2)}) collective-permute-start(bf16[384,256]{1,0:T(8,128)(2,1)S(1)} %get-tuple-element.44), channel_id=1, source_target_pairs={{0,2},{1,3},{2,0},{3,1},{4,6},{5,7},{6,4},{7,5},{8,10},{9,11},{10,... | collective-permute-start | bytes 589832 | tf_op jit(solution)/shard_map/ppermute | solution.py:570
  73.6 12.7 %collective-permute-start.13 = (bf16[48,4608]{1,0:T(8,128)(2,1)S(1)}, bf16[48,4608]{1,0:T(8,128)(2,1)S(1)}, u32[]{:S(2)}, u32[]{:S(2)}) collective-permute-start(bf16[48,4608]{1,0:T(8,128)(2,1)S(1)} %copy-done.1), channel_id=1, source_target_pairs={{0,8},{4,12},{8,0},{12,4},{1,9},{5,13},{9,1},{13,5},{2,10},{6,14},... | collective-permute-start | bytes 1327112 | tf_op jit(solution)/shard_map/ppermute | solution.py:563
  75.1 6.5 %collective-permute-start.8 = (bf16[384,256]{1,0:T(8,128)(2,1)S(1)}, bf16[384,256]{1,0:T(8,128)(2,1)S(1)}, u32[]{:S(2)}, u32[]{:S(2)}) collective-permute-start(bf16[384,256]{1,0:T(8,128)(2,1)S(1)} %get-tuple-element.44), channel_id=1, source_target_pairs={{0,3},{1,0},{2,1},{3,2},{4,7},{5,4},{6,5},{7,6},{8,11},{9,8},{10,9... | collective-permute-start | bytes 589832 | tf_op jit(solution)/shard_map/ppermute | solution.py:570
  76.7 16.0 %collective-permute-start.14 = (bf16[48,4608]{1,0:T(8,128)(2,1)S(1)}, bf16[48,4608]{1,0:T(8,128)(2,1)S(1)}, u32[]{:S(2)}, u32[]{:S(2)}) collective-permute-start(bf16[48,4608]{1,0:T(8,128)(2,1)S(1)} %collective-permute-done.11.refs_1_), channel_id=1, source_target_pairs={{0,16},{16,0},{1,17},{17,1},{2,18},{18,2},{3,19},{19,3},{4,20},{20... | collective-permute-start | bytes 1327112 | tf_op jit(solution)/shard_map/ppermute | solution.py:563
  86.3 11.0 %collective-permute-start.15 = (bf16[48,4608]{1,0:T(8,128)(2,1)S(1)}, bf16[48,4608]{1,0:T(8,128)(2,1)S(1)}, u32[]{:S(2)}, u32[]{:S(2)}) collective-permute-start(bf16[48,4608]{1,0:T(8,128)(2,1)S(1)} %collective-permute-done.13.refs_2_), channel_id=1, source_target_pairs={{0,16},{16,0},{1,17},{17,1},{2,18},{18,2},{3,19},{19,3},{4,20},{20... | collective-permute-start | bytes 1327112 | tf_op jit(solution)/shard_map/ppermute | solution.py:563
  86.9 5.9 %collective-permute-start.9 = (bf16[384,256]{1,0:T(8,128)(2,1)}, bf16[384,256]{1,0:T(8,128)(2,1)S(1)}, u32[]{:S(2)}, u32[]{:S(2)}) collective-permute-start(bf16[384,256]{1,0:T(8,128)(2,1)} %get-tuple-element.49), channel_id=1, source_target_pairs={{0,8},{4,12},{8,0},{12,4},{1,9},{5,13},{9,1},{13,5},{2,10},{6,14},... | collective-permute-start | bytes 589832 | tf_op jit(solution)/shard_map/ppermute | solution.py:563
  100.8 4.0 %collective-permute-start.16 = (bf16[192,4608]{1,0:T(8,128)(2,1)}, bf16[192,4608]{1,0:T(8,128)(2,1)S(1)}, u32[]{:S(2)}, u32[]{:S(2)}) collective-permute-start(bf16[192,4608]{1,0:T(8,128)(2,1)} %get-tuple-element.57), channel_id=1, source_target_pairs={{0,4},{4,0},{8,12},{12,8},{1,5},{5,1},{9,13},{13,9},{2,6},{6,2},{1... | collective-permute-start | bytes 5308424 | tf_op jit(solution)/shard_map/ppermute | solution.py:563
where the time goes:
time: 109 us; the launch traced here: 107 us
  waiting for transfers between devices  44.5 us (41%)
  Pallas kernels  37.7 us (35%)
  starting transfers between devices  21.8 us (20%)
  other arithmetic  3.16 us (3%)
    pallas_call x11, Pallas kernels, call(): pl.pallas_call(kernel, in_specs=in_specs, out_specs=[spec for _, _, spec...  37.7 us
    ppermute x11, waiting for transfers between devices, flipped(): return lax.ppermute(array, axis, [(i, i ^ bit) for i in range(size)])  23.6 us
    ppermute x6, waiting for transfers between devices, along_line(): lax.ppermute(array, 'seq', [(i, (i + by) % size) for i in range(size)])  20.9 us
    ppermute x6, starting transfers between devices, along_line(): lax.ppermute(array, 'seq', [(i, (i + by) % size) for i in range(size)])  11.4 us
    ppermute x11, starting transfers between devices, flipped(): return lax.ppermute(array, axis, [(i, i ^ bit) for i in range(size)])  10.5 us
  transfers between devices with their start and end apart: 17, of which 11 were waited for; matrix products, arithmetic and copies ran while one was open for 3% of the time, Pallas kernels for 26%

commit v1 on v0

--- a/solution.py
+++ b/solution.py
@@ -572,6 +572,15 @@
     return parts
 
 
+def along_ring(array):
+    size = lax.axis_size("seq")
+    parts, part = [array[None]], array
+    for _ in range(1, size):
+        part = lax.ppermute(part, "seq", [(i, (i + 1) % size) for i in range(size)])
+        parts.append(Came(part[None]))
+    return parts
+
+
 def came(parts):
     return [part.array for part in parts if isinstance(part, Came)]
 
@@ -607,7 +616,7 @@
     q_near, kv_near = qkv([own, Came(partner)], weights, trig, 0)
     near = along_line(kv_near)
     half = w_out.shape[0] // 2
-    w_cut = cut(table, group_at, after(w_out, kv_near), [half // 4, half * 3 // 8, half * 3 // 8])
+    w_cut = cut(table, group_at, after(w_out, kv_near), [half // 4] * 4)
     q_near = after(q_near, *w_cut)
     (near_state,) = attention(
         [Step(0, 0, others, same=0)], table, [q_near], [near_chunk], [near], [near_chunk], [None]
@@ -615,12 +624,18 @@
 
     away = after(away, *near_state)
     q_far, kv_far = qkv([Came(away), Came(flipped(away, "tp", 1))], weights, trig, block_rows)
-    far = along_line(kv_far)
+    far = along_ring(kv_far)
 
     fetched = lambda piece, *others: flipped(after(piece, *others), "tp", 2)
     swap = lambda array: flipped(array, "groups", 1)
     w_far = [fetched(piece, away) for piece in w_cut[:2]]
     w_far[0] = after(w_far[0], kv_far)
+    w_far.append(fetched(w_cut[2], w_far[0]))
+    w_other = [swap(w_far[0])]
+    w_far[1] = after(w_far[1], came(far)[0], w_other[0])
+    w_far.append(fetched(w_cut[3], w_far[1]))
+    w_other.append(swap(w_far[1]))
+
     near_state, far_state = attention(
         [Step(1, 1, [], same=0), Step(1, 0, everyone), Step(0, 1, [0])],
         table,
@@ -630,9 +645,8 @@
         [near_chunk, far_chunk],
         [near_state, None],
     )
-    w_other = [swap(w_far[0])]
-    w_far[1] = after(w_far[1], *far_state, *came(far)[:2], w_other[0])
-    w_far.append(fetched(w_cut[2], w_far[1]))
+    w_far[2] = after(w_far[2], *far_state, w_other[1])
+    w_other.append(swap(w_far[2]))
     attended, gone = attention(
         [Step(1, 0, others), Step(0, 0, others)],
         table,
@@ -645,8 +659,7 @@
     )
     gone = flipped(gone, "tp", 2)
     near_sum = output_near(attended, w_out)
-    w_far[2] = after(w_far[2], attended)
-    w_other += [swap(piece) for piece in w_far[1:]]
+    w_other.append(swap(after(w_far[3], attended)))
     pieces = [Came(piece) for piece in w_far + w_other]
     sent, w_laid = output_send(table, group_at, Came(gone), near_sum, pieces)
     received = flipped(sent, "tp", 1)

time: 109 us -> 102 us (0.936); the launches traced: 107 us -> 102 us
  waiting for transfers between devices: 44.5 us -> 38.1 us
  Pallas kernels: 37.7 us -> 40 us
    ppermute x0 -> x3, waiting for transfers between devices: none -> 12.3 us  [along_ring(): part = lax.ppermute(part, 'seq', [(i, (i + 1) % size) for i in range(size)])]
    ppermute x6 -> x3, waiting for transfers between devices: 20.9 us -> 9.19 us  [along_line(): lax.ppermute(array, 'seq', [(i, (i + by) % size) for i in range(size)])]
    ppermute x11 -> x13, waiting for transfers between devices: 23.6 us -> 16.6 us  [flipped(): return lax.ppermute(array, axis, [(i, i ^ bit) for i in range(size)])]
    ppermute x6 -> x3, starting transfers between devices: 11.4 us -> 5.57 us  [along_line(): lax.ppermute(array, 'seq', [(i, (i + by) % size) for i in range(size)])]
    ppermute x11 -> x13, starting transfers between devices: 10.5 us -> 13.6 us  [flipped(): return lax.ppermute(array, axis, [(i, i ^ bit) for i in range(size)])]
    pallas_call x11, Pallas kernels: 37.7 us -> 40 us  [call(): pl.pallas_call(kernel, in_specs=in_specs, out_specs=[spec for _, _, spec...]
    ppermute x0 -> x3, starting transfers between devices: none -> 1.58 us  [along_ring(): part = lax.ppermute(part, 'seq', [(i, (i + 1) % size) for i in range(size)])]
  transfers between devices with their start and end apart: 17 -> 19, of which waited for: 11 -> 10; matrix products, arithmetic and copies ran while one was open for 3% -> 3% of each run, Pallas kernels for 26% -> 31%
where the time goes in v1:
time: 102 us
  Pallas kernels  40 us (39%)
  waiting for transfers between devices  38.1 us (37%)
  starting transfers between devices  20.8 us (20%)
  other arithmetic  3.15 us (3%)
    pallas_call x11, Pallas kernels, call(): pl.pallas_call(kernel, in_specs=in_specs, out_specs=[spec for _, _, spec...  40 us
    ppermute x13, waiting for transfers between devices, flipped(): return lax.ppermute(array, axis, [(i, i ^ bit) for i in range(size)])  16.6 us
    ppermute x13, starting transfers between devices, flipped(): return lax.ppermute(array, axis, [(i, i ^ bit) for i in range(size)])  13.6 us
    ppermute x3, waiting for transfers between devices, along_ring(): part = lax.ppermute(part, 'seq', [(i, (i + 1) % size) for i in range(size)])  12.3 us
    ppermute x3, waiting for transfers between devices, along_line(): lax.ppermute(array, 'seq', [(i, (i + by) % size) for i in range(size)])  9.19 us
    ppermute x3, starting transfers between devices, along_line(): lax.ppermute(array, 'seq', [(i, (i + by) % size) for i in range(size)])  5.57 us
  transfers between devices with their start and end apart: 19, of which 10 were waited for; matrix products, arithmetic and copies ran while one was open for 3% of the time, Pallas kernels for 31%

profile of v1, /device:TPU:0, one launch (start us, length us, event | category | flops | bytes accessed | tf_op | source)
XLA Modules:
  0.0 102.3 jit_solution(11577966655856178559)
XLA Ops:
  0.0 3.1 %norm_rows.1.refs_0_ = bf16[192,4608]{1,0:T(8,128)(2,1)} custom-call(bf16[192,4608]{1,0:T(8,128)(2,1)} %hidden.3, f32[4608]{0:T(1024)} %gain.2), custom_call_target="tpu_custom_call" | custom-call | flops 1 | bytes 1 | tf_op jit(solution)/shard_map/norm_rows/pallas_call | solution.py:38
  3.7 2.6 %collective-permute-start.1 = (bf16[192,4608]{1,0:T(8,128)(2,1)}, bf16[192,4608]{1,0:T(8,128)(2,1)S(1)}, u32[]{:S(2)}, u32[]{:S(2)}) collective-permute-start(bf16[192,4608]{1,0:T(8,128)(2,1)} %norm_rows.1.refs_0_), channel_id=1, source_target_pairs={{0,8},{4,12},{8,0},{12,4},{1,9},{5,13},{9,1},{13,5},{2,10},{6,14},... | collective-permute-start | bytes 5308424 | tf_op jit(solution)/shard_map/ppermute | solution.py:563
  6.7 1.4 %multiply_cosine_fusion = (f32[768,64]{1,0:T(8,128)S(1)}, f32[768,64]{1,0:T(8,128)S(1)}, f32[768,64]{1,0:T(8,128)S(1)}) fusion(f32[768]{0:T(1024)S(1)} %add_convert_fusion, f32[64]{0:T(128)S(1)} %multiply_power_fusion), kind=kLoop, calls=%fused_computation.2 | loop fusion | flops 98304 | bytes 593152 | tf_op jit(solution)/shard_map/cos | solution.py:552
  8.1 1.3 %pad_maximum_fusion.trig = f32[768,256]{1,0:T(8,128)} fusion(f32[768,64]{1,0:T(8,128)S(1)} %get-tuple-element.71, f32[768,64]{1,0:T(8,128)S(1)} %get-tuple-element.70, f32[768,64]{1,0:T(8,128)S(1)} %get-tuple-element.69), kind=kLoop, calls=%fused_computation | loop fusion | flops 589824 | bytes 1376256 | tf_op jit(solution)/shard_map/concatenate | solution.py:553
  9.4 4.4 %qkv.2 = (bf16[2,384,128]{2,1,0:T(8,128)(2,1)S(1)}, bf16[384,256]{1,0:T(8,128)(2,1)S(1)}) custom-call(f32[768,256]{1,0:T(8,128)} %pad_maximum_fusion.trig, bf16[4608,256]{1,0:T(8,128)(2,1)} %wq.3, bf16[4608,128]{1,0:T(8,128)(2,1)} %wk.3, bf16[4608,128]{1,0:T(8,128)(2,1)} %wv.3, bf16[192,4608]{1,0:T(8,128)(2,1)} %norm_rows.1.refs_0_, ...), custom_call_target="tpu_custom_call" | custom-call | flops 1 | bytes 1 | tf_op jit(solution)/shard_map/qkv/pallas_call | solution.py:38
  13.8 1.6 %collective-permute-start.2 = (bf16[384,256]{1,0:T(8,128)(2,1)S(1)}, bf16[384,256]{1,0:T(8,128)(2,1)S(1)}, u32[]{:S(2)}, u32[]{:S(2)}) collective-permute-start(bf16[384,256]{1,0:T(8,128)(2,1)S(1)} %get-tuple-element.37), channel_id=1, source_target_pairs={{0,1},{1,2},{2,3},{3,0},{4,5},{5,6},{6,7},{7,4},{8,9},{9,10},{10,1... | collective-permute-start | bytes 589832 | tf_op jit(solution)/shard_map/ppermute | solution.py:570
  15.4 2.6 %collective-permute-start.3 = (bf16[384,256]{1,0:T(8,128)(2,1)S(1)}, bf16[384,256]{1,0:T(8,128)(2,1)S(1)}, u32[]{:S(2)}, u32[]{:S(2)}) collective-permute-start(bf16[384,256]{1,0:T(8,128)(2,1)S(1)} %get-tuple-element.37), channel_id=1, source_target_pairs={{0,2},{1,3},{2,0},{3,1},{4,6},{5,7},{6,4},{7,5},{8,10},{9,11},{10,... | collective-permute-start | bytes 589832 | tf_op jit(solution)/shard_map/ppermute | solution.py:570
  18.0 1.3 %collective-permute-start.4 = (bf16[384,256]{1,0:T(8,128)(2,1)S(1)}, bf16[384,256]{1,0:T(8,128)(2,1)S(1)}, u32[]{:S(2)}, u32[]{:S(2)}) collective-permute-start(bf16[384,256]{1,0:T(8,128)(2,1)S(1)} %get-tuple-element.37), channel_id=1, source_target_pairs={{0,3},{1,0},{2,1},{3,2},{4,7},{5,4},{6,5},{7,6},{8,11},{9,8},{10,9... | collective-permute-start | bytes 589832 | tf_op jit(solution)/shard_map/ppermute | solution.py:570
  19.4 2.6 %cut_weights.1 = (bf16[32,4608]{1,0:T(8,128)(2,1)}, bf16[32,4608]{1,0:T(8,128)(2,1)}, bf16[32,4608]{1,0:T(8,128)(2,1)}, bf16[32,4608]{1,0:T(8,128)(2,1)}) custom-call(s32[10]{0:T(128)S(1)} %pad_add_fusion.1.table, bf16[256,4608]{1,0:T(8,128)(2,1)} %weights_hbm.1), custom_call_target="tpu_custom_call" | custom-call | flops 1 | bytes 1 | tf_op jit(solution)/shard_map/cut_weights/pallas_call | solution.py:38
  22.1 1.5 %collective-permute-done.2 = bf16[384,256]{1,0:T(8,128)(2,1)S(1)} collective-permute-done((bf16[384,256]{1,0:T(8,128)(2,1)S(1)}, bf16[384,256]{1,0:T(8,128)(2,1)S(1)}, u32[]{:S(2)}, u32[]{:S(2)}) %collective-permute-start.2) | collective-permute-done | bytes 196640 | tf_op jit(solution)/shard_map/ppermute | solution.py:570
  23.5 7.7 %collective-permute-done.3 = bf16[384,256]{1,0:T(8,128)(2,1)S(1)} collective-permute-done((bf16[384,256]{1,0:T(8,128)(2,1)S(1)}, bf16[384,256]{1,0:T(8,128)(2,1)S(1)}, u32[]{:S(2)}, u32[]{:S(2)}) %collective-permute-start.3) | collective-permute-done | bytes 196640 | tf_op jit(solution)/shard_map/ppermute | solution.py:570
  31.3 4.3 %attention.3 = (f32[3,8,256]{2,1,0:T(8,128)S(1)}, f32[3,144,256]{2,1,0:T(8,128)S(1)}) custom-call(s32[10]{0:T(128)S(1)} %pad_add_fusion.1.table, bf16[2,384,128]{2,1,0:T(8,128)(2,1)S(1)} %get-tuple-element.43.refs_0_, bf16[1,384,256]{2,1,0:T(8,128)(2,1)S(1)} %bitcast.14, bf16[1,384,256]{2,1,0:T(8,128)(2,1)S(1)} %bitcast.16, ...), custom_call_target="tpu_custom_call" | custom-call | flops 1 | bytes 1 | tf_op jit(solution)/shard_map/attention/pallas_call | solution.py:38
  35.6 10.1 %collective-permute-done.1.refs_0_ = bf16[192,4608]{1,0:T(8,128)(2,1)S(1)} collective-permute-done((bf16[192,4608]{1,0:T(8,128)(2,1)}, bf16[192,4608]{1,0:T(8,128)(2,1)S(1)}, u32[]{:S(2)}, u32[]{:S(2)}) %collective-permute-start.1) | collective-permute-done | bytes 1769504 | tf_op jit(solution)/shard_map/ppermute | solution.py:563
  45.7 1.8 %collective-permute-start.10 = (bf16[32,4608]{1,0:T(8,128)(2,1)}, bf16[32,4608]{1,0:T(8,128)(2,1)S(1)}, u32[]{:S(2)}, u32[]{:S(2)}) collective-permute-start(bf16[32,4608]{1,0:T(8,128)(2,1)} %get-tuple-element.55), channel_id=1, source_target_pairs={{0,8},{4,12},{8,0},{12,4},{1,9},{5,13},{9,1},{13,5},{2,10},{6,14},... | collective-permute-start | bytes 884744 | tf_op jit(solution)/shard_map/ppermute | solution.py:563
  47.8 1.6 %collective-permute-done.5.refs_1_ = bf16[192,4608]{1,0:T(8,128)(2,1)S(1)} collective-permute-done((bf16[192,4608]{1,0:T(8,128)(2,1)S(1)}, bf16[192,4608]{1,0:T(8,128)(2,1)S(1)}, u32[]{:S(2)}, u32[]{:S(2)}) %collective-permute-start.5) | collective-permute-done | bytes 1769504 | tf_op jit(solution)/shard_map/ppermute | solution.py:563
  49.4 4.1 %qkv.3 = (bf16[2,384,128]{2,1,0:T(8,128)(2,1)S(1)}, bf16[384,256]{1,0:T(8,128)(2,1)S(1)}) custom-call(f32[768,256]{1,0:T(8,128)} %pad_maximum_fusion.trig, bf16[4608,256]{1,0:T(8,128)(2,1)} %wq.3, bf16[4608,128]{1,0:T(8,128)(2,1)} %wk.3, bf16[4608,128]{1,0:T(8,128)(2,1)} %wv.3, bf16[192,4608]{1,0:T(8,128)(2,1)S(1)} %collective-permute-done.1.refs_0_, ...), custom_call_target="tpu_custom_call" | custom-call | flops 1 | bytes 1 | tf_op jit(solution)/shard_map/qkv/pallas_call | solution.py:38
  53.5 2.2 %collective-permute-done.10.refs_0_ = bf16[32,4608]{1,0:T(8,128)(2,1)S(1)} collective-permute-done((bf16[32,4608]{1,0:T(8,128)(2,1)}, bf16[32,4608]{1,0:T(8,128)(2,1)S(1)}, u32[]{:S(2)}, u32[]{:S(2)}) %collective-permute-start.10) | collective-permute-done | bytes 294944 | tf_op jit(solution)/shard_map/ppermute | solution.py:563
  55.8 1.7 %collective-permute-start.12 = (bf16[32,4608]{1,0:T(8,128)(2,1)S(1)}, bf16[32,4608]{1,0:T(8,128)(2,1)S(1)}, u32[]{:S(2)}, u32[]{:S(2)}) collective-permute-start(bf16[32,4608]{1,0:T(8,128)(2,1)S(1)} %collective-permute-done.10.refs_0_), channel_id=1, source_target_pairs={{0,16},{16,0},{1,17},{17,1},{2,18},{18,2},{3,19},{19,3},{4,20},{20... | collective-permute-start | bytes 884744 | tf_op jit(solution)/shard_map/ppermute | solution.py:563
  57.5 1.6 %collective-permute-start.6 = (bf16[384,256]{1,0:T(8,128)(2,1)S(1)}, bf16[384,256]{1,0:T(8,128)(2,1)S(1)}, u32[]{:S(2)}, u32[]{:S(2)}) collective-permute-start(bf16[384,256]{1,0:T(8,128)(2,1)S(1)} %get-tuple-element.48), channel_id=1, source_target_pairs={{0,1},{1,2},{2,3},{3,0},{4,5},{5,6},{6,7},{7,4},{8,9},{9,10},{10,1... | collective-permute-start | bytes 589832 | tf_op jit(solution)/shard_map/ppermute | solution.py:579
  59.1 6.0 %collective-permute-done.6 = bf16[384,256]{1,0:T(8,128)(2,1)S(1)} collective-permute-done((bf16[384,256]{1,0:T(8,128)(2,1)S(1)}, bf16[384,256]{1,0:T(8,128)(2,1)S(1)}, u32[]{:S(2)}, u32[]{:S(2)}) %collective-permute-start.6) | collective-permute-done | bytes 196640 | tf_op jit(solution)/shard_map/ppermute | solution.py:579
  65.1 1.5 %collective-permute-start.13 = (bf16[32,4608]{1,0:T(8,128)(2,1)S(1)}, bf16[32,4608]{1,0:T(8,128)(2,1)S(1)}, u32[]{:S(2)}, u32[]{:S(2)}) collective-permute-start(bf16[32,4608]{1,0:T(8,128)(2,1)S(1)} %copy-done.2), channel_id=1, source_target_pairs={{0,8},{4,12},{8,0},{12,4},{1,9},{5,13},{9,1},{13,5},{2,10},{6,14},... | collective-permute-start | bytes 884744 | tf_op jit(solution)/shard_map/ppermute | solution.py:563
  67.7 4.9 %collective-permute-done.7 = bf16[384,256]{1,0:T(8,128)(2,1)S(1)} collective-permute-done((bf16[384,256]{1,0:T(8,128)(2,1)S(1)}, bf16[384,256]{1,0:T(8,128)(2,1)S(1)}, u32[]{:S(2)}, u32[]{:S(2)}) %collective-permute-start.7) | collective-permute-done | bytes 196640 | tf_op jit(solution)/shard_map/ppermute | solution.py:579
  72.6 5.5 %attention.4 = (f32[3,8,256]{2,1,0:T(8,128)S(1)}, f32[3,144,256]{2,1,0:T(8,128)S(1)}, f32[3,8,256]{2,1,0:T(8,128)S(1)}, f32[3,144,256]{2,1,0:T(8,128)S(1)}) custom-call(s32[10]{0:T(128)S(1)} %pad_add_fusion.1.table, bf16[2,384,128]{2,1,0:T(8,128)(2,1)S(1)} %get-tuple-element.43.refs_0_, ...), custom_call_target="tpu_custom_call", output_to_operand_aliasing={{0}: (8, {}), {1}: (9, {})} | custom-call | flops 1 | bytes 1 | tf_op jit(solution)/shard_map/attention/pallas_call | solution.py:38
  78.6 1.4 %collective-permute-done.8 = bf16[384,256]{1,0:T(8,128)(2,1)S(1)} collective-permute-done((bf16[384,256]{1,0:T(8,128)(2,1)S(1)}, bf16[384,256]{1,0:T(8,128)(2,1)S(1)}, u32[]{:S(2)}, u32[]{:S(2)}) %collective-permute-start.8) | collective-permute-done | bytes 196640 | tf_op jit(solution)/shard_map/ppermute | solution.py:579
  80.0 5.3 %attention.5 = (bf16[384,256]{1,0:T(8,128)(2,1)}, bf16[384,256]{1,0:T(8,128)(2,1)}, f32[3,8,256]{2,1,0:T(8,128)S(1)}, f32[3,144,256]{2,1,0:T(8,128)S(1)}, f32[3,...) custom-call(s32[10]{0:T(128)S(1)} %pad_add_fusion.1.table, ...), custom_call_target="tpu_custom_call", output_to_operand_aliasing={{2}: (7, {}), {3}: (8, {}), {4}: (9, {}), {5}: (10, {})} | custom-call | flops 1 | bytes 1 | tf_op jit(solution)/shard_map/attention/pallas_call | solution.py:38
  85.3 0.6 collective-permute-start.17
  85.9 2.9 %collective-permute-start.9 = (bf16[384,256]{1,0:T(8,128)(2,1)}, bf16[384,256]{1,0:T(8,128)(2,1)S(1)}, u32[]{:S(2)}, u32[]{:S(2)}) collective-permute-start(bf16[384,256]{1,0:T(8,128)(2,1)} %get-tuple-element.53), channel_id=1, source_target_pairs={{0,8},{4,12},{8,0},{12,4},{1,9},{5,13},{9,1},{13,5},{2,10},{6,14},... | collective-permute-start | bytes 589832 | tf_op jit(solution)/shard_map/ppermute | solution.py:563
  88.8 3.4 %output_near.1.near = f32[384,4608]{1,0:T(8,128)S(1)} custom-call(bf16[384,256]{1,0:T(8,128)(2,1)} %get-tuple-element.54.left_hbm, bf16[256,4608]{1,0:T(8,128)(2,1)} %weights_hbm.1), custom_call_target="tpu_custom_call" | custom-call | flops 1 | bytes 1 | tf_op jit(solution)/shard_map/output_near/pallas_call | solution.py:38
  92.7 2.9 %output_send.1 = (bf16[192,4608]{1,0:T(8,128)(2,1)}, bf16[256,4608]{1,0:T(8,128)(2,1)S(1)}) custom-call(s32[10]{0:T(128)S(1)} %pad_add_fusion.1.table, bf16[384,256]{1,0:T(8,128)(2,1)S(1)} %collective-permute-done.9.left_hbm, f32[384,4608]{1,0:T(8,128)S(1)} %output_near.1.near, bf16[32,4608]{1,0:T(8,128)(2,1)S(1)} %collective-permute-done.10.refs_0_, ...), custom_call_target="tpu_custom_call" | custom-call | flops 1 | bytes 1 | tf_op jit(solution)/shard_map/output_send/pallas_call | solution.py:38
  95.7 1.7 %output_keep.1 = (f32[192,4608]{1,0:T(8,128)S(1)}, bf16[192,4608]{1,0:T(8,128)(2,1)S(1)}) custom-call(bf16[384,256]{1,0:T(8,128)(2,1)S(1)} %collective-permute-done.9.left_hbm, bf16[192,4608]{1,0:T(8,128)(2,1)} %hidden.3, f32[384,4608]{1,0:T(8,128)S(1)} %output_near.1.near, bf16[256,4608]{1,0:T(8,128)(2,1)S(1)} %get-tuple-element.64.weights), custom_call_target="tpu_custom_call" | custom-call | flops 1 | bytes 1 | tf_op jit(solution)/shard_map/output_keep/pallas_call | solution.py:38
  97.4 2.1 %collective-permute-done.18.received = bf16[192,4608]{1,0:T(8,128)(2,1)S(1)} collective-permute-done((bf16[192,4608]{1,0:T(8,128)(2,1)}, bf16[192,4608]{1,0:T(8,128)(2,1)S(1)}, u32[]{:S(2)}, u32[]{:S(2)}) %collective-permute-start.18) | collective-permute-done | bytes 1769504 | tf_op jit(solution)/shard_map/ppermute | solution.py:563
  99.6 2.6 %output_norm.1 = bf16[192,4608]{1,0:T(8,128)(2,1)} custom-call(bf16[192,4608]{1,0:T(8,128)(2,1)S(1)} %collective-permute-done.18.received, bf16[192,4608]{1,0:T(8,128)(2,1)S(1)} %get-tuple-element.65.hidden, f32[192,4608]{1,0:T(8,128)S(1)} %get-tuple-element.66.kept, f32[4608]{0:T(1024)} %gain.3), custom_call_target="tpu_custom_call" | custom-call | flops 1 | bytes 1 | tf_op jit(solution)/shard_map/output_norm/pallas_call | solution.py:38
  (34 shorter events, 3.5 us)
Async XLA Ops:
  0.0 6.3 %copy-start = (s32[8]{0:T(128)S(1)}, s32[8]{0:T(128)}, u32[]{:S(2)}) copy-start(s32[8]{0:T(128)} %param.15) | copy-start | bytes 100
  3.1 6.2 %collective-permute-start = (bf16[192,4608]{1,0:T(8,128)(2,1)}, bf16[192,4608]{1,0:T(8,128)(2,1)}, u32[]{:S(2)}, u32[]{:S(2)}) collective-permute-start(bf16[192,4608]{1,0:T(8,128)(2,1)} %norm_rows.1.refs_0_), channel_id=1, source_target_pairs={{0,4},{4,0},{8,12},{12,8},{1,5},{5,1},{9,13},{13,9},{2,6},{6,2},{1... | collective-permute-start | bytes 5308424 | tf_op jit(solution)/shard_map/ppermute | solution.py:563
  3.7 42.0 %collective-permute-start.1 = (bf16[192,4608]{1,0:T(8,128)(2,1)}, bf16[192,4608]{1,0:T(8,128)(2,1)S(1)}, u32[]{:S(2)}, u32[]{:S(2)}) collective-permute-start(bf16[192,4608]{1,0:T(8,128)(2,1)} %norm_rows.1.refs_0_), channel_id=1, source_target_pairs={{0,8},{4,12},{8,0},{12,4},{1,9},{5,13},{9,1},{13,5},{2,10},{6,14},... | collective-permute-start | bytes 5308424 | tf_op jit(solution)/shard_map/ppermute | solution.py:563
  13.8 9.7 %collective-permute-start.2 = (bf16[384,256]{1,0:T(8,128)(2,1)S(1)}, bf16[384,256]{1,0:T(8,128)(2,1)S(1)}, u32[]{:S(2)}, u32[]{:S(2)}) collective-permute-start(bf16[384,256]{1,0:T(8,128)(2,1)S(1)} %get-tuple-element.37), channel_id=1, source_target_pairs={{0,1},{1,2},{2,3},{3,0},{4,5},{5,6},{6,7},{7,4},{8,9},{9,10},{10,1... | collective-permute-start | bytes 589832 | tf_op jit(solution)/shard_map/ppermute | solution.py:570
  15.4 15.8 %collective-permute-start.3 = (bf16[384,256]{1,0:T(8,128)(2,1)S(1)}, bf16[384,256]{1,0:T(8,128)(2,1)S(1)}, u32[]{:S(2)}, u32[]{:S(2)}) collective-permute-start(bf16[384,256]{1,0:T(8,128)(2,1)S(1)} %get-tuple-element.37), channel_id=1, source_target_pairs={{0,2},{1,3},{2,0},{3,1},{4,6},{5,7},{6,4},{7,5},{8,10},{9,11},{10,... | collective-permute-start | bytes 589832 | tf_op jit(solution)/shard_map/ppermute | solution.py:570
  18.0 13.2 %collective-permute-start.4 = (bf16[384,256]{1,0:T(8,128)(2,1)S(1)}, bf16[384,256]{1,0:T(8,128)(2,1)S(1)}, u32[]{:S(2)}, u32[]{:S(2)}) collective-permute-start(bf16[384,256]{1,0:T(8,128)(2,1)S(1)} %get-tuple-element.37), channel_id=1, source_target_pairs={{0,3},{1,0},{2,1},{3,2},{4,7},{5,4},{6,5},{7,6},{8,11},{9,8},{10,9... | collective-permute-start | bytes 589832 | tf_op jit(solution)/shard_map/ppermute | solution.py:570
  45.7 19.4 %copy-start.2 = (bf16[32,4608]{1,0:T(8,128)(2,1)S(1)}, bf16[32,4608]{1,0:T(8,128)(2,1)}, u32[]{:S(2)}) copy-start(bf16[32,4608]{1,0:T(8,128)(2,1)} %get-tuple-element.59) | copy-start | bytes 884740
  45.7 21.5 %copy-start.1 = (bf16[32,4608]{1,0:T(8,128)(2,1)S(1)}, bf16[32,4608]{1,0:T(8,128)(2,1)}, u32[]{:S(2)}) copy-start(bf16[32,4608]{1,0:T(8,128)(2,1)} %get-tuple-element.61) | copy-start | bytes 884740
  45.7 3.7 %collective-permute-start.5 = (bf16[192,4608]{1,0:T(8,128)(2,1)S(1)}, bf16[192,4608]{1,0:T(8,128)(2,1)S(1)}, u32[]{:S(2)}, u32[]{:S(2)}) collective-permute-start(bf16[192,4608]{1,0:T(8,128)(2,1)S(1)} %collective-permute-done.1.refs_0_), channel_id=1, source_target_pairs={{0,4},{4,0},{8,12},{12,8},{1,5},{5,1},{9,13},{13,9},{2,6},{6,2},{1... | collective-permute-start | bytes 5308424 | tf_op jit(solution)/shard_map/ppermute | solution.py:563
  45.7 10.1 %collective-permute-start.10 = (bf16[32,4608]{1,0:T(8,128)(2,1)}, bf16[32,4608]{1,0:T(8,128)(2,1)S(1)}, u32[]{:S(2)}, u32[]{:S(2)}) collective-permute-start(bf16[32,4608]{1,0:T(8,128)(2,1)} %get-tuple-element.55), channel_id=1, source_target_pairs={{0,8},{4,12},{8,0},{12,4},{1,9},{5,13},{9,1},{13,5},{2,10},{6,14},... | collective-permute-start | bytes 884744 | tf_op jit(solution)/shard_map/ppermute | solution.py:563
  47.5 19.1 %collective-permute-start.11 = (bf16[32,4608]{1,0:T(8,128)(2,1)}, bf16[32,4608]{1,0:T(8,128)(2,1)S(1)}, u32[]{:S(2)}, u32[]{:S(2)}) collective-permute-start(bf16[32,4608]{1,0:T(8,128)(2,1)} %get-tuple-element.57), channel_id=1, source_target_pairs={{0,8},{4,12},{8,0},{12,4},{1,9},{5,13},{9,1},{13,5},{2,10},{6,14},... | collective-permute-start | bytes 884744 | tf_op jit(solution)/shard_map/ppermute | solution.py:563
  55.8 10.9 %collective-permute-start.12 = (bf16[32,4608]{1,0:T(8,128)(2,1)S(1)}, bf16[32,4608]{1,0:T(8,128)(2,1)S(1)}, u32[]{:S(2)}, u32[]{:S(2)}) collective-permute-start(bf16[32,4608]{1,0:T(8,128)(2,1)S(1)} %collective-permute-done.10.refs_0_), channel_id=1, source_target_pairs={{0,16},{16,0},{1,17},{17,1},{2,18},{18,2},{3,19},{19,3},{4,20},{20... | collective-permute-start | bytes 884744 | tf_op jit(solution)/shard_map/ppermute | solution.py:563
  57.5 7.6 %collective-permute-start.6 = (bf16[384,256]{1,0:T(8,128)(2,1)S(1)}, bf16[384,256]{1,0:T(8,128)(2,1)S(1)}, u32[]{:S(2)}, u32[]{:S(2)}) collective-permute-start(bf16[384,256]{1,0:T(8,128)(2,1)S(1)} %get-tuple-element.48), channel_id=1, source_target_pairs={{0,1},{1,2},{2,3},{3,0},{4,5},{5,6},{6,7},{7,4},{8,9},{9,10},{10,1... | collective-permute-start | bytes 589832 | tf_op jit(solution)/shard_map/ppermute | solution.py:579
  65.1 7.5 %collective-permute-start.7 = (bf16[384,256]{1,0:T(8,128)(2,1)S(1)}, bf16[384,256]{1,0:T(8,128)(2,1)S(1)}, u32[]{:S(2)}, u32[]{:S(2)}) collective-permute-start(bf16[384,256]{1,0:T(8,128)(2,1)S(1)} %collective-permute-done.6), channel_id=1, source_target_pairs={{0,1},{1,2},{2,3},{3,0},{4,5},{5,6},{6,7},{7,4},{8,9},{9,10},{10,1... | collective-permute-start | bytes 589832 | tf_op jit(solution)/shard_map/ppermute | solution.py:579
  65.1 12.9 %collective-permute-start.13 = (bf16[32,4608]{1,0:T(8,128)(2,1)S(1)}, bf16[32,4608]{1,0:T(8,128)(2,1)S(1)}, u32[]{:S(2)}, u32[]{:S(2)}) collective-permute-start(bf16[32,4608]{1,0:T(8,128)(2,1)S(1)} %copy-done.2), channel_id=1, source_target_pairs={{0,8},{4,12},{8,0},{12,4},{1,9},{5,13},{9,1},{13,5},{2,10},{6,14},... | collective-permute-start | bytes 884744 | tf_op jit(solution)/shard_map/ppermute | solution.py:563
  66.6 11.4 %collective-permute-start.14 = (bf16[32,4608]{1,0:T(8,128)(2,1)S(1)}, bf16[32,4608]{1,0:T(8,128)(2,1)S(1)}, u32[]{:S(2)}, u32[]{:S(2)}) collective-permute-start(bf16[32,4608]{1,0:T(8,128)(2,1)S(1)} %collective-permute-done.11.refs_1_), channel_id=1, source_target_pairs={{0,16},{16,0},{1,17},{17,1},{2,18},{18,2},{3,19},{19,3},{4,20},{20... | collective-permute-start | bytes 884744 | tf_op jit(solution)/shard_map/ppermute | solution.py:563
  67.2 18.2 %collective-permute-start.15 = (bf16[32,4608]{1,0:T(8,128)(2,1)S(1)}, bf16[32,4608]{1,0:T(8,128)(2,1)S(1)}, u32[]{:S(2)}, u32[]{:S(2)}) collective-permute-start(bf16[32,4608]{1,0:T(8,128)(2,1)S(1)} %copy-done.1), channel_id=1, source_target_pairs={{0,8},{4,12},{8,0},{12,4},{1,9},{5,13},{9,1},{13,5},{2,10},{6,14},... | collective-permute-start | bytes 884744 | tf_op jit(solution)/shard_map/ppermute | solution.py:563
  72.5 7.5 %collective-permute-start.8 = (bf16[384,256]{1,0:T(8,128)(2,1)S(1)}, bf16[384,256]{1,0:T(8,128)(2,1)S(1)}, u32[]{:S(2)}, u32[]{:S(2)}) collective-permute-start(bf16[384,256]{1,0:T(8,128)(2,1)S(1)} %collective-permute-done.7), channel_id=1, source_target_pairs={{0,1},{1,2},{2,3},{3,0},{4,5},{5,6},{6,7},{7,4},{8,9},{9,10},{10,1... | collective-permute-start | bytes 589832 | tf_op jit(solution)/shard_map/ppermute | solution.py:579
  78.0 14.6 %collective-permute-start.16 = (bf16[32,4608]{1,0:T(8,128)(2,1)S(1)}, bf16[32,4608]{1,0:T(8,128)(2,1)S(1)}, u32[]{:S(2)}, u32[]{:S(2)}) collective-permute-start(bf16[32,4608]{1,0:T(8,128)(2,1)S(1)} %collective-permute-done.13.refs_2_), channel_id=1, source_target_pairs={{0,16},{16,0},{1,17},{17,1},{2,18},{18,2},{3,19},{19,3},{4,20},{20... | collective-permute-start | bytes 884744 | tf_op jit(solution)/shard_map/ppermute | solution.py:563
  85.3 7.3 %collective-permute-start.17 = (bf16[32,4608]{1,0:T(8,128)(2,1)S(1)}, bf16[32,4608]{1,0:T(8,128)(2,1)S(1)}, u32[]{:S(2)}, u32[]{:S(2)}) collective-permute-start(bf16[32,4608]{1,0:T(8,128)(2,1)S(1)} %collective-permute-done.15.refs_3_), channel_id=1, source_target_pairs={{0,16},{16,0},{1,17},{17,1},{2,18},{18,2},{3,19},{19,3},{4,20},{20... | collective-permute-start | bytes 884744 | tf_op jit(solution)/shard_map/ppermute | solution.py:563
  85.9 6.7 %collective-permute-start.9 = (bf16[384,256]{1,0:T(8,128)(2,1)}, bf16[384,256]{1,0:T(8,128)(2,1)S(1)}, u32[]{:S(2)}, u32[]{:S(2)}) collective-permute-start(bf16[384,256]{1,0:T(8,128)(2,1)} %get-tuple-element.53), channel_id=1, source_target_pairs={{0,8},{4,12},{8,0},{12,4},{1,9},{5,13},{9,1},{13,5},{2,10},{6,14},... | collective-permute-start | bytes 589832 | tf_op jit(solution)/shard_map/ppermute | solution.py:563
  95.6 4.0 %collective-permute-start.18 = (bf16[192,4608]{1,0:T(8,128)(2,1)}, bf16[192,4608]{1,0:T(8,128)(2,1)S(1)}, u32[]{:S(2)}, u32[]{:S(2)}) collective-permute-start(bf16[192,4608]{1,0:T(8,128)(2,1)} %get-tuple-element.63), channel_id=1, source_target_pairs={{0,4},{4,0},{8,12},{12,8},{1,5},{5,1},{9,13},{13,9},{2,6},{6,2},{1... | collective-permute-start | bytes 5308424 | tf_op jit(solution)/shard_map/ppermute | solution.py:563

commit v2 on v1

--- a/solution.py
+++ b/solution.py
@@ -108,24 +108,12 @@
     )
 
 
-def rotate_into(product, angles, q, kv):
-    cos, sin = angles[:, :HD], angles[:, HD:]
-    queries = product.shape[1] - 2 * HD
-
-    def rotated(at):
-        y = product[:, at : at + HD]
-        return y * cos + pltpu.roll(y, HD // 2, 1) * sin
-
-    factor = ATT_SCALAR ** (-0.5) * math.log2(math.e)
-    kv[:, :HD] = rotated(queries).astype(jnp.bfloat16)
-    kv[:, HD:] = product[:, queries + HD :].astype(jnp.bfloat16)
-    for head in range(queries // HD):
-        q[head] = (rotated(head * HD) * factor).astype(jnp.bfloat16)
-
-
-def qkv_kernel(count, first, chunks, trig, wq, wk, wv, *refs):
-    parts = refs[:count]
-    q, kv, weights, rows, angles, semaphores = refs[count:]
+def qkv_kernel(count, kinds, first, chunks, trig, *refs):
+    refs = list(refs)
+    take = lambda n: [refs.pop(0) for _ in range(n)]
+    given, parts = take(len(kinds)), take(count)
+    q, kv = take(1)[0] if "q" in kinds else None, take(1)[0] if "k" in kinds else None
+    weights, rows, angles, semaphores = refs
     copies, waits = Copies(semaphores), []
     depth = weights.shape[0] // chunks
     for chunk in range(chunks):
@@ -134,7 +122,7 @@
             target = rows.at[pl.ds(put, part.shape[0]), span]
             here.append(copies.start(part.at[:, span], target))
             put += part.shape[0]
-        for weight in (wq, wk, wv):
+        for weight in given:
             target = weights.at[span, pl.ds(column, weight.shape[1])]
             here.append(copies.start(weight.at[span], target))
             column += weight.shape[1]
@@ -148,27 +136,43 @@
         term = jnp.dot(rows[:, span], weights[span, :], preferred_element_type=jnp.float32)
         product = term if product is None else product + term
     late.wait()
-    rotate_into(product, angles, q, kv)
-
-
-def qkv(parts, weights, trig, first, chunks=6):
+    cos, sin = angles[:, :HD], angles[:, HD:]
+
+    def rotated(at):
+        y = product[:, at : at + HD]
+        return y * cos + pltpu.roll(y, HD // 2, 1) * sin
+
+    factor = ATT_SCALAR ** (-0.5) * math.log2(math.e)
+    if kv is not None:
+        begin = product.shape[1] - 2 * HD
+        kv[:, :HD] = rotated(begin).astype(jnp.bfloat16)
+        kv[:, HD:] = product[:, begin + HD :].astype(jnp.bfloat16)
+    if q is not None:
+        for head in range(q.shape[0]):
+            q[head] = (rotated(head * HD) * factor).astype(jnp.bfloat16)
+
+
+def qkv(parts, weights, kinds, trig, first, chunks=6):
+    given = [weights["qkv".index(kind)] for kind in kinds]
     total, width = sum(part.shape[0] for part in parts), parts[0].shape[1]
-    columns = sum(weight.shape[1] for weight in weights)
-    heads, bf16 = columns // HD - 2, jnp.bfloat16
+    columns = sum(weight.shape[1] for weight in given)
+    heads, bf16 = weights[0].shape[1] // HD, jnp.bfloat16
+    outs = [((heads, total, HD), bf16, VMEM)] * ("q" in kinds)
+    outs += [((total, 2 * HD), bf16, VMEM)] * ("k" in kinds)
     return call(
-        functools.partial(qkv_kernel, len(parts), first, chunks),
-        "qkv",
+        functools.partial(qkv_kernel, len(parts), kinds, first, chunks),
+        "project_" + kinds,
         14,
-        [HBM] * (4 + len(parts)),
-        [((heads, total, HD), bf16, VMEM), ((total, 2 * HD), bf16, VMEM)],
+        [HBM] * (1 + len(given) + len(parts)),
+        outs,
         [
             pltpu.VMEM((width, columns), bf16),
             pltpu.VMEM((total, width), bf16),
             pltpu.VMEM((total, 2 * HD), jnp.float32),
-            pltpu.SemaphoreType.DMA((1 + (len(parts) + 3) * chunks,)),
+            pltpu.SemaphoreType.DMA((1 + (len(parts) + len(given)) * chunks,)),
         ],
         trig,
-        *weights,
+        *given,
         *parts,
     )
 
@@ -613,26 +617,27 @@
     partner = flipped(own, "tp", 1)
 
     weights = (wq, wk, wv)
-    q_near, kv_near = qkv([own, Came(partner)], weights, trig, 0)
+    q_near, kv_near = qkv([own, Came(partner)], weights, "qkv", trig, 0)
     near = along_line(kv_near)
     half = w_out.shape[0] // 2
-    w_cut = cut(table, group_at, after(w_out, kv_near), [half // 4] * 4)
+    w_cut = cut(table, group_at, after(w_out, kv_near), [half // 4, half // 4, half * 3 // 8, half // 8])
     q_near = after(q_near, *w_cut)
     (near_state,) = attention(
         [Step(0, 0, others, same=0)], table, [q_near], [near_chunk], [near], [near_chunk], [None]
     )
 
     away = after(away, *near_state)
-    q_far, kv_far = qkv([Came(away), Came(flipped(away, "tp", 1))], weights, trig, block_rows)
+    rows_far = [Came(away), Came(flipped(away, "tp", 1))]
+    (kv_far,) = qkv(rows_far, weights, "kv", trig, block_rows)
+    rows_far[1] = Came(after(rows_far[1].array, kv_far))
+    (q_far,) = qkv(rows_far, weights, "q", trig, block_rows)
     far = along_ring(kv_far)
 
     fetched = lambda piece, *others: flipped(after(piece, *others), "tp", 2)
     swap = lambda array: flipped(array, "groups", 1)
-    w_far = [fetched(piece, away) for piece in w_cut[:2]]
-    w_far[0] = after(w_far[0], kv_far)
-    w_far.append(fetched(w_cut[2], w_far[0]))
-    w_other = [swap(w_far[0])]
-    w_far[1] = after(w_far[1], came(far)[0], w_other[0])
+    w_far = [fetched(piece, away) for piece in w_cut[:3]]
+    w_other = [swap(after(w_far[0], q_far))]
+    w_far[1] = after(w_far[1], w_other[0], came(far)[1])
     w_far.append(fetched(w_cut[3], w_far[1]))
     w_other.append(swap(w_far[1]))
 
@@ -645,7 +650,7 @@
         [near_chunk, far_chunk],
         [near_state, None],
     )
-    w_far[2] = after(w_far[2], *far_state, w_other[1])
+    w_far[2] = after(w_far[2], w_other[1], *far_state, came(far)[-1])
     w_other.append(swap(w_far[2]))
     attended, gone = attention(
         [Step(1, 0, others), Step(0, 0, others)],
@@ -682,7 +687,7 @@
     qs, keys_values, weights = [], [], (wq, wk, wv)
     for at in range(2):
         first = at * block_rows
-        q, kv = qkv([normed[first : first + block_rows]], weights, trig, first)
+        q, kv = qkv([normed[first : first + block_rows]], weights, "qkv", trig, first)
         qs.append(q)
         keys_values.append(kv)
     kv = lax.all_gather(jnp.stack(keys_values), "seq")[line].reshape(-1, block_rows, 2 * HD)

time: 102 us -> 102 us (level)
  waiting for transfers between devices: 38.1 us -> 32.1 us
  local copies, waits for them, and re-layouts: 0.01 us -> 2.72 us
  starting transfers between devices: 20.8 us -> 23.4 us
    ppermute x3, waiting for transfers between devices: 12.3 us -> 5.8 us  [along_ring(): part = lax.ppermute(part, 'seq', [(i, (i + 1) % size) for i in range(size)])]
    unnamed x6 -> x12, local copies, waits for them, and re-layouts: 0.01 us -> 2.72 us
    ppermute x3, starting transfers between devices: 1.58 us -> 3.28 us  [along_ring(): part = lax.ppermute(part, 'seq', [(i, (i + 1) % size) for i in range(size)])]
    pallas_call x11 -> x12, Pallas kernels: 40 us -> 40.5 us  [call(): pl.pallas_call(kernel, in_specs=in_specs, out_specs=[spec for _, _, spec...]
where the time goes in v2:
time: 102 us
  Pallas kernels  40.5 us (40%)
  waiting for transfers between devices  32.1 us (31%)
  starting transfers between devices  23.4 us (23%)
  other arithmetic  3.16 us (3%)
  local copies, waits for them, and re-layouts  2.72 us (3%)
    pallas_call x12, Pallas kernels, call(): pl.pallas_call(kernel, in_specs=in_specs, out_specs=[spec for _, _, spec...  40.5 us
    ppermute x13, waiting for transfers between devices, flipped(): return lax.ppermute(array, axis, [(i, i ^ bit) for i in range(size)])  17.1 us
    ppermute x13, starting transfers between devices, flipped(): return lax.ppermute(array, axis, [(i, i ^ bit) for i in range(size)])  14.6 us
    ppermute x3, waiting for transfers between devices, along_line(): lax.ppermute(array, 'seq', [(i, (i + by) % size) for i in range(size)])  9.17 us
    ppermute x3, waiting for transfers between devices, along_ring(): part = lax.ppermute(part, 'seq', [(i, (i + 1) % size) for i in range(size)])  5.8 us
    ppermute x3, starting transfers between devices, along_line(): lax.ppermute(array, 'seq', [(i, (i + by) % size) for i in range(size)])  5.57 us
    ppermute x3, starting transfers between devices, along_ring(): part = lax.ppermute(part, 'seq', [(i, (i + 1) % size) for i in range(size)])  3.28 us
    unnamed x12, local copies, waits for them, and re-layouts  2.72 us
  transfers between devices with their start and end apart: 19, of which 10 were waited for; matrix products, arithmetic and copies ran while one was open for 3% of the time, Pallas kernels for 31%

profile of v2, /device:TPU:0, one launch (start us, length us, event | category | flops | bytes accessed | tf_op | source)
XLA Modules:
  0.0 102.2 jit_solution(2679471577475101981)
XLA Ops:
  0.0 3.1 %norm_rows.1.refs_3_ = bf16[192,4608]{1,0:T(8,128)(2,1)} custom-call(bf16[192,4608]{1,0:T(8,128)(2,1)} %hidden.3, f32[4608]{0:T(1024)} %gain.2), custom_call_target="tpu_custom_call" | custom-call | flops 1 | bytes 1 | tf_op jit(solution)/shard_map/norm_rows/pallas_call | solution.py:38
  3.7 2.6 %collective-permute-start.1 = (bf16[192,4608]{1,0:T(8,128)(2,1)}, bf16[192,4608]{1,0:T(8,128)(2,1)S(1)}, u32[]{:S(2)}, u32[]{:S(2)}) collective-permute-start(bf16[192,4608]{1,0:T(8,128)(2,1)} %norm_rows.1.refs_3_), channel_id=1, source_target_pairs={{0,8},{4,12},{8,0},{12,4},{1,9},{5,13},{9,1},{13,5},{2,10},{6,14},... | collective-permute-start | bytes 5308424 | tf_op jit(solution)/shard_map/ppermute | solution.py:567
  6.7 1.4 %multiply_cosine_fusion = (f32[768,64]{1,0:T(8,128)S(1)}, f32[768,64]{1,0:T(8,128)S(1)}, f32[768,64]{1,0:T(8,128)S(1)}) fusion(f32[768]{0:T(1024)S(1)} %add_convert_fusion, f32[64]{0:T(128)S(1)} %multiply_power_fusion), kind=kLoop, calls=%fused_computation.2 | loop fusion | flops 98304 | bytes 593152 | tf_op jit(solution)/shard_map/cos | solution.py:556
  10.6 1.5 %copy-done.1 = bf16[192,4608]{1,0:T(8,128)(2,1)S(1)} copy-done((bf16[192,4608]{1,0:T(8,128)(2,1)S(1)}, bf16[192,4608]{1,0:T(8,128)(2,1)}, u32[]{:S(2)}) %copy-start.1) | copy-done | bytes 1769496
  12.1 4.2 %project_qkv.1 = (bf16[2,384,128]{2,1,0:T(8,128)(2,1)S(1)}, bf16[384,256]{1,0:T(8,128)(2,1)S(1)}) custom-call(f32[768,256]{1,0:T(8,128)} %pad_maximum_fusion.trig, bf16[4608,256]{1,0:T(8,128)(2,1)} %refs_0_.5, bf16[4608,128]{1,0:T(8,128)(2,1)} %refs_0_.4, bf16[4608,128]{1,0:T(8,128)(2,1)} %refs_1_.3, bf16[192,4608]{1,0:T(8,128)(2,1)} %norm_rows.1.refs_3_, ...), custom_call_target="tpu_custom_call" | custom-call | flops 1 | bytes 1 | tf_op jit(solution)/shard_map/project_qkv/pallas_call | solution.py:38
  16.3 1.6 %collective-permute-start.2 = (bf16[384,256]{1,0:T(8,128)(2,1)S(1)}, bf16[384,256]{1,0:T(8,128)(2,1)S(1)}, u32[]{:S(2)}, u32[]{:S(2)}) collective-permute-start(bf16[384,256]{1,0:T(8,128)(2,1)S(1)} %get-tuple-element.36), channel_id=1, source_target_pairs={{0,1},{1,2},{2,3},{3,0},{4,5},{5,6},{6,7},{7,4},{8,9},{9,10},{10,1... | collective-permute-start | bytes 589832 | tf_op jit(solution)/shard_map/ppermute | solution.py:574
  18.0 2.6 %collective-permute-start.3 = (bf16[384,256]{1,0:T(8,128)(2,1)S(1)}, bf16[384,256]{1,0:T(8,128)(2,1)S(1)}, u32[]{:S(2)}, u32[]{:S(2)}) collective-permute-start(bf16[384,256]{1,0:T(8,128)(2,1)S(1)} %get-tuple-element.36), channel_id=1, source_target_pairs={{0,2},{1,3},{2,0},{3,1},{4,6},{5,7},{6,4},{7,5},{8,10},{9,11},{10,... | collective-permute-start | bytes 589832 | tf_op jit(solution)/shard_map/ppermute | solution.py:574
  20.6 1.3 %collective-permute-start.4 = (bf16[384,256]{1,0:T(8,128)(2,1)S(1)}, bf16[384,256]{1,0:T(8,128)(2,1)S(1)}, u32[]{:S(2)}, u32[]{:S(2)}) collective-permute-start(bf16[384,256]{1,0:T(8,128)(2,1)S(1)} %get-tuple-element.36), channel_id=1, source_target_pairs={{0,3},{1,0},{2,1},{3,2},{4,7},{5,4},{6,5},{7,6},{8,11},{9,8},{10,9... | collective-permute-start | bytes 589832 | tf_op jit(solution)/shard_map/ppermute | solution.py:574
  22.0 2.6 %cut_weights.1 = (bf16[32,4608]{1,0:T(8,128)(2,1)}, bf16[32,4608]{1,0:T(8,128)(2,1)}, bf16[48,4608]{1,0:T(8,128)(2,1)}, bf16[16,4608]{1,0:T(8,128)(2,1)}) custom-call(s32[10]{0:T(128)S(1)} %pad_add_fusion.1.table, bf16[256,4608]{1,0:T(8,128)(2,1)} %weights_hbm.1), custom_call_target="tpu_custom_call" | custom-call | flops 1 | bytes 1 | tf_op jit(solution)/shard_map/cut_weights/pallas_call | solution.py:38
  24.6 1.4 %collective-permute-done.2 = bf16[384,256]{1,0:T(8,128)(2,1)S(1)} collective-permute-done((bf16[384,256]{1,0:T(8,128)(2,1)S(1)}, bf16[384,256]{1,0:T(8,128)(2,1)S(1)}, u32[]{:S(2)}, u32[]{:S(2)}) %collective-permute-start.2) | collective-permute-done | bytes 196640 | tf_op jit(solution)/shard_map/ppermute | solution.py:574
  26.1 7.7 %collective-permute-done.3 = bf16[384,256]{1,0:T(8,128)(2,1)S(1)} collective-permute-done((bf16[384,256]{1,0:T(8,128)(2,1)S(1)}, bf16[384,256]{1,0:T(8,128)(2,1)S(1)}, u32[]{:S(2)}, u32[]{:S(2)}) %collective-permute-start.3) | collective-permute-done | bytes 196640 | tf_op jit(solution)/shard_map/ppermute | solution.py:574
  33.8 4.3 %attention.3 = (f32[3,8,256]{2,1,0:T(8,128)S(1)}, f32[3,144,256]{2,1,0:T(8,128)S(1)}) custom-call(s32[10]{0:T(128)S(1)} %pad_add_fusion.1.table, bf16[2,384,128]{2,1,0:T(8,128)(2,1)S(1)} %get-tuple-element.42.refs_0_, bf16[1,384,256]{2,1,0:T(8,128)(2,1)S(1)} %bitcast.16, bf16[1,384,256]{2,1,0:T(8,128)(2,1)S(1)} %bitcast.18, ...), custom_call_target="tpu_custom_call" | custom-call | flops 1 | bytes 1 | tf_op jit(solution)/shard_map/attention/pallas_call | solution.py:38
  38.1 7.6 %collective-permute-done.1.refs_2_.refs_1_ = bf16[192,4608]{1,0:T(8,128)(2,1)S(1)} collective-permute-done((bf16[192,4608]{1,0:T(8,128)(2,1)}, bf16[192,4608]{1,0:T(8,128)(2,1)S(1)}, u32[]{:S(2)}, u32[]{:S(2)}) %collective-permute-start.1) | collective-permute-done | bytes 1769504 | tf_op jit(solution)/shard_map/ppermute | solution.py:567
  45.7 1.8 %collective-permute-start.10 = (bf16[32,4608]{1,0:T(8,128)(2,1)}, bf16[32,4608]{1,0:T(8,128)(2,1)S(1)}, u32[]{:S(2)}, u32[]{:S(2)}) collective-permute-start(bf16[32,4608]{1,0:T(8,128)(2,1)} %get-tuple-element.53), channel_id=1, source_target_pairs={{0,8},{4,12},{8,0},{12,4},{1,9},{5,13},{9,1},{13,5},{2,10},{6,14},... | collective-permute-start | bytes 884744 | tf_op jit(solution)/shard_map/ppermute | solution.py:567
  47.4 1.9 %collective-permute-done.5.refs_3_.refs_2_ = bf16[192,4608]{1,0:T(8,128)(2,1)S(1)} collective-permute-done((bf16[192,4608]{1,0:T(8,128)(2,1)S(1)}, bf16[192,4608]{1,0:T(8,128)(2,1)S(1)}, u32[]{:S(2)}, u32[]{:S(2)}) %collective-permute-start.5) | collective-permute-done | bytes 1769504 | tf_op jit(solution)/shard_map/ppermute | solution.py:567
  49.4 3.8 %project_kv.1 = bf16[384,256]{1,0:T(8,128)(2,1)S(1)} custom-call(f32[768,256]{1,0:T(8,128)} %pad_maximum_fusion.trig, bf16[4608,128]{1,0:T(8,128)(2,1)} %refs_0_.4, bf16[4608,128]{1,0:T(8,128)(2,1)} %refs_1_.3, bf16[192,4608]{1,0:T(8,128)(2,1)S(1)} %collective-permute-done.1.refs_2_.refs_1_, bf16[192,4608]{1,0:T(8,128)(2,1)S(1)} %collective-permute-done.5.refs_3_.refs_2_), custom_call_target="tpu_custom_call" | custom-call | flops 1 | bytes 1 | tf_op jit(solution)/shard_map/project_kv/pallas_call | solution.py:38
  53.2 1.9 %collective-permute-start.6 = (bf16[384,256]{1,0:T(8,128)(2,1)S(1)}, bf16[384,256]{1,0:T(8,128)(2,1)S(1)}, u32[]{:S(2)}, u32[]{:S(2)}) collective-permute-start(bf16[384,256]{1,0:T(8,128)(2,1)S(1)} %project_kv.1), channel_id=1, source_target_pairs={{0,1},{1,2},{2,3},{3,0},{4,5},{5,6},{6,7},{7,4},{8,9},{9,10},{10,1... | collective-permute-start | bytes 589832 | tf_op jit(solution)/shard_map/ppermute | solution.py:583
  55.1 1.5 %collective-permute-start.11 = (bf16[32,4608]{1,0:T(8,128)(2,1)S(1)}, bf16[32,4608]{1,0:T(8,128)(2,1)S(1)}, u32[]{:S(2)}, u32[]{:S(2)}) collective-permute-start(bf16[32,4608]{1,0:T(8,128)(2,1)S(1)} %copy-done.4), channel_id=1, source_target_pairs={{0,8},{4,12},{8,0},{12,4},{1,9},{5,13},{9,1},{13,5},{2,10},{6,14},... | collective-permute-start | bytes 884744 | tf_op jit(solution)/shard_map/ppermute | solution.py:567
  56.6 3.7 %project_q.1.refs_1_ = bf16[2,384,128]{2,1,0:T(8,128)(2,1)S(1)} custom-call(f32[768,256]{1,0:T(8,128)} %pad_maximum_fusion.trig, bf16[4608,256]{1,0:T(8,128)(2,1)} %refs_0_.5, bf16[192,4608]{1,0:T(8,128)(2,1)S(1)} %collective-permute-done.1.refs_2_.refs_1_, bf16[192,4608]{1,0:T(8,128)(2,1)S(1)} %collective-permute-done.5.refs_3_.refs_2_), custom_call_target="tpu_custom_call" | custom-call | flops 1 | bytes 1 | tf_op jit(solution)/shard_map/project_q/pallas_call | solution.py:38
  60.4 1.6 %collective-permute-start.12 = (bf16[32,4608]{1,0:T(8,128)(2,1)S(1)}, bf16[32,4608]{1,0:T(8,128)(2,1)S(1)}, u32[]{:S(2)}, u32[]{:S(2)}) collective-permute-start(bf16[32,4608]{1,0:T(8,128)(2,1)S(1)} %collective-permute-done.10.refs_0_), channel_id=1, source_target_pairs={{0,16},{16,0},{1,17},{17,1},{2,18},{18,2},{3,19},{19,3},{4,20},{20... | collective-permute-start | bytes 884744 | tf_op jit(solution)/shard_map/ppermute | solution.py:567
  64.0 4.9 %collective-permute-done.12.refs_4_ = bf16[32,4608]{1,0:T(8,128)(2,1)S(1)} collective-permute-done((bf16[32,4608]{1,0:T(8,128)(2,1)S(1)}, bf16[32,4608]{1,0:T(8,128)(2,1)S(1)}, u32[]{:S(2)}, u32[]{:S(2)}) %collective-permute-start.12) | collective-permute-done | bytes 294944 | tf_op jit(solution)/shard_map/ppermute | solution.py:567
  68.9 1.6 %collective-permute-done.7 = bf16[384,256]{1,0:T(8,128)(2,1)S(1)} collective-permute-done((bf16[384,256]{1,0:T(8,128)(2,1)S(1)}, bf16[384,256]{1,0:T(8,128)(2,1)S(1)}, u32[]{:S(2)}, u32[]{:S(2)}) %collective-permute-start.7) | collective-permute-done | bytes 196640 | tf_op jit(solution)/shard_map/ppermute | solution.py:583
  72.0 3.4 %attention.4 = (f32[3,8,256]{2,1,0:T(8,128)S(1)}, f32[3,144,256]{2,1,0:T(8,128)S(1)}, f32[3,8,256]{2,1,0:T(8,128)S(1)}, f32[3,144,256]{2,1,0:T(8,128)S(1)}) custom-call(s32[10]{0:T(128)S(1)} %pad_add_fusion.1.table, bf16[2,384,128]{2,1,0:T(8,128)(2,1)S(1)} %get-tuple-element.42.refs_0_, ...), custom_call_target="tpu_custom_call", output_to_operand_aliasing={{0}: (8, {}), {1}: (9, {})} | custom-call | flops 1 | bytes 1 | tf_op jit(solution)/shard_map/attention/pallas_call | solution.py:38
  75.5 3.8 %collective-permute-done.8 = bf16[384,256]{1,0:T(8,128)(2,1)S(1)} collective-permute-done((bf16[384,256]{1,0:T(8,128)(2,1)S(1)}, bf16[384,256]{1,0:T(8,128)(2,1)S(1)}, u32[]{:S(2)}, u32[]{:S(2)}) %collective-permute-start.8) | collective-permute-done | bytes 196640 | tf_op jit(solution)/shard_map/ppermute | solution.py:583
  80.1 1.3 %collective-permute-start.15 = (bf16[16,4608]{1,0:T(8,128)(2,1)S(1)}, bf16[16,4608]{1,0:T(8,128)(2,1)S(1)}, u32[]{:S(2)}, u32[]{:S(2)}) collective-permute-start(bf16[16,4608]{1,0:T(8,128)(2,1)S(1)} %copy-done.5), channel_id=1, source_target_pairs={{0,8},{4,12},{8,0},{12,4},{1,9},{5,13},{9,1},{13,5},{2,10},{6,14},... | collective-permute-start | bytes 442376 | tf_op jit(solution)/shard_map/ppermute | solution.py:567
  81.3 3.9 %attention.5 = (bf16[384,256]{1,0:T(8,128)(2,1)}, bf16[384,256]{1,0:T(8,128)(2,1)}, f32[3,8,256]{2,1,0:T(8,128)S(1)}, f32[3,144,256]{2,1,0:T(8,128)S(1)}, f32[3,...) custom-call(s32[10]{0:T(128)S(1)} %pad_add_fusion.1.table, ...), custom_call_target="tpu_custom_call", output_to_operand_aliasing={{2}: (7, {}), {3}: (8, {}), {4}: (9, {}), {5}: (10, {})} | custom-call | flops 1 | bytes 1 | tf_op jit(solution)/shard_map/attention/pallas_call | solution.py:38
  85.3 1.5 %collective-permute-start.9 = (bf16[384,256]{1,0:T(8,128)(2,1)}, bf16[384,256]{1,0:T(8,128)(2,1)S(1)}, u32[]{:S(2)}, u32[]{:S(2)}) collective-permute-start(bf16[384,256]{1,0:T(8,128)(2,1)} %get-tuple-element.51), channel_id=1, source_target_pairs={{0,8},{4,12},{8,0},{12,4},{1,9},{5,13},{9,1},{13,5},{2,10},{6,14},... | collective-permute-start | bytes 589832 | tf_op jit(solution)/shard_map/ppermute | solution.py:567
  88.0 3.4 %output_near.1.near = f32[384,4608]{1,0:T(8,128)S(1)} custom-call(bf16[384,256]{1,0:T(8,128)(2,1)} %get-tuple-element.52.left_hbm, bf16[256,4608]{1,0:T(8,128)(2,1)} %weights_hbm.1), custom_call_target="tpu_custom_call" | custom-call | flops 1 | bytes 1 | tf_op jit(solution)/shard_map/output_near/pallas_call | solution.py:38
  91.9 3.6 %output_send.1 = (bf16[192,4608]{1,0:T(8,128)(2,1)}, bf16[256,4608]{1,0:T(8,128)(2,1)S(1)}) custom-call(s32[10]{0:T(128)S(1)} %pad_add_fusion.1.table, bf16[384,256]{1,0:T(8,128)(2,1)S(1)} %collective-permute-done.9.left_hbm, f32[384,4608]{1,0:T(8,128)S(1)} %output_near.1.near, bf16[32,4608]{1,0:T(8,128)(2,1)S(1)} %collective-permute-done.10.refs_0_, ...), custom_call_target="tpu_custom_call" | custom-call | flops 1 | bytes 1 | tf_op jit(solution)/shard_map/output_send/pallas_call | solution.py:38
  95.6 1.7 %output_keep.1 = (f32[192,4608]{1,0:T(8,128)S(1)}, bf16[192,4608]{1,0:T(8,128)(2,1)S(1)}) custom-call(bf16[384,256]{1,0:T(8,128)(2,1)S(1)} %collective-permute-done.9.left_hbm, bf16[192,4608]{1,0:T(8,128)(2,1)} %hidden.3, f32[384,4608]{1,0:T(8,128)S(1)} %output_near.1.near, bf16[256,4608]{1,0:T(8,128)(2,1)S(1)} %get-tuple-element.62.weights), custom_call_target="tpu_custom_call" | custom-call | flops 1 | bytes 1 | tf_op jit(solution)/shard_map/output_keep/pallas_call | solution.py:38
  97.3 2.1 %collective-permute-done.18.received = bf16[192,4608]{1,0:T(8,128)(2,1)S(1)} collective-permute-done((bf16[192,4608]{1,0:T(8,128)(2,1)}, bf16[192,4608]{1,0:T(8,128)(2,1)S(1)}, u32[]{:S(2)}, u32[]{:S(2)}) %collective-permute-start.18) | collective-permute-done | bytes 1769504 | tf_op jit(solution)/shard_map/ppermute | solution.py:567
  99.5 2.6 %output_norm.1 = bf16[192,4608]{1,0:T(8,128)(2,1)} custom-call(bf16[192,4608]{1,0:T(8,128)(2,1)S(1)} %collective-permute-done.18.received, bf16[192,4608]{1,0:T(8,128)(2,1)S(1)} %get-tuple-element.63.hidden, f32[192,4608]{1,0:T(8,128)S(1)} %get-tuple-element.64.kept, f32[4608]{0:T(1024)} %gain.3), custom_call_target="tpu_custom_call" | custom-call | flops 1 | bytes 1 | tf_op jit(solution)/shard_map/output_norm/pallas_call | solution.py:38
  (41 shorter events, 9.7 us)
Async XLA Ops:
  0.0 6.3 %copy-start.2 = (s32[8]{0:T(128)S(1)}, s32[8]{0:T(128)}, u32[]{:S(2)}) copy-start(s32[8]{0:T(128)} %param.15) | copy-start | bytes 100
  3.1 6.2 %collective-permute-start = (bf16[192,4608]{1,0:T(8,128)(2,1)}, bf16[192,4608]{1,0:T(8,128)(2,1)S(1)}, u32[]{:S(2)}, u32[]{:S(2)}) collective-permute-start(bf16[192,4608]{1,0:T(8,128)(2,1)} %norm_rows.1.refs_3_), channel_id=1, source_target_pairs={{0,4},{4,0},{8,12},{12,8},{1,5},{5,1},{9,13},{13,9},{2,6},{6,2},{1... | collective-permute-start | bytes 5308424 | tf_op jit(solution)/shard_map/ppermute | solution.py:567
  3.7 42.0 %collective-permute-start.1 = (bf16[192,4608]{1,0:T(8,128)(2,1)}, bf16[192,4608]{1,0:T(8,128)(2,1)S(1)}, u32[]{:S(2)}, u32[]{:S(2)}) collective-permute-start(bf16[192,4608]{1,0:T(8,128)(2,1)} %norm_rows.1.refs_3_), channel_id=1, source_target_pairs={{0,8},{4,12},{8,0},{12,4},{1,9},{5,13},{9,1},{13,5},{2,10},{6,14},... | collective-permute-start | bytes 5308424 | tf_op jit(solution)/shard_map/ppermute | solution.py:567
  9.4 1.2 %copy-start = (bf16[192,4608]{1,0:T(8,128)(2,1)}, bf16[192,4608]{1,0:T(8,128)(2,1)S(1)}, u32[]{:S(2)}) copy-start(bf16[192,4608]{1,0:T(8,128)(2,1)S(1)} %collective-permute-done.refs_4_) | copy-start | bytes 5308420
  10.6 1.5 %copy-start.1 = (bf16[192,4608]{1,0:T(8,128)(2,1)S(1)}, bf16[192,4608]{1,0:T(8,128)(2,1)}, u32[]{:S(2)}) copy-start(bf16[192,4608]{1,0:T(8,128)(2,1)} %copy-done) | copy-start | bytes 5308420
  16.3 9.7 %collective-permute-start.2 = (bf16[384,256]{1,0:T(8,128)(2,1)S(1)}, bf16[384,256]{1,0:T(8,128)(2,1)S(1)}, u32[]{:S(2)}, u32[]{:S(2)}) collective-permute-start(bf16[384,256]{1,0:T(8,128)(2,1)S(1)} %get-tuple-element.36), channel_id=1, source_target_pairs={{0,1},{1,2},{2,3},{3,0},{4,5},{5,6},{6,7},{7,4},{8,9},{9,10},{10,1... | collective-permute-start | bytes 589832 | tf_op jit(solution)/shard_map/ppermute | solution.py:574
  18.0 15.8 %collective-permute-start.3 = (bf16[384,256]{1,0:T(8,128)(2,1)S(1)}, bf16[384,256]{1,0:T(8,128)(2,1)S(1)}, u32[]{:S(2)}, u32[]{:S(2)}) collective-permute-start(bf16[384,256]{1,0:T(8,128)(2,1)S(1)} %get-tuple-element.36), channel_id=1, source_target_pairs={{0,2},{1,3},{2,0},{3,1},{4,6},{5,7},{6,4},{7,5},{8,10},{9,11},{10,... | collective-permute-start | bytes 589832 | tf_op jit(solution)/shard_map/ppermute | solution.py:574
  20.6 13.2 %collective-permute-start.4 = (bf16[384,256]{1,0:T(8,128)(2,1)S(1)}, bf16[384,256]{1,0:T(8,128)(2,1)S(1)}, u32[]{:S(2)}, u32[]{:S(2)}) collective-permute-start(bf16[384,256]{1,0:T(8,128)(2,1)S(1)} %get-tuple-element.36), channel_id=1, source_target_pairs={{0,3},{1,0},{2,1},{3,2},{4,7},{5,4},{6,5},{7,6},{8,11},{9,8},{10,9... | collective-permute-start | bytes 589832 | tf_op jit(solution)/shard_map/ppermute | solution.py:574
  45.7 9.4 %copy-start.4 = (bf16[32,4608]{1,0:T(8,128)(2,1)S(1)}, bf16[32,4608]{1,0:T(8,128)(2,1)}, u32[]{:S(2)}) copy-start(bf16[32,4608]{1,0:T(8,128)(2,1)} %get-tuple-element.54) | copy-start | bytes 884740
  45.7 3.7 %collective-permute-start.5 = (bf16[192,4608]{1,0:T(8,128)(2,1)S(1)}, bf16[192,4608]{1,0:T(8,128)(2,1)S(1)}, u32[]{:S(2)}, u32[]{:S(2)}) collective-permute-start(bf16[192,4608]{1,0:T(8,128)(2,1)S(1)} %collective-permute-done.1.refs_2_.refs_1_), channel_id=1, source_target_pairs={{0,4},{4,0},{8,12},{12,8},{1,5},{5,1},{9,13},{13,9},{2,6},{6,2},{1... | collective-permute-start | bytes 5308424 | tf_op jit(solution)/shard_map/ppermute | solution.py:567
  45.7 14.7 %collective-permute-start.10 = (bf16[32,4608]{1,0:T(8,128)(2,1)}, bf16[32,4608]{1,0:T(8,128)(2,1)S(1)}, u32[]{:S(2)}, u32[]{:S(2)}) collective-permute-start(bf16[32,4608]{1,0:T(8,128)(2,1)} %get-tuple-element.53), channel_id=1, source_target_pairs={{0,8},{4,12},{8,0},{12,4},{1,9},{5,13},{9,1},{13,5},{2,10},{6,14},... | collective-permute-start | bytes 884744 | tf_op jit(solution)/shard_map/ppermute | solution.py:567
  53.2 10.3 %copy-start.3 = (bf16[48,4608]{1,0:T(8,128)(2,1)S(1)}, bf16[48,4608]{1,0:T(8,128)(2,1)}, u32[]{:S(2)}) copy-start(bf16[48,4608]{1,0:T(8,128)(2,1)} %get-tuple-element.57) | copy-start | bytes 1327108
  53.2 9.1 %collective-permute-start.6 = (bf16[384,256]{1,0:T(8,128)(2,1)S(1)}, bf16[384,256]{1,0:T(8,128)(2,1)S(1)}, u32[]{:S(2)}, u32[]{:S(2)}) collective-permute-start(bf16[384,256]{1,0:T(8,128)(2,1)S(1)} %project_kv.1), channel_id=1, source_target_pairs={{0,1},{1,2},{2,3},{3,0},{4,5},{5,6},{6,7},{7,4},{8,9},{9,10},{10,1... | collective-permute-start | bytes 589832 | tf_op jit(solution)/shard_map/ppermute | solution.py:583
  55.1 8.9 %collective-permute-start.11 = (bf16[32,4608]{1,0:T(8,128)(2,1)S(1)}, bf16[32,4608]{1,0:T(8,128)(2,1)S(1)}, u32[]{:S(2)}, u32[]{:S(2)}) collective-permute-start(bf16[32,4608]{1,0:T(8,128)(2,1)S(1)} %copy-done.4), channel_id=1, source_target_pairs={{0,8},{4,12},{8,0},{12,4},{1,9},{5,13},{9,1},{13,5},{2,10},{6,14},... | collective-permute-start | bytes 884744 | tf_op jit(solution)/shard_map/ppermute | solution.py:567
  60.4 19.7 %copy-start.5 = (bf16[16,4608]{1,0:T(8,128)(2,1)S(1)}, bf16[16,4608]{1,0:T(8,128)(2,1)}, u32[]{:S(2)}) copy-start(bf16[16,4608]{1,0:T(8,128)(2,1)} %get-tuple-element.59) | copy-start | bytes 442372
  60.4 8.6 %collective-permute-start.12 = (bf16[32,4608]{1,0:T(8,128)(2,1)S(1)}, bf16[32,4608]{1,0:T(8,128)(2,1)S(1)}, u32[]{:S(2)}, u32[]{:S(2)}) collective-permute-start(bf16[32,4608]{1,0:T(8,128)(2,1)S(1)} %collective-permute-done.10.refs_0_), channel_id=1, source_target_pairs={{0,16},{16,0},{1,17},{17,1},{2,18},{18,2},{3,19},{19,3},{4,20},{20... | collective-permute-start | bytes 884744 | tf_op jit(solution)/shard_map/ppermute | solution.py:567
  62.3 8.2 %collective-permute-start.7 = (bf16[384,256]{1,0:T(8,128)(2,1)S(1)}, bf16[384,256]{1,0:T(8,128)(2,1)S(1)}, u32[]{:S(2)}, u32[]{:S(2)}) collective-permute-start(bf16[384,256]{1,0:T(8,128)(2,1)S(1)} %collective-permute-done.6), channel_id=1, source_target_pairs={{0,1},{1,2},{2,3},{3,0},{4,5},{5,6},{6,7},{7,4},{8,9},{9,10},{10,1... | collective-permute-start | bytes 589832 | tf_op jit(solution)/shard_map/ppermute | solution.py:583
  63.5 11.9 %collective-permute-start.13 = (bf16[48,4608]{1,0:T(8,128)(2,1)S(1)}, bf16[48,4608]{1,0:T(8,128)(2,1)S(1)}, u32[]{:S(2)}, u32[]{:S(2)}) collective-permute-start(bf16[48,4608]{1,0:T(8,128)(2,1)S(1)} %copy-done.3), channel_id=1, source_target_pairs={{0,8},{4,12},{8,0},{12,4},{1,9},{5,13},{9,1},{13,5},{2,10},{6,14},... | collective-permute-start | bytes 1327112 | tf_op jit(solution)/shard_map/ppermute | solution.py:567
  70.6 8.7 %collective-permute-start.14 = (bf16[32,4608]{1,0:T(8,128)(2,1)S(1)}, bf16[32,4608]{1,0:T(8,128)(2,1)S(1)}, u32[]{:S(2)}, u32[]{:S(2)}) collective-permute-start(bf16[32,4608]{1,0:T(8,128)(2,1)S(1)} %collective-permute-done.11.refs_1_), channel_id=1, source_target_pairs={{0,16},{16,0},{1,17},{17,1},{2,18},{18,2},{3,19},{19,3},{4,20},{20... | collective-permute-start | bytes 884744 | tf_op jit(solution)/shard_map/ppermute | solution.py:567
  71.8 7.5 %collective-permute-start.8 = (bf16[384,256]{1,0:T(8,128)(2,1)S(1)}, bf16[384,256]{1,0:T(8,128)(2,1)S(1)}, u32[]{:S(2)}, u32[]{:S(2)}) collective-permute-start(bf16[384,256]{1,0:T(8,128)(2,1)S(1)} %collective-permute-done.7), channel_id=1, source_target_pairs={{0,1},{1,2},{2,3},{3,0},{4,5},{5,6},{6,7},{7,4},{8,9},{9,10},{10,1... | collective-permute-start | bytes 589832 | tf_op jit(solution)/shard_map/ppermute | solution.py:583
  79.3 12.6 %collective-permute-start.16 = (bf16[48,4608]{1,0:T(8,128)(2,1)S(1)}, bf16[48,4608]{1,0:T(8,128)(2,1)S(1)}, u32[]{:S(2)}, u32[]{:S(2)}) collective-permute-start(bf16[48,4608]{1,0:T(8,128)(2,1)S(1)} %collective-permute-done.13.refs_2_), channel_id=1, source_target_pairs={{0,16},{16,0},{1,17},{17,1},{2,18},{18,2},{3,19},{19,3},{4,20},{20... | collective-permute-start | bytes 1327112 | tf_op jit(solution)/shard_map/ppermute | solution.py:567
  80.1 6.7 %collective-permute-start.15 = (bf16[16,4608]{1,0:T(8,128)(2,1)S(1)}, bf16[16,4608]{1,0:T(8,128)(2,1)S(1)}, u32[]{:S(2)}, u32[]{:S(2)}) collective-permute-start(bf16[16,4608]{1,0:T(8,128)(2,1)S(1)} %copy-done.5), channel_id=1, source_target_pairs={{0,8},{4,12},{8,0},{12,4},{1,9},{5,13},{9,1},{13,5},{2,10},{6,14},... | collective-permute-start | bytes 442376 | tf_op jit(solution)/shard_map/ppermute | solution.py:567
  85.3 6.6 %collective-permute-start.9 = (bf16[384,256]{1,0:T(8,128)(2,1)}, bf16[384,256]{1,0:T(8,128)(2,1)S(1)}, u32[]{:S(2)}, u32[]{:S(2)}) collective-permute-start(bf16[384,256]{1,0:T(8,128)(2,1)} %get-tuple-element.51), channel_id=1, source_target_pairs={{0,8},{4,12},{8,0},{12,4},{1,9},{5,13},{9,1},{13,5},{2,10},{6,14},... | collective-permute-start | bytes 589832 | tf_op jit(solution)/shard_map/ppermute | solution.py:567
  86.8 5.1 %collective-permute-start.17 = (bf16[16,4608]{1,0:T(8,128)(2,1)S(1)}, bf16[16,4608]{1,0:T(8,128)(2,1)S(1)}, u32[]{:S(2)}, u32[]{:S(2)}) collective-permute-start(bf16[16,4608]{1,0:T(8,128)(2,1)S(1)} %collective-permute-done.15.refs_3_), channel_id=1, source_target_pairs={{0,16},{16,0},{1,17},{17,1},{2,18},{18,2},{3,19},{19,3},{4,20},{20... | collective-permute-start | bytes 442376 | tf_op jit(solution)/shard_map/ppermute | solution.py:567
  95.5 4.0 %collective-permute-start.18 = (bf16[192,4608]{1,0:T(8,128)(2,1)}, bf16[192,4608]{1,0:T(8,128)(2,1)S(1)}, u32[]{:S(2)}, u32[]{:S(2)}) collective-permute-start(bf16[192,4608]{1,0:T(8,128)(2,1)} %get-tuple-element.61), channel_id=1, source_target_pairs={{0,4},{4,0},{8,12},{12,8},{1,5},{5,1},{9,13},{13,9},{2,6},{6,2},{1... | collective-permute-start | bytes 5308424 | tf_op jit(solution)/shard_map/ppermute | solution.py:567

commit v3 on v2

--- a/solution.py
+++ b/solution.py
@@ -152,7 +152,7 @@
             q[head] = (rotated(head * HD) * factor).astype(jnp.bfloat16)
 
 
-def qkv(parts, weights, kinds, trig, first, chunks=6):
+def qkv(parts, weights, kinds, trig, first, chunks=3):
     given = [weights["qkv".index(kind)] for kind in kinds]
     total, width = sum(part.shape[0] for part in parts), parts[0].shape[1]
     columns = sum(weight.shape[1] for weight in given)
@@ -620,17 +620,16 @@
     q_near, kv_near = qkv([own, Came(partner)], weights, "qkv", trig, 0)
     near = along_line(kv_near)
     half = w_out.shape[0] // 2
-    w_cut = cut(table, group_at, after(w_out, kv_near), [half // 4, half // 4, half * 3 // 8, half // 8])
+    w_cut = cut(table, group_at, after(w_out, kv_near), [half // 4, half * 3 // 8, half // 4, half // 8])
     q_near = after(q_near, *w_cut)
     (near_state,) = attention(
         [Step(0, 0, others, same=0)], table, [q_near], [near_chunk], [near], [near_chunk], [None]
     )
 
     away = after(away, *near_state)
-    rows_far = [Came(away), Came(flipped(away, "tp", 1))]
-    (kv_far,) = qkv(rows_far, weights, "kv", trig, block_rows)
-    rows_far[1] = Came(after(rows_far[1].array, kv_far))
-    (q_far,) = qkv(rows_far, weights, "q", trig, block_rows)
+    q_far, kv_far = qkv(
+        [Came(away), Came(flipped(away, "tp", 1))], weights, "qkv", trig, block_rows
+    )
     far = along_ring(kv_far)
 
     fetched = lambda piece, *others: flipped(after(piece, *others), "tp", 2)

time: 102 us -> 105 us (1.029)
  waiting for transfers between devices: 32.1 us -> 40.3 us
  local copies, waits for them, and re-layouts: 2.72 us -> 0.01 us
  starting transfers between devices: 23.4 us -> 21.3 us
    ppermute x3, waiting for transfers between devices: 5.8 us -> 12.8 us  [along_ring(): part = lax.ppermute(part, 'seq', [(i, (i + 1) % size) for i in range(size)])]
    unnamed x12 -> x6, local copies, waits for them, and re-layouts: 2.72 us -> 0.01 us
    ppermute x3, starting transfers between devices: 3.28 us -> 1.87 us  [along_ring(): part = lax.ppermute(part, 'seq', [(i, (i + 1) % size) for i in range(size)])]
    ppermute x13, waiting for transfers between devices: 17.1 us -> 18.3 us  [flipped(): return lax.ppermute(array, axis, [(i, i ^ bit) for i in range(size)])]
    pallas_call x12 -> x11, Pallas kernels: 40.5 us -> 40 us  [call(): pl.pallas_call(kernel, in_specs=in_specs, out_specs=[spec for _, _, spec...]
  transfers between devices with their start and end apart: 19 -> 19, of which waited for: 10 -> 14; matrix products, arithmetic and copies ran while one was open for 3% -> 3% of each run, Pallas kernels for 31% -> 29%
where the time goes in v3:
time: 105 us
  waiting for transfers between devices  40.3 us (38%)
  Pallas kernels  40 us (38%)
  starting transfers between devices  21.3 us (20%)
  other arithmetic  3.15 us (3%)
    pallas_call x11, Pallas kernels, call(): pl.pallas_call(kernel, in_specs=in_specs, out_specs=[spec for _, _, spec...  40 us
    ppermute x13, waiting for transfers between devices, flipped(): return lax.ppermute(array, axis, [(i, i ^ bit) for i in range(size)])  18.3 us
    ppermute x13, starting transfers between devices, flipped(): return lax.ppermute(array, axis, [(i, i ^ bit) for i in range(size)])  13.8 us
    ppermute x3, waiting for transfers between devices, along_ring(): part = lax.ppermute(part, 'seq', [(i, (i + 1) % size) for i in range(size)])  12.8 us
    ppermute x3, waiting for transfers between devices, along_line(): lax.ppermute(array, 'seq', [(i, (i + by) % size) for i in range(size)])  9.14 us
    ppermute x3, starting transfers between devices, along_line(): lax.ppermute(array, 'seq', [(i, (i + by) % size) for i in range(size)])  5.56 us
  transfers between devices with their start and end apart: 19, of which 14 were waited for; matrix products, arithmetic and copies ran while one was open for 3% of the time, Pallas kernels for 29%

profile of v3, /device:TPU:0, one launch (start us, length us, event | category | flops | bytes accessed | tf_op | source)
XLA Modules:
  0.0 105.0 jit_solution(8860469200251025789)
XLA Ops:
  0.0 3.1 %norm_rows.1.refs_3_ = bf16[192,4608]{1,0:T(8,128)(2,1)} custom-call(bf16[192,4608]{1,0:T(8,128)(2,1)} %hidden.3, f32[4608]{0:T(1024)} %gain.2), custom_call_target="tpu_custom_call" | custom-call | flops 1 | bytes 1 | tf_op jit(solution)/shard_map/norm_rows/pallas_call | solution.py:38
  3.7 2.6 %collective-permute-start.1 = (bf16[192,4608]{1,0:T(8,128)(2,1)}, bf16[192,4608]{1,0:T(8,128)(2,1)S(1)}, u32[]{:S(2)}, u32[]{:S(2)}) collective-permute-start(bf16[192,4608]{1,0:T(8,128)(2,1)} %norm_rows.1.refs_3_), channel_id=1, source_target_pairs={{0,8},{4,12},{8,0},{12,4},{1,9},{5,13},{9,1},{13,5},{2,10},{6,14},... | collective-permute-start | bytes 5308424 | tf_op jit(solution)/shard_map/ppermute | solution.py:567
  6.7 1.4 %multiply_cosine_fusion = (f32[768,64]{1,0:T(8,128)S(1)}, f32[768,64]{1,0:T(8,128)S(1)}, f32[768,64]{1,0:T(8,128)S(1)}) fusion(f32[768]{0:T(1024)S(1)} %add_convert_fusion, f32[64]{0:T(128)S(1)} %multiply_power_fusion), kind=kLoop, calls=%fused_computation.2 | loop fusion | flops 98304 | bytes 593152 | tf_op jit(solution)/shard_map/cos | solution.py:556
  8.1 1.3 %pad_maximum_fusion.trig = f32[768,256]{1,0:T(8,128)} fusion(f32[768,64]{1,0:T(8,128)S(1)} %get-tuple-element.71, f32[768,64]{1,0:T(8,128)S(1)} %get-tuple-element.70, f32[768,64]{1,0:T(8,128)S(1)} %get-tuple-element.69), kind=kLoop, calls=%fused_computation | loop fusion | flops 589824 | bytes 1376256 | tf_op jit(solution)/shard_map/concatenate | solution.py:557
  9.4 4.9 %project_qkv.2 = (bf16[2,384,128]{2,1,0:T(8,128)(2,1)S(1)}, bf16[384,256]{1,0:T(8,128)(2,1)S(1)}) custom-call(f32[768,256]{1,0:T(8,128)} %pad_maximum_fusion.trig, bf16[4608,256]{1,0:T(8,128)(2,1)} %refs_0_.3, bf16[4608,128]{1,0:T(8,128)(2,1)} %refs_1_.3, bf16[4608,128]{1,0:T(8,128)(2,1)} %refs_2_.3, bf16[192,4608]{1,0:T(8,128)(2,1)} %norm_rows.1.refs_3_, ...), custom_call_target="tpu_custom_call" | custom-call | flops 1 | bytes 1 | tf_op jit(solution)/shard_map/project_qkv/pallas_call | solution.py:38
  14.3 1.6 %collective-permute-start.2 = (bf16[384,256]{1,0:T(8,128)(2,1)S(1)}, bf16[384,256]{1,0:T(8,128)(2,1)S(1)}, u32[]{:S(2)}, u32[]{:S(2)}) collective-permute-start(bf16[384,256]{1,0:T(8,128)(2,1)S(1)} %get-tuple-element.37), channel_id=1, source_target_pairs={{0,1},{1,2},{2,3},{3,0},{4,5},{5,6},{6,7},{7,4},{8,9},{9,10},{10,1... | collective-permute-start | bytes 589832 | tf_op jit(solution)/shard_map/ppermute | solution.py:574
  16.0 2.6 %collective-permute-start.3 = (bf16[384,256]{1,0:T(8,128)(2,1)S(1)}, bf16[384,256]{1,0:T(8,128)(2,1)S(1)}, u32[]{:S(2)}, u32[]{:S(2)}) collective-permute-start(bf16[384,256]{1,0:T(8,128)(2,1)S(1)} %get-tuple-element.37), channel_id=1, source_target_pairs={{0,2},{1,3},{2,0},{3,1},{4,6},{5,7},{6,4},{7,5},{8,10},{9,11},{10,... | collective-permute-start | bytes 589832 | tf_op jit(solution)/shard_map/ppermute | solution.py:574
  18.5 1.3 %collective-permute-start.4 = (bf16[384,256]{1,0:T(8,128)(2,1)S(1)}, bf16[384,256]{1,0:T(8,128)(2,1)S(1)}, u32[]{:S(2)}, u32[]{:S(2)}) collective-permute-start(bf16[384,256]{1,0:T(8,128)(2,1)S(1)} %get-tuple-element.37), channel_id=1, source_target_pairs={{0,3},{1,0},{2,1},{3,2},{4,7},{5,4},{6,5},{7,6},{8,11},{9,8},{10,9... | collective-permute-start | bytes 589832 | tf_op jit(solution)/shard_map/ppermute | solution.py:574
  20.0 2.7 %cut_weights.1 = (bf16[32,4608]{1,0:T(8,128)(2,1)}, bf16[48,4608]{1,0:T(8,128)(2,1)}, bf16[32,4608]{1,0:T(8,128)(2,1)}, bf16[16,4608]{1,0:T(8,128)(2,1)}) custom-call(s32[10]{0:T(128)S(1)} %pad_add_fusion.1.table, bf16[256,4608]{1,0:T(8,128)(2,1)} %weights_hbm.1), custom_call_target="tpu_custom_call" | custom-call | flops 1 | bytes 1 | tf_op jit(solution)/shard_map/cut_weights/pallas_call | solution.py:38
  22.6 1.4 %collective-permute-done.2 = bf16[384,256]{1,0:T(8,128)(2,1)S(1)} collective-permute-done((bf16[384,256]{1,0:T(8,128)(2,1)S(1)}, bf16[384,256]{1,0:T(8,128)(2,1)S(1)}, u32[]{:S(2)}, u32[]{:S(2)}) %collective-permute-start.2) | collective-permute-done | bytes 196640 | tf_op jit(solution)/shard_map/ppermute | solution.py:574
  24.1 7.7 %collective-permute-done.3 = bf16[384,256]{1,0:T(8,128)(2,1)S(1)} collective-permute-done((bf16[384,256]{1,0:T(8,128)(2,1)S(1)}, bf16[384,256]{1,0:T(8,128)(2,1)S(1)}, u32[]{:S(2)}, u32[]{:S(2)}) %collective-permute-start.3) | collective-permute-done | bytes 196640 | tf_op jit(solution)/shard_map/ppermute | solution.py:574
  31.8 3.6 %attention.3 = (f32[3,8,256]{2,1,0:T(8,128)S(1)}, f32[3,144,256]{2,1,0:T(8,128)S(1)}) custom-call(s32[10]{0:T(128)S(1)} %pad_add_fusion.1.table, bf16[2,384,128]{2,1,0:T(8,128)(2,1)S(1)} %get-tuple-element.43.refs_0_, bf16[1,384,256]{2,1,0:T(8,128)(2,1)S(1)} %bitcast.14, bf16[1,384,256]{2,1,0:T(8,128)(2,1)S(1)} %bitcast.16, ...), custom_call_target="tpu_custom_call" | custom-call | flops 1 | bytes 1 | tf_op jit(solution)/shard_map/attention/pallas_call | solution.py:38
  35.4 10.2 %collective-permute-done.1.refs_3_ = bf16[192,4608]{1,0:T(8,128)(2,1)S(1)} collective-permute-done((bf16[192,4608]{1,0:T(8,128)(2,1)}, bf16[192,4608]{1,0:T(8,128)(2,1)S(1)}, u32[]{:S(2)}, u32[]{:S(2)}) %collective-permute-start.1) | collective-permute-done | bytes 1769504 | tf_op jit(solution)/shard_map/ppermute | solution.py:567
  45.7 1.8 %collective-permute-start.10 = (bf16[32,4608]{1,0:T(8,128)(2,1)}, bf16[32,4608]{1,0:T(8,128)(2,1)S(1)}, u32[]{:S(2)}, u32[]{:S(2)}) collective-permute-start(bf16[32,4608]{1,0:T(8,128)(2,1)} %get-tuple-element.55), channel_id=1, source_target_pairs={{0,8},{4,12},{8,0},{12,4},{1,9},{5,13},{9,1},{13,5},{2,10},{6,14},... | collective-permute-start | bytes 884744 | tf_op jit(solution)/shard_map/ppermute | solution.py:567
  47.7 1.7 %collective-permute-done.5.refs_4_ = bf16[192,4608]{1,0:T(8,128)(2,1)S(1)} collective-permute-done((bf16[192,4608]{1,0:T(8,128)(2,1)S(1)}, bf16[192,4608]{1,0:T(8,128)(2,1)S(1)}, u32[]{:S(2)}, u32[]{:S(2)}) %collective-permute-start.5) | collective-permute-done | bytes 1769504 | tf_op jit(solution)/shard_map/ppermute | solution.py:567
  49.4 4.3 %project_qkv.3 = (bf16[2,384,128]{2,1,0:T(8,128)(2,1)S(1)}, bf16[384,256]{1,0:T(8,128)(2,1)S(1)}) custom-call(f32[768,256]{1,0:T(8,128)} %pad_maximum_fusion.trig, bf16[4608,256]{1,0:T(8,128)(2,1)} %refs_0_.3, bf16[4608,128]{1,0:T(8,128)(2,1)} %refs_1_.3, bf16[4608,128]{1,0:T(8,128)(2,1)} %refs_2_.3, bf16[192,4608]{1,0:T(8,128)(2,1)S(1)} %collective-permute-done.1.refs_3_, ...), custom_call_target="tpu_custom_call" | custom-call | flops 1 | bytes 1 | tf_op jit(solution)/shard_map/project_qkv/pallas_call | solution.py:38
  53.7 1.9 %collective-permute-start.6 = (bf16[384,256]{1,0:T(8,128)(2,1)S(1)}, bf16[384,256]{1,0:T(8,128)(2,1)S(1)}, u32[]{:S(2)}, u32[]{:S(2)}) collective-permute-start(bf16[384,256]{1,0:T(8,128)(2,1)S(1)} %get-tuple-element.48), channel_id=1, source_target_pairs={{0,1},{1,2},{2,3},{3,0},{4,5},{5,6},{6,7},{7,4},{8,9},{9,10},{10,1... | collective-permute-start | bytes 589832 | tf_op jit(solution)/shard_map/ppermute | solution.py:583
  55.7 1.7 %collective-permute-start.12 = (bf16[32,4608]{1,0:T(8,128)(2,1)S(1)}, bf16[32,4608]{1,0:T(8,128)(2,1)S(1)}, u32[]{:S(2)}, u32[]{:S(2)}) collective-permute-start(bf16[32,4608]{1,0:T(8,128)(2,1)S(1)} %collective-permute-done.10.refs_0_), channel_id=1, source_target_pairs={{0,16},{16,0},{1,17},{17,1},{2,18},{18,2},{3,19},{19,3},{4,20},{20... | collective-permute-start | bytes 884744 | tf_op jit(solution)/shard_map/ppermute | solution.py:567
  57.4 5.4 %collective-permute-done.6 = bf16[384,256]{1,0:T(8,128)(2,1)S(1)} collective-permute-done((bf16[384,256]{1,0:T(8,128)(2,1)S(1)}, bf16[384,256]{1,0:T(8,128)(2,1)S(1)}, u32[]{:S(2)}, u32[]{:S(2)}) %collective-permute-start.6) | collective-permute-done | bytes 196640 | tf_op jit(solution)/shard_map/ppermute | solution.py:583
  62.8 2.0 %collective-permute-done.11.refs_1_ = bf16[48,4608]{1,0:T(8,128)(2,1)S(1)} collective-permute-done((bf16[48,4608]{1,0:T(8,128)(2,1)}, bf16[48,4608]{1,0:T(8,128)(2,1)S(1)}, u32[]{:S(2)}, u32[]{:S(2)}) %collective-permute-start.11) | collective-permute-done | bytes 442400 | tf_op jit(solution)/shard_map/ppermute | solution.py:567
  64.8 6.2 %collective-permute-done.7 = bf16[384,256]{1,0:T(8,128)(2,1)S(1)} collective-permute-done((bf16[384,256]{1,0:T(8,128)(2,1)S(1)}, bf16[384,256]{1,0:T(8,128)(2,1)S(1)}, u32[]{:S(2)}, u32[]{:S(2)}) %collective-permute-start.7) | collective-permute-done | bytes 196640 | tf_op jit(solution)/shard_map/ppermute | solution.py:583
  71.0 1.2 %collective-permute-start.14 = (bf16[48,4608]{1,0:T(8,128)(2,1)S(1)}, bf16[48,4608]{1,0:T(8,128)(2,1)S(1)}, u32[]{:S(2)}, u32[]{:S(2)}) collective-permute-start(bf16[48,4608]{1,0:T(8,128)(2,1)S(1)} %collective-permute-done.11.refs_1_), channel_id=1, source_target_pairs={{0,16},{16,0},{1,17},{17,1},{2,18},{18,2},{3,19},{19,3},{4,20},{20... | collective-permute-start | bytes 1327112 | tf_op jit(solution)/shard_map/ppermute | solution.py:567
  72.3 1.5 %collective-permute-start.13 = (bf16[32,4608]{1,0:T(8,128)(2,1)S(1)}, bf16[32,4608]{1,0:T(8,128)(2,1)S(1)}, u32[]{:S(2)}, u32[]{:S(2)}) collective-permute-start(bf16[32,4608]{1,0:T(8,128)(2,1)S(1)} %copy-done.1), channel_id=1, source_target_pairs={{0,8},{4,12},{8,0},{12,4},{1,9},{5,13},{9,1},{13,5},{2,10},{6,14},... | collective-permute-start | bytes 884744 | tf_op jit(solution)/shard_map/ppermute | solution.py:567
  73.8 4.1 %attention.4 = (f32[3,8,256]{2,1,0:T(8,128)S(1)}, f32[3,144,256]{2,1,0:T(8,128)S(1)}, f32[3,8,256]{2,1,0:T(8,128)S(1)}, f32[3,144,256]{2,1,0:T(8,128)S(1)}) custom-call(s32[10]{0:T(128)S(1)} %pad_add_fusion.1.table, bf16[2,384,128]{2,1,0:T(8,128)(2,1)S(1)} %get-tuple-element.43.refs_0_, ...), custom_call_target="tpu_custom_call", output_to_operand_aliasing={{0}: (8, {}), {1}: (9, {})} | custom-call | flops 1 | bytes 1 | tf_op jit(solution)/shard_map/attention/pallas_call | solution.py:38
  77.9 1.9 %collective-permute-start.15 = (bf16[16,4608]{1,0:T(8,128)(2,1)S(1)}, bf16[16,4608]{1,0:T(8,128)(2,1)S(1)}, u32[]{:S(2)}, u32[]{:S(2)}) collective-permute-start(bf16[16,4608]{1,0:T(8,128)(2,1)S(1)} %copy-done.2), channel_id=1, source_target_pairs={{0,8},{4,12},{8,0},{12,4},{1,9},{5,13},{9,1},{13,5},{2,10},{6,14},... | collective-permute-start | bytes 442376 | tf_op jit(solution)/shard_map/ppermute | solution.py:567
  80.1 1.2 %collective-permute-done.8 = bf16[384,256]{1,0:T(8,128)(2,1)S(1)} collective-permute-done((bf16[384,256]{1,0:T(8,128)(2,1)S(1)}, bf16[384,256]{1,0:T(8,128)(2,1)S(1)}, u32[]{:S(2)}, u32[]{:S(2)}) %collective-permute-start.8) | collective-permute-done | bytes 196640 | tf_op jit(solution)/shard_map/ppermute | solution.py:583
  82.8 6.0 %attention.5 = (bf16[384,256]{1,0:T(8,128)(2,1)}, bf16[384,256]{1,0:T(8,128)(2,1)}, f32[3,8,256]{2,1,0:T(8,128)S(1)}, f32[3,144,256]{2,1,0:T(8,128)S(1)}, f32[3,...) custom-call(s32[10]{0:T(128)S(1)} %pad_add_fusion.1.table, ...), custom_call_target="tpu_custom_call", output_to_operand_aliasing={{2}: (7, {}), {3}: (8, {}), {4}: (9, {}), {5}: (10, {})} | custom-call | flops 1 | bytes 1 | tf_op jit(solution)/shard_map/attention/pallas_call | solution.py:38
  90.0 3.4 %output_near.1.near = f32[384,4608]{1,0:T(8,128)S(1)} custom-call(bf16[384,256]{1,0:T(8,128)(2,1)} %get-tuple-element.54.left_hbm, bf16[256,4608]{1,0:T(8,128)(2,1)} %weights_hbm.1), custom_call_target="tpu_custom_call" | custom-call | flops 1 | bytes 1 | tf_op jit(solution)/shard_map/output_near/pallas_call | solution.py:38
  94.7 3.6 %output_send.1 = (bf16[192,4608]{1,0:T(8,128)(2,1)}, bf16[256,4608]{1,0:T(8,128)(2,1)S(1)}) custom-call(s32[10]{0:T(128)S(1)} %pad_add_fusion.1.table, bf16[384,256]{1,0:T(8,128)(2,1)S(1)} %collective-permute-done.9.left_hbm, f32[384,4608]{1,0:T(8,128)S(1)} %output_near.1.near, bf16[32,4608]{1,0:T(8,128)(2,1)S(1)} %collective-permute-done.10.refs_0_, ...), custom_call_target="tpu_custom_call" | custom-call | flops 1 | bytes 1 | tf_op jit(solution)/shard_map/output_send/pallas_call | solution.py:38
  98.4 1.7 %output_keep.1 = (f32[192,4608]{1,0:T(8,128)S(1)}, bf16[192,4608]{1,0:T(8,128)(2,1)S(1)}) custom-call(bf16[384,256]{1,0:T(8,128)(2,1)S(1)} %collective-permute-done.9.left_hbm, bf16[192,4608]{1,0:T(8,128)(2,1)} %hidden.3, f32[384,4608]{1,0:T(8,128)S(1)} %output_near.1.near, bf16[256,4608]{1,0:T(8,128)(2,1)S(1)} %get-tuple-element.64.weights), custom_call_target="tpu_custom_call" | custom-call | flops 1 | bytes 1 | tf_op jit(solution)/shard_map/output_keep/pallas_call | solution.py:38
  100.1 2.1 %collective-permute-done.18.received = bf16[192,4608]{1,0:T(8,128)(2,1)S(1)} collective-permute-done((bf16[192,4608]{1,0:T(8,128)(2,1)}, bf16[192,4608]{1,0:T(8,128)(2,1)S(1)}, u32[]{:S(2)}, u32[]{:S(2)}) %collective-permute-start.18) | collective-permute-done | bytes 1769504 | tf_op jit(solution)/shard_map/ppermute | solution.py:567
  102.3 2.6 %output_norm.1 = bf16[192,4608]{1,0:T(8,128)(2,1)} custom-call(bf16[192,4608]{1,0:T(8,128)(2,1)S(1)} %collective-permute-done.18.received, bf16[192,4608]{1,0:T(8,128)(2,1)S(1)} %get-tuple-element.65.hidden, f32[192,4608]{1,0:T(8,128)S(1)} %get-tuple-element.66.kept, f32[4608]{0:T(1024)} %gain.3), custom_call_target="tpu_custom_call" | custom-call | flops 1 | bytes 1 | tf_op jit(solution)/shard_map/output_norm/pallas_call | solution.py:38
  (34 shorter events, 5.8 us)
Async XLA Ops:
  0.0 6.3 %copy-start = (s32[8]{0:T(128)S(1)}, s32[8]{0:T(128)}, u32[]{:S(2)}) copy-start(s32[8]{0:T(128)} %param.15) | copy-start | bytes 100
  3.1 6.2 %collective-permute-start = (bf16[192,4608]{1,0:T(8,128)(2,1)}, bf16[192,4608]{1,0:T(8,128)(2,1)}, u32[]{:S(2)}, u32[]{:S(2)}) collective-permute-start(bf16[192,4608]{1,0:T(8,128)(2,1)} %norm_rows.1.refs_3_), channel_id=1, source_target_pairs={{0,4},{4,0},{8,12},{12,8},{1,5},{5,1},{9,13},{13,9},{2,6},{6,2},{1... | collective-permute-start | bytes 5308424 | tf_op jit(solution)/shard_map/ppermute | solution.py:567
  3.7 42.0 %collective-permute-start.1 = (bf16[192,4608]{1,0:T(8,128)(2,1)}, bf16[192,4608]{1,0:T(8,128)(2,1)S(1)}, u32[]{:S(2)}, u32[]{:S(2)}) collective-permute-start(bf16[192,4608]{1,0:T(8,128)(2,1)} %norm_rows.1.refs_3_), channel_id=1, source_target_pairs={{0,8},{4,12},{8,0},{12,4},{1,9},{5,13},{9,1},{13,5},{2,10},{6,14},... | collective-permute-start | bytes 5308424 | tf_op jit(solution)/shard_map/ppermute | solution.py:567
  14.3 9.7 %collective-permute-start.2 = (bf16[384,256]{1,0:T(8,128)(2,1)S(1)}, bf16[384,256]{1,0:T(8,128)(2,1)S(1)}, u32[]{:S(2)}, u32[]{:S(2)}) collective-permute-start(bf16[384,256]{1,0:T(8,128)(2,1)S(1)} %get-tuple-element.37), channel_id=1, source_target_pairs={{0,1},{1,2},{2,3},{3,0},{4,5},{5,6},{6,7},{7,4},{8,9},{9,10},{10,1... | collective-permute-start | bytes 589832 | tf_op jit(solution)/shard_map/ppermute | solution.py:574
  16.0 15.8 %collective-permute-start.3 = (bf16[384,256]{1,0:T(8,128)(2,1)S(1)}, bf16[384,256]{1,0:T(8,128)(2,1)S(1)}, u32[]{:S(2)}, u32[]{:S(2)}) collective-permute-start(bf16[384,256]{1,0:T(8,128)(2,1)S(1)} %get-tuple-element.37), channel_id=1, source_target_pairs={{0,2},{1,3},{2,0},{3,1},{4,6},{5,7},{6,4},{7,5},{8,10},{9,11},{10,... | collective-permute-start | bytes 589832 | tf_op jit(solution)/shard_map/ppermute | solution.py:574
  18.5 13.2 %collective-permute-start.4 = (bf16[384,256]{1,0:T(8,128)(2,1)S(1)}, bf16[384,256]{1,0:T(8,128)(2,1)S(1)}, u32[]{:S(2)}, u32[]{:S(2)}) collective-permute-start(bf16[384,256]{1,0:T(8,128)(2,1)S(1)} %get-tuple-element.37), channel_id=1, source_target_pairs={{0,3},{1,0},{2,1},{3,2},{4,7},{5,4},{6,5},{7,6},{8,11},{9,8},{10,9... | collective-permute-start | bytes 589832 | tf_op jit(solution)/shard_map/ppermute | solution.py:574
  45.7 26.6 %copy-start.1 = (bf16[32,4608]{1,0:T(8,128)(2,1)S(1)}, bf16[32,4608]{1,0:T(8,128)(2,1)}, u32[]{:S(2)}) copy-start(bf16[32,4608]{1,0:T(8,128)(2,1)} %get-tuple-element.59) | copy-start | bytes 884740
  45.7 3.7 %collective-permute-start.5 = (bf16[192,4608]{1,0:T(8,128)(2,1)S(1)}, bf16[192,4608]{1,0:T(8,128)(2,1)S(1)}, u32[]{:S(2)}, u32[]{:S(2)}) collective-permute-start(bf16[192,4608]{1,0:T(8,128)(2,1)S(1)} %collective-permute-done.1.refs_3_), channel_id=1, source_target_pairs={{0,4},{4,0},{8,12},{12,8},{1,5},{5,1},{9,13},{13,9},{2,6},{6,2},{1... | collective-permute-start | bytes 5308424 | tf_op jit(solution)/shard_map/ppermute | solution.py:567
  45.7 10.0 %collective-permute-start.10 = (bf16[32,4608]{1,0:T(8,128)(2,1)}, bf16[32,4608]{1,0:T(8,128)(2,1)S(1)}, u32[]{:S(2)}, u32[]{:S(2)}) collective-permute-start(bf16[32,4608]{1,0:T(8,128)(2,1)} %get-tuple-element.55), channel_id=1, source_target_pairs={{0,8},{4,12},{8,0},{12,4},{1,9},{5,13},{9,1},{13,5},{2,10},{6,14},... | collective-permute-start | bytes 884744 | tf_op jit(solution)/shard_map/ppermute | solution.py:567
  47.4 17.4 %collective-permute-start.11 = (bf16[48,4608]{1,0:T(8,128)(2,1)}, bf16[48,4608]{1,0:T(8,128)(2,1)S(1)}, u32[]{:S(2)}, u32[]{:S(2)}) collective-permute-start(bf16[48,4608]{1,0:T(8,128)(2,1)} %get-tuple-element.56), channel_id=1, source_target_pairs={{0,8},{4,12},{8,0},{12,4},{1,9},{5,13},{9,1},{13,5},{2,10},{6,14},... | collective-permute-start | bytes 1327112 | tf_op jit(solution)/shard_map/ppermute | solution.py:567
  53.7 24.2 %copy-start.2 = (bf16[16,4608]{1,0:T(8,128)(2,1)S(1)}, bf16[16,4608]{1,0:T(8,128)(2,1)}, u32[]{:S(2)}) copy-start(bf16[16,4608]{1,0:T(8,128)(2,1)} %get-tuple-element.61) | copy-start | bytes 442372
  53.7 9.1 %collective-permute-start.6 = (bf16[384,256]{1,0:T(8,128)(2,1)S(1)}, bf16[384,256]{1,0:T(8,128)(2,1)S(1)}, u32[]{:S(2)}, u32[]{:S(2)}) collective-permute-start(bf16[384,256]{1,0:T(8,128)(2,1)S(1)} %get-tuple-element.48), channel_id=1, source_target_pairs={{0,1},{1,2},{2,3},{3,0},{4,5},{5,6},{6,7},{7,4},{8,9},{9,10},{10,1... | collective-permute-start | bytes 589832 | tf_op jit(solution)/shard_map/ppermute | solution.py:583
  55.7 9.1 %collective-permute-start.12 = (bf16[32,4608]{1,0:T(8,128)(2,1)S(1)}, bf16[32,4608]{1,0:T(8,128)(2,1)S(1)}, u32[]{:S(2)}, u32[]{:S(2)}) collective-permute-start(bf16[32,4608]{1,0:T(8,128)(2,1)S(1)} %collective-permute-done.10.refs_0_), channel_id=1, source_target_pairs={{0,16},{16,0},{1,17},{17,1},{2,18},{18,2},{3,19},{19,3},{4,20},{20... | collective-permute-start | bytes 884744 | tf_op jit(solution)/shard_map/ppermute | solution.py:567
  62.8 8.2 %collective-permute-start.7 = (bf16[384,256]{1,0:T(8,128)(2,1)S(1)}, bf16[384,256]{1,0:T(8,128)(2,1)S(1)}, u32[]{:S(2)}, u32[]{:S(2)}) collective-permute-start(bf16[384,256]{1,0:T(8,128)(2,1)S(1)} %collective-permute-done.6), channel_id=1, source_target_pairs={{0,1},{1,2},{2,3},{3,0},{4,5},{5,6},{6,7},{7,4},{8,9},{9,10},{10,1... | collective-permute-start | bytes 589832 | tf_op jit(solution)/shard_map/ppermute | solution.py:583
  71.0 10.8 %collective-permute-start.14 = (bf16[48,4608]{1,0:T(8,128)(2,1)S(1)}, bf16[48,4608]{1,0:T(8,128)(2,1)S(1)}, u32[]{:S(2)}, u32[]{:S(2)}) collective-permute-start(bf16[48,4608]{1,0:T(8,128)(2,1)S(1)} %collective-permute-done.11.refs_1_), channel_id=1, source_target_pairs={{0,16},{16,0},{1,17},{17,1},{2,18},{18,2},{3,19},{19,3},{4,20},{20... | collective-permute-start | bytes 1327112 | tf_op jit(solution)/shard_map/ppermute | solution.py:567
  72.3 7.8 %collective-permute-start.13 = (bf16[32,4608]{1,0:T(8,128)(2,1)S(1)}, bf16[32,4608]{1,0:T(8,128)(2,1)S(1)}, u32[]{:S(2)}, u32[]{:S(2)}) collective-permute-start(bf16[32,4608]{1,0:T(8,128)(2,1)S(1)} %copy-done.1), channel_id=1, source_target_pairs={{0,8},{4,12},{8,0},{12,4},{1,9},{5,13},{9,1},{13,5},{2,10},{6,14},... | collective-permute-start | bytes 884744 | tf_op jit(solution)/shard_map/ppermute | solution.py:567
  73.8 7.5 %collective-permute-start.8 = (bf16[384,256]{1,0:T(8,128)(2,1)S(1)}, bf16[384,256]{1,0:T(8,128)(2,1)S(1)}, u32[]{:S(2)}, u32[]{:S(2)}) collective-permute-start(bf16[384,256]{1,0:T(8,128)(2,1)S(1)} %collective-permute-done.7), channel_id=1, source_target_pairs={{0,1},{1,2},{2,3},{3,0},{4,5},{5,6},{6,7},{7,4},{8,9},{9,10},{10,1... | collective-permute-start | bytes 589832 | tf_op jit(solution)/shard_map/ppermute | solution.py:583
  77.9 11.1 %collective-permute-start.15 = (bf16[16,4608]{1,0:T(8,128)(2,1)S(1)}, bf16[16,4608]{1,0:T(8,128)(2,1)S(1)}, u32[]{:S(2)}, u32[]{:S(2)}) collective-permute-start(bf16[16,4608]{1,0:T(8,128)(2,1)S(1)} %copy-done.2), channel_id=1, source_target_pairs={{0,8},{4,12},{8,0},{12,4},{1,9},{5,13},{9,1},{13,5},{2,10},{6,14},... | collective-permute-start | bytes 442376 | tf_op jit(solution)/shard_map/ppermute | solution.py:567
  81.8 12.9 %collective-permute-start.16 = (bf16[32,4608]{1,0:T(8,128)(2,1)S(1)}, bf16[32,4608]{1,0:T(8,128)(2,1)S(1)}, u32[]{:S(2)}, u32[]{:S(2)}) collective-permute-start(bf16[32,4608]{1,0:T(8,128)(2,1)S(1)} %collective-permute-done.13.refs_2_), channel_id=1, source_target_pairs={{0,16},{16,0},{1,17},{17,1},{2,18},{18,2},{3,19},{19,3},{4,20},{20... | collective-permute-start | bytes 884744 | tf_op jit(solution)/shard_map/ppermute | solution.py:567
  88.8 5.9 %collective-permute-start.9 = (bf16[384,256]{1,0:T(8,128)(2,1)}, bf16[384,256]{1,0:T(8,128)(2,1)S(1)}, u32[]{:S(2)}, u32[]{:S(2)}) collective-permute-start(bf16[384,256]{1,0:T(8,128)(2,1)} %get-tuple-element.53), channel_id=1, source_target_pairs={{0,8},{4,12},{8,0},{12,4},{1,9},{5,13},{9,1},{13,5},{2,10},{6,14},... | collective-permute-start | bytes 589832 | tf_op jit(solution)/shard_map/ppermute | solution.py:567
  89.0 5.1 %collective-permute-start.17 = (bf16[16,4608]{1,0:T(8,128)(2,1)S(1)}, bf16[16,4608]{1,0:T(8,128)(2,1)S(1)}, u32[]{:S(2)}, u32[]{:S(2)}) collective-permute-start(bf16[16,4608]{1,0:T(8,128)(2,1)S(1)} %collective-permute-done.15.refs_3_), channel_id=1, source_target_pairs={{0,16},{16,0},{1,17},{17,1},{2,18},{18,2},{3,19},{19,3},{4,20},{20... | collective-permute-start | bytes 442376 | tf_op jit(solution)/shard_map/ppermute | solution.py:567
  98.3 4.0 %collective-permute-start.18 = (bf16[192,4608]{1,0:T(8,128)(2,1)}, bf16[192,4608]{1,0:T(8,128)(2,1)S(1)}, u32[]{:S(2)}, u32[]{:S(2)}) collective-permute-start(bf16[192,4608]{1,0:T(8,128)(2,1)} %get-tuple-element.63), channel_id=1, source_target_pairs={{0,4},{4,0},{8,12},{12,8},{1,5},{5,1},{9,13},{13,9},{2,6},{6,2},{1... | collective-permute-start | bytes 5308424 | tf_op jit(solution)/shard_map/ppermute | solution.py:567

commit v4 on v1

--- a/solution.py
+++ b/solution.py
@@ -59,13 +59,16 @@
         return copy
 
 
-def norm_kernel(cuts, pieces, hidden, gain, *refs):
+def norm_kernel(cuts, pieces, first, hidden, gain, *refs):
     parts, (gains, rows, staged, semaphores) = refs[: len(cuts)], refs[len(cuts) :]
     copies = Copies(semaphores)
-    count, width = hidden.shape
+    count, width = rows.shape
     step = count // pieces
     spans = [pl.ds(at * step, step) for at in range(pieces)]
-    ins = [copies.start(hidden.at[span], rows.at[span]) for span in spans]
+    ins = [
+        copies.start(hidden.at[pl.ds(first + at * step, step)], rows.at[span])
+        for at, span in enumerate(spans)
+    ]
     copies.start(gain, gains).wait()
     scale = gains[...].reshape(1, width)
     outs = []
@@ -88,11 +91,11 @@
         copy.wait()
 
 
-def norm(hidden, gain, cuts, pieces=3):
-    rows, width = hidden.shape
+def norm(hidden, gain, first, cuts, pieces=3):
+    rows, width = sum(cuts), hidden.shape[1]
     bf16 = jnp.bfloat16
     return call(
-        functools.partial(norm_kernel, cuts, pieces),
+        functools.partial(norm_kernel, cuts, pieces, first),
         "norm_rows",
         8,
         [HBM, HBM],
@@ -108,24 +111,9 @@
     )
 
 
-def rotate_into(product, angles, q, kv):
-    cos, sin = angles[:, :HD], angles[:, HD:]
-    queries = product.shape[1] - 2 * HD
-
-    def rotated(at):
-        y = product[:, at : at + HD]
-        return y * cos + pltpu.roll(y, HD // 2, 1) * sin
-
-    factor = ATT_SCALAR ** (-0.5) * math.log2(math.e)
-    kv[:, :HD] = rotated(queries).astype(jnp.bfloat16)
-    kv[:, HD:] = product[:, queries + HD :].astype(jnp.bfloat16)
-    for head in range(queries // HD):
-        q[head] = (rotated(head * HD) * factor).astype(jnp.bfloat16)
-
-
-def qkv_kernel(count, first, chunks, trig, wq, wk, wv, *refs):
-    parts = refs[:count]
-    q, kv, weights, rows, angles, semaphores = refs[count:]
+def qkv_kernel(places, first, chunks, held, trig, wq, wk, wv, *refs):
+    parts, refs = refs[: len(places)], refs[len(places) + 2 * held :]
+    q, kv, weights, rows, angles, semaphores = refs
     copies, waits = Copies(semaphores), []
     depth = weights.shape[0] // chunks
     for chunk in range(chunks):
@@ -139,7 +127,12 @@
             here.append(copies.start(weight.at[span], target))
             column += weight.shape[1]
         waits.append(here)
-    late = copies.start(trig.at[pl.ds(first, put)], angles)
+    late, put = [], 0
+    for part, place in zip(parts, places):
+        count = part.shape[0]
+        source = trig.at[pl.ds(first + place, count)]
+        late.append(copies.start(source, angles.at[pl.ds(put, count)]))
+        put += count
     product = None
     for chunk, here in enumerate(waits):
         for copy in here:
@@ -147,29 +140,51 @@
         span = pl.ds(chunk * depth, depth)
         term = jnp.dot(rows[:, span], weights[span, :], preferred_element_type=jnp.float32)
         product = term if product is None else product + term
-    late.wait()
-    rotate_into(product, angles, q, kv)
-
-
-def qkv(parts, weights, trig, first, chunks=6):
-    total, width = sum(part.shape[0] for part in parts), parts[0].shape[1]
+    for copy in late:
+        copy.wait()
+    cos, sin = angles[:, :HD], angles[:, HD:]
+    queries = product.shape[1] - 2 * HD
+
+    def rotated(at):
+        y = product[:, at : at + HD]
+        return y * cos + pltpu.roll(y, HD // 2, 1) * sin
+
+    factor = ATT_SCALAR ** (-0.5) * math.log2(math.e)
+    keys = rotated(queries).astype(jnp.bfloat16)
+    values = product[:, queries + HD :].astype(jnp.bfloat16)
+    heads = [(rotated(at) * factor).astype(jnp.bfloat16) for at in range(0, queries, HD)]
+    put = 0
+    for part, place in zip(parts, places):
+        count = part.shape[0]
+        kv[place : place + count, :HD] = keys[put : put + count]
+        kv[place : place + count, HD:] = values[put : put + count]
+        for head, rotated_head in enumerate(heads):
+            q[head, place : place + count, :] = rotated_head[put : put + count]
+        put += count
+
+
+def qkv(parts, places, total, weights, trig, first, held=(), chunks=4):
+    rows, width = sum(part.shape[0] for part in parts), parts[0].shape[1]
     columns = sum(weight.shape[1] for weight in weights)
-    heads, bf16 = columns // HD - 2, jnp.bfloat16
+    heads, bf16 = weights[0].shape[1] // HD, jnp.bfloat16
+    given = 4 + len(parts)
     return call(
-        functools.partial(qkv_kernel, len(parts), first, chunks),
+        functools.partial(qkv_kernel, places, first, chunks, bool(held)),
         "qkv",
         14,
-        [HBM] * (4 + len(parts)),
+        [HBM] * given + [VMEM] * len(held),
         [((heads, total, HD), bf16, VMEM), ((total, 2 * HD), bf16, VMEM)],
         [
             pltpu.VMEM((width, columns), bf16),
-            pltpu.VMEM((total, width), bf16),
-            pltpu.VMEM((total, 2 * HD), jnp.float32),
-            pltpu.SemaphoreType.DMA((1 + (len(parts) + 3) * chunks,)),
+            pltpu.VMEM((rows, width), bf16),
+            pltpu.VMEM((rows, 2 * HD), jnp.float32),
+            pltpu.SemaphoreType.DMA((len(parts) + (len(parts) + 3) * chunks,)),
         ],
         trig,
         *weights,
         *parts,
+        *held,
+        aliases={given + at: at for at in range(len(held))},
     )
 
 
@@ -608,27 +623,48 @@
     near_chunk, far_chunk = Chunk(near_at, runs, rows), Chunk(far_at, runs, rows)
     others, everyone = list(range(1, lines)), list(range(lines))
 
-    own = norm(hidden, pre_gain, [rows])[0]
-    away = flipped(own, "tp", 2)
-    partner = flipped(own, "tp", 1)
+    half = rows // 2
+    own = [norm(hidden, pre_gain, at * half, [half])[0] for at in range(2)]
+    away = [flipped(part, "tp", 2) for part in own]
+    partner = [Came(flipped(part, "tp", 1)) for part in own]
 
     weights = (wq, wk, wv)
-    q_near, kv_near = qkv([own, Came(partner)], weights, trig, 0)
+    places = [0, half, rows, rows + half]
+    q_near, kv_near = qkv([*own, *partner], places, block_rows, weights, trig, 0)
     near = along_line(kv_near)
-    half = w_out.shape[0] // 2
-    w_cut = cut(table, group_at, after(w_out, kv_near), [half // 4] * 4)
+    w_cut = cut(table, group_at, after(w_out, kv_near), [w_out.shape[0] // 8] * 4)
     q_near = after(q_near, *w_cut)
     (near_state,) = attention(
         [Step(0, 0, others, same=0)], table, [q_near], [near_chunk], [near], [near_chunk], [None]
     )
 
-    away = after(away, *near_state)
-    q_far, kv_far = qkv([Came(away), Came(flipped(away, "tp", 1))], weights, trig, block_rows)
+    away[0] = after(away[0], *near_state)
+    quarter = half // 2
+    swapped = [flipped(away[0][at : at + quarter], "tp", 1) for at in (0, quarter)]
+    held = qkv(
+        [Came(away[0]), *[Came(part) for part in swapped]],
+        [0, rows, rows + quarter],
+        block_rows,
+        weights,
+        trig,
+        block_rows,
+    )
+    away[1] = after(away[1], *held)
+    held = qkv(
+        [Came(away[1]), Came(flipped(away[1], "tp", 1))],
+        [half, rows + half],
+        block_rows,
+        weights,
+        trig,
+        block_rows,
+        held,
+    )
+    q_far, kv_far = held
     far = along_ring(kv_far)
 
     fetched = lambda piece, *others: flipped(after(piece, *others), "tp", 2)
     swap = lambda array: flipped(array, "groups", 1)
-    w_far = [fetched(piece, away) for piece in w_cut[:2]]
+    w_far = [fetched(piece, away[1]) for piece in w_cut[:2]]
     w_far[0] = after(w_far[0], kv_far)
     w_far.append(fetched(w_cut[2], w_far[0]))
     w_other = [swap(w_far[0])]
@@ -675,14 +711,15 @@
     block_rows = rows * lax.axis_size("tp") // 2
     starts = lookup(block_of, block) * block_rows
     table = jnp.concatenate([jnp.zeros(2, jnp.int32), starts])
-    normed = norm(hidden, pre_gain, [rows], 1)[0]
+    normed = norm(hidden, pre_gain, 0, [rows], 1)[0]
     normed = lax.all_gather(normed, "tp", axis=0, tiled=True)
     place = jnp.arange(block_rows, dtype=jnp.int32)
     trig = rotary_table((starts[:2, None] + place).reshape(-1))
     qs, keys_values, weights = [], [], (wq, wk, wv)
     for at in range(2):
         first = at * block_rows
-        q, kv = qkv([normed[first : first + block_rows]], weights, trig, first)
+        rows_here = [normed[first : first + block_rows]]
+        q, kv = qkv(rows_here, [0], block_rows, weights, trig, first)
         qs.append(q)
         keys_values.append(kv)
     kv = lax.all_gather(jnp.stack(keys_values), "seq")[line].reshape(-1, block_rows, 2 * HD)

time: 102 us -> 102 us (level)
  waiting for transfers between devices: 38.1 us -> 32 us
  Pallas kernels: 40 us -> 45.8 us
    pallas_call x11 -> x13, Pallas kernels: 40 us -> 45.8 us  [call(): pl.pallas_call(kernel, in_specs=in_specs, out_specs=[spec for _, _, spec...]
    ppermute x13 -> x17, waiting for transfers between devices: 16.6 us -> 10.9 us  [flipped(): return lax.ppermute(array, axis, [(i, i ^ bit) for i in range(size)])]
    ppermute x13 -> x17, starting transfers between devices: 13.6 us -> 13.6 us  [flipped(): return lax.ppermute(array, axis, [(i, i ^ bit) for i in range(size)])]
  transfers between devices with their start and end apart: 19 -> 23, of which waited for: 10 -> 13; matrix products, arithmetic and copies ran while one was open for 3% -> 3% of each run, Pallas kernels for 31% -> 37%
where the time goes in v4:
time: 102 us
  Pallas kernels  45.8 us (45%)
  waiting for transfers between devices  32 us (31%)
  starting transfers between devices  20.7 us (20%)
  other arithmetic  3.15 us (3%)
    pallas_call x13, Pallas kernels, call(): pl.pallas_call(kernel, in_specs=in_specs, out_specs=[spec for _, _, spec...  45.8 us
    ppermute x17, starting transfers between devices, flipped(): return lax.ppermute(array, axis, [(i, i ^ bit) for i in range(size)])  13.6 us
    ppermute x3, waiting for transfers between devices, along_ring(): part = lax.ppermute(part, 'seq', [(i, (i + 1) % size) for i in range(size)])  12.3 us
    ppermute x17, waiting for transfers between devices, flipped(): return lax.ppermute(array, axis, [(i, i ^ bit) for i in range(size)])  10.9 us
    ppermute x3, waiting for transfers between devices, along_line(): lax.ppermute(array, 'seq', [(i, (i + by) % size) for i in range(size)])  8.87 us
    ppermute x3, starting transfers between devices, along_line(): lax.ppermute(array, 'seq', [(i, (i + by) % size) for i in range(size)])  5.57 us
  transfers between devices with their start and end apart: 23, of which 13 were waited for; matrix products, arithmetic and copies ran while one was open for 3% of the time, Pallas kernels for 37%

profile of v4, /device:TPU:0, one launch (start us, length us, event | category | flops | bytes accessed | tf_op | source)
XLA Modules:
  0.0 102.2 jit_solution(16973224255272251438)
XLA Ops:
  0.0 2.3 %norm_rows.2.refs_0_ = bf16[96,4608]{1,0:T(8,128)(2,1)} custom-call(bf16[192,4608]{1,0:T(8,128)(2,1)} %hidden.5, f32[4608]{0:T(1024)} %gain.4), custom_call_target="tpu_custom_call" | custom-call | flops 1 | bytes 1 | tf_op jit(solution)/shard_map/norm_rows/pallas_call | solution.py:38
  2.9 2.6 %collective-permute-start.3 = (bf16[96,4608]{1,0:T(8,128)(2,1)}, bf16[96,4608]{1,0:T(8,128)(2,1)S(1)}, u32[]{:S(2)}, u32[]{:S(2)}) collective-permute-start(bf16[96,4608]{1,0:T(8,128)(2,1)} %norm_rows.2.refs_0_), channel_id=1, source_target_pairs={{0,8},{4,12},{8,0},{12,4},{1,9},{5,13},{9,1},{13,5},{2,10},{6,14},... | collective-permute-start | bytes 2654216 | tf_op jit(solution)/shard_map/ppermute | solution.py:578
  5.4 2.3 %norm_rows.3.refs_1_ = bf16[96,4608]{1,0:T(8,128)(2,1)} custom-call(bf16[192,4608]{1,0:T(8,128)(2,1)} %hidden.5, f32[4608]{0:T(1024)} %gain.4), custom_call_target="tpu_custom_call" | custom-call | flops 1 | bytes 1 | tf_op jit(solution)/shard_map/norm_rows/pallas_call | solution.py:38
  8.4 1.4 %multiply_cosine_fusion = (f32[768,64]{1,0:T(8,128)S(1)}, f32[768,64]{1,0:T(8,128)S(1)}, f32[768,64]{1,0:T(8,128)S(1)}) fusion(f32[768]{0:T(1024)S(1)} %add_convert_fusion, f32[64]{0:T(128)S(1)} %multiply_power_fusion), kind=kLoop, calls=%fused_computation.2 | loop fusion | flops 98304 | bytes 593152 | tf_op jit(solution)/shard_map/cos | solution.py:567
  9.9 1.3 %pad_maximum_fusion.trig = f32[768,256]{1,0:T(8,128)} fusion(f32[768,64]{1,0:T(8,128)S(1)} %get-tuple-element.79, f32[768,64]{1,0:T(8,128)S(1)} %get-tuple-element.78, f32[768,64]{1,0:T(8,128)S(1)} %get-tuple-element.77), kind=kLoop, calls=%fused_computation | loop fusion | flops 589824 | bytes 1376256 | tf_op jit(solution)/shard_map/concatenate | solution.py:568
  11.2 4.8 %qkv.3 = (bf16[2,384,128]{2,1,0:T(8,128)(2,1)S(1)}, bf16[384,256]{1,0:T(8,128)(2,1)S(1)}) custom-call(f32[768,256]{1,0:T(8,128)} %pad_maximum_fusion.trig, bf16[4608,256]{1,0:T(8,128)(2,1)} %wq.5, bf16[4608,128]{1,0:T(8,128)(2,1)} %wk.5, bf16[4608,128]{1,0:T(8,128)(2,1)} %wv.5, bf16[96,4608]{1,0:T(8,128)(2,1)} %norm_rows.2.refs_0_, ...), custom_call_target="tpu_custom_call" | custom-call | flops 1 | bytes 1 | tf_op jit(solution)/shard_map/qkv/pallas_call | solution.py:38
  16.0 1.6 %collective-permute-start.4 = (bf16[384,256]{1,0:T(8,128)(2,1)S(1)}, bf16[384,256]{1,0:T(8,128)(2,1)S(1)}, u32[]{:S(2)}, u32[]{:S(2)}) collective-permute-start(bf16[384,256]{1,0:T(8,128)(2,1)S(1)} %get-tuple-element.40), channel_id=1, source_target_pairs={{0,1},{1,2},{2,3},{3,0},{4,5},{5,6},{6,7},{7,4},{8,9},{9,10},{10,1... | collective-permute-start | bytes 589832 | tf_op jit(solution)/shard_map/ppermute | solution.py:585
  17.6 2.6 %collective-permute-start.5 = (bf16[384,256]{1,0:T(8,128)(2,1)S(1)}, bf16[384,256]{1,0:T(8,128)(2,1)S(1)}, u32[]{:S(2)}, u32[]{:S(2)}) collective-permute-start(bf16[384,256]{1,0:T(8,128)(2,1)S(1)} %get-tuple-element.40), channel_id=1, source_target_pairs={{0,2},{1,3},{2,0},{3,1},{4,6},{5,7},{6,4},{7,5},{8,10},{9,11},{10,... | collective-permute-start | bytes 589832 | tf_op jit(solution)/shard_map/ppermute | solution.py:585
  20.2 1.3 %collective-permute-start.6 = (bf16[384,256]{1,0:T(8,128)(2,1)S(1)}, bf16[384,256]{1,0:T(8,128)(2,1)S(1)}, u32[]{:S(2)}, u32[]{:S(2)}) collective-permute-start(bf16[384,256]{1,0:T(8,128)(2,1)S(1)} %get-tuple-element.40), channel_id=1, source_target_pairs={{0,3},{1,0},{2,1},{3,2},{4,7},{5,4},{6,5},{7,6},{8,11},{9,8},{10,9... | collective-permute-start | bytes 589832 | tf_op jit(solution)/shard_map/ppermute | solution.py:585
  22.1 2.6 %cut_weights.1 = (bf16[32,4608]{1,0:T(8,128)(2,1)}, bf16[32,4608]{1,0:T(8,128)(2,1)}, bf16[32,4608]{1,0:T(8,128)(2,1)}, bf16[32,4608]{1,0:T(8,128)(2,1)}) custom-call(s32[10]{0:T(128)S(1)} %pad_add_fusion.1.table, bf16[256,4608]{1,0:T(8,128)(2,1)} %weights_hbm.1), custom_call_target="tpu_custom_call" | custom-call | flops 1 | bytes 1 | tf_op jit(solution)/shard_map/cut_weights/pallas_call | solution.py:38
  25.7 7.9 %collective-permute-done.5 = bf16[384,256]{1,0:T(8,128)(2,1)S(1)} collective-permute-done((bf16[384,256]{1,0:T(8,128)(2,1)S(1)}, bf16[384,256]{1,0:T(8,128)(2,1)S(1)}, u32[]{:S(2)}, u32[]{:S(2)}) %collective-permute-start.5) | collective-permute-done | bytes 196640 | tf_op jit(solution)/shard_map/ppermute | solution.py:585
  33.6 4.3 %attention.3 = (f32[3,8,256]{2,1,0:T(8,128)S(1)}, f32[3,144,256]{2,1,0:T(8,128)S(1)}) custom-call(s32[10]{0:T(128)S(1)} %pad_add_fusion.1.table, bf16[2,384,128]{2,1,0:T(8,128)(2,1)S(1)} %get-tuple-element.46.refs_0_, bf16[1,384,256]{2,1,0:T(8,128)(2,1)S(1)} %bitcast.16, bf16[1,384,256]{2,1,0:T(8,128)(2,1)S(1)} %bitcast.18, ...), custom_call_target="tpu_custom_call" | custom-call | flops 1 | bytes 1 | tf_op jit(solution)/shard_map/attention/pallas_call | solution.py:38
  38.6 1.3 %collective-permute-done.7.refs_1_ = bf16[48,4608]{1,0:T(8,128)(2,1)S(1)} collective-permute-done((bf16[48,4608]{1,0:T(8,128)(2,1)S(1)}, bf16[48,4608]{1,0:T(8,128)(2,1)S(1)}, u32[]{:S(2)}, u32[]{:S(2)}) %collective-permute-start.7) | collective-permute-done | bytes 442400 | tf_op jit(solution)/shard_map/ppermute | solution.py:578
  40.5 3.4 %qkv.4 = (bf16[2,384,128]{2,1,0:T(8,128)(2,1)S(1)}, bf16[384,256]{1,0:T(8,128)(2,1)S(1)}) custom-call(f32[768,256]{1,0:T(8,128)} %pad_maximum_fusion.trig, bf16[4608,256]{1,0:T(8,128)(2,1)} %wq.5, bf16[4608,128]{1,0:T(8,128)(2,1)} %wk.5, bf16[4608,128]{1,0:T(8,128)(2,1)} %wv.5, bf16[96,4608]{1,0:T(8,128)(2,1)S(1)} %collective-permute-done.3.refs_0_, ...), custom_call_target="tpu_custom_call" | custom-call | flops 1 | bytes 1 | tf_op jit(solution)/shard_map/qkv/pallas_call | solution.py:38
  43.8 1.0 collective-permute-done.2.refs_0_
  44.9 1.8 %collective-permute-start.14 = (bf16[32,4608]{1,0:T(8,128)(2,1)S(1)}, bf16[32,4608]{1,0:T(8,128)(2,1)S(1)}, u32[]{:S(2)}, u32[]{:S(2)}) collective-permute-start(bf16[32,4608]{1,0:T(8,128)(2,1)S(1)} %copy-done.4), channel_id=1, source_target_pairs={{0,8},{4,12},{8,0},{12,4},{1,9},{5,13},{9,1},{13,5},{2,10},{6,14},... | collective-permute-start | bytes 884744 | tf_op jit(solution)/shard_map/ppermute | solution.py:578
  47.3 3.3 %qkv.5 = (bf16[2,384,128]{2,1,0:T(8,128)(2,1)S(1)}, bf16[384,256]{1,0:T(8,128)(2,1)S(1)}) custom-call(f32[768,256]{1,0:T(8,128)} %pad_maximum_fusion.trig, bf16[4608,256]{1,0:T(8,128)(2,1)} %wq.5, bf16[4608,128]{1,0:T(8,128)(2,1)} %wk.5, bf16[4608,128]{1,0:T(8,128)(2,1)} %wv.5, ...), custom_call_target="tpu_custom_call", output_to_operand_aliasing={{0}: (6, {}), {1}: (7, {})} | custom-call | flops 1 | bytes 1 | tf_op jit(solution)/shard_map/qkv/pallas_call | solution.py:38
  50.6 4.2 %collective-permute-done.14.refs_0_ = bf16[32,4608]{1,0:T(8,128)(2,1)S(1)} collective-permute-done((bf16[32,4608]{1,0:T(8,128)(2,1)S(1)}, bf16[32,4608]{1,0:T(8,128)(2,1)S(1)}, u32[]{:S(2)}, u32[]{:S(2)}) %collective-permute-start.14) | collective-permute-done | bytes 294944 | tf_op jit(solution)/shard_map/ppermute | solution.py:578
  54.8 1.7 %collective-permute-start.16 = (bf16[32,4608]{1,0:T(8,128)(2,1)S(1)}, bf16[32,4608]{1,0:T(8,128)(2,1)S(1)}, u32[]{:S(2)}, u32[]{:S(2)}) collective-permute-start(bf16[32,4608]{1,0:T(8,128)(2,1)S(1)} %collective-permute-done.14.refs_0_), channel_id=1, source_target_pairs={{0,16},{16,0},{1,17},{17,1},{2,18},{18,2},{3,19},{19,3},{4,20},{20... | collective-permute-start | bytes 884744 | tf_op jit(solution)/shard_map/ppermute | solution.py:578
  56.5 1.6 %collective-permute-start.10 = (bf16[384,256]{1,0:T(8,128)(2,1)S(1)}, bf16[384,256]{1,0:T(8,128)(2,1)S(1)}, u32[]{:S(2)}, u32[]{:S(2)}) collective-permute-start(bf16[384,256]{1,0:T(8,128)(2,1)S(1)} %get-tuple-element.54), channel_id=1, source_target_pairs={{0,1},{1,2},{2,3},{3,0},{4,5},{5,6},{6,7},{7,4},{8,9},{9,10},{10,1... | collective-permute-start | bytes 589832 | tf_op jit(solution)/shard_map/ppermute | solution.py:594
  58.1 6.0 %collective-permute-done.10 = bf16[384,256]{1,0:T(8,128)(2,1)S(1)} collective-permute-done((bf16[384,256]{1,0:T(8,128)(2,1)S(1)}, bf16[384,256]{1,0:T(8,128)(2,1)S(1)}, u32[]{:S(2)}, u32[]{:S(2)}) %collective-permute-start.10) | collective-permute-done | bytes 196640 | tf_op jit(solution)/shard_map/ppermute | solution.py:594
  64.1 1.5 %collective-permute-start.17 = (bf16[32,4608]{1,0:T(8,128)(2,1)S(1)}, bf16[32,4608]{1,0:T(8,128)(2,1)S(1)}, u32[]{:S(2)}, u32[]{:S(2)}) collective-permute-start(bf16[32,4608]{1,0:T(8,128)(2,1)S(1)} %copy-done.2), channel_id=1, source_target_pairs={{0,8},{4,12},{8,0},{12,4},{1,9},{5,13},{9,1},{13,5},{2,10},{6,14},... | collective-permute-start | bytes 884744 | tf_op jit(solution)/shard_map/ppermute | solution.py:578
  66.6 4.9 %collective-permute-done.11 = bf16[384,256]{1,0:T(8,128)(2,1)S(1)} collective-permute-done((bf16[384,256]{1,0:T(8,128)(2,1)S(1)}, bf16[384,256]{1,0:T(8,128)(2,1)S(1)}, u32[]{:S(2)}, u32[]{:S(2)}) %collective-permute-start.11) | collective-permute-done | bytes 196640 | tf_op jit(solution)/shard_map/ppermute | solution.py:594
  71.5 5.5 %attention.4 = (f32[3,8,256]{2,1,0:T(8,128)S(1)}, f32[3,144,256]{2,1,0:T(8,128)S(1)}, f32[3,8,256]{2,1,0:T(8,128)S(1)}, f32[3,144,256]{2,1,0:T(8,128)S(1)}) custom-call(s32[10]{0:T(128)S(1)} %pad_add_fusion.1.table, bf16[2,384,128]{2,1,0:T(8,128)(2,1)S(1)} %get-tuple-element.46.refs_0_, ...), custom_call_target="tpu_custom_call", output_to_operand_aliasing={{0}: (8, {}), {1}: (9, {})} | custom-call | flops 1 | bytes 1 | tf_op jit(solution)/shard_map/attention/pallas_call | solution.py:38
  77.6 1.4 %collective-permute-done.12 = bf16[384,256]{1,0:T(8,128)(2,1)S(1)} collective-permute-done((bf16[384,256]{1,0:T(8,128)(2,1)S(1)}, bf16[384,256]{1,0:T(8,128)(2,1)S(1)}, u32[]{:S(2)}, u32[]{:S(2)}) %collective-permute-start.12) | collective-permute-done | bytes 196640 | tf_op jit(solution)/shard_map/ppermute | solution.py:594
  79.0 6.6 %attention.5 = (bf16[384,256]{1,0:T(8,128)(2,1)}, bf16[384,256]{1,0:T(8,128)(2,1)}, f32[3,8,256]{2,1,0:T(8,128)S(1)}, f32[3,144,256]{2,1,0:T(8,128)S(1)}, f32[3,...) custom-call(s32[10]{0:T(128)S(1)} %pad_add_fusion.1.table, ...), custom_call_target="tpu_custom_call", output_to_operand_aliasing={{2}: (7, {}), {3}: (8, {}), {4}: (9, {}), {5}: (10, {})} | custom-call | flops 1 | bytes 1 | tf_op jit(solution)/shard_map/attention/pallas_call | solution.py:38
  86.2 1.5 %collective-permute-start.13 = (bf16[384,256]{1,0:T(8,128)(2,1)}, bf16[384,256]{1,0:T(8,128)(2,1)S(1)}, u32[]{:S(2)}, u32[]{:S(2)}) collective-permute-start(bf16[384,256]{1,0:T(8,128)(2,1)} %get-tuple-element.59), channel_id=1, source_target_pairs={{0,8},{4,12},{8,0},{12,4},{1,9},{5,13},{9,1},{13,5},{2,10},{6,14},... | collective-permute-start | bytes 589832 | tf_op jit(solution)/shard_map/ppermute | solution.py:578
  87.8 3.4 %output_near.1.near = f32[384,4608]{1,0:T(8,128)S(1)} custom-call(bf16[384,256]{1,0:T(8,128)(2,1)} %get-tuple-element.60.left_hbm, bf16[256,4608]{1,0:T(8,128)(2,1)} %weights_hbm.1), custom_call_target="tpu_custom_call" | custom-call | flops 1 | bytes 1 | tf_op jit(solution)/shard_map/output_near/pallas_call | solution.py:38
  92.4 3.0 %output_send.1 = (bf16[192,4608]{1,0:T(8,128)(2,1)}, bf16[256,4608]{1,0:T(8,128)(2,1)S(1)}) custom-call(s32[10]{0:T(128)S(1)} %pad_add_fusion.1.table, bf16[384,256]{1,0:T(8,128)(2,1)S(1)} %collective-permute-done.13.left_hbm, f32[384,4608]{1,0:T(8,128)S(1)} %output_near.1.near, bf16[32,4608]{1,0:T(8,128)(2,1)S(1)} %collective-permute-done.14.refs_0_, ...), custom_call_target="tpu_custom_call" | custom-call | flops 1 | bytes 1 | tf_op jit(solution)/shard_map/output_send/pallas_call | solution.py:38
  95.5 1.7 %output_keep.1 = (f32[192,4608]{1,0:T(8,128)S(1)}, bf16[192,4608]{1,0:T(8,128)(2,1)S(1)}) custom-call(bf16[384,256]{1,0:T(8,128)(2,1)S(1)} %collective-permute-done.13.left_hbm, bf16[192,4608]{1,0:T(8,128)(2,1)} %hidden.5, f32[384,4608]{1,0:T(8,128)S(1)} %output_near.1.near, bf16[256,4608]{1,0:T(8,128)(2,1)S(1)} %get-tuple-element.70.weights), custom_call_target="tpu_custom_call" | custom-call | flops 1 | bytes 1 | tf_op jit(solution)/shard_map/output_keep/pallas_call | solution.py:38
  97.2 2.1 %collective-permute-done.22.received = bf16[192,4608]{1,0:T(8,128)(2,1)S(1)} collective-permute-done((bf16[192,4608]{1,0:T(8,128)(2,1)}, bf16[192,4608]{1,0:T(8,128)(2,1)S(1)}, u32[]{:S(2)}, u32[]{:S(2)}) %collective-permute-start.22) | collective-permute-done | bytes 1769504 | tf_op jit(solution)/shard_map/ppermute | solution.py:578
  99.4 2.7 %output_norm.1 = bf16[192,4608]{1,0:T(8,128)(2,1)} custom-call(bf16[192,4608]{1,0:T(8,128)(2,1)S(1)} %collective-permute-done.22.received, bf16[192,4608]{1,0:T(8,128)(2,1)S(1)} %get-tuple-element.71.hidden, f32[192,4608]{1,0:T(8,128)S(1)} %get-tuple-element.72.kept, f32[4608]{0:T(1024)} %gain.5), custom_call_target="tpu_custom_call" | custom-call | flops 1 | bytes 1 | tf_op jit(solution)/shard_map/output_norm/pallas_call | solution.py:38
  (49 shorter events, 8.1 us)
Async XLA Ops:
  2.3 5.7 %copy-start = (s32[8]{0:T(128)S(1)}, s32[8]{0:T(128)}, u32[]{:S(2)}) copy-start(s32[8]{0:T(128)} %param.15) | copy-start | bytes 100
  2.3 8.8 %collective-permute-start = (bf16[96,4608]{1,0:T(8,128)(2,1)}, bf16[96,4608]{1,0:T(8,128)(2,1)S(1)}, u32[]{:S(2)}, u32[]{:S(2)}) collective-permute-start(bf16[96,4608]{1,0:T(8,128)(2,1)} %norm_rows.2.refs_0_), channel_id=1, source_target_pairs={{0,4},{4,0},{8,12},{12,8},{1,5},{5,1},{9,13},{13,9},{2,6},{6,2},{1... | collective-permute-start | bytes 2654216 | tf_op jit(solution)/shard_map/ppermute | solution.py:578
  2.9 35.1 %collective-permute-start.3 = (bf16[96,4608]{1,0:T(8,128)(2,1)}, bf16[96,4608]{1,0:T(8,128)(2,1)S(1)}, u32[]{:S(2)}, u32[]{:S(2)}) collective-permute-start(bf16[96,4608]{1,0:T(8,128)(2,1)} %norm_rows.2.refs_0_), channel_id=1, source_target_pairs={{0,8},{4,12},{8,0},{12,4},{1,9},{5,13},{9,1},{13,5},{2,10},{6,14},... | collective-permute-start | bytes 2654216 | tf_op jit(solution)/shard_map/ppermute | solution.py:578
  7.8 3.4 %collective-permute-start.1 = (bf16[96,4608]{1,0:T(8,128)(2,1)}, bf16[96,4608]{1,0:T(8,128)(2,1)S(1)}, u32[]{:S(2)}, u32[]{:S(2)}) collective-permute-start(bf16[96,4608]{1,0:T(8,128)(2,1)} %norm_rows.3.refs_1_), channel_id=1, source_target_pairs={{0,4},{4,0},{8,12},{12,8},{1,5},{5,1},{9,13},{13,9},{2,6},{6,2},{1... | collective-permute-start | bytes 2654216 | tf_op jit(solution)/shard_map/ppermute | solution.py:578
  16.0 9.7 %collective-permute-start.4 = (bf16[384,256]{1,0:T(8,128)(2,1)S(1)}, bf16[384,256]{1,0:T(8,128)(2,1)S(1)}, u32[]{:S(2)}, u32[]{:S(2)}) collective-permute-start(bf16[384,256]{1,0:T(8,128)(2,1)S(1)} %get-tuple-element.40), channel_id=1, source_target_pairs={{0,1},{1,2},{2,3},{3,0},{4,5},{5,6},{6,7},{7,4},{8,9},{9,10},{10,1... | collective-permute-start | bytes 589832 | tf_op jit(solution)/shard_map/ppermute | solution.py:585
  17.6 16.0 %collective-permute-start.5 = (bf16[384,256]{1,0:T(8,128)(2,1)S(1)}, bf16[384,256]{1,0:T(8,128)(2,1)S(1)}, u32[]{:S(2)}, u32[]{:S(2)}) collective-permute-start(bf16[384,256]{1,0:T(8,128)(2,1)S(1)} %get-tuple-element.40), channel_id=1, source_target_pairs={{0,2},{1,3},{2,0},{3,1},{4,6},{5,7},{6,4},{7,5},{8,10},{9,11},{10,... | collective-permute-start | bytes 589832 | tf_op jit(solution)/shard_map/ppermute | solution.py:585
  20.2 13.4 %collective-permute-start.6 = (bf16[384,256]{1,0:T(8,128)(2,1)S(1)}, bf16[384,256]{1,0:T(8,128)(2,1)S(1)}, u32[]{:S(2)}, u32[]{:S(2)}) collective-permute-start(bf16[384,256]{1,0:T(8,128)(2,1)S(1)} %get-tuple-element.40), channel_id=1, source_target_pairs={{0,3},{1,0},{2,1},{3,2},{4,7},{5,4},{6,5},{7,6},{8,11},{9,8},{10,9... | collective-permute-start | bytes 589832 | tf_op jit(solution)/shard_map/ppermute | solution.py:585
  21.5 23.3 %collective-permute-start.2 = (bf16[96,4608]{1,0:T(8,128)(2,1)}, bf16[96,4608]{1,0:T(8,128)(2,1)S(1)}, u32[]{:S(2)}, u32[]{:S(2)}) collective-permute-start(bf16[96,4608]{1,0:T(8,128)(2,1)} %norm_rows.3.refs_1_), channel_id=1, source_target_pairs={{0,8},{4,12},{8,0},{12,4},{1,9},{5,13},{9,1},{13,5},{2,10},{6,14},... | collective-permute-start | bytes 2654216 | tf_op jit(solution)/shard_map/ppermute | solution.py:578
  38.0 1.9 %collective-permute-start.7 = (bf16[48,4608]{1,0:T(8,128)(2,1)S(1)}, bf16[48,4608]{1,0:T(8,128)(2,1)S(1)}, u32[]{:S(2)}, u32[]{:S(2)}) collective-permute-start(bf16[48,4608]{1,0:T(8,128)(2,1)S(1)} %get-tuple-element.76), channel_id=1, source_target_pairs={{0,4},{4,0},{8,12},{12,8},{1,5},{5,1},{9,13},{13,9},{2,6},{6,2},{1... | collective-permute-start | bytes 1327112 | tf_op jit(solution)/shard_map/ppermute | solution.py:578
  38.1 6.8 %copy-start.4 = (bf16[32,4608]{1,0:T(8,128)(2,1)S(1)}, bf16[32,4608]{1,0:T(8,128)(2,1)}, u32[]{:S(2)}) copy-start(bf16[32,4608]{1,0:T(8,128)(2,1)} %get-tuple-element.61) | copy-start | bytes 884740
  38.1 8.6 %copy-start.3 = (bf16[32,4608]{1,0:T(8,128)(2,1)S(1)}, bf16[32,4608]{1,0:T(8,128)(2,1)}, u32[]{:S(2)}) copy-start(bf16[32,4608]{1,0:T(8,128)(2,1)} %get-tuple-element.63) | copy-start | bytes 884740
  38.1 2.4 %collective-permute-start.8 = (bf16[48,4608]{1,0:T(8,128)(2,1)S(1)}, bf16[48,4608]{1,0:T(8,128)(2,1)S(1)}, u32[]{:S(2)}, u32[]{:S(2)}) collective-permute-start(bf16[48,4608]{1,0:T(8,128)(2,1)S(1)} %get-tuple-element.75), channel_id=1, source_target_pairs={{0,4},{4,0},{8,12},{12,8},{1,5},{5,1},{9,13},{13,9},{2,6},{6,2},{1... | collective-permute-start | bytes 1327112 | tf_op jit(solution)/shard_map/ppermute | solution.py:578
  44.9 19.2 %copy-start.2 = (bf16[32,4608]{1,0:T(8,128)(2,1)S(1)}, bf16[32,4608]{1,0:T(8,128)(2,1)}, u32[]{:S(2)}) copy-start(bf16[32,4608]{1,0:T(8,128)(2,1)} %get-tuple-element.65) | copy-start | bytes 884740
  44.9 21.3 %copy-start.1 = (bf16[32,4608]{1,0:T(8,128)(2,1)S(1)}, bf16[32,4608]{1,0:T(8,128)(2,1)}, u32[]{:S(2)}) copy-start(bf16[32,4608]{1,0:T(8,128)(2,1)} %get-tuple-element.67) | copy-start | bytes 884740
  44.9 2.4 %collective-permute-start.9 = (bf16[96,4608]{1,0:T(8,128)(2,1)S(1)}, bf16[96,4608]{1,0:T(8,128)(2,1)S(1)}, u32[]{:S(2)}, u32[]{:S(2)}) collective-permute-start(bf16[96,4608]{1,0:T(8,128)(2,1)S(1)} %collective-permute-done.2.refs_0_), channel_id=1, source_target_pairs={{0,4},{4,0},{8,12},{12,8},{1,5},{5,1},{9,13},{13,9},{2,6},{6,2},{1... | collective-permute-start | bytes 2654216 | tf_op jit(solution)/shard_map/ppermute | solution.py:578
  44.9 9.9 %collective-permute-start.14 = (bf16[32,4608]{1,0:T(8,128)(2,1)S(1)}, bf16[32,4608]{1,0:T(8,128)(2,1)S(1)}, u32[]{:S(2)}, u32[]{:S(2)}) collective-permute-start(bf16[32,4608]{1,0:T(8,128)(2,1)S(1)} %copy-done.4), channel_id=1, source_target_pairs={{0,8},{4,12},{8,0},{12,4},{1,9},{5,13},{9,1},{13,5},{2,10},{6,14},... | collective-permute-start | bytes 884744 | tf_op jit(solution)/shard_map/ppermute | solution.py:578
  46.7 18.9 %collective-permute-start.15 = (bf16[32,4608]{1,0:T(8,128)(2,1)S(1)}, bf16[32,4608]{1,0:T(8,128)(2,1)S(1)}, u32[]{:S(2)}, u32[]{:S(2)}) collective-permute-start(bf16[32,4608]{1,0:T(8,128)(2,1)S(1)} %copy-done.3), channel_id=1, source_target_pairs={{0,8},{4,12},{8,0},{12,4},{1,9},{5,13},{9,1},{13,5},{2,10},{6,14},... | collective-permute-start | bytes 884744 | tf_op jit(solution)/shard_map/ppermute | solution.py:578
  54.8 10.9 %collective-permute-start.16 = (bf16[32,4608]{1,0:T(8,128)(2,1)S(1)}, bf16[32,4608]{1,0:T(8,128)(2,1)S(1)}, u32[]{:S(2)}, u32[]{:S(2)}) collective-permute-start(bf16[32,4608]{1,0:T(8,128)(2,1)S(1)} %collective-permute-done.14.refs_0_), channel_id=1, source_target_pairs={{0,16},{16,0},{1,17},{17,1},{2,18},{18,2},{3,19},{19,3},{4,20},{20... | collective-permute-start | bytes 884744 | tf_op jit(solution)/shard_map/ppermute | solution.py:578
  56.5 7.6 %collective-permute-start.10 = (bf16[384,256]{1,0:T(8,128)(2,1)S(1)}, bf16[384,256]{1,0:T(8,128)(2,1)S(1)}, u32[]{:S(2)}, u32[]{:S(2)}) collective-permute-start(bf16[384,256]{1,0:T(8,128)(2,1)S(1)} %get-tuple-element.54), channel_id=1, source_target_pairs={{0,1},{1,2},{2,3},{3,0},{4,5},{5,6},{6,7},{7,4},{8,9},{9,10},{10,1... | collective-permute-start | bytes 589832 | tf_op jit(solution)/shard_map/ppermute | solution.py:594
  64.1 7.5 %collective-permute-start.11 = (bf16[384,256]{1,0:T(8,128)(2,1)S(1)}, bf16[384,256]{1,0:T(8,128)(2,1)S(1)}, u32[]{:S(2)}, u32[]{:S(2)}) collective-permute-start(bf16[384,256]{1,0:T(8,128)(2,1)S(1)} %collective-permute-done.10), channel_id=1, source_target_pairs={{0,1},{1,2},{2,3},{3,0},{4,5},{5,6},{6,7},{7,4},{8,9},{9,10},{10,1... | collective-permute-start | bytes 589832 | tf_op jit(solution)/shard_map/ppermute | solution.py:594
  64.1 12.9 %collective-permute-start.17 = (bf16[32,4608]{1,0:T(8,128)(2,1)S(1)}, bf16[32,4608]{1,0:T(8,128)(2,1)S(1)}, u32[]{:S(2)}, u32[]{:S(2)}) collective-permute-start(bf16[32,4608]{1,0:T(8,128)(2,1)S(1)} %copy-done.2), channel_id=1, source_target_pairs={{0,8},{4,12},{8,0},{12,4},{1,9},{5,13},{9,1},{13,5},{2,10},{6,14},... | collective-permute-start | bytes 884744 | tf_op jit(solution)/shard_map/ppermute | solution.py:578
  65.6 11.4 %collective-permute-start.18 = (bf16[32,4608]{1,0:T(8,128)(2,1)S(1)}, bf16[32,4608]{1,0:T(8,128)(2,1)S(1)}, u32[]{:S(2)}, u32[]{:S(2)}) collective-permute-start(bf16[32,4608]{1,0:T(8,128)(2,1)S(1)} %collective-permute-done.15.refs_1_), channel_id=1, source_target_pairs={{0,16},{16,0},{1,17},{17,1},{2,18},{18,2},{3,19},{19,3},{4,20},{20... | collective-permute-start | bytes 884744 | tf_op jit(solution)/shard_map/ppermute | solution.py:578
  66.2 19.5 %collective-permute-start.19 = (bf16[32,4608]{1,0:T(8,128)(2,1)S(1)}, bf16[32,4608]{1,0:T(8,128)(2,1)S(1)}, u32[]{:S(2)}, u32[]{:S(2)}) collective-permute-start(bf16[32,4608]{1,0:T(8,128)(2,1)S(1)} %copy-done.1), channel_id=1, source_target_pairs={{0,8},{4,12},{8,0},{12,4},{1,9},{5,13},{9,1},{13,5},{2,10},{6,14},... | collective-permute-start | bytes 884744 | tf_op jit(solution)/shard_map/ppermute | solution.py:578
  71.5 7.5 %collective-permute-start.12 = (bf16[384,256]{1,0:T(8,128)(2,1)S(1)}, bf16[384,256]{1,0:T(8,128)(2,1)S(1)}, u32[]{:S(2)}, u32[]{:S(2)}) collective-permute-start(bf16[384,256]{1,0:T(8,128)(2,1)S(1)} %collective-permute-done.11), channel_id=1, source_target_pairs={{0,1},{1,2},{2,3},{3,0},{4,5},{5,6},{6,7},{7,4},{8,9},{9,10},{10,1... | collective-permute-start | bytes 589832 | tf_op jit(solution)/shard_map/ppermute | solution.py:594
  77.0 15.1 %collective-permute-start.20 = (bf16[32,4608]{1,0:T(8,128)(2,1)S(1)}, bf16[32,4608]{1,0:T(8,128)(2,1)S(1)}, u32[]{:S(2)}, u32[]{:S(2)}) collective-permute-start(bf16[32,4608]{1,0:T(8,128)(2,1)S(1)} %collective-permute-done.17.refs_2_), channel_id=1, source_target_pairs={{0,16},{16,0},{1,17},{17,1},{2,18},{18,2},{3,19},{19,3},{4,20},{20... | collective-permute-start | bytes 884744 | tf_op jit(solution)/shard_map/ppermute | solution.py:578
  85.6 6.8 %collective-permute-start.21 = (bf16[32,4608]{1,0:T(8,128)(2,1)S(1)}, bf16[32,4608]{1,0:T(8,128)(2,1)S(1)}, u32[]{:S(2)}, u32[]{:S(2)}) collective-permute-start(bf16[32,4608]{1,0:T(8,128)(2,1)S(1)} %collective-permute-done.19.refs_3_), channel_id=1, source_target_pairs={{0,16},{16,0},{1,17},{17,1},{2,18},{18,2},{3,19},{19,3},{4,20},{20... | collective-permute-start | bytes 884744 | tf_op jit(solution)/shard_map/ppermute | solution.py:578
  86.2 5.9 %collective-permute-start.13 = (bf16[384,256]{1,0:T(8,128)(2,1)}, bf16[384,256]{1,0:T(8,128)(2,1)S(1)}, u32[]{:S(2)}, u32[]{:S(2)}) collective-permute-start(bf16[384,256]{1,0:T(8,128)(2,1)} %get-tuple-element.59), channel_id=1, source_target_pairs={{0,8},{4,12},{8,0},{12,4},{1,9},{5,13},{9,1},{13,5},{2,10},{6,14},... | collective-permute-start | bytes 589832 | tf_op jit(solution)/shard_map/ppermute | solution.py:578
  95.4 4.0 %collective-permute-start.22 = (bf16[192,4608]{1,0:T(8,128)(2,1)}, bf16[192,4608]{1,0:T(8,128)(2,1)S(1)}, u32[]{:S(2)}, u32[]{:S(2)}) collective-permute-start(bf16[192,4608]{1,0:T(8,128)(2,1)} %get-tuple-element.69), channel_id=1, source_target_pairs={{0,4},{4,0},{8,12},{12,8},{1,5},{5,1},{9,13},{13,9},{2,6},{6,2},{1... | collective-permute-start | bytes 5308424 | tf_op jit(solution)/shard_map/ppermute | solution.py:578

commit v5 on v4

--- a/solution.py
+++ b/solution.py
@@ -665,12 +665,9 @@
     fetched = lambda piece, *others: flipped(after(piece, *others), "tp", 2)
     swap = lambda array: flipped(array, "groups", 1)
     w_far = [fetched(piece, away[1]) for piece in w_cut[:2]]
-    w_far[0] = after(w_far[0], kv_far)
-    w_far.append(fetched(w_cut[2], w_far[0]))
-    w_other = [swap(w_far[0])]
-    w_far[1] = after(w_far[1], came(far)[0], w_other[0])
-    w_far.append(fetched(w_cut[3], w_far[1]))
-    w_other.append(swap(w_far[1]))
+    w_far[:2] = [after(piece, came(far)[0]) for piece in w_far]
+    w_far += [fetched(piece, before) for piece, before in zip(w_cut[2:], w_far[:2])]
+    w_other = [swap(piece) for piece in w_far[:2]]
 
     near_state, far_state = attention(
         [Step(1, 1, [], same=0), Step(1, 0, everyone), Step(0, 1, [0])],
@@ -681,7 +678,7 @@
         [near_chunk, far_chunk],
         [near_state, None],
     )
-    w_far[2] = after(w_far[2], *far_state, w_other[1])
+    w_far[2] = after(w_far[2], *far_state, *w_other)
     w_other.append(swap(w_far[2]))
     attended, gone = attention(
         [Step(1, 0, others), Step(0, 0, others)],

time: 102 us -> 98.8 us (0.969)
  waiting for transfers between devices: 32 us -> 25.4 us
  starting transfers between devices: 20.7 us -> 24.9 us
  Pallas kernels: 45.8 us -> 44.5 us
    ppermute x17, waiting for transfers between devices: 10.9 us -> 7.41 us  [flipped(): return lax.ppermute(array, axis, [(i, i ^ bit) for i in range(size)])]
    ppermute x3, waiting for transfers between devices: 12.3 us -> 9.14 us  [along_ring(): part = lax.ppermute(part, 'seq', [(i, (i + 1) % size) for i in range(size)])]
    ppermute x3, starting transfers between devices: 1.57 us -> 4.13 us  [along_ring(): part = lax.ppermute(part, 'seq', [(i, (i + 1) % size) for i in range(size)])]
    ppermute x17, starting transfers between devices: 13.6 us -> 15.2 us  [flipped(): return lax.ppermute(array, axis, [(i, i ^ bit) for i in range(size)])]
    pallas_call x13, Pallas kernels: 45.8 us -> 44.5 us  [call(): pl.pallas_call(kernel, in_specs=in_specs, out_specs=[spec for _, _, spec...]
  transfers between devices with their start and end apart: 23 -> 23, of which waited for: 13 -> 11; matrix products, arithmetic and copies ran while one was open for 3% -> 3% of each run, Pallas kernels for 37% -> 37%
where the time goes in v5:
time: 98.8 us; the launch traced here: 98.5 us
  Pallas kernels  44.5 us (45%)
  waiting for transfers between devices  25.4 us (26%)
  starting transfers between devices  24.9 us (25%)
  other arithmetic  3.15 us (3%)
    pallas_call x13, Pallas kernels, call(): pl.pallas_call(kernel, in_specs=in_specs, out_specs=[spec for _, _, spec...  44.5 us
    ppermute x17, starting transfers between devices, flipped(): return lax.ppermute(array, axis, [(i, i ^ bit) for i in range(size)])  15.2 us
    ppermute x3, waiting for transfers between devices, along_ring(): part = lax.ppermute(part, 'seq', [(i, (i + 1) % size) for i in range(size)])  9.14 us
    ppermute x3, waiting for transfers between devices, along_line(): lax.ppermute(array, 'seq', [(i, (i + by) % size) for i in range(size)])  8.87 us
    ppermute x17, waiting for transfers between devices, flipped(): return lax.ppermute(array, axis, [(i, i ^ bit) for i in range(size)])  7.41 us
    ppermute x3, starting transfers between devices, along_line(): lax.ppermute(array, 'seq', [(i, (i + by) % size) for i in range(size)])  5.57 us
    ppermute x3, starting transfers between devices, along_ring(): part = lax.ppermute(part, 'seq', [(i, (i + 1) % size) for i in range(size)])  4.13 us
  transfers between devices with their start and end apart: 23, of which 11 were waited for; matrix products, arithmetic and copies ran while one was open for 3% of the time, Pallas kernels for 37%

profile of v5, /device:TPU:0, one launch (start us, length us, event | category | flops | bytes accessed | tf_op | source)
XLA Modules:
  0.0 98.5 jit_solution(8272555663273306992)
XLA Ops:
  0.0 2.3 %norm_rows.2.refs_0_ = bf16[96,4608]{1,0:T(8,128)(2,1)} custom-call(bf16[192,4608]{1,0:T(8,128)(2,1)} %hidden.5, f32[4608]{0:T(1024)} %gain.4), custom_call_target="tpu_custom_call" | custom-call | flops 1 | bytes 1 | tf_op jit(solution)/shard_map/norm_rows/pallas_call | solution.py:38
  2.9 2.6 %collective-permute-start.3 = (bf16[96,4608]{1,0:T(8,128)(2,1)}, bf16[96,4608]{1,0:T(8,128)(2,1)S(1)}, u32[]{:S(2)}, u32[]{:S(2)}) collective-permute-start(bf16[96,4608]{1,0:T(8,128)(2,1)} %norm_rows.2.refs_0_), channel_id=1, source_target_pairs={{0,8},{4,12},{8,0},{12,4},{1,9},{5,13},{9,1},{13,5},{2,10},{6,14},... | collective-permute-start | bytes 2654216 | tf_op jit(solution)/shard_map/ppermute | solution.py:578
  5.4 2.3 %norm_rows.3.refs_1_ = bf16[96,4608]{1,0:T(8,128)(2,1)} custom-call(bf16[192,4608]{1,0:T(8,128)(2,1)} %hidden.5, f32[4608]{0:T(1024)} %gain.4), custom_call_target="tpu_custom_call" | custom-call | flops 1 | bytes 1 | tf_op jit(solution)/shard_map/norm_rows/pallas_call | solution.py:38
  8.4 1.4 %multiply_cosine_fusion = (f32[768,64]{1,0:T(8,128)S(1)}, f32[768,64]{1,0:T(8,128)S(1)}, f32[768,64]{1,0:T(8,128)S(1)}) fusion(f32[768]{0:T(1024)S(1)} %add_convert_fusion, f32[64]{0:T(128)S(1)} %multiply_power_fusion), kind=kLoop, calls=%fused_computation.2 | loop fusion | flops 98304 | bytes 593152 | tf_op jit(solution)/shard_map/cos | solution.py:567
  9.9 1.3 %pad_maximum_fusion.trig = f32[768,256]{1,0:T(8,128)} fusion(f32[768,64]{1,0:T(8,128)S(1)} %get-tuple-element.79, f32[768,64]{1,0:T(8,128)S(1)} %get-tuple-element.78, f32[768,64]{1,0:T(8,128)S(1)} %get-tuple-element.77), kind=kLoop, calls=%fused_computation | loop fusion | flops 589824 | bytes 1376256 | tf_op jit(solution)/shard_map/concatenate | solution.py:568
  11.2 4.8 %qkv.3 = (bf16[2,384,128]{2,1,0:T(8,128)(2,1)S(1)}, bf16[384,256]{1,0:T(8,128)(2,1)S(1)}) custom-call(f32[768,256]{1,0:T(8,128)} %pad_maximum_fusion.trig, bf16[4608,256]{1,0:T(8,128)(2,1)} %wq.5, bf16[4608,128]{1,0:T(8,128)(2,1)} %wk.5, bf16[4608,128]{1,0:T(8,128)(2,1)} %wv.5, bf16[96,4608]{1,0:T(8,128)(2,1)} %norm_rows.2.refs_0_, ...), custom_call_target="tpu_custom_call" | custom-call | flops 1 | bytes 1 | tf_op jit(solution)/shard_map/qkv/pallas_call | solution.py:38
  16.0 1.6 %collective-permute-start.4 = (bf16[384,256]{1,0:T(8,128)(2,1)S(1)}, bf16[384,256]{1,0:T(8,128)(2,1)S(1)}, u32[]{:S(2)}, u32[]{:S(2)}) collective-permute-start(bf16[384,256]{1,0:T(8,128)(2,1)S(1)} %get-tuple-element.40), channel_id=1, source_target_pairs={{0,1},{1,2},{2,3},{3,0},{4,5},{5,6},{6,7},{7,4},{8,9},{9,10},{10,1... | collective-permute-start | bytes 589832 | tf_op jit(solution)/shard_map/ppermute | solution.py:585
  17.6 2.6 %collective-permute-start.5 = (bf16[384,256]{1,0:T(8,128)(2,1)S(1)}, bf16[384,256]{1,0:T(8,128)(2,1)S(1)}, u32[]{:S(2)}, u32[]{:S(2)}) collective-permute-start(bf16[384,256]{1,0:T(8,128)(2,1)S(1)} %get-tuple-element.40), channel_id=1, source_target_pairs={{0,2},{1,3},{2,0},{3,1},{4,6},{5,7},{6,4},{7,5},{8,10},{9,11},{10,... | collective-permute-start | bytes 589832 | tf_op jit(solution)/shard_map/ppermute | solution.py:585
  20.2 1.3 %collective-permute-start.6 = (bf16[384,256]{1,0:T(8,128)(2,1)S(1)}, bf16[384,256]{1,0:T(8,128)(2,1)S(1)}, u32[]{:S(2)}, u32[]{:S(2)}) collective-permute-start(bf16[384,256]{1,0:T(8,128)(2,1)S(1)} %get-tuple-element.40), channel_id=1, source_target_pairs={{0,3},{1,0},{2,1},{3,2},{4,7},{5,4},{6,5},{7,6},{8,11},{9,8},{10,9... | collective-permute-start | bytes 589832 | tf_op jit(solution)/shard_map/ppermute | solution.py:585
  22.1 2.6 %cut_weights.1 = (bf16[32,4608]{1,0:T(8,128)(2,1)}, bf16[32,4608]{1,0:T(8,128)(2,1)}, bf16[32,4608]{1,0:T(8,128)(2,1)}, bf16[32,4608]{1,0:T(8,128)(2,1)}) custom-call(s32[10]{0:T(128)S(1)} %pad_add_fusion.1.table, bf16[256,4608]{1,0:T(8,128)(2,1)} %weights_hbm.1), custom_call_target="tpu_custom_call" | custom-call | flops 1 | bytes 1 | tf_op jit(solution)/shard_map/cut_weights/pallas_call | solution.py:38
  25.7 7.9 %collective-permute-done.5 = bf16[384,256]{1,0:T(8,128)(2,1)S(1)} collective-permute-done((bf16[384,256]{1,0:T(8,128)(2,1)S(1)}, bf16[384,256]{1,0:T(8,128)(2,1)S(1)}, u32[]{:S(2)}, u32[]{:S(2)}) %collective-permute-start.5) | collective-permute-done | bytes 196640 | tf_op jit(solution)/shard_map/ppermute | solution.py:585
  33.6 4.3 %attention.3 = (f32[3,8,256]{2,1,0:T(8,128)S(1)}, f32[3,144,256]{2,1,0:T(8,128)S(1)}) custom-call(s32[10]{0:T(128)S(1)} %pad_add_fusion.1.table, bf16[2,384,128]{2,1,0:T(8,128)(2,1)S(1)} %get-tuple-element.46.refs_0_, bf16[1,384,256]{2,1,0:T(8,128)(2,1)S(1)} %bitcast.16, bf16[1,384,256]{2,1,0:T(8,128)(2,1)S(1)} %bitcast.18, ...), custom_call_target="tpu_custom_call" | custom-call | flops 1 | bytes 1 | tf_op jit(solution)/shard_map/attention/pallas_call | solution.py:38
  38.6 1.3 %collective-permute-done.7.refs_1_ = bf16[48,4608]{1,0:T(8,128)(2,1)S(1)} collective-permute-done((bf16[48,4608]{1,0:T(8,128)(2,1)S(1)}, bf16[48,4608]{1,0:T(8,128)(2,1)S(1)}, u32[]{:S(2)}, u32[]{:S(2)}) %collective-permute-start.7) | collective-permute-done | bytes 442400 | tf_op jit(solution)/shard_map/ppermute | solution.py:578
  40.5 3.4 %qkv.4 = (bf16[2,384,128]{2,1,0:T(8,128)(2,1)S(1)}, bf16[384,256]{1,0:T(8,128)(2,1)S(1)}) custom-call(f32[768,256]{1,0:T(8,128)} %pad_maximum_fusion.trig, bf16[4608,256]{1,0:T(8,128)(2,1)} %wq.5, bf16[4608,128]{1,0:T(8,128)(2,1)} %wk.5, bf16[4608,128]{1,0:T(8,128)(2,1)} %wv.5, bf16[96,4608]{1,0:T(8,128)(2,1)S(1)} %collective-permute-done.3.refs_0_, ...), custom_call_target="tpu_custom_call" | custom-call | flops 1 | bytes 1 | tf_op jit(solution)/shard_map/qkv/pallas_call | solution.py:38
  43.8 1.0 %collective-permute-done.2.refs_0_ = bf16[96,4608]{1,0:T(8,128)(2,1)S(1)} collective-permute-done((bf16[96,4608]{1,0:T(8,128)(2,1)}, bf16[96,4608]{1,0:T(8,128)(2,1)S(1)}, u32[]{:S(2)}, u32[]{:S(2)}) %collective-permute-start.2) | collective-permute-done | bytes 884768 | tf_op jit(solution)/shard_map/ppermute | solution.py:578
  44.9 1.8 %collective-permute-start.14 = (bf16[32,4608]{1,0:T(8,128)(2,1)S(1)}, bf16[32,4608]{1,0:T(8,128)(2,1)S(1)}, u32[]{:S(2)}, u32[]{:S(2)}) collective-permute-start(bf16[32,4608]{1,0:T(8,128)(2,1)S(1)} %copy-done.4), channel_id=1, source_target_pairs={{0,8},{4,12},{8,0},{12,4},{1,9},{5,13},{9,1},{13,5},{2,10},{6,14},... | collective-permute-start | bytes 884744 | tf_op jit(solution)/shard_map/ppermute | solution.py:578
  47.3 3.3 %qkv.5 = (bf16[2,384,128]{2,1,0:T(8,128)(2,1)S(1)}, bf16[384,256]{1,0:T(8,128)(2,1)S(1)}) custom-call(f32[768,256]{1,0:T(8,128)} %pad_maximum_fusion.trig, bf16[4608,256]{1,0:T(8,128)(2,1)} %wq.5, bf16[4608,128]{1,0:T(8,128)(2,1)} %wk.5, bf16[4608,128]{1,0:T(8,128)(2,1)} %wv.5, ...), custom_call_target="tpu_custom_call", output_to_operand_aliasing={{0}: (6, {}), {1}: (7, {})} | custom-call | flops 1 | bytes 1 | tf_op jit(solution)/shard_map/qkv/pallas_call | solution.py:38
  50.6 3.1 %collective-permute-start.10 = (bf16[384,256]{1,0:T(8,128)(2,1)S(1)}, bf16[384,256]{1,0:T(8,128)(2,1)S(1)}, u32[]{:S(2)}, u32[]{:S(2)}) collective-permute-start(bf16[384,256]{1,0:T(8,128)(2,1)S(1)} %get-tuple-element.54), channel_id=1, source_target_pairs={{0,1},{1,2},{2,3},{3,0},{4,5},{5,6},{6,7},{7,4},{8,9},{9,10},{10,1... | collective-permute-start | bytes 589832 | tf_op jit(solution)/shard_map/ppermute | solution.py:594
  53.7 6.0 %collective-permute-done.10 = bf16[384,256]{1,0:T(8,128)(2,1)S(1)} collective-permute-done((bf16[384,256]{1,0:T(8,128)(2,1)S(1)}, bf16[384,256]{1,0:T(8,128)(2,1)S(1)}, u32[]{:S(2)}, u32[]{:S(2)}) %collective-permute-start.10) | collective-permute-done | bytes 196640 | tf_op jit(solution)/shard_map/ppermute | solution.py:594
  60.7 1.5 %collective-permute-start.17 = (bf16[32,4608]{1,0:T(8,128)(2,1)S(1)}, bf16[32,4608]{1,0:T(8,128)(2,1)S(1)}, u32[]{:S(2)}, u32[]{:S(2)}) collective-permute-start(bf16[32,4608]{1,0:T(8,128)(2,1)S(1)} %collective-permute-done.14.refs_0_), channel_id=1, source_target_pairs={{0,16},{16,0},{1,17},{17,1},{2,18},{18,2},{3,19},{19,3},{4,20},{20... | collective-permute-start | bytes 884744 | tf_op jit(solution)/shard_map/ppermute | solution.py:578
  63.3 1.5 %collective-permute-start.19 = (bf16[32,4608]{1,0:T(8,128)(2,1)S(1)}, bf16[32,4608]{1,0:T(8,128)(2,1)S(1)}, u32[]{:S(2)}, u32[]{:S(2)}) collective-permute-start(bf16[32,4608]{1,0:T(8,128)(2,1)S(1)} %copy-done.1), channel_id=1, source_target_pairs={{0,8},{4,12},{8,0},{12,4},{1,9},{5,13},{9,1},{13,5},{2,10},{6,14},... | collective-permute-start | bytes 884744 | tf_op jit(solution)/shard_map/ppermute | solution.py:578
  64.7 3.2 %collective-permute-done.11 = bf16[384,256]{1,0:T(8,128)(2,1)S(1)} collective-permute-done((bf16[384,256]{1,0:T(8,128)(2,1)S(1)}, bf16[384,256]{1,0:T(8,128)(2,1)S(1)}, u32[]{:S(2)}, u32[]{:S(2)}) %collective-permute-start.11) | collective-permute-done | bytes 196640 | tf_op jit(solution)/shard_map/ppermute | solution.py:594
  67.9 5.5 %attention.4 = (f32[3,8,256]{2,1,0:T(8,128)S(1)}, f32[3,144,256]{2,1,0:T(8,128)S(1)}, f32[3,8,256]{2,1,0:T(8,128)S(1)}, f32[3,144,256]{2,1,0:T(8,128)S(1)}) custom-call(s32[10]{0:T(128)S(1)} %pad_add_fusion.1.table, bf16[2,384,128]{2,1,0:T(8,128)(2,1)S(1)} %get-tuple-element.46.refs_0_, ...), custom_call_target="tpu_custom_call", output_to_operand_aliasing={{0}: (8, {}), {1}: (9, {})} | custom-call | flops 1 | bytes 1 | tf_op jit(solution)/shard_map/attention/pallas_call | solution.py:38
  73.4 1.5 %collective-permute-done.18.refs_5_ = bf16[32,4608]{1,0:T(8,128)(2,1)S(1)} collective-permute-done((bf16[32,4608]{1,0:T(8,128)(2,1)S(1)}, bf16[32,4608]{1,0:T(8,128)(2,1)S(1)}, u32[]{:S(2)}, u32[]{:S(2)}) %collective-permute-start.18) | collective-permute-done | bytes 294944 | tf_op jit(solution)/shard_map/ppermute | solution.py:578
  74.9 1.5 %collective-permute-start.20 = (bf16[32,4608]{1,0:T(8,128)(2,1)S(1)}, bf16[32,4608]{1,0:T(8,128)(2,1)S(1)}, u32[]{:S(2)}, u32[]{:S(2)}) collective-permute-start(bf16[32,4608]{1,0:T(8,128)(2,1)S(1)} %collective-permute-done.16.refs_2_), channel_id=1, source_target_pairs={{0,16},{16,0},{1,17},{17,1},{2,18},{18,2},{3,19},{19,3},{4,20},{20... | collective-permute-start | bytes 884744 | tf_op jit(solution)/shard_map/ppermute | solution.py:578
  76.4 5.3 %attention.5 = (bf16[384,256]{1,0:T(8,128)(2,1)}, bf16[384,256]{1,0:T(8,128)(2,1)}, f32[3,8,256]{2,1,0:T(8,128)S(1)}, f32[3,144,256]{2,1,0:T(8,128)S(1)}, f32[3,...) custom-call(s32[10]{0:T(128)S(1)} %pad_add_fusion.1.table, ...), custom_call_target="tpu_custom_call", output_to_operand_aliasing={{2}: (7, {}), {3}: (8, {}), {4}: (9, {}), {5}: (10, {})} | custom-call | flops 1 | bytes 1 | tf_op jit(solution)/shard_map/attention/pallas_call | solution.py:38
  82.3 2.5 %collective-permute-start.13 = (bf16[384,256]{1,0:T(8,128)(2,1)}, bf16[384,256]{1,0:T(8,128)(2,1)S(1)}, u32[]{:S(2)}, u32[]{:S(2)}) collective-permute-start(bf16[384,256]{1,0:T(8,128)(2,1)} %get-tuple-element.59), channel_id=1, source_target_pairs={{0,8},{4,12},{8,0},{12,4},{1,9},{5,13},{9,1},{13,5},{2,10},{6,14},... | collective-permute-start | bytes 589832 | tf_op jit(solution)/shard_map/ppermute | solution.py:578
  84.8 3.4 %output_near.1.near = f32[384,4608]{1,0:T(8,128)S(1)} custom-call(bf16[384,256]{1,0:T(8,128)(2,1)} %get-tuple-element.60.left_hbm, bf16[256,4608]{1,0:T(8,128)(2,1)} %weights_hbm.1), custom_call_target="tpu_custom_call" | custom-call | flops 1 | bytes 1 | tf_op jit(solution)/shard_map/output_near/pallas_call | solution.py:38
  88.7 3.0 %output_send.1 = (bf16[192,4608]{1,0:T(8,128)(2,1)}, bf16[256,4608]{1,0:T(8,128)(2,1)S(1)}) custom-call(s32[10]{0:T(128)S(1)} %pad_add_fusion.1.table, bf16[384,256]{1,0:T(8,128)(2,1)S(1)} %collective-permute-done.13.left_hbm, f32[384,4608]{1,0:T(8,128)S(1)} %output_near.1.near, bf16[32,4608]{1,0:T(8,128)(2,1)S(1)} %collective-permute-done.14.refs_0_, ...), custom_call_target="tpu_custom_call" | custom-call | flops 1 | bytes 1 | tf_op jit(solution)/shard_map/output_send/pallas_call | solution.py:38
  91.8 1.7 %output_keep.1 = (f32[192,4608]{1,0:T(8,128)S(1)}, bf16[192,4608]{1,0:T(8,128)(2,1)S(1)}) custom-call(bf16[384,256]{1,0:T(8,128)(2,1)S(1)} %collective-permute-done.13.left_hbm, bf16[192,4608]{1,0:T(8,128)(2,1)} %hidden.5, f32[384,4608]{1,0:T(8,128)S(1)} %output_near.1.near, bf16[256,4608]{1,0:T(8,128)(2,1)S(1)} %get-tuple-element.70.weights), custom_call_target="tpu_custom_call" | custom-call | flops 1 | bytes 1 | tf_op jit(solution)/shard_map/output_keep/pallas_call | solution.py:38
  93.5 2.1 %collective-permute-done.22.received = bf16[192,4608]{1,0:T(8,128)(2,1)S(1)} collective-permute-done((bf16[192,4608]{1,0:T(8,128)(2,1)}, bf16[192,4608]{1,0:T(8,128)(2,1)S(1)}, u32[]{:S(2)}, u32[]{:S(2)}) %collective-permute-start.22) | collective-permute-done | bytes 1769504 | tf_op jit(solution)/shard_map/ppermute | solution.py:578
  95.7 2.7 %output_norm.1 = bf16[192,4608]{1,0:T(8,128)(2,1)} custom-call(bf16[192,4608]{1,0:T(8,128)(2,1)S(1)} %collective-permute-done.22.received, bf16[192,4608]{1,0:T(8,128)(2,1)S(1)} %get-tuple-element.71.hidden, f32[192,4608]{1,0:T(8,128)S(1)} %get-tuple-element.72.kept, f32[4608]{0:T(1024)} %gain.5), custom_call_target="tpu_custom_call" | custom-call | flops 1 | bytes 1 | tf_op jit(solution)/shard_map/output_norm/pallas_call | solution.py:38
  (49 shorter events, 7.8 us)
Async XLA Ops:
  2.3 5.7 %copy-start = (s32[8]{0:T(128)S(1)}, s32[8]{0:T(128)}, u32[]{:S(2)}) copy-start(s32[8]{0:T(128)} %param.15) | copy-start | bytes 100
  2.3 8.8 %collective-permute-start = (bf16[96,4608]{1,0:T(8,128)(2,1)}, bf16[96,4608]{1,0:T(8,128)(2,1)S(1)}, u32[]{:S(2)}, u32[]{:S(2)}) collective-permute-start(bf16[96,4608]{1,0:T(8,128)(2,1)} %norm_rows.2.refs_0_), channel_id=1, source_target_pairs={{0,4},{4,0},{8,12},{12,8},{1,5},{5,1},{9,13},{13,9},{2,6},{6,2},{1... | collective-permute-start | bytes 2654216 | tf_op jit(solution)/shard_map/ppermute | solution.py:578
  2.9 35.1 %collective-permute-start.3 = (bf16[96,4608]{1,0:T(8,128)(2,1)}, bf16[96,4608]{1,0:T(8,128)(2,1)S(1)}, u32[]{:S(2)}, u32[]{:S(2)}) collective-permute-start(bf16[96,4608]{1,0:T(8,128)(2,1)} %norm_rows.2.refs_0_), channel_id=1, source_target_pairs={{0,8},{4,12},{8,0},{12,4},{1,9},{5,13},{9,1},{13,5},{2,10},{6,14},... | collective-permute-start | bytes 2654216 | tf_op jit(solution)/shard_map/ppermute | solution.py:578
  7.8 3.4 %collective-permute-start.1 = (bf16[96,4608]{1,0:T(8,128)(2,1)}, bf16[96,4608]{1,0:T(8,128)(2,1)S(1)}, u32[]{:S(2)}, u32[]{:S(2)}) collective-permute-start(bf16[96,4608]{1,0:T(8,128)(2,1)} %norm_rows.3.refs_1_), channel_id=1, source_target_pairs={{0,4},{4,0},{8,12},{12,8},{1,5},{5,1},{9,13},{13,9},{2,6},{6,2},{1... | collective-permute-start | bytes 2654216 | tf_op jit(solution)/shard_map/ppermute | solution.py:578
  16.0 9.7 %collective-permute-start.4 = (bf16[384,256]{1,0:T(8,128)(2,1)S(1)}, bf16[384,256]{1,0:T(8,128)(2,1)S(1)}, u32[]{:S(2)}, u32[]{:S(2)}) collective-permute-start(bf16[384,256]{1,0:T(8,128)(2,1)S(1)} %get-tuple-element.40), channel_id=1, source_target_pairs={{0,1},{1,2},{2,3},{3,0},{4,5},{5,6},{6,7},{7,4},{8,9},{9,10},{10,1... | collective-permute-start | bytes 589832 | tf_op jit(solution)/shard_map/ppermute | solution.py:585
  17.6 16.0 %collective-permute-start.5 = (bf16[384,256]{1,0:T(8,128)(2,1)S(1)}, bf16[384,256]{1,0:T(8,128)(2,1)S(1)}, u32[]{:S(2)}, u32[]{:S(2)}) collective-permute-start(bf16[384,256]{1,0:T(8,128)(2,1)S(1)} %get-tuple-element.40), channel_id=1, source_target_pairs={{0,2},{1,3},{2,0},{3,1},{4,6},{5,7},{6,4},{7,5},{8,10},{9,11},{10,... | collective-permute-start | bytes 589832 | tf_op jit(solution)/shard_map/ppermute | solution.py:585
  20.2 13.4 %collective-permute-start.6 = (bf16[384,256]{1,0:T(8,128)(2,1)S(1)}, bf16[384,256]{1,0:T(8,128)(2,1)S(1)}, u32[]{:S(2)}, u32[]{:S(2)}) collective-permute-start(bf16[384,256]{1,0:T(8,128)(2,1)S(1)} %get-tuple-element.40), channel_id=1, source_target_pairs={{0,3},{1,0},{2,1},{3,2},{4,7},{5,4},{6,5},{7,6},{8,11},{9,8},{10,9... | collective-permute-start | bytes 589832 | tf_op jit(solution)/shard_map/ppermute | solution.py:585
  21.5 23.3 %collective-permute-start.2 = (bf16[96,4608]{1,0:T(8,128)(2,1)}, bf16[96,4608]{1,0:T(8,128)(2,1)S(1)}, u32[]{:S(2)}, u32[]{:S(2)}) collective-permute-start(bf16[96,4608]{1,0:T(8,128)(2,1)} %norm_rows.3.refs_1_), channel_id=1, source_target_pairs={{0,8},{4,12},{8,0},{12,4},{1,9},{5,13},{9,1},{13,5},{2,10},{6,14},... | collective-permute-start | bytes 2654216 | tf_op jit(solution)/shard_map/ppermute | solution.py:578
  38.0 1.9 %collective-permute-start.7 = (bf16[48,4608]{1,0:T(8,128)(2,1)S(1)}, bf16[48,4608]{1,0:T(8,128)(2,1)S(1)}, u32[]{:S(2)}, u32[]{:S(2)}) collective-permute-start(bf16[48,4608]{1,0:T(8,128)(2,1)S(1)} %get-tuple-element.76), channel_id=1, source_target_pairs={{0,4},{4,0},{8,12},{12,8},{1,5},{5,1},{9,13},{13,9},{2,6},{6,2},{1... | collective-permute-start | bytes 1327112 | tf_op jit(solution)/shard_map/ppermute | solution.py:578
  38.1 6.8 %copy-start.4 = (bf16[32,4608]{1,0:T(8,128)(2,1)S(1)}, bf16[32,4608]{1,0:T(8,128)(2,1)}, u32[]{:S(2)}) copy-start(bf16[32,4608]{1,0:T(8,128)(2,1)} %get-tuple-element.61) | copy-start | bytes 884740
  38.1 8.6 %copy-start.3 = (bf16[32,4608]{1,0:T(8,128)(2,1)S(1)}, bf16[32,4608]{1,0:T(8,128)(2,1)}, u32[]{:S(2)}) copy-start(bf16[32,4608]{1,0:T(8,128)(2,1)} %get-tuple-element.63) | copy-start | bytes 884740
  38.1 2.4 %collective-permute-start.8 = (bf16[48,4608]{1,0:T(8,128)(2,1)S(1)}, bf16[48,4608]{1,0:T(8,128)(2,1)S(1)}, u32[]{:S(2)}, u32[]{:S(2)}) collective-permute-start(bf16[48,4608]{1,0:T(8,128)(2,1)S(1)} %get-tuple-element.75), channel_id=1, source_target_pairs={{0,4},{4,0},{8,12},{12,8},{1,5},{5,1},{9,13},{13,9},{2,6},{6,2},{1... | collective-permute-start | bytes 1327112 | tf_op jit(solution)/shard_map/ppermute | solution.py:578
  44.9 17.3 %copy-start.2 = (bf16[32,4608]{1,0:T(8,128)(2,1)S(1)}, bf16[32,4608]{1,0:T(8,128)(2,1)}, u32[]{:S(2)}) copy-start(bf16[32,4608]{1,0:T(8,128)(2,1)} %get-tuple-element.65) | copy-start | bytes 884740
  44.9 18.4 %copy-start.1 = (bf16[32,4608]{1,0:T(8,128)(2,1)S(1)}, bf16[32,4608]{1,0:T(8,128)(2,1)}, u32[]{:S(2)}) copy-start(bf16[32,4608]{1,0:T(8,128)(2,1)} %get-tuple-element.67) | copy-start | bytes 884740
  44.9 2.4 %collective-permute-start.9 = (bf16[96,4608]{1,0:T(8,128)(2,1)S(1)}, bf16[96,4608]{1,0:T(8,128)(2,1)S(1)}, u32[]{:S(2)}, u32[]{:S(2)}) collective-permute-start(bf16[96,4608]{1,0:T(8,128)(2,1)S(1)} %collective-permute-done.2.refs_0_), channel_id=1, source_target_pairs={{0,4},{4,0},{8,12},{12,8},{1,5},{5,1},{9,13},{13,9},{2,6},{6,2},{1... | collective-permute-start | bytes 2654216 | tf_op jit(solution)/shard_map/ppermute | solution.py:578
  44.9 15.8 %collective-permute-start.14 = (bf16[32,4608]{1,0:T(8,128)(2,1)S(1)}, bf16[32,4608]{1,0:T(8,128)(2,1)S(1)}, u32[]{:S(2)}, u32[]{:S(2)}) collective-permute-start(bf16[32,4608]{1,0:T(8,128)(2,1)S(1)} %copy-done.4), channel_id=1, source_target_pairs={{0,8},{4,12},{8,0},{12,4},{1,9},{5,13},{9,1},{13,5},{2,10},{6,14},... | collective-permute-start | bytes 884744 | tf_op jit(solution)/shard_map/ppermute | solution.py:578
  46.7 16.0 %collective-permute-start.15 = (bf16[32,4608]{1,0:T(8,128)(2,1)S(1)}, bf16[32,4608]{1,0:T(8,128)(2,1)S(1)}, u32[]{:S(2)}, u32[]{:S(2)}) collective-permute-start(bf16[32,4608]{1,0:T(8,128)(2,1)S(1)} %copy-done.3), channel_id=1, source_target_pairs={{0,8},{4,12},{8,0},{12,4},{1,9},{5,13},{9,1},{13,5},{2,10},{6,14},... | collective-permute-start | bytes 884744 | tf_op jit(solution)/shard_map/ppermute | solution.py:578
  50.6 9.1 %collective-permute-start.10 = (bf16[384,256]{1,0:T(8,128)(2,1)S(1)}, bf16[384,256]{1,0:T(8,128)(2,1)S(1)}, u32[]{:S(2)}, u32[]{:S(2)}) collective-permute-start(bf16[384,256]{1,0:T(8,128)(2,1)S(1)} %get-tuple-element.54), channel_id=1, source_target_pairs={{0,1},{1,2},{2,3},{3,0},{4,5},{5,6},{6,7},{7,4},{8,9},{9,10},{10,1... | collective-permute-start | bytes 589832 | tf_op jit(solution)/shard_map/ppermute | solution.py:594
  59.7 8.2 %collective-permute-start.11 = (bf16[384,256]{1,0:T(8,128)(2,1)S(1)}, bf16[384,256]{1,0:T(8,128)(2,1)S(1)}, u32[]{:S(2)}, u32[]{:S(2)}) collective-permute-start(bf16[384,256]{1,0:T(8,128)(2,1)S(1)} %collective-permute-done.10), channel_id=1, source_target_pairs={{0,1},{1,2},{2,3},{3,0},{4,5},{5,6},{6,7},{7,4},{8,9},{9,10},{10,1... | collective-permute-start | bytes 589832 | tf_op jit(solution)/shard_map/ppermute | solution.py:594
  60.7 12.7 %collective-permute-start.17 = (bf16[32,4608]{1,0:T(8,128)(2,1)S(1)}, bf16[32,4608]{1,0:T(8,128)(2,1)S(1)}, u32[]{:S(2)}, u32[]{:S(2)}) collective-permute-start(bf16[32,4608]{1,0:T(8,128)(2,1)S(1)} %collective-permute-done.14.refs_0_), channel_id=1, source_target_pairs={{0,16},{16,0},{1,17},{17,1},{2,18},{18,2},{3,19},{19,3},{4,20},{20... | collective-permute-start | bytes 884744 | tf_op jit(solution)/shard_map/ppermute | solution.py:578
  62.2 11.2 %collective-permute-start.16 = (bf16[32,4608]{1,0:T(8,128)(2,1)S(1)}, bf16[32,4608]{1,0:T(8,128)(2,1)S(1)}, u32[]{:S(2)}, u32[]{:S(2)}) collective-permute-start(bf16[32,4608]{1,0:T(8,128)(2,1)S(1)} %copy-done.2), channel_id=1, source_target_pairs={{0,8},{4,12},{8,0},{12,4},{1,9},{5,13},{9,1},{13,5},{2,10},{6,14},... | collective-permute-start | bytes 884744 | tf_op jit(solution)/shard_map/ppermute | solution.py:578
  62.7 12.2 %collective-permute-start.18 = (bf16[32,4608]{1,0:T(8,128)(2,1)S(1)}, bf16[32,4608]{1,0:T(8,128)(2,1)S(1)}, u32[]{:S(2)}, u32[]{:S(2)}) collective-permute-start(bf16[32,4608]{1,0:T(8,128)(2,1)S(1)} %collective-permute-done.15.refs_1_), channel_id=1, source_target_pairs={{0,16},{16,0},{1,17},{17,1},{2,18},{18,2},{3,19},{19,3},{4,20},{20... | collective-permute-start | bytes 884744 | tf_op jit(solution)/shard_map/ppermute | solution.py:578
  63.3 18.5 %collective-permute-start.19 = (bf16[32,4608]{1,0:T(8,128)(2,1)S(1)}, bf16[32,4608]{1,0:T(8,128)(2,1)S(1)}, u32[]{:S(2)}, u32[]{:S(2)}) collective-permute-start(bf16[32,4608]{1,0:T(8,128)(2,1)S(1)} %copy-done.1), channel_id=1, source_target_pairs={{0,8},{4,12},{8,0},{12,4},{1,9},{5,13},{9,1},{13,5},{2,10},{6,14},... | collective-permute-start | bytes 884744 | tf_op jit(solution)/shard_map/ppermute | solution.py:578
  67.9 8.5 %collective-permute-start.12 = (bf16[384,256]{1,0:T(8,128)(2,1)S(1)}, bf16[384,256]{1,0:T(8,128)(2,1)S(1)}, u32[]{:S(2)}, u32[]{:S(2)}) collective-permute-start(bf16[384,256]{1,0:T(8,128)(2,1)S(1)} %collective-permute-done.11), channel_id=1, source_target_pairs={{0,1},{1,2},{2,3},{3,0},{4,5},{5,6},{6,7},{7,4},{8,9},{9,10},{10,1... | collective-permute-start | bytes 589832 | tf_op jit(solution)/shard_map/ppermute | solution.py:594
  74.9 13.3 %collective-permute-start.20 = (bf16[32,4608]{1,0:T(8,128)(2,1)S(1)}, bf16[32,4608]{1,0:T(8,128)(2,1)S(1)}, u32[]{:S(2)}, u32[]{:S(2)}) collective-permute-start(bf16[32,4608]{1,0:T(8,128)(2,1)S(1)} %collective-permute-done.16.refs_2_), channel_id=1, source_target_pairs={{0,16},{16,0},{1,17},{17,1},{2,18},{18,2},{3,19},{19,3},{4,20},{20... | collective-permute-start | bytes 884744 | tf_op jit(solution)/shard_map/ppermute | solution.py:578
  81.7 7.0 %collective-permute-start.21 = (bf16[32,4608]{1,0:T(8,128)(2,1)S(1)}, bf16[32,4608]{1,0:T(8,128)(2,1)S(1)}, u32[]{:S(2)}, u32[]{:S(2)}) collective-permute-start(bf16[32,4608]{1,0:T(8,128)(2,1)S(1)} %collective-permute-done.19.refs_3_), channel_id=1, source_target_pairs={{0,16},{16,0},{1,17},{17,1},{2,18},{18,2},{3,19},{19,3},{4,20},{20... | collective-permute-start | bytes 884744 | tf_op jit(solution)/shard_map/ppermute | solution.py:578
  82.3 6.4 %collective-permute-start.13 = (bf16[384,256]{1,0:T(8,128)(2,1)}, bf16[384,256]{1,0:T(8,128)(2,1)S(1)}, u32[]{:S(2)}, u32[]{:S(2)}) collective-permute-start(bf16[384,256]{1,0:T(8,128)(2,1)} %get-tuple-element.59), channel_id=1, source_target_pairs={{0,8},{4,12},{8,0},{12,4},{1,9},{5,13},{9,1},{13,5},{2,10},{6,14},... | collective-permute-start | bytes 589832 | tf_op jit(solution)/shard_map/ppermute | solution.py:578
  91.7 4.0 %collective-permute-start.22 = (bf16[192,4608]{1,0:T(8,128)(2,1)}, bf16[192,4608]{1,0:T(8,128)(2,1)S(1)}, u32[]{:S(2)}, u32[]{:S(2)}) collective-permute-start(bf16[192,4608]{1,0:T(8,128)(2,1)} %get-tuple-element.69), channel_id=1, source_target_pairs={{0,4},{4,0},{8,12},{12,8},{1,5},{5,1},{9,13},{13,9},{2,6},{6,2},{1... | collective-permute-start | bytes 5308424 | tf_op jit(solution)/shard_map/ppermute | solution.py:578

commit v6 on v4

--- a/solution.py
+++ b/solution.py
@@ -587,10 +587,12 @@
     return parts
 
 
-def along_ring(array):
+def along_ring(array, beside):
     size = lax.axis_size("seq")
     parts, part = [array[None]], array
-    for _ in range(1, size):
+    for step in range(1, size):
+        if step == size - 1:
+            part = after(part, beside)
         part = lax.ppermute(part, "seq", [(i, (i + 1) % size) for i in range(size)])
         parts.append(Came(part[None]))
     return parts
@@ -660,16 +662,15 @@
         held,
     )
     q_far, kv_far = held
-    far = along_ring(kv_far)
 
     fetched = lambda piece, *others: flipped(after(piece, *others), "tp", 2)
     swap = lambda array: flipped(array, "groups", 1)
     w_far = [fetched(piece, away[1]) for piece in w_cut[:2]]
     w_far[0] = after(w_far[0], kv_far)
-    w_far.append(fetched(w_cut[2], w_far[0]))
     w_other = [swap(w_far[0])]
-    w_far[1] = after(w_far[1], came(far)[0], w_other[0])
-    w_far.append(fetched(w_cut[3], w_far[1]))
+    far = along_ring(kv_far, w_other[0])
+    w_far[1] = after(w_far[1], came(far)[0])
+    w_far += [fetched(piece, before) for piece, before in zip(w_cut[2:], w_far[:2])]
     w_other.append(swap(w_far[1]))
 
     near_state, far_state = attention(
@@ -681,7 +682,7 @@
         [near_chunk, far_chunk],
         [near_state, None],
     )
-    w_far[2] = after(w_far[2], *far_state, w_other[1])
+    w_far[2] = after(w_far[2], *far_state)
     w_other.append(swap(w_far[2]))
     attended, gone = attention(
         [Step(1, 0, others), Step(0, 0, others)],
@@ -695,7 +696,7 @@
     )
     gone = flipped(gone, "tp", 2)
     near_sum = output_near(attended, w_out)
-    w_other.append(swap(after(w_far[3], attended)))
+    w_other.append(swap(after(w_far[3], attended, w_other[1])))
     pieces = [Came(piece) for piece in w_far + w_other]
     sent, w_laid = output_send(table, group_at, Came(gone), near_sum, pieces)
     received = flipped(sent, "tp", 1)

time: 102 us -> 99.2 us (0.973)
  waiting for transfers between devices: 32 us -> 26 us
  starting transfers between devices: 20.7 us -> 24.2 us
    ppermute x3, waiting for transfers between devices: 12.3 us -> 8.33 us  [along_ring(): part = lax.ppermute(part, 'seq', [(i, (i + 1) % size) for i in range(size)])]
    ppermute x3, starting transfers between devices: 1.57 us -> 4.16 us  [along_ring(): part = lax.ppermute(part, 'seq', [(i, (i + 1) % size) for i in range(size)])]
    ppermute x17, waiting for transfers between devices: 10.9 us -> 8.84 us  [flipped(): return lax.ppermute(array, axis, [(i, i ^ bit) for i in range(size)])]
  transfers between devices with their start and end apart: 23 -> 23, of which waited for: 13 -> 12; matrix products, arithmetic and copies ran while one was open for 3% -> 3% of each run, Pallas kernels for 37% -> 38%
where the time goes in v6:
time: 99.2 us; the launch traced here: 99 us
  Pallas kernels  45.2 us (46%)
  waiting for transfers between devices  26 us (26%)
  starting transfers between devices  24.2 us (24%)
  other arithmetic  3.15 us (3%)
    pallas_call x13, Pallas kernels, call(): pl.pallas_call(kernel, in_specs=in_specs, out_specs=[spec for _, _, spec...  45.2 us
    ppermute x17, starting transfers between devices, flipped(): return lax.ppermute(array, axis, [(i, i ^ bit) for i in range(size)])  14.4 us
    ppermute x3, waiting for transfers between devices, along_line(): lax.ppermute(array, 'seq', [(i, (i + by) % size) for i in range(size)])  8.85 us
    ppermute x17, waiting for transfers between devices, flipped(): return lax.ppermute(array, axis, [(i, i ^ bit) for i in range(size)])  8.84 us
    ppermute x3, waiting for transfers between devices, along_ring(): part = lax.ppermute(part, 'seq', [(i, (i + 1) % size) for i in range(size)])  8.33 us
    ppermute x3, starting transfers between devices, along_line(): lax.ppermute(array, 'seq', [(i, (i + by) % size) for i in range(size)])  5.57 us
    ppermute x3, starting transfers between devices, along_ring(): part = lax.ppermute(part, 'seq', [(i, (i + 1) % size) for i in range(size)])  4.16 us
  transfers between devices with their start and end apart: 23, of which 12 were waited for; matrix products, arithmetic and copies ran while one was open for 3% of the time, Pallas kernels for 38%

profile of v6, /device:TPU:0, one launch (start us, length us, event | category | flops | bytes accessed | tf_op | source)
XLA Modules:
  0.0 99.0 jit_solution(3843983667471965046)
XLA Ops:
  0.0 2.3 %norm_rows.2.refs_0_ = bf16[96,4608]{1,0:T(8,128)(2,1)} custom-call(bf16[192,4608]{1,0:T(8,128)(2,1)} %hidden.5, f32[4608]{0:T(1024)} %gain.4), custom_call_target="tpu_custom_call" | custom-call | flops 1 | bytes 1 | tf_op jit(solution)/shard_map/norm_rows/pallas_call | solution.py:38
  2.9 2.6 %collective-permute-start.3 = (bf16[96,4608]{1,0:T(8,128)(2,1)}, bf16[96,4608]{1,0:T(8,128)(2,1)S(1)}, u32[]{:S(2)}, u32[]{:S(2)}) collective-permute-start(bf16[96,4608]{1,0:T(8,128)(2,1)} %norm_rows.2.refs_0_), channel_id=1, source_target_pairs={{0,8},{4,12},{8,0},{12,4},{1,9},{5,13},{9,1},{13,5},{2,10},{6,14},... | collective-permute-start | bytes 2654216 | tf_op jit(solution)/shard_map/ppermute | solution.py:578
  5.4 2.3 %norm_rows.3.refs_1_ = bf16[96,4608]{1,0:T(8,128)(2,1)} custom-call(bf16[192,4608]{1,0:T(8,128)(2,1)} %hidden.5, f32[4608]{0:T(1024)} %gain.4), custom_call_target="tpu_custom_call" | custom-call | flops 1 | bytes 1 | tf_op jit(solution)/shard_map/norm_rows/pallas_call | solution.py:38
  8.4 1.4 %multiply_cosine_fusion = (f32[768,64]{1,0:T(8,128)S(1)}, f32[768,64]{1,0:T(8,128)S(1)}, f32[768,64]{1,0:T(8,128)S(1)}) fusion(f32[768]{0:T(1024)S(1)} %add_convert_fusion, f32[64]{0:T(128)S(1)} %multiply_power_fusion), kind=kLoop, calls=%fused_computation.2 | loop fusion | flops 98304 | bytes 593152 | tf_op jit(solution)/shard_map/cos | solution.py:567
  11.2 4.8 %qkv.3 = (bf16[2,384,128]{2,1,0:T(8,128)(2,1)S(1)}, bf16[384,256]{1,0:T(8,128)(2,1)S(1)}) custom-call(f32[768,256]{1,0:T(8,128)} %pad_maximum_fusion.trig, bf16[4608,256]{1,0:T(8,128)(2,1)} %wq.5, bf16[4608,128]{1,0:T(8,128)(2,1)} %wk.5, bf16[4608,128]{1,0:T(8,128)(2,1)} %wv.5, bf16[96,4608]{1,0:T(8,128)(2,1)} %norm_rows.2.refs_0_, ...), custom_call_target="tpu_custom_call" | custom-call | flops 1 | bytes 1 | tf_op jit(solution)/shard_map/qkv/pallas_call | solution.py:38
  16.0 1.6 %collective-permute-start.4 = (bf16[384,256]{1,0:T(8,128)(2,1)S(1)}, bf16[384,256]{1,0:T(8,128)(2,1)S(1)}, u32[]{:S(2)}, u32[]{:S(2)}) collective-permute-start(bf16[384,256]{1,0:T(8,128)(2,1)S(1)} %get-tuple-element.41), channel_id=1, source_target_pairs={{0,1},{1,2},{2,3},{3,0},{4,5},{5,6},{6,7},{7,4},{8,9},{9,10},{10,1... | collective-permute-start | bytes 589832 | tf_op jit(solution)/shard_map/ppermute | solution.py:585
  17.6 2.6 %collective-permute-start.5 = (bf16[384,256]{1,0:T(8,128)(2,1)S(1)}, bf16[384,256]{1,0:T(8,128)(2,1)S(1)}, u32[]{:S(2)}, u32[]{:S(2)}) collective-permute-start(bf16[384,256]{1,0:T(8,128)(2,1)S(1)} %get-tuple-element.41), channel_id=1, source_target_pairs={{0,2},{1,3},{2,0},{3,1},{4,6},{5,7},{6,4},{7,5},{8,10},{9,11},{10,... | collective-permute-start | bytes 589832 | tf_op jit(solution)/shard_map/ppermute | solution.py:585
  20.2 1.3 %collective-permute-start.6 = (bf16[384,256]{1,0:T(8,128)(2,1)S(1)}, bf16[384,256]{1,0:T(8,128)(2,1)S(1)}, u32[]{:S(2)}, u32[]{:S(2)}) collective-permute-start(bf16[384,256]{1,0:T(8,128)(2,1)S(1)} %get-tuple-element.41), channel_id=1, source_target_pairs={{0,3},{1,0},{2,1},{3,2},{4,7},{5,4},{6,5},{7,6},{8,11},{9,8},{10,9... | collective-permute-start | bytes 589832 | tf_op jit(solution)/shard_map/ppermute | solution.py:585
  22.1 2.6 %cut_weights.1 = (bf16[32,4608]{1,0:T(8,128)(2,1)}, bf16[32,4608]{1,0:T(8,128)(2,1)}, bf16[32,4608]{1,0:T(8,128)(2,1)}, bf16[32,4608]{1,0:T(8,128)(2,1)}) custom-call(s32[10]{0:T(128)S(1)} %pad_add_fusion.1.table, bf16[256,4608]{1,0:T(8,128)(2,1)} %weights_hbm.1), custom_call_target="tpu_custom_call" | custom-call | flops 1 | bytes 1 | tf_op jit(solution)/shard_map/cut_weights/pallas_call | solution.py:38
  25.7 7.9 %collective-permute-done.5 = bf16[384,256]{1,0:T(8,128)(2,1)S(1)} collective-permute-done((bf16[384,256]{1,0:T(8,128)(2,1)S(1)}, bf16[384,256]{1,0:T(8,128)(2,1)S(1)}, u32[]{:S(2)}, u32[]{:S(2)}) %collective-permute-start.5) | collective-permute-done | bytes 196640 | tf_op jit(solution)/shard_map/ppermute | solution.py:585
  33.6 4.3 %attention.3 = (f32[3,8,256]{2,1,0:T(8,128)S(1)}, f32[3,144,256]{2,1,0:T(8,128)S(1)}) custom-call(s32[10]{0:T(128)S(1)} %pad_add_fusion.1.table, bf16[2,384,128]{2,1,0:T(8,128)(2,1)S(1)} %get-tuple-element.47.refs_0_, bf16[1,384,256]{2,1,0:T(8,128)(2,1)S(1)} %bitcast.16, bf16[1,384,256]{2,1,0:T(8,128)(2,1)S(1)} %bitcast.18, ...), custom_call_target="tpu_custom_call" | custom-call | flops 1 | bytes 1 | tf_op jit(solution)/shard_map/attention/pallas_call | solution.py:38
  38.6 1.3 %collective-permute-done.7.refs_1_ = bf16[48,4608]{1,0:T(8,128)(2,1)S(1)} collective-permute-done((bf16[48,4608]{1,0:T(8,128)(2,1)S(1)}, bf16[48,4608]{1,0:T(8,128)(2,1)S(1)}, u32[]{:S(2)}, u32[]{:S(2)}) %collective-permute-start.7) | collective-permute-done | bytes 442400 | tf_op jit(solution)/shard_map/ppermute | solution.py:578
  40.5 3.4 %qkv.4 = (bf16[2,384,128]{2,1,0:T(8,128)(2,1)S(1)}, bf16[384,256]{1,0:T(8,128)(2,1)S(1)}) custom-call(f32[768,256]{1,0:T(8,128)} %pad_maximum_fusion.trig, bf16[4608,256]{1,0:T(8,128)(2,1)} %wq.5, bf16[4608,128]{1,0:T(8,128)(2,1)} %wk.5, bf16[4608,128]{1,0:T(8,128)(2,1)} %wv.5, bf16[96,4608]{1,0:T(8,128)(2,1)S(1)} %collective-permute-done.3.refs_0_, ...), custom_call_target="tpu_custom_call" | custom-call | flops 1 | bytes 1 | tf_op jit(solution)/shard_map/qkv/pallas_call | solution.py:38
  44.9 1.8 %collective-permute-start.12 = (bf16[32,4608]{1,0:T(8,128)(2,1)S(1)}, bf16[32,4608]{1,0:T(8,128)(2,1)S(1)}, u32[]{:S(2)}, u32[]{:S(2)}) collective-permute-start(bf16[32,4608]{1,0:T(8,128)(2,1)S(1)} %copy-done.4), channel_id=1, source_target_pairs={{0,8},{4,12},{8,0},{12,4},{1,9},{5,13},{9,1},{13,5},{2,10},{6,14},... | collective-permute-start | bytes 884744 | tf_op jit(solution)/shard_map/ppermute | solution.py:578
  47.3 3.3 %qkv.5 = (bf16[2,384,128]{2,1,0:T(8,128)(2,1)S(1)}, bf16[384,256]{1,0:T(8,128)(2,1)S(1)}) custom-call(f32[768,256]{1,0:T(8,128)} %pad_maximum_fusion.trig, bf16[4608,256]{1,0:T(8,128)(2,1)} %wq.5, bf16[4608,128]{1,0:T(8,128)(2,1)} %wk.5, bf16[4608,128]{1,0:T(8,128)(2,1)} %wv.5, ...), custom_call_target="tpu_custom_call", output_to_operand_aliasing={{0}: (6, {}), {1}: (7, {})} | custom-call | flops 1 | bytes 1 | tf_op jit(solution)/shard_map/qkv/pallas_call | solution.py:38
  50.6 3.2 %collective-permute-start.10 = (bf16[384,256]{1,0:T(8,128)(2,1)S(1)}, bf16[384,256]{1,0:T(8,128)(2,1)S(1)}, u32[]{:S(2)}, u32[]{:S(2)}) collective-permute-start(bf16[384,256]{1,0:T(8,128)(2,1)S(1)} %get-tuple-element.55), channel_id=1, source_target_pairs={{0,1},{1,2},{2,3},{3,0},{4,5},{5,6},{6,7},{7,4},{8,9},{9,10},{10,1... | collective-permute-start | bytes 589832 | tf_op jit(solution)/shard_map/ppermute | solution.py:596
  54.3 1.7 %collective-permute-start.13 = (bf16[32,4608]{1,0:T(8,128)(2,1)S(1)}, bf16[32,4608]{1,0:T(8,128)(2,1)S(1)}, u32[]{:S(2)}, u32[]{:S(2)}) collective-permute-start(bf16[32,4608]{1,0:T(8,128)(2,1)S(1)} %collective-permute-done.12.refs_0_), channel_id=1, source_target_pairs={{0,16},{16,0},{1,17},{17,1},{2,18},{18,2},{3,19},{19,3},{4,20},{20... | collective-permute-start | bytes 884744 | tf_op jit(solution)/shard_map/ppermute | solution.py:578
  56.0 3.6 %collective-permute-done.10 = bf16[384,256]{1,0:T(8,128)(2,1)S(1)} collective-permute-done((bf16[384,256]{1,0:T(8,128)(2,1)S(1)}, bf16[384,256]{1,0:T(8,128)(2,1)S(1)}, u32[]{:S(2)}, u32[]{:S(2)}) %collective-permute-start.10) | collective-permute-done | bytes 196640 | tf_op jit(solution)/shard_map/ppermute | solution.py:596
  61.2 1.5 %collective-permute-done.16.refs_1_ = bf16[32,4608]{1,0:T(8,128)(2,1)S(1)} collective-permute-done((bf16[32,4608]{1,0:T(8,128)(2,1)S(1)}, bf16[32,4608]{1,0:T(8,128)(2,1)S(1)}, u32[]{:S(2)}, u32[]{:S(2)}) %collective-permute-start.16) | collective-permute-done | bytes 294944 | tf_op jit(solution)/shard_map/ppermute | solution.py:578
  63.0 1.5 %collective-permute-start.19 = (bf16[32,4608]{1,0:T(8,128)(2,1)S(1)}, bf16[32,4608]{1,0:T(8,128)(2,1)S(1)}, u32[]{:S(2)}, u32[]{:S(2)}) collective-permute-start(bf16[32,4608]{1,0:T(8,128)(2,1)S(1)} %collective-permute-done.16.refs_1_), channel_id=1, source_target_pairs={{0,16},{16,0},{1,17},{17,1},{2,18},{18,2},{3,19},{19,3},{4,20},{20... | collective-permute-start | bytes 884744 | tf_op jit(solution)/shard_map/ppermute | solution.py:578
  64.5 3.4 %collective-permute-done.11 = bf16[384,256]{1,0:T(8,128)(2,1)S(1)} collective-permute-done((bf16[384,256]{1,0:T(8,128)(2,1)S(1)}, bf16[384,256]{1,0:T(8,128)(2,1)S(1)}, u32[]{:S(2)}, u32[]{:S(2)}) %collective-permute-start.11) | collective-permute-done | bytes 196640 | tf_op jit(solution)/shard_map/ppermute | solution.py:596
  67.9 4.8 %attention.4 = (f32[3,8,256]{2,1,0:T(8,128)S(1)}, f32[3,144,256]{2,1,0:T(8,128)S(1)}, f32[3,8,256]{2,1,0:T(8,128)S(1)}, f32[3,144,256]{2,1,0:T(8,128)S(1)}) custom-call(s32[10]{0:T(128)S(1)} %pad_add_fusion.1.table, bf16[2,384,128]{2,1,0:T(8,128)(2,1)S(1)} %get-tuple-element.47.refs_0_, ...), custom_call_target="tpu_custom_call", output_to_operand_aliasing={{0}: (8, {}), {1}: (9, {})} | custom-call | flops 1 | bytes 1 | tf_op jit(solution)/shard_map/attention/pallas_call | solution.py:38
  72.7 1.3 %collective-permute-start.20 = (bf16[32,4608]{1,0:T(8,128)(2,1)S(1)}, bf16[32,4608]{1,0:T(8,128)(2,1)S(1)}, u32[]{:S(2)}, u32[]{:S(2)}) collective-permute-start(bf16[32,4608]{1,0:T(8,128)(2,1)S(1)} %collective-permute-done.17.refs_2_), channel_id=1, source_target_pairs={{0,16},{16,0},{1,17},{17,1},{2,18},{18,2},{3,19},{19,3},{4,20},{20... | collective-permute-start | bytes 884744 | tf_op jit(solution)/shard_map/ppermute | solution.py:578
  74.0 1.3 %collective-permute-done.14 = bf16[384,256]{1,0:T(8,128)(2,1)S(1)} collective-permute-done((bf16[384,256]{1,0:T(8,128)(2,1)S(1)}, bf16[384,256]{1,0:T(8,128)(2,1)S(1)}, u32[]{:S(2)}, u32[]{:S(2)}) %collective-permute-start.14) | collective-permute-done | bytes 196640 | tf_op jit(solution)/shard_map/ppermute | solution.py:596
  75.4 6.6 %attention.5 = (bf16[384,256]{1,0:T(8,128)(2,1)}, bf16[384,256]{1,0:T(8,128)(2,1)}, f32[3,8,256]{2,1,0:T(8,128)S(1)}, f32[3,144,256]{2,1,0:T(8,128)S(1)}, f32[3,...) custom-call(s32[10]{0:T(128)S(1)} %pad_add_fusion.1.table, ...), custom_call_target="tpu_custom_call", output_to_operand_aliasing={{2}: (7, {}), {3}: (8, {}), {4}: (9, {}), {5}: (10, {})} | custom-call | flops 1 | bytes 1 | tf_op jit(solution)/shard_map/attention/pallas_call | solution.py:38
  82.0 1.3 %collective-permute-start.21 = (bf16[32,4608]{1,0:T(8,128)(2,1)S(1)}, bf16[32,4608]{1,0:T(8,128)(2,1)S(1)}, u32[]{:S(2)}, u32[]{:S(2)}) collective-permute-start(bf16[32,4608]{1,0:T(8,128)(2,1)S(1)} %collective-permute-done.18.refs_3_), channel_id=1, source_target_pairs={{0,16},{16,0},{1,17},{17,1},{2,18},{18,2},{3,19},{19,3},{4,20},{20... | collective-permute-start | bytes 884744 | tf_op jit(solution)/shard_map/ppermute | solution.py:578
  84.2 3.4 %output_near.1.near = f32[384,4608]{1,0:T(8,128)S(1)} custom-call(bf16[384,256]{1,0:T(8,128)(2,1)} %get-tuple-element.64.left_hbm, bf16[256,4608]{1,0:T(8,128)(2,1)} %weights_hbm.1), custom_call_target="tpu_custom_call" | custom-call | flops 1 | bytes 1 | tf_op jit(solution)/shard_map/output_near/pallas_call | solution.py:38
  87.6 1.7 %collective-permute-done.15.left_hbm = bf16[384,256]{1,0:T(8,128)(2,1)S(1)} collective-permute-done((bf16[384,256]{1,0:T(8,128)(2,1)}, bf16[384,256]{1,0:T(8,128)(2,1)S(1)}, u32[]{:S(2)}, u32[]{:S(2)}) %collective-permute-start.15) | collective-permute-done | bytes 196640 | tf_op jit(solution)/shard_map/ppermute | solution.py:578
  89.2 3.0 %output_send.1 = (bf16[192,4608]{1,0:T(8,128)(2,1)}, bf16[256,4608]{1,0:T(8,128)(2,1)S(1)}) custom-call(s32[10]{0:T(128)S(1)} %pad_add_fusion.1.table, bf16[384,256]{1,0:T(8,128)(2,1)S(1)} %collective-permute-done.15.left_hbm, f32[384,4608]{1,0:T(8,128)S(1)} %output_near.1.near, bf16[32,4608]{1,0:T(8,128)(2,1)S(1)} %collective-permute-done.12.refs_0_, ...), custom_call_target="tpu_custom_call" | custom-call | flops 1 | bytes 1 | tf_op jit(solution)/shard_map/output_send/pallas_call | solution.py:38
  92.3 1.7 %output_keep.1 = (f32[192,4608]{1,0:T(8,128)S(1)}, bf16[192,4608]{1,0:T(8,128)(2,1)S(1)}) custom-call(bf16[384,256]{1,0:T(8,128)(2,1)S(1)} %collective-permute-done.15.left_hbm, bf16[192,4608]{1,0:T(8,128)(2,1)} %hidden.5, f32[384,4608]{1,0:T(8,128)S(1)} %output_near.1.near, bf16[256,4608]{1,0:T(8,128)(2,1)S(1)} %get-tuple-element.72.weights), custom_call_target="tpu_custom_call" | custom-call | flops 1 | bytes 1 | tf_op jit(solution)/shard_map/output_keep/pallas_call | solution.py:38
  94.1 2.1 %collective-permute-done.22.received = bf16[192,4608]{1,0:T(8,128)(2,1)S(1)} collective-permute-done((bf16[192,4608]{1,0:T(8,128)(2,1)}, bf16[192,4608]{1,0:T(8,128)(2,1)S(1)}, u32[]{:S(2)}, u32[]{:S(2)}) %collective-permute-start.22) | collective-permute-done | bytes 1769504 | tf_op jit(solution)/shard_map/ppermute | solution.py:578
  96.2 2.7 %output_norm.1 = bf16[192,4608]{1,0:T(8,128)(2,1)} custom-call(bf16[192,4608]{1,0:T(8,128)(2,1)S(1)} %collective-permute-done.22.received, bf16[192,4608]{1,0:T(8,128)(2,1)S(1)} %get-tuple-element.73.hidden, f32[192,4608]{1,0:T(8,128)S(1)} %get-tuple-element.74.kept, f32[4608]{0:T(1024)} %gain.5), custom_call_target="tpu_custom_call" | custom-call | flops 1 | bytes 1 | tf_op jit(solution)/shard_map/output_norm/pallas_call | solution.py:38
  (49 shorter events, 10.1 us)
Async XLA Ops:
  2.3 5.7 %copy-start = (s32[8]{0:T(128)S(1)}, s32[8]{0:T(128)}, u32[]{:S(2)}) copy-start(s32[8]{0:T(128)} %param.15) | copy-start | bytes 100
  2.3 8.8 %collective-permute-start = (bf16[96,4608]{1,0:T(8,128)(2,1)}, bf16[96,4608]{1,0:T(8,128)(2,1)S(1)}, u32[]{:S(2)}, u32[]{:S(2)}) collective-permute-start(bf16[96,4608]{1,0:T(8,128)(2,1)} %norm_rows.2.refs_0_), channel_id=1, source_target_pairs={{0,4},{4,0},{8,12},{12,8},{1,5},{5,1},{9,13},{13,9},{2,6},{6,2},{1... | collective-permute-start | bytes 2654216 | tf_op jit(solution)/shard_map/ppermute | solution.py:578
  2.9 35.1 %collective-permute-start.3 = (bf16[96,4608]{1,0:T(8,128)(2,1)}, bf16[96,4608]{1,0:T(8,128)(2,1)S(1)}, u32[]{:S(2)}, u32[]{:S(2)}) collective-permute-start(bf16[96,4608]{1,0:T(8,128)(2,1)} %norm_rows.2.refs_0_), channel_id=1, source_target_pairs={{0,8},{4,12},{8,0},{12,4},{1,9},{5,13},{9,1},{13,5},{2,10},{6,14},... | collective-permute-start | bytes 2654216 | tf_op jit(solution)/shard_map/ppermute | solution.py:578
  7.8 3.4 %collective-permute-start.1 = (bf16[96,4608]{1,0:T(8,128)(2,1)}, bf16[96,4608]{1,0:T(8,128)(2,1)S(1)}, u32[]{:S(2)}, u32[]{:S(2)}) collective-permute-start(bf16[96,4608]{1,0:T(8,128)(2,1)} %norm_rows.3.refs_1_), channel_id=1, source_target_pairs={{0,4},{4,0},{8,12},{12,8},{1,5},{5,1},{9,13},{13,9},{2,6},{6,2},{1... | collective-permute-start | bytes 2654216 | tf_op jit(solution)/shard_map/ppermute | solution.py:578
  16.0 9.7 %collective-permute-start.4 = (bf16[384,256]{1,0:T(8,128)(2,1)S(1)}, bf16[384,256]{1,0:T(8,128)(2,1)S(1)}, u32[]{:S(2)}, u32[]{:S(2)}) collective-permute-start(bf16[384,256]{1,0:T(8,128)(2,1)S(1)} %get-tuple-element.41), channel_id=1, source_target_pairs={{0,1},{1,2},{2,3},{3,0},{4,5},{5,6},{6,7},{7,4},{8,9},{9,10},{10,1... | collective-permute-start | bytes 589832 | tf_op jit(solution)/shard_map/ppermute | solution.py:585
  17.6 16.0 %collective-permute-start.5 = (bf16[384,256]{1,0:T(8,128)(2,1)S(1)}, bf16[384,256]{1,0:T(8,128)(2,1)S(1)}, u32[]{:S(2)}, u32[]{:S(2)}) collective-permute-start(bf16[384,256]{1,0:T(8,128)(2,1)S(1)} %get-tuple-element.41), channel_id=1, source_target_pairs={{0,2},{1,3},{2,0},{3,1},{4,6},{5,7},{6,4},{7,5},{8,10},{9,11},{10,... | collective-permute-start | bytes 589832 | tf_op jit(solution)/shard_map/ppermute | solution.py:585
  20.2 13.4 %collective-permute-start.6 = (bf16[384,256]{1,0:T(8,128)(2,1)S(1)}, bf16[384,256]{1,0:T(8,128)(2,1)S(1)}, u32[]{:S(2)}, u32[]{:S(2)}) collective-permute-start(bf16[384,256]{1,0:T(8,128)(2,1)S(1)} %get-tuple-element.41), channel_id=1, source_target_pairs={{0,3},{1,0},{2,1},{3,2},{4,7},{5,4},{6,5},{7,6},{8,11},{9,8},{10,9... | collective-permute-start | bytes 589832 | tf_op jit(solution)/shard_map/ppermute | solution.py:585
  21.5 23.3 %collective-permute-start.2 = (bf16[96,4608]{1,0:T(8,128)(2,1)}, bf16[96,4608]{1,0:T(8,128)(2,1)S(1)}, u32[]{:S(2)}, u32[]{:S(2)}) collective-permute-start(bf16[96,4608]{1,0:T(8,128)(2,1)} %norm_rows.3.refs_1_), channel_id=1, source_target_pairs={{0,8},{4,12},{8,0},{12,4},{1,9},{5,13},{9,1},{13,5},{2,10},{6,14},... | collective-permute-start | bytes 2654216 | tf_op jit(solution)/shard_map/ppermute | solution.py:578
  38.0 1.9 %collective-permute-start.7 = (bf16[48,4608]{1,0:T(8,128)(2,1)S(1)}, bf16[48,4608]{1,0:T(8,128)(2,1)S(1)}, u32[]{:S(2)}, u32[]{:S(2)}) collective-permute-start(bf16[48,4608]{1,0:T(8,128)(2,1)S(1)} %get-tuple-element.78), channel_id=1, source_target_pairs={{0,4},{4,0},{8,12},{12,8},{1,5},{5,1},{9,13},{13,9},{2,6},{6,2},{1... | collective-permute-start | bytes 1327112 | tf_op jit(solution)/shard_map/ppermute | solution.py:578
  38.1 6.8 %copy-start.4 = (bf16[32,4608]{1,0:T(8,128)(2,1)S(1)}, bf16[32,4608]{1,0:T(8,128)(2,1)}, u32[]{:S(2)}) copy-start(bf16[32,4608]{1,0:T(8,128)(2,1)} %get-tuple-element.56) | copy-start | bytes 884740
  38.1 2.4 %collective-permute-start.8 = (bf16[48,4608]{1,0:T(8,128)(2,1)S(1)}, bf16[48,4608]{1,0:T(8,128)(2,1)S(1)}, u32[]{:S(2)}, u32[]{:S(2)}) collective-permute-start(bf16[48,4608]{1,0:T(8,128)(2,1)S(1)} %get-tuple-element.77), channel_id=1, source_target_pairs={{0,4},{4,0},{8,12},{12,8},{1,5},{5,1},{9,13},{13,9},{2,6},{6,2},{1... | collective-permute-start | bytes 1327112 | tf_op jit(solution)/shard_map/ppermute | solution.py:578
  44.9 8.9 %copy-start.3 = (bf16[32,4608]{1,0:T(8,128)(2,1)S(1)}, bf16[32,4608]{1,0:T(8,128)(2,1)}, u32[]{:S(2)}) copy-start(bf16[32,4608]{1,0:T(8,128)(2,1)} %get-tuple-element.65) | copy-start | bytes 884740
  44.9 15.8 %copy-start.2 = (bf16[32,4608]{1,0:T(8,128)(2,1)S(1)}, bf16[32,4608]{1,0:T(8,128)(2,1)}, u32[]{:S(2)}) copy-start(bf16[32,4608]{1,0:T(8,128)(2,1)} %get-tuple-element.67) | copy-start | bytes 884740
  44.9 17.8 %copy-start.1 = (bf16[32,4608]{1,0:T(8,128)(2,1)S(1)}, bf16[32,4608]{1,0:T(8,128)(2,1)}, u32[]{:S(2)}) copy-start(bf16[32,4608]{1,0:T(8,128)(2,1)} %get-tuple-element.69) | copy-start | bytes 884740
  44.9 2.4 %collective-permute-start.9 = (bf16[96,4608]{1,0:T(8,128)(2,1)S(1)}, bf16[96,4608]{1,0:T(8,128)(2,1)S(1)}, u32[]{:S(2)}, u32[]{:S(2)}) collective-permute-start(bf16[96,4608]{1,0:T(8,128)(2,1)S(1)} %collective-permute-done.2.refs_0_), channel_id=1, source_target_pairs={{0,4},{4,0},{8,12},{12,8},{1,5},{5,1},{9,13},{13,9},{2,6},{6,2},{1... | collective-permute-start | bytes 2654216 | tf_op jit(solution)/shard_map/ppermute | solution.py:578
  44.9 9.4 %collective-permute-start.12 = (bf16[32,4608]{1,0:T(8,128)(2,1)S(1)}, bf16[32,4608]{1,0:T(8,128)(2,1)S(1)}, u32[]{:S(2)}, u32[]{:S(2)}) collective-permute-start(bf16[32,4608]{1,0:T(8,128)(2,1)S(1)} %copy-done.4), channel_id=1, source_target_pairs={{0,8},{4,12},{8,0},{12,4},{1,9},{5,13},{9,1},{13,5},{2,10},{6,14},... | collective-permute-start | bytes 884744 | tf_op jit(solution)/shard_map/ppermute | solution.py:578
  50.6 9.1 %collective-permute-start.10 = (bf16[384,256]{1,0:T(8,128)(2,1)S(1)}, bf16[384,256]{1,0:T(8,128)(2,1)S(1)}, u32[]{:S(2)}, u32[]{:S(2)}) collective-permute-start(bf16[384,256]{1,0:T(8,128)(2,1)S(1)} %get-tuple-element.55), channel_id=1, source_target_pairs={{0,1},{1,2},{2,3},{3,0},{4,5},{5,6},{6,7},{7,4},{8,9},{9,10},{10,1... | collective-permute-start | bytes 589832 | tf_op jit(solution)/shard_map/ppermute | solution.py:596
  53.8 8.9 %collective-permute-start.16 = (bf16[32,4608]{1,0:T(8,128)(2,1)S(1)}, bf16[32,4608]{1,0:T(8,128)(2,1)S(1)}, u32[]{:S(2)}, u32[]{:S(2)}) collective-permute-start(bf16[32,4608]{1,0:T(8,128)(2,1)S(1)} %copy-done.3), channel_id=1, source_target_pairs={{0,8},{4,12},{8,0},{12,4},{1,9},{5,13},{9,1},{13,5},{2,10},{6,14},... | collective-permute-start | bytes 884744 | tf_op jit(solution)/shard_map/ppermute | solution.py:578
  54.3 10.2 %collective-permute-start.13 = (bf16[32,4608]{1,0:T(8,128)(2,1)S(1)}, bf16[32,4608]{1,0:T(8,128)(2,1)S(1)}, u32[]{:S(2)}, u32[]{:S(2)}) collective-permute-start(bf16[32,4608]{1,0:T(8,128)(2,1)S(1)} %collective-permute-done.12.refs_0_), channel_id=1, source_target_pairs={{0,16},{16,0},{1,17},{17,1},{2,18},{18,2},{3,19},{19,3},{4,20},{20... | collective-permute-start | bytes 884744 | tf_op jit(solution)/shard_map/ppermute | solution.py:578
  59.7 8.2 %collective-permute-start.11 = (bf16[384,256]{1,0:T(8,128)(2,1)S(1)}, bf16[384,256]{1,0:T(8,128)(2,1)S(1)}, u32[]{:S(2)}, u32[]{:S(2)}) collective-permute-start(bf16[384,256]{1,0:T(8,128)(2,1)S(1)} %collective-permute-done.10), channel_id=1, source_target_pairs={{0,1},{1,2},{2,3},{3,0},{4,5},{5,6},{6,7},{7,4},{8,9},{9,10},{10,1... | collective-permute-start | bytes 589832 | tf_op jit(solution)/shard_map/ppermute | solution.py:596
  60.7 12.0 %collective-permute-start.17 = (bf16[32,4608]{1,0:T(8,128)(2,1)S(1)}, bf16[32,4608]{1,0:T(8,128)(2,1)S(1)}, u32[]{:S(2)}, u32[]{:S(2)}) collective-permute-start(bf16[32,4608]{1,0:T(8,128)(2,1)S(1)} %copy-done.2), channel_id=1, source_target_pairs={{0,8},{4,12},{8,0},{12,4},{1,9},{5,13},{9,1},{13,5},{2,10},{6,14},... | collective-permute-start | bytes 884744 | tf_op jit(solution)/shard_map/ppermute | solution.py:578
  62.7 19.3 %collective-permute-start.18 = (bf16[32,4608]{1,0:T(8,128)(2,1)S(1)}, bf16[32,4608]{1,0:T(8,128)(2,1)S(1)}, u32[]{:S(2)}, u32[]{:S(2)}) collective-permute-start(bf16[32,4608]{1,0:T(8,128)(2,1)S(1)} %copy-done.1), channel_id=1, source_target_pairs={{0,8},{4,12},{8,0},{12,4},{1,9},{5,13},{9,1},{13,5},{2,10},{6,14},... | collective-permute-start | bytes 884744 | tf_op jit(solution)/shard_map/ppermute | solution.py:578
  63.0 19.0 %collective-permute-start.19 = (bf16[32,4608]{1,0:T(8,128)(2,1)S(1)}, bf16[32,4608]{1,0:T(8,128)(2,1)S(1)}, u32[]{:S(2)}, u32[]{:S(2)}) collective-permute-start(bf16[32,4608]{1,0:T(8,128)(2,1)S(1)} %collective-permute-done.16.refs_1_), channel_id=1, source_target_pairs={{0,16},{16,0},{1,17},{17,1},{2,18},{18,2},{3,19},{19,3},{4,20},{20... | collective-permute-start | bytes 884744 | tf_op jit(solution)/shard_map/ppermute | solution.py:578
  67.9 7.5 %collective-permute-start.14 = (bf16[384,256]{1,0:T(8,128)(2,1)S(1)}, bf16[384,256]{1,0:T(8,128)(2,1)S(1)}, u32[]{:S(2)}, u32[]{:S(2)}) collective-permute-start(bf16[384,256]{1,0:T(8,128)(2,1)S(1)} %collective-permute-done.11), channel_id=1, source_target_pairs={{0,1},{1,2},{2,3},{3,0},{4,5},{5,6},{6,7},{7,4},{8,9},{9,10},{10,1... | collective-permute-start | bytes 589832 | tf_op jit(solution)/shard_map/ppermute | solution.py:596
  72.7 14.9 %collective-permute-start.20 = (bf16[32,4608]{1,0:T(8,128)(2,1)S(1)}, bf16[32,4608]{1,0:T(8,128)(2,1)S(1)}, u32[]{:S(2)}, u32[]{:S(2)}) collective-permute-start(bf16[32,4608]{1,0:T(8,128)(2,1)S(1)} %collective-permute-done.17.refs_2_), channel_id=1, source_target_pairs={{0,16},{16,0},{1,17},{17,1},{2,18},{18,2},{3,19},{19,3},{4,20},{20... | collective-permute-start | bytes 884744 | tf_op jit(solution)/shard_map/ppermute | solution.py:578
  82.0 7.2 %collective-permute-start.21 = (bf16[32,4608]{1,0:T(8,128)(2,1)S(1)}, bf16[32,4608]{1,0:T(8,128)(2,1)S(1)}, u32[]{:S(2)}, u32[]{:S(2)}) collective-permute-start(bf16[32,4608]{1,0:T(8,128)(2,1)S(1)} %collective-permute-done.18.refs_3_), channel_id=1, source_target_pairs={{0,16},{16,0},{1,17},{17,1},{2,18},{18,2},{3,19},{19,3},{4,20},{20... | collective-permute-start | bytes 884744 | tf_op jit(solution)/shard_map/ppermute | solution.py:578
  83.4 5.9 %collective-permute-start.15 = (bf16[384,256]{1,0:T(8,128)(2,1)}, bf16[384,256]{1,0:T(8,128)(2,1)S(1)}, u32[]{:S(2)}, u32[]{:S(2)}) collective-permute-start(bf16[384,256]{1,0:T(8,128)(2,1)} %get-tuple-element.63), channel_id=1, source_target_pairs={{0,8},{4,12},{8,0},{12,4},{1,9},{5,13},{9,1},{13,5},{2,10},{6,14},... | collective-permute-start | bytes 589832 | tf_op jit(solution)/shard_map/ppermute | solution.py:578
  92.2 4.0 %collective-permute-start.22 = (bf16[192,4608]{1,0:T(8,128)(2,1)}, bf16[192,4608]{1,0:T(8,128)(2,1)S(1)}, u32[]{:S(2)}, u32[]{:S(2)}) collective-permute-start(bf16[192,4608]{1,0:T(8,128)(2,1)} %get-tuple-element.71), channel_id=1, source_target_pairs={{0,4},{4,0},{8,12},{12,8},{1,5},{5,1},{9,13},{13,9},{2,6},{6,2},{1... | collective-permute-start | bytes 5308424 | tf_op jit(solution)/shard_map/ppermute | solution.py:578

commit v7 on v6

--- a/solution.py
+++ b/solution.py
@@ -365,34 +365,43 @@
 
 
 def cut_kernel(sizes, at, table, weights, *refs):
-    outs, (held, semaphores) = refs[: len(sizes)], refs[len(sizes) :]
+    outs, (held, semaphores) = refs[: len(sizes) + 1], refs[len(sizes) + 1 :]
     copies = Copies(semaphores)
-    half = sum(sizes)
+    half = weights.shape[0] // 2
     first = pl.multiple_of(table[at] * half, half)
+    split = sum(sizes)
+    rest = half - split
     ins, put = [], 0
     for size in sizes:
         target = held.at[pl.ds(put, size)]
         ins.append((copies.start(weights.at[pl.ds(first + put, size)], target), target))
         put += size
-    stores = []
-    for (copy, piece), out in zip(ins, outs):
-        copy.wait()
-        stores.append(copies.start(piece, out))
+    both = held.at[pl.ds(split, 2 * rest)]
+    for side in range(2):
+        source = weights.at[pl.ds(side * half + split, rest)]
+        copy = copies.start(source, held.at[pl.ds(split + side * rest, rest)])
+        ins.append((copy, both if side else None))
+    outs, stores = list(outs), []
+    for copy, piece in ins:
+        copy.wait()
+        if piece is not None:
+            stores.append(copies.start(piece, outs.pop(0)))
     for copy in stores:
         copy.wait()
 
 
 def cut(table, at, weights, sizes):
     depth, width = weights.shape
+    rest = depth // 2 - sum(sizes)
     return call(
         functools.partial(cut_kernel, sizes, at),
         "cut_weights",
         4,
         [SMEM, HBM],
-        [((size, width), weights.dtype, HBM) for size in sizes],
+        [((size, width), weights.dtype, HBM) for size in [*sizes, 2 * rest]],
         [
-            pltpu.VMEM((depth // 2, width), weights.dtype),
-            pltpu.SemaphoreType.DMA((2 * len(sizes),)),
+            pltpu.VMEM((depth // 2 + rest, width), weights.dtype),
+            pltpu.SemaphoreType.DMA((2 * len(sizes) + 3,)),
         ],
         table,
         weights,
@@ -429,19 +438,22 @@
     )[0]
 
 
-def send_kernel(at, chunks, table, left_hbm, near, *refs):
-    count = len(refs) - 5
-    pieces, (out, weights, left, staged, semaphores) = refs[:count], refs[count:]
+def send_kernel(at, splits, chunks, table, left_hbm, near, *refs):
+    pieces, refs = refs[: 2 * splits + 1], refs[2 * splits + 1 :]
+    out, weights, left, staged, semaphores = refs
     copies = Copies(semaphores)
     depth, width = weights.shape
-    step = width // chunks
+    half, step = depth // 2, width // chunks
     first = copies.start(left_hbm, left)
     waits, put = [], 0
-    for index, piece in enumerate(pieces):
-        half = table[at] if index < count // 2 else 1 - table[at]
-        row = pl.multiple_of(half * (depth // 2) + put % (depth // 2), 16)
-        waits.append(copies.start(piece, weights.at[pl.ds(row, piece.shape[0])]))
-        put += piece.shape[0]
+    for own, other in zip(pieces[:splits], pieces[splits:-1]):
+        for piece, side in ((own, table[at]), (other, 1 - table[at])):
+            row = pl.multiple_of(side * half + put, 16)
+            waits.append(copies.start(piece, weights.at[pl.ds(row, piece.shape[0])]))
+        put += own.shape[0]
+    for side in range(2):
+        source = pieces[-1].at[pl.ds(side * (half - put), half - put)]
+        waits.append(copies.start(source, weights.at[pl.ds(side * half + put, half - put)]))
     for copy in waits:
         copy.wait()
     first.wait()
@@ -462,7 +474,7 @@
     (rows, width), columns = near.shape, left.shape[1]
     half, bf16 = (rows // 2, width), jnp.bfloat16
     return call(
-        functools.partial(send_kernel, at, chunks),
+        functools.partial(send_kernel, at, len(pieces) // 2, chunks),
         "output_send",
         8,
         [SMEM, HBM, VMEM] + [HBM] * len(pieces),
@@ -470,7 +482,7 @@
         [
             pltpu.VMEM(left.shape, bf16),
             pltpu.VMEM(half, bf16),
-            pltpu.SemaphoreType.DMA((1 + len(pieces) + chunks,)),
+            pltpu.SemaphoreType.DMA((2 + len(pieces) + chunks,)),
         ],
         table,
         left,
@@ -634,7 +646,9 @@
     places = [0, half, rows, rows + half]
     q_near, kv_near = qkv([*own, *partner], places, block_rows, weights, trig, 0)
     near = along_line(kv_near)
-    w_cut = cut(table, group_at, after(w_out, kv_near), [w_out.shape[0] // 8] * 4)
+    eighth = w_out.shape[0] // 8
+    sizes = [eighth, eighth * 3 // 2, eighth]
+    w_cut = cut(table, group_at, after(w_out, kv_near), sizes)
     q_near = after(q_near, *w_cut)
     (near_state,) = attention(
         [Step(0, 0, others, same=0)], table, [q_near], [near_chunk], [near], [near_chunk], [None]
@@ -684,20 +698,16 @@
     )
     w_far[2] = after(w_far[2], *far_state)
     w_other.append(swap(w_far[2]))
-    attended, gone = attention(
-        [Step(1, 0, others), Step(0, 0, others)],
-        table,
-        [q_near, q_far],
-        [near_chunk, far_chunk],
-        [far],
-        [far_chunk],
-        [near_state, far_state],
-        final=[[0], [1]],
+    rest = [Step(0, 0, others)]
+    (gone,) = attention(
+        rest, table, [q_far], [far_chunk], [far], [far_chunk], [far_state], final=[[0]]
     )
     gone = flipped(gone, "tp", 2)
+    (attended,) = attention(
+        rest, table, [q_near], [near_chunk], [far], [far_chunk], [near_state], final=[[0]]
+    )
     near_sum = output_near(attended, w_out)
-    w_other.append(swap(after(w_far[3], attended, w_other[1])))
-    pieces = [Came(piece) for piece in w_far + w_other]
+    pieces = [Came(piece) for piece in w_far[:3] + w_other + w_far[3:]]
     sent, w_laid = output_send(table, group_at, Came(gone), near_sum, pieces)
     received = flipped(sent, "tp", 1)
     kept, held = output_keep(Came(gone), hidden, near_sum, w_laid)

time: 99.2 us -> 98.3 us (level); the launches traced: 99 us -> 99.4 us
  starting transfers between devices: 24.2 us -> 26.9 us
  waiting for transfers between devices: 26 us -> 23.4 us
    ppermute x17 -> x16, starting transfers between devices: 14.4 us -> 18.3 us  [flipped(): return lax.ppermute(array, axis, [(i, i ^ bit) for i in range(size)])]
    ppermute x3, waiting for transfers between devices: 8.33 us -> 5.16 us  [along_ring(): part = lax.ppermute(part, 'seq', [(i, (i + 1) % size) for i in range(size)])]
    ppermute x3, starting transfers between devices: 4.16 us -> 3.04 us  [along_ring(): part = lax.ppermute(part, 'seq', [(i, (i + 1) % size) for i in range(size)])]
    ppermute x17 -> x16, waiting for transfers between devices: 8.84 us -> 9.49 us  [flipped(): return lax.ppermute(array, axis, [(i, i ^ bit) for i in range(size)])]
    pallas_call x13 -> x14, Pallas kernels: 45.2 us -> 45.4 us  [call(): pl.pallas_call(kernel, in_specs=in_specs, out_specs=[spec for _, _, spec...]
  transfers between devices with their start and end apart: 23 -> 22, of which waited for: 12 -> 11; matrix products, arithmetic and copies ran while one was open for 3% -> 3% of each run, Pallas kernels for 38% -> 37%
where the time goes in v7:
time: 98.3 us; the launch traced here: 99.4 us
  Pallas kernels  45.4 us (46%)
  starting transfers between devices  26.9 us (27%)
  waiting for transfers between devices  23.4 us (24%)
  other arithmetic  3.15 us (3%)
    pallas_call x14, Pallas kernels, call(): pl.pallas_call(kernel, in_specs=in_specs, out_specs=[spec for _, _, spec...  45.4 us
    ppermute x16, starting transfers between devices, flipped(): return lax.ppermute(array, axis, [(i, i ^ bit) for i in range(size)])  18.3 us
    ppermute x16, waiting for transfers between devices, flipped(): return lax.ppermute(array, axis, [(i, i ^ bit) for i in range(size)])  9.49 us
    ppermute x3, waiting for transfers between devices, along_line(): lax.ppermute(array, 'seq', [(i, (i + by) % size) for i in range(size)])  8.74 us
    ppermute x3, starting transfers between devices, along_line(): lax.ppermute(array, 'seq', [(i, (i + by) % size) for i in range(size)])  5.57 us
    ppermute x3, waiting for transfers between devices, along_ring(): part = lax.ppermute(part, 'seq', [(i, (i + 1) % size) for i in range(size)])  5.16 us
    ppermute x3, starting transfers between devices, along_ring(): part = lax.ppermute(part, 'seq', [(i, (i + 1) % size) for i in range(size)])  3.04 us
  transfers between devices with their start and end apart: 22, of which 11 were waited for; matrix products, arithmetic and copies ran while one was open for 3% of the time, Pallas kernels for 37%

profile of v7, /device:TPU:0, one launch (start us, length us, event | category | flops | bytes accessed | tf_op | source)
XLA Modules:
  0.0 99.4 jit_solution(14714009101299949891)
XLA Ops:
  0.0 2.3 %norm_rows.3.refs_0_ = bf16[96,4608]{1,0:T(8,128)(2,1)} custom-call(bf16[192,4608]{1,0:T(8,128)(2,1)} %hidden.5, f32[4608]{0:T(1024)} %gain.4), custom_call_target="tpu_custom_call" | custom-call | flops 1 | bytes 1 | tf_op jit(solution)/shard_map/norm_rows/pallas_call | solution.py:38
  2.9 2.6 %collective-permute-start.1 = (bf16[96,4608]{1,0:T(8,128)(2,1)}, bf16[96,4608]{1,0:T(8,128)(2,1)S(1)}, u32[]{:S(2)}, u32[]{:S(2)}) collective-permute-start(bf16[96,4608]{1,0:T(8,128)(2,1)} %norm_rows.3.refs_0_), channel_id=1, source_target_pairs={{0,8},{4,12},{8,0},{12,4},{1,9},{5,13},{9,1},{13,5},{2,10},{6,14},... | collective-permute-start | bytes 2654216 | tf_op jit(solution)/shard_map/ppermute | solution.py:590
  5.5 2.3 %norm_rows.2.refs_1_ = bf16[96,4608]{1,0:T(8,128)(2,1)} custom-call(bf16[192,4608]{1,0:T(8,128)(2,1)} %hidden.5, f32[4608]{0:T(1024)} %gain.4), custom_call_target="tpu_custom_call" | custom-call | flops 1 | bytes 1 | tf_op jit(solution)/shard_map/norm_rows/pallas_call | solution.py:38
  8.4 1.4 %multiply_cosine_fusion = (f32[768,64]{1,0:T(8,128)S(1)}, f32[768,64]{1,0:T(8,128)S(1)}, f32[768,64]{1,0:T(8,128)S(1)}) fusion(f32[768]{0:T(1024)S(1)} %add_convert_fusion, f32[64]{0:T(128)S(1)} %multiply_power_fusion), kind=kLoop, calls=%fused_computation.2 | loop fusion | flops 98304 | bytes 593152 | tf_op jit(solution)/shard_map/cos | solution.py:579
  11.2 4.8 %qkv.3 = (bf16[2,384,128]{2,1,0:T(8,128)(2,1)S(1)}, bf16[384,256]{1,0:T(8,128)(2,1)S(1)}) custom-call(f32[768,256]{1,0:T(8,128)} %pad_maximum_fusion.trig, bf16[4608,256]{1,0:T(8,128)(2,1)} %wq.5, bf16[4608,128]{1,0:T(8,128)(2,1)} %wk.5, bf16[4608,128]{1,0:T(8,128)(2,1)} %wv.5, bf16[96,4608]{1,0:T(8,128)(2,1)} %norm_rows.3.refs_0_, ...), custom_call_target="tpu_custom_call" | custom-call | flops 1 | bytes 1 | tf_op jit(solution)/shard_map/qkv/pallas_call | solution.py:38
  16.0 1.6 %collective-permute-start.4 = (bf16[384,256]{1,0:T(8,128)(2,1)S(1)}, bf16[384,256]{1,0:T(8,128)(2,1)S(1)}, u32[]{:S(2)}, u32[]{:S(2)}) collective-permute-start(bf16[384,256]{1,0:T(8,128)(2,1)S(1)} %get-tuple-element.40), channel_id=1, source_target_pairs={{0,1},{1,2},{2,3},{3,0},{4,5},{5,6},{6,7},{7,4},{8,9},{9,10},{10,1... | collective-permute-start | bytes 589832 | tf_op jit(solution)/shard_map/ppermute | solution.py:597
  17.6 2.6 %collective-permute-start.5 = (bf16[384,256]{1,0:T(8,128)(2,1)S(1)}, bf16[384,256]{1,0:T(8,128)(2,1)S(1)}, u32[]{:S(2)}, u32[]{:S(2)}) collective-permute-start(bf16[384,256]{1,0:T(8,128)(2,1)S(1)} %get-tuple-element.40), channel_id=1, source_target_pairs={{0,2},{1,3},{2,0},{3,1},{4,6},{5,7},{6,4},{7,5},{8,10},{9,11},{10,... | collective-permute-start | bytes 589832 | tf_op jit(solution)/shard_map/ppermute | solution.py:597
  20.2 1.3 %collective-permute-start.6 = (bf16[384,256]{1,0:T(8,128)(2,1)S(1)}, bf16[384,256]{1,0:T(8,128)(2,1)S(1)}, u32[]{:S(2)}, u32[]{:S(2)}) collective-permute-start(bf16[384,256]{1,0:T(8,128)(2,1)S(1)} %get-tuple-element.40), channel_id=1, source_target_pairs={{0,3},{1,0},{2,1},{3,2},{4,7},{5,4},{6,5},{7,6},{8,11},{9,8},{10,9... | collective-permute-start | bytes 589832 | tf_op jit(solution)/shard_map/ppermute | solution.py:597
  22.1 2.7 %cut_weights.1 = (bf16[32,4608]{1,0:T(8,128)(2,1)}, bf16[48,4608]{1,0:T(8,128)(2,1)}, bf16[32,4608]{1,0:T(8,128)(2,1)}, bf16[32,4608]{1,0:T(8,128)(2,1)}) custom-call(s32[10]{0:T(128)S(1)} %pad_add_fusion.1.table, bf16[256,4608]{1,0:T(8,128)(2,1)} %weights_hbm.1), custom_call_target="tpu_custom_call" | custom-call | flops 1 | bytes 1 | tf_op jit(solution)/shard_map/cut_weights/pallas_call | solution.py:38
  25.7 7.9 %collective-permute-done.5 = bf16[384,256]{1,0:T(8,128)(2,1)S(1)} collective-permute-done((bf16[384,256]{1,0:T(8,128)(2,1)S(1)}, bf16[384,256]{1,0:T(8,128)(2,1)S(1)}, u32[]{:S(2)}, u32[]{:S(2)}) %collective-permute-start.5) | collective-permute-done | bytes 196640 | tf_op jit(solution)/shard_map/ppermute | solution.py:597
  33.6 4.3 %attention.4 = (f32[3,8,256]{2,1,0:T(8,128)S(1)}, f32[3,144,256]{2,1,0:T(8,128)S(1)}) custom-call(s32[10]{0:T(128)S(1)} %pad_add_fusion.1.table, bf16[2,384,128]{2,1,0:T(8,128)(2,1)S(1)} %get-tuple-element.46.refs_0_, bf16[1,384,256]{2,1,0:T(8,128)(2,1)S(1)} %bitcast.17, bf16[1,384,256]{2,1,0:T(8,128)(2,1)S(1)} %bitcast.19, ...), custom_call_target="tpu_custom_call" | custom-call | flops 1 | bytes 1 | tf_op jit(solution)/shard_map/attention/pallas_call | solution.py:38
  40.5 3.4 %qkv.4 = (bf16[2,384,128]{2,1,0:T(8,128)(2,1)S(1)}, bf16[384,256]{1,0:T(8,128)(2,1)S(1)}) custom-call(f32[768,256]{1,0:T(8,128)} %pad_maximum_fusion.trig, bf16[4608,256]{1,0:T(8,128)(2,1)} %wq.5, bf16[4608,128]{1,0:T(8,128)(2,1)} %wk.5, bf16[4608,128]{1,0:T(8,128)(2,1)} %wv.5, bf16[96,4608]{1,0:T(8,128)(2,1)S(1)} %collective-permute-done.1.refs_0_, ...), custom_call_target="tpu_custom_call" | custom-call | flops 1 | bytes 1 | tf_op jit(solution)/shard_map/qkv/pallas_call | solution.py:38
  44.9 1.8 %collective-permute-start.12 = (bf16[32,4608]{1,0:T(8,128)(2,1)S(1)}, bf16[32,4608]{1,0:T(8,128)(2,1)S(1)}, u32[]{:S(2)}, u32[]{:S(2)}) collective-permute-start(bf16[32,4608]{1,0:T(8,128)(2,1)S(1)} %copy-done.4), channel_id=1, source_target_pairs={{0,8},{4,12},{8,0},{12,4},{1,9},{5,13},{9,1},{13,5},{2,10},{6,14},... | collective-permute-start | bytes 884744 | tf_op jit(solution)/shard_map/ppermute | solution.py:590
  47.3 3.3 %qkv.5 = (bf16[2,384,128]{2,1,0:T(8,128)(2,1)S(1)}, bf16[384,256]{1,0:T(8,128)(2,1)S(1)}) custom-call(f32[768,256]{1,0:T(8,128)} %pad_maximum_fusion.trig, bf16[4608,256]{1,0:T(8,128)(2,1)} %wq.5, bf16[4608,128]{1,0:T(8,128)(2,1)} %wk.5, bf16[4608,128]{1,0:T(8,128)(2,1)} %wv.5, ...), custom_call_target="tpu_custom_call", output_to_operand_aliasing={{0}: (6, {}), {1}: (7, {})} | custom-call | flops 1 | bytes 1 | tf_op jit(solution)/shard_map/qkv/pallas_call | solution.py:38
  50.6 2.4 %collective-permute-start.10 = (bf16[384,256]{1,0:T(8,128)(2,1)S(1)}, bf16[384,256]{1,0:T(8,128)(2,1)S(1)}, u32[]{:S(2)}, u32[]{:S(2)}) collective-permute-start(bf16[384,256]{1,0:T(8,128)(2,1)S(1)} %get-tuple-element.54), channel_id=1, source_target_pairs={{0,1},{1,2},{2,3},{3,0},{4,5},{5,6},{6,7},{7,4},{8,9},{9,10},{10,1... | collective-permute-start | bytes 589832 | tf_op jit(solution)/shard_map/ppermute | solution.py:608
  53.1 1.7 %collective-permute-done.12.refs_0_ = bf16[32,4608]{1,0:T(8,128)(2,1)S(1)} collective-permute-done((bf16[32,4608]{1,0:T(8,128)(2,1)S(1)}, bf16[32,4608]{1,0:T(8,128)(2,1)S(1)}, u32[]{:S(2)}, u32[]{:S(2)}) %collective-permute-start.12) | collective-permute-done | bytes 294944 | tf_op jit(solution)/shard_map/ppermute | solution.py:590
  54.8 1.7 %collective-permute-start.13 = (bf16[32,4608]{1,0:T(8,128)(2,1)S(1)}, bf16[32,4608]{1,0:T(8,128)(2,1)S(1)}, u32[]{:S(2)}, u32[]{:S(2)}) collective-permute-start(bf16[32,4608]{1,0:T(8,128)(2,1)S(1)} %collective-permute-done.12.refs_0_), channel_id=1, source_target_pairs={{0,16},{16,0},{1,17},{17,1},{2,18},{18,2},{3,19},{19,3},{4,20},{20... | collective-permute-start | bytes 884744 | tf_op jit(solution)/shard_map/ppermute | solution.py:590
  56.5 3.2 %collective-permute-done.10 = bf16[384,256]{1,0:T(8,128)(2,1)S(1)} collective-permute-done((bf16[384,256]{1,0:T(8,128)(2,1)S(1)}, bf16[384,256]{1,0:T(8,128)(2,1)S(1)}, u32[]{:S(2)}, u32[]{:S(2)}) %collective-permute-start.10) | collective-permute-done | bytes 196640 | tf_op jit(solution)/shard_map/ppermute | solution.py:608
  60.0 1.9 %collective-permute-start.17 = (bf16[32,4608]{1,0:T(8,128)(2,1)S(1)}, bf16[32,4608]{1,0:T(8,128)(2,1)S(1)}, u32[]{:S(2)}, u32[]{:S(2)}) collective-permute-start(bf16[32,4608]{1,0:T(8,128)(2,1)S(1)} %copy-done.3), channel_id=1, source_target_pairs={{0,8},{4,12},{8,0},{12,4},{1,9},{5,13},{9,1},{13,5},{2,10},{6,14},... | collective-permute-start | bytes 884744 | tf_op jit(solution)/shard_map/ppermute | solution.py:590
  61.9 2.4 %collective-permute-done.16.refs_1_ = bf16[48,4608]{1,0:T(8,128)(2,1)S(1)} collective-permute-done((bf16[48,4608]{1,0:T(8,128)(2,1)S(1)}, bf16[48,4608]{1,0:T(8,128)(2,1)S(1)}, u32[]{:S(2)}, u32[]{:S(2)}) %collective-permute-start.16) | collective-permute-done | bytes 442400 | tf_op jit(solution)/shard_map/ppermute | solution.py:590
  64.2 1.7 %collective-permute-start.18 = (bf16[48,4608]{1,0:T(8,128)(2,1)S(1)}, bf16[48,4608]{1,0:T(8,128)(2,1)S(1)}, u32[]{:S(2)}, u32[]{:S(2)}) collective-permute-start(bf16[48,4608]{1,0:T(8,128)(2,1)S(1)} %collective-permute-done.16.refs_1_), channel_id=1, source_target_pairs={{0,16},{16,0},{1,17},{17,1},{2,18},{18,2},{3,19},{19,3},{4,20},{20... | collective-permute-start | bytes 1327112 | tf_op jit(solution)/shard_map/ppermute | solution.py:590
  66.0 1.9 %collective-permute-done.11 = bf16[384,256]{1,0:T(8,128)(2,1)S(1)} collective-permute-done((bf16[384,256]{1,0:T(8,128)(2,1)S(1)}, bf16[384,256]{1,0:T(8,128)(2,1)S(1)}, u32[]{:S(2)}, u32[]{:S(2)}) %collective-permute-start.11) | collective-permute-done | bytes 196640 | tf_op jit(solution)/shard_map/ppermute | solution.py:608
  68.2 4.1 %attention.5 = (f32[3,8,256]{2,1,0:T(8,128)S(1)}, f32[3,144,256]{2,1,0:T(8,128)S(1)}, f32[3,8,256]{2,1,0:T(8,128)S(1)}, f32[3,144,256]{2,1,0:T(8,128)S(1)}) custom-call(s32[10]{0:T(128)S(1)} %pad_add_fusion.1.table, bf16[2,384,128]{2,1,0:T(8,128)(2,1)S(1)} %get-tuple-element.46.refs_0_, ...), custom_call_target="tpu_custom_call", output_to_operand_aliasing={{0}: (8, {}), {1}: (9, {})} | custom-call | flops 1 | bytes 1 | tf_op jit(solution)/shard_map/attention/pallas_call | solution.py:38
  72.3 3.3 %collective-permute-start.20 = (bf16[32,4608]{1,0:T(8,128)(2,1)S(1)}, bf16[32,4608]{1,0:T(8,128)(2,1)S(1)}, u32[]{:S(2)}, u32[]{:S(2)}) collective-permute-start(bf16[32,4608]{1,0:T(8,128)(2,1)S(1)} %copy-done.2), channel_id=1, source_target_pairs={{0,8},{4,12},{8,0},{12,4},{1,9},{5,13},{9,1},{13,5},{2,10},{6,14},... | collective-permute-start | bytes 884744 | tf_op jit(solution)/shard_map/ppermute | solution.py:590
  76.3 2.5 %attention.6 = (bf16[384,256]{1,0:T(8,128)(2,1)}, f32[3,8,256]{2,1,0:T(8,128)S(1)}, f32[3,144,256]{2,1,0:T(8,128)S(1)}) custom-call(s32[10]{0:T(128)S(1)} %pad_add_fusion.1.table, bf16[2,384,128]{2,1,0:T(8,128)(2,1)S(1)} %get-tuple-element.53.refs_1_.refs_0_, bf16[1,384,256]{2,1,0:T(8,128)(2,1)S(1)} %bitcast.15, ...), custom_call_target="tpu_custom_call", output_to_operand_aliasing={{1}: (6, {}), {2}: (7, {})} | custom-call | flops 1 | bytes 1 | tf_op jit(solution)/shard_map/attention/pallas_call | solution.py:38
  78.7 2.5 %collective-permute-start.15 = (bf16[384,256]{1,0:T(8,128)(2,1)}, bf16[384,256]{1,0:T(8,128)(2,1)S(1)}, u32[]{:S(2)}, u32[]{:S(2)}) collective-permute-start(bf16[384,256]{1,0:T(8,128)(2,1)} %get-tuple-element.60), channel_id=1, source_target_pairs={{0,8},{4,12},{8,0},{12,4},{1,9},{5,13},{9,1},{13,5},{2,10},{6,14},... | collective-permute-start | bytes 589832 | tf_op jit(solution)/shard_map/ppermute | solution.py:590
  81.3 4.5 %attention.7 = (bf16[384,256]{1,0:T(8,128)(2,1)}, f32[3,8,256]{2,1,0:T(8,128)S(1)}, f32[3,144,256]{2,1,0:T(8,128)S(1)}) custom-call(s32[10]{0:T(128)S(1)} %pad_add_fusion.1.table, bf16[2,384,128]{2,1,0:T(8,128)(2,1)S(1)} %get-tuple-element.46.refs_0_, bf16[1,384,256]{2,1,0:T(8,128)(2,1)S(1)} %bitcast.16, ...), custom_call_target="tpu_custom_call", output_to_operand_aliasing={{1}: (6, {}), {2}: (7, {})} | custom-call | flops 1 | bytes 1 | tf_op jit(solution)/shard_map/attention/pallas_call | solution.py:38
  85.7 3.4 %output_near.1.near = f32[384,4608]{1,0:T(8,128)S(1)} custom-call(bf16[384,256]{1,0:T(8,128)(2,1)} %get-tuple-element.63.left_hbm, bf16[256,4608]{1,0:T(8,128)(2,1)} %weights_hbm.1), custom_call_target="tpu_custom_call" | custom-call | flops 1 | bytes 1 | tf_op jit(solution)/shard_map/output_near/pallas_call | solution.py:38
  89.1 3.6 %output_send.1 = (bf16[192,4608]{1,0:T(8,128)(2,1)}, bf16[256,4608]{1,0:T(8,128)(2,1)S(1)}) custom-call(s32[10]{0:T(128)S(1)} %pad_add_fusion.1.table, bf16[384,256]{1,0:T(8,128)(2,1)S(1)} %collective-permute-done.15.left_hbm, f32[384,4608]{1,0:T(8,128)S(1)} %output_near.1.near, bf16[32,4608]{1,0:T(8,128)(2,1)S(1)} %collective-permute-done.12.refs_0_, ...), custom_call_target="tpu_custom_call" | custom-call | flops 1 | bytes 1 | tf_op jit(solution)/shard_map/output_send/pallas_call | solution.py:38
  92.8 1.7 %output_keep.1 = (f32[192,4608]{1,0:T(8,128)S(1)}, bf16[192,4608]{1,0:T(8,128)(2,1)S(1)}) custom-call(bf16[384,256]{1,0:T(8,128)(2,1)S(1)} %collective-permute-done.15.left_hbm, bf16[192,4608]{1,0:T(8,128)(2,1)} %hidden.5, f32[384,4608]{1,0:T(8,128)S(1)} %output_near.1.near, bf16[256,4608]{1,0:T(8,128)(2,1)S(1)} %get-tuple-element.70.weights), custom_call_target="tpu_custom_call" | custom-call | flops 1 | bytes 1 | tf_op jit(solution)/shard_map/output_keep/pallas_call | solution.py:38
  94.6 2.1 %collective-permute-done.21.received = bf16[192,4608]{1,0:T(8,128)(2,1)S(1)} collective-permute-done((bf16[192,4608]{1,0:T(8,128)(2,1)}, bf16[192,4608]{1,0:T(8,128)(2,1)S(1)}, u32[]{:S(2)}, u32[]{:S(2)}) %collective-permute-start.21) | collective-permute-done | bytes 1769504 | tf_op jit(solution)/shard_map/ppermute | solution.py:590
  96.7 2.6 %output_norm.1 = bf16[192,4608]{1,0:T(8,128)(2,1)} custom-call(bf16[192,4608]{1,0:T(8,128)(2,1)S(1)} %collective-permute-done.21.received, bf16[192,4608]{1,0:T(8,128)(2,1)S(1)} %get-tuple-element.71.hidden, f32[192,4608]{1,0:T(8,128)S(1)} %get-tuple-element.72.kept, f32[4608]{0:T(1024)} %gain.5), custom_call_target="tpu_custom_call" | custom-call | flops 1 | bytes 1 | tf_op jit(solution)/shard_map/output_norm/pallas_call | solution.py:38
  (48 shorter events, 9.3 us)
Async XLA Ops:
  2.3 5.7 %copy-start = (s32[8]{0:T(128)S(1)}, s32[8]{0:T(128)}, u32[]{:S(2)}) copy-start(s32[8]{0:T(128)} %param.15) | copy-start | bytes 100
  2.4 8.8 %collective-permute-start.2 = (bf16[96,4608]{1,0:T(8,128)(2,1)}, bf16[96,4608]{1,0:T(8,128)(2,1)S(1)}, u32[]{:S(2)}, u32[]{:S(2)}) collective-permute-start(bf16[96,4608]{1,0:T(8,128)(2,1)} %norm_rows.3.refs_0_), channel_id=1, source_target_pairs={{0,4},{4,0},{8,12},{12,8},{1,5},{5,1},{9,13},{13,9},{2,6},{6,2},{1... | collective-permute-start | bytes 2654216 | tf_op jit(solution)/shard_map/ppermute | solution.py:590
  2.9 35.0 %collective-permute-start.1 = (bf16[96,4608]{1,0:T(8,128)(2,1)}, bf16[96,4608]{1,0:T(8,128)(2,1)S(1)}, u32[]{:S(2)}, u32[]{:S(2)}) collective-permute-start(bf16[96,4608]{1,0:T(8,128)(2,1)} %norm_rows.3.refs_0_), channel_id=1, source_target_pairs={{0,8},{4,12},{8,0},{12,4},{1,9},{5,13},{9,1},{13,5},{2,10},{6,14},... | collective-permute-start | bytes 2654216 | tf_op jit(solution)/shard_map/ppermute | solution.py:590
  7.8 3.4 %collective-permute-start.3 = (bf16[96,4608]{1,0:T(8,128)(2,1)}, bf16[96,4608]{1,0:T(8,128)(2,1)S(1)}, u32[]{:S(2)}, u32[]{:S(2)}) collective-permute-start(bf16[96,4608]{1,0:T(8,128)(2,1)} %norm_rows.2.refs_1_), channel_id=1, source_target_pairs={{0,4},{4,0},{8,12},{12,8},{1,5},{5,1},{9,13},{13,9},{2,6},{6,2},{1... | collective-permute-start | bytes 2654216 | tf_op jit(solution)/shard_map/ppermute | solution.py:590
  16.0 9.7 %collective-permute-start.4 = (bf16[384,256]{1,0:T(8,128)(2,1)S(1)}, bf16[384,256]{1,0:T(8,128)(2,1)S(1)}, u32[]{:S(2)}, u32[]{:S(2)}) collective-permute-start(bf16[384,256]{1,0:T(8,128)(2,1)S(1)} %get-tuple-element.40), channel_id=1, source_target_pairs={{0,1},{1,2},{2,3},{3,0},{4,5},{5,6},{6,7},{7,4},{8,9},{9,10},{10,1... | collective-permute-start | bytes 589832 | tf_op jit(solution)/shard_map/ppermute | solution.py:597
  17.6 16.0 %collective-permute-start.5 = (bf16[384,256]{1,0:T(8,128)(2,1)S(1)}, bf16[384,256]{1,0:T(8,128)(2,1)S(1)}, u32[]{:S(2)}, u32[]{:S(2)}) collective-permute-start(bf16[384,256]{1,0:T(8,128)(2,1)S(1)} %get-tuple-element.40), channel_id=1, source_target_pairs={{0,2},{1,3},{2,0},{3,1},{4,6},{5,7},{6,4},{7,5},{8,10},{9,11},{10,... | collective-permute-start | bytes 589832 | tf_op jit(solution)/shard_map/ppermute | solution.py:597
  20.2 13.4 %collective-permute-start.6 = (bf16[384,256]{1,0:T(8,128)(2,1)S(1)}, bf16[384,256]{1,0:T(8,128)(2,1)S(1)}, u32[]{:S(2)}, u32[]{:S(2)}) collective-permute-start(bf16[384,256]{1,0:T(8,128)(2,1)S(1)} %get-tuple-element.40), channel_id=1, source_target_pairs={{0,3},{1,0},{2,1},{3,2},{4,7},{5,4},{6,5},{7,6},{8,11},{9,8},{10,9... | collective-permute-start | bytes 589832 | tf_op jit(solution)/shard_map/ppermute | solution.py:597
  21.5 23.3 %collective-permute-start = (bf16[96,4608]{1,0:T(8,128)(2,1)}, bf16[96,4608]{1,0:T(8,128)(2,1)S(1)}, u32[]{:S(2)}, u32[]{:S(2)}) collective-permute-start(bf16[96,4608]{1,0:T(8,128)(2,1)} %norm_rows.2.refs_1_), channel_id=1, source_target_pairs={{0,8},{4,12},{8,0},{12,4},{1,9},{5,13},{9,1},{13,5},{2,10},{6,14},... | collective-permute-start | bytes 2654216 | tf_op jit(solution)/shard_map/ppermute | solution.py:590
  38.0 1.9 %collective-permute-start.7 = (bf16[48,4608]{1,0:T(8,128)(2,1)S(1)}, bf16[48,4608]{1,0:T(8,128)(2,1)S(1)}, u32[]{:S(2)}, u32[]{:S(2)}) collective-permute-start(bf16[48,4608]{1,0:T(8,128)(2,1)S(1)} %get-tuple-element.76), channel_id=1, source_target_pairs={{0,4},{4,0},{8,12},{12,8},{1,5},{5,1},{9,13},{13,9},{2,6},{6,2},{1... | collective-permute-start | bytes 1327112 | tf_op jit(solution)/shard_map/ppermute | solution.py:590
  38.1 6.8 %copy-start.4 = (bf16[32,4608]{1,0:T(8,128)(2,1)S(1)}, bf16[32,4608]{1,0:T(8,128)(2,1)}, u32[]{:S(2)}) copy-start(bf16[32,4608]{1,0:T(8,128)(2,1)} %get-tuple-element.55) | copy-start | bytes 884740
  38.1 8.6 %copy-start.1 = (bf16[48,4608]{1,0:T(8,128)(2,1)S(1)}, bf16[48,4608]{1,0:T(8,128)(2,1)}, u32[]{:S(2)}) copy-start(bf16[48,4608]{1,0:T(8,128)(2,1)} %get-tuple-element.64) | copy-start | bytes 1327108
  38.1 2.4 %collective-permute-start.8 = (bf16[48,4608]{1,0:T(8,128)(2,1)S(1)}, bf16[48,4608]{1,0:T(8,128)(2,1)S(1)}, u32[]{:S(2)}, u32[]{:S(2)}) collective-permute-start(bf16[48,4608]{1,0:T(8,128)(2,1)S(1)} %get-tuple-element.75), channel_id=1, source_target_pairs={{0,4},{4,0},{8,12},{12,8},{1,5},{5,1},{9,13},{13,9},{2,6},{6,2},{1... | collective-permute-start | bytes 1327112 | tf_op jit(solution)/shard_map/ppermute | solution.py:590
  44.9 15.1 %copy-start.3 = (bf16[32,4608]{1,0:T(8,128)(2,1)S(1)}, bf16[32,4608]{1,0:T(8,128)(2,1)}, u32[]{:S(2)}) copy-start(bf16[32,4608]{1,0:T(8,128)(2,1)} %get-tuple-element.66) | copy-start | bytes 884740
  44.9 2.4 %collective-permute-start.9 = (bf16[96,4608]{1,0:T(8,128)(2,1)S(1)}, bf16[96,4608]{1,0:T(8,128)(2,1)S(1)}, u32[]{:S(2)}, u32[]{:S(2)}) collective-permute-start(bf16[96,4608]{1,0:T(8,128)(2,1)S(1)} %collective-permute-done.refs_0_), channel_id=1, source_target_pairs={{0,4},{4,0},{8,12},{12,8},{1,5},{5,1},{9,13},{13,9},{2,6},{6,2},{1... | collective-permute-start | bytes 2654216 | tf_op jit(solution)/shard_map/ppermute | solution.py:590
  44.9 9.9 %collective-permute-start.12 = (bf16[32,4608]{1,0:T(8,128)(2,1)S(1)}, bf16[32,4608]{1,0:T(8,128)(2,1)S(1)}, u32[]{:S(2)}, u32[]{:S(2)}) collective-permute-start(bf16[32,4608]{1,0:T(8,128)(2,1)S(1)} %copy-done.4), channel_id=1, source_target_pairs={{0,8},{4,12},{8,0},{12,4},{1,9},{5,13},{9,1},{13,5},{2,10},{6,14},... | collective-permute-start | bytes 884744 | tf_op jit(solution)/shard_map/ppermute | solution.py:590
  46.7 17.5 %collective-permute-start.16 = (bf16[48,4608]{1,0:T(8,128)(2,1)S(1)}, bf16[48,4608]{1,0:T(8,128)(2,1)S(1)}, u32[]{:S(2)}, u32[]{:S(2)}) collective-permute-start(bf16[48,4608]{1,0:T(8,128)(2,1)S(1)} %copy-done.1), channel_id=1, source_target_pairs={{0,8},{4,12},{8,0},{12,4},{1,9},{5,13},{9,1},{13,5},{2,10},{6,14},... | collective-permute-start | bytes 1327112 | tf_op jit(solution)/shard_map/ppermute | solution.py:590
  50.6 21.7 %copy-start.2 = (bf16[32,4608]{1,0:T(8,128)(2,1)S(1)}, bf16[32,4608]{1,0:T(8,128)(2,1)}, u32[]{:S(2)}) copy-start(bf16[32,4608]{1,0:T(8,128)(2,1)} %get-tuple-element.68) | copy-start | bytes 884740
  50.6 9.1 %collective-permute-start.10 = (bf16[384,256]{1,0:T(8,128)(2,1)S(1)}, bf16[384,256]{1,0:T(8,128)(2,1)S(1)}, u32[]{:S(2)}, u32[]{:S(2)}) collective-permute-start(bf16[384,256]{1,0:T(8,128)(2,1)S(1)} %get-tuple-element.54), channel_id=1, source_target_pairs={{0,1},{1,2},{2,3},{3,0},{4,5},{5,6},{6,7},{7,4},{8,9},{9,10},{10,1... | collective-permute-start | bytes 589832 | tf_op jit(solution)/shard_map/ppermute | solution.py:608
  54.8 11.2 %collective-permute-start.13 = (bf16[32,4608]{1,0:T(8,128)(2,1)S(1)}, bf16[32,4608]{1,0:T(8,128)(2,1)S(1)}, u32[]{:S(2)}, u32[]{:S(2)}) collective-permute-start(bf16[32,4608]{1,0:T(8,128)(2,1)S(1)} %collective-permute-done.12.refs_0_), channel_id=1, source_target_pairs={{0,16},{16,0},{1,17},{17,1},{2,18},{18,2},{3,19},{19,3},{4,20},{20... | collective-permute-start | bytes 884744 | tf_op jit(solution)/shard_map/ppermute | solution.py:590
  59.7 8.2 %collective-permute-start.11 = (bf16[384,256]{1,0:T(8,128)(2,1)S(1)}, bf16[384,256]{1,0:T(8,128)(2,1)S(1)}, u32[]{:S(2)}, u32[]{:S(2)}) collective-permute-start(bf16[384,256]{1,0:T(8,128)(2,1)S(1)} %collective-permute-done.10), channel_id=1, source_target_pairs={{0,1},{1,2},{2,3},{3,0},{4,5},{5,6},{6,7},{7,4},{8,9},{9,10},{10,1... | collective-permute-start | bytes 589832 | tf_op jit(solution)/shard_map/ppermute | solution.py:608
  60.0 15.6 %collective-permute-start.17 = (bf16[32,4608]{1,0:T(8,128)(2,1)S(1)}, bf16[32,4608]{1,0:T(8,128)(2,1)S(1)}, u32[]{:S(2)}, u32[]{:S(2)}) collective-permute-start(bf16[32,4608]{1,0:T(8,128)(2,1)S(1)} %copy-done.3), channel_id=1, source_target_pairs={{0,8},{4,12},{8,0},{12,4},{1,9},{5,13},{9,1},{13,5},{2,10},{6,14},... | collective-permute-start | bytes 884744 | tf_op jit(solution)/shard_map/ppermute | solution.py:590
  64.2 24.9 %collective-permute-start.18 = (bf16[48,4608]{1,0:T(8,128)(2,1)S(1)}, bf16[48,4608]{1,0:T(8,128)(2,1)S(1)}, u32[]{:S(2)}, u32[]{:S(2)}) collective-permute-start(bf16[48,4608]{1,0:T(8,128)(2,1)S(1)} %collective-permute-done.16.refs_1_), channel_id=1, source_target_pairs={{0,16},{16,0},{1,17},{17,1},{2,18},{18,2},{3,19},{19,3},{4,20},{20... | collective-permute-start | bytes 1327112 | tf_op jit(solution)/shard_map/ppermute | solution.py:590
  67.9 8.3 %collective-permute-start.14 = (bf16[384,256]{1,0:T(8,128)(2,1)S(1)}, bf16[384,256]{1,0:T(8,128)(2,1)S(1)}, u32[]{:S(2)}, u32[]{:S(2)}) collective-permute-start(bf16[384,256]{1,0:T(8,128)(2,1)S(1)} %collective-permute-done.11), channel_id=1, source_target_pairs={{0,1},{1,2},{2,3},{3,0},{4,5},{5,6},{6,7},{7,4},{8,9},{9,10},{10,1... | collective-permute-start | bytes 589832 | tf_op jit(solution)/shard_map/ppermute | solution.py:608
  72.3 16.8 %collective-permute-start.20 = (bf16[32,4608]{1,0:T(8,128)(2,1)S(1)}, bf16[32,4608]{1,0:T(8,128)(2,1)S(1)}, u32[]{:S(2)}, u32[]{:S(2)}) collective-permute-start(bf16[32,4608]{1,0:T(8,128)(2,1)S(1)} %copy-done.2), channel_id=1, source_target_pairs={{0,8},{4,12},{8,0},{12,4},{1,9},{5,13},{9,1},{13,5},{2,10},{6,14},... | collective-permute-start | bytes 884744 | tf_op jit(solution)/shard_map/ppermute | solution.py:590
  75.6 13.5 %collective-permute-start.19 = (bf16[32,4608]{1,0:T(8,128)(2,1)S(1)}, bf16[32,4608]{1,0:T(8,128)(2,1)S(1)}, u32[]{:S(2)}, u32[]{:S(2)}) collective-permute-start(bf16[32,4608]{1,0:T(8,128)(2,1)S(1)} %collective-permute-done.17.refs_2_), channel_id=1, source_target_pairs={{0,16},{16,0},{1,17},{17,1},{2,18},{18,2},{3,19},{19,3},{4,20},{20... | collective-permute-start | bytes 884744 | tf_op jit(solution)/shard_map/ppermute | solution.py:590
  78.7 10.4 %collective-permute-start.15 = (bf16[384,256]{1,0:T(8,128)(2,1)}, bf16[384,256]{1,0:T(8,128)(2,1)S(1)}, u32[]{:S(2)}, u32[]{:S(2)}) collective-permute-start(bf16[384,256]{1,0:T(8,128)(2,1)} %get-tuple-element.60), channel_id=1, source_target_pairs={{0,8},{4,12},{8,0},{12,4},{1,9},{5,13},{9,1},{13,5},{2,10},{6,14},... | collective-permute-start | bytes 589832 | tf_op jit(solution)/shard_map/ppermute | solution.py:590
  92.7 4.0 %collective-permute-start.21 = (bf16[192,4608]{1,0:T(8,128)(2,1)}, bf16[192,4608]{1,0:T(8,128)(2,1)S(1)}, u32[]{:S(2)}, u32[]{:S(2)}) collective-permute-start(bf16[192,4608]{1,0:T(8,128)(2,1)} %get-tuple-element.69), channel_id=1, source_target_pairs={{0,4},{4,0},{8,12},{12,8},{1,5},{5,1},{9,13},{13,9},{2,6},{6,2},{1... | collective-permute-start | bytes 5308424 | tf_op jit(solution)/shard_map/ppermute | solution.py:590

commit v8 on v7

--- a/solution.py
+++ b/solution.py
@@ -219,7 +219,7 @@
     take(2 * (count - len(fresh)))
     outs = take(len(final))
     states = [take(2) for _ in range(count)]
-    kvs, staged = take(len(group_parts)), take(len(final))
+    kvs = take(len(group_parts))
     (semaphores,) = refs
     copies = Copies(semaphores)
     core = table[0]
@@ -308,8 +308,7 @@
 
     for group in list(waits):
         ready(group)
-    stores = []
-    for out, stage, order in zip(outs, staged, final):
+    for out, order in zip(outs, final):
         put = 0
         for q in order:
             acc, heads = states[q][1], qs[q].shape[0]
@@ -318,13 +317,10 @@
                 rows = acc[at, :HD, :] / acc[at, HD : HD + 1, :]
                 rows = rows.T.astype(jnp.bfloat16)
                 for head in range(heads):
-                    stage[put : put + tile, head * HD : (head + 1) * HD] = rows[
+                    out[put : put + tile, head * HD : (head + 1) * HD] = rows[
                         head * tile : (head + 1) * tile
                     ]
                 put += tile
-        stores.append(copies.start(stage, out))
-    for copy in stores:
-        copy.wait()
 
 
 def attention(plan, table, qs, q_chunks, groups, k_chunks, state, final=()):
@@ -336,12 +332,11 @@
         shapes += [(rows // tile, deep, heads * tile) for deep in (8, HD + ONES)]
     width = qs[0].shape[0] * HD
     sums = [sum(qs[q].shape[1] for q in order) for order in final]
-    outs = [((rows, width), jnp.bfloat16, HBM) for rows in sums]
+    outs = [((rows, width), jnp.bfloat16, VMEM) for rows in sums]
     scratch = []
     for parts in groups:
         slots = sum(part.shape[0] for part in parts)
         scratch.append(pltpu.VMEM((slots,) + parts[0].shape[1:], jnp.bfloat16))
-    scratch += [pltpu.VMEM((rows, width), jnp.bfloat16) for rows in sums]
     parts = [part for parts in groups for part in parts]
     sizes = [len(parts) for parts in groups]
     inputs, aliases = [table, *qs, *parts], {}
@@ -355,7 +350,7 @@
         10,
         [SMEM] + [VMEM] * (len(inputs) - 1),
         outs + [(shape, jnp.float32, VMEM) for shape in shapes],
-        scratch + [pltpu.SemaphoreType.DMA((len(parts) + len(outs),))],
+        scratch + [pltpu.SemaphoreType.DMA((len(parts),))],
         *inputs,
         aliases=aliases,
     )
@@ -408,31 +403,27 @@
     )
 
 
-def near_kernel(chunks, left_hbm, weights_hbm, out, left, weights, semaphores):
+def near_kernel(chunks, left, weights_hbm, out, weights, semaphores):
     copies = Copies(semaphores)
     step = out.shape[1] // chunks
-    first = copies.start(left_hbm, left)
     lanes = [pl.ds(chunk * step, step) for chunk in range(chunks)]
     waits = [copies.start(weights_hbm.at[:, at], weights.at[:, at]) for at in lanes]
-    first.wait()
     for at, copy in zip(lanes, waits):
         copy.wait()
-        out[:, at] = jnp.dot(left[...], weights[:, at], preferred_element_type=jnp.float32)
+        out[:, at] = jnp.dot(
+            left[...], weights[:, at], preferred_element_type=jnp.float32
+        ).astype(jnp.bfloat16)
 
 
 def output_near(left, weights, chunks=6):
-    (rows, columns), width = left.shape, weights.shape[1]
+    rows, width = left.shape[0], weights.shape[1]
     return call(
         functools.partial(near_kernel, chunks),
         "output_near",
         8,
-        [HBM] * 2,
-        [((rows, width), jnp.float32, VMEM)],
-        [
-            pltpu.VMEM(left.shape, left.dtype),
-            pltpu.VMEM(weights.shape, weights.dtype),
-            pltpu.SemaphoreType.DMA((1 + chunks,)),
-        ],
+        [VMEM, HBM],
+        [((rows, width), jnp.bfloat16, VMEM)],
+        [pltpu.VMEM(weights.shape, weights.dtype), pltpu.SemaphoreType.DMA((chunks,))],
         left,
         weights,
     )[0]
@@ -462,7 +453,7 @@
     for chunk in range(chunks):
         span = pl.ds(chunk * step, step)
         staged[:, span] = (
-            near[half:, span]
+            near[half:, span].astype(jnp.float32)
             + jnp.dot(left[half:, :], weights[:, span], preferred_element_type=jnp.float32)
         ).astype(jnp.bfloat16)
         stores.append(copies.start(staged.at[:, span], out.at[:, span]))
@@ -498,7 +489,7 @@
     half, step = left.shape[0] // 2, out.shape[1] // chunks
     for chunk in range(chunks):
         span = pl.ds(chunk * step, step)
-        out[:, span] = near[:half, span] + jnp.dot(
+        out[:, span] = near[:half, span].astype(jnp.float32) + jnp.dot(
             left[:half, :], weights[:, span], preferred_element_type=jnp.float32
         )
     late.wait()

time: 98.3 us -> 96.6 us (0.983); the launches traced: 99.4 us -> 96.1 us
  starting transfers between devices: 26.9 us -> 21.8 us
  waiting for transfers between devices: 23.4 us -> 27.4 us
  Pallas kernels: 45.4 us -> 43.3 us
    ppermute x16, starting transfers between devices: 18.3 us -> 13.6 us  [flipped(): return lax.ppermute(array, axis, [(i, i ^ bit) for i in range(size)])]
    ppermute x3, waiting for transfers between devices: 8.74 us -> 12.9 us  [along_line(): lax.ppermute(array, 'seq', [(i, (i + by) % size) for i in range(size)])]
    pallas_call x14, Pallas kernels: 45.4 us -> 43.3 us  [call(): pl.pallas_call(kernel, in_specs=in_specs, out_specs=[spec for _, _, spec...]
  transfers between devices with their start and end apart: 22 -> 22, of which waited for: 11 -> 10; matrix products, arithmetic and copies ran while one was open for 3% -> 3% of each run, Pallas kernels for 37% -> 36%
where the time goes in v8:
time: 96.6 us; the launch traced here: 96.1 us
  Pallas kernels  43.3 us (45%)
  waiting for transfers between devices  27.4 us (28%)
  starting transfers between devices  21.8 us (23%)
  other arithmetic  3.15 us (3%)
    pallas_call x14, Pallas kernels, call(): pl.pallas_call(kernel, in_specs=in_specs, out_specs=[spec for _, _, spec...  43.3 us
    ppermute x16, starting transfers between devices, flipped(): return lax.ppermute(array, axis, [(i, i ^ bit) for i in range(size)])  13.6 us
    ppermute x3, waiting for transfers between devices, along_line(): lax.ppermute(array, 'seq', [(i, (i + by) % size) for i in range(size)])  12.9 us
    ppermute x16, waiting for transfers between devices, flipped(): return lax.ppermute(array, axis, [(i, i ^ bit) for i in range(size)])  9.99 us
    ppermute x3, starting transfers between devices, along_line(): lax.ppermute(array, 'seq', [(i, (i + by) % size) for i in range(size)])  4.67 us
    ppermute x3, waiting for transfers between devices, along_ring(): part = lax.ppermute(part, 'seq', [(i, (i + 1) % size) for i in range(size)])  4.55 us
    ppermute x3, starting transfers between devices, along_ring(): part = lax.ppermute(part, 'seq', [(i, (i + 1) % size) for i in range(size)])  3.48 us
  transfers between devices with their start and end apart: 22, of which 10 were waited for; matrix products, arithmetic and copies ran while one was open for 3% of the time, Pallas kernels for 36%

profile of v8, /device:TPU:0, one launch (start us, length us, event | category | flops | bytes accessed | tf_op | source)
XLA Modules:
  0.0 96.1 jit_solution(12721621737275900039)
XLA Ops:
  0.0 2.3 %norm_rows.3.refs_0_ = bf16[96,4608]{1,0:T(8,128)(2,1)} custom-call(bf16[192,4608]{1,0:T(8,128)(2,1)} %hidden.5, f32[4608]{0:T(1024)} %gain.4), custom_call_target="tpu_custom_call" | custom-call | flops 1 | bytes 1 | tf_op jit(solution)/shard_map/norm_rows/pallas_call | solution.py:38
  2.9 2.6 %collective-permute-start.1 = (bf16[96,4608]{1,0:T(8,128)(2,1)}, bf16[96,4608]{1,0:T(8,128)(2,1)S(1)}, u32[]{:S(2)}, u32[]{:S(2)}) collective-permute-start(bf16[96,4608]{1,0:T(8,128)(2,1)} %norm_rows.3.refs_0_), channel_id=1, source_target_pairs={{0,8},{4,12},{8,0},{12,4},{1,9},{5,13},{9,1},{13,5},{2,10},{6,14},... | collective-permute-start | bytes 2654216 | tf_op jit(solution)/shard_map/ppermute | solution.py:581
  5.5 2.3 %norm_rows.2.refs_1_ = bf16[96,4608]{1,0:T(8,128)(2,1)} custom-call(bf16[192,4608]{1,0:T(8,128)(2,1)} %hidden.5, f32[4608]{0:T(1024)} %gain.4), custom_call_target="tpu_custom_call" | custom-call | flops 1 | bytes 1 | tf_op jit(solution)/shard_map/norm_rows/pallas_call | solution.py:38
  8.4 1.4 %multiply_cosine_fusion = (f32[768,64]{1,0:T(8,128)S(1)}, f32[768,64]{1,0:T(8,128)S(1)}, f32[768,64]{1,0:T(8,128)S(1)}) fusion(f32[768]{0:T(1024)S(1)} %add_convert_fusion, f32[64]{0:T(128)S(1)} %multiply_power_fusion), kind=kLoop, calls=%fused_computation.2 | loop fusion | flops 98304 | bytes 593152 | tf_op jit(solution)/shard_map/cos | solution.py:570
  9.9 1.3 %pad_maximum_fusion.trig = f32[768,256]{1,0:T(8,128)} fusion(f32[768,64]{1,0:T(8,128)S(1)} %get-tuple-element.79, f32[768,64]{1,0:T(8,128)S(1)} %get-tuple-element.78, f32[768,64]{1,0:T(8,128)S(1)} %get-tuple-element.77), kind=kLoop, calls=%fused_computation | loop fusion | flops 589824 | bytes 1376256 | tf_op jit(solution)/shard_map/concatenate | solution.py:571
  11.2 4.8 %qkv.3 = (bf16[2,384,128]{2,1,0:T(8,128)(2,1)S(1)}, bf16[384,256]{1,0:T(8,128)(2,1)S(1)}) custom-call(f32[768,256]{1,0:T(8,128)} %pad_maximum_fusion.trig, bf16[4608,256]{1,0:T(8,128)(2,1)} %wq.5, bf16[4608,128]{1,0:T(8,128)(2,1)} %wk.5, bf16[4608,128]{1,0:T(8,128)(2,1)} %wv.5, bf16[96,4608]{1,0:T(8,128)(2,1)} %norm_rows.3.refs_0_, ...), custom_call_target="tpu_custom_call" | custom-call | flops 1 | bytes 1 | tf_op jit(solution)/shard_map/qkv/pallas_call | solution.py:38
  16.0 3.7 %collective-permute-start.6 = (bf16[384,256]{1,0:T(8,128)(2,1)S(1)}, bf16[384,256]{1,0:T(8,128)(2,1)S(1)}, u32[]{:S(2)}, u32[]{:S(2)}) collective-permute-start(bf16[384,256]{1,0:T(8,128)(2,1)S(1)} %get-tuple-element.40), channel_id=1, source_target_pairs={{0,3},{1,0},{2,1},{3,2},{4,7},{5,4},{6,5},{7,6},{8,11},{9,8},{10,9... | collective-permute-start | bytes 589832 | tf_op jit(solution)/shard_map/ppermute | solution.py:588
  19.6 1.0 %collective-permute-start.4 = (bf16[384,256]{1,0:T(8,128)(2,1)S(1)}, bf16[384,256]{1,0:T(8,128)(2,1)S(1)}, u32[]{:S(2)}, u32[]{:S(2)}) collective-permute-start(bf16[384,256]{1,0:T(8,128)(2,1)S(1)} %get-tuple-element.40), channel_id=1, source_target_pairs={{0,1},{1,2},{2,3},{3,0},{4,5},{5,6},{6,7},{7,4},{8,9},{9,10},{10,1... | collective-permute-start | bytes 589832 | tf_op jit(solution)/shard_map/ppermute | solution.py:588
  21.2 2.7 %cut_weights.1 = (bf16[32,4608]{1,0:T(8,128)(2,1)}, bf16[48,4608]{1,0:T(8,128)(2,1)}, bf16[32,4608]{1,0:T(8,128)(2,1)}, bf16[32,4608]{1,0:T(8,128)(2,1)}) custom-call(s32[10]{0:T(128)S(1)} %pad_add_fusion.1.table, bf16[256,4608]{1,0:T(8,128)(2,1)} %weights_hbm.1), custom_call_target="tpu_custom_call" | custom-call | flops 1 | bytes 1 | tf_op jit(solution)/shard_map/cut_weights/pallas_call | solution.py:38
  24.9 11.9 %collective-permute-done.5 = bf16[384,256]{1,0:T(8,128)(2,1)S(1)} collective-permute-done((bf16[384,256]{1,0:T(8,128)(2,1)S(1)}, bf16[384,256]{1,0:T(8,128)(2,1)S(1)}, u32[]{:S(2)}, u32[]{:S(2)}) %collective-permute-start.5) | collective-permute-done | bytes 196640 | tf_op jit(solution)/shard_map/ppermute | solution.py:588
  36.8 2.9 %attention.4 = (f32[3,8,256]{2,1,0:T(8,128)S(1)}, f32[3,144,256]{2,1,0:T(8,128)S(1)}) custom-call(s32[10]{0:T(128)S(1)} %pad_add_fusion.1.table, bf16[2,384,128]{2,1,0:T(8,128)(2,1)S(1)} %get-tuple-element.46.refs_0_, bf16[1,384,256]{2,1,0:T(8,128)(2,1)S(1)} %bitcast.17, bf16[1,384,256]{2,1,0:T(8,128)(2,1)S(1)} %bitcast.23, ...), custom_call_target="tpu_custom_call" | custom-call | flops 1 | bytes 1 | tf_op jit(solution)/shard_map/attention/pallas_call | solution.py:38
  40.4 1.3 %collective-permute-done.8.refs_2_ = bf16[48,4608]{1,0:T(8,128)(2,1)S(1)} collective-permute-done((bf16[48,4608]{1,0:T(8,128)(2,1)S(1)}, bf16[48,4608]{1,0:T(8,128)(2,1)S(1)}, u32[]{:S(2)}, u32[]{:S(2)}) %collective-permute-start.8) | collective-permute-done | bytes 442400 | tf_op jit(solution)/shard_map/ppermute | solution.py:581
  42.3 3.4 %qkv.4 = (bf16[2,384,128]{2,1,0:T(8,128)(2,1)S(1)}, bf16[384,256]{1,0:T(8,128)(2,1)S(1)}) custom-call(f32[768,256]{1,0:T(8,128)} %pad_maximum_fusion.trig, bf16[4608,256]{1,0:T(8,128)(2,1)} %wq.5, bf16[4608,128]{1,0:T(8,128)(2,1)} %wk.5, bf16[4608,128]{1,0:T(8,128)(2,1)} %wv.5, bf16[96,4608]{1,0:T(8,128)(2,1)S(1)} %collective-permute-done.1.refs_0_, ...), custom_call_target="tpu_custom_call" | custom-call | flops 1 | bytes 1 | tf_op jit(solution)/shard_map/qkv/pallas_call | solution.py:38
  46.0 1.2 %collective-permute-start.12 = (bf16[32,4608]{1,0:T(8,128)(2,1)S(1)}, bf16[32,4608]{1,0:T(8,128)(2,1)S(1)}, u32[]{:S(2)}, u32[]{:S(2)}) collective-permute-start(bf16[32,4608]{1,0:T(8,128)(2,1)S(1)} %copy-done.4), channel_id=1, source_target_pairs={{0,8},{4,12},{8,0},{12,4},{1,9},{5,13},{9,1},{13,5},{2,10},{6,14},... | collective-permute-start | bytes 884744 | tf_op jit(solution)/shard_map/ppermute | solution.py:581
  48.2 3.3 %qkv.5 = (bf16[2,384,128]{2,1,0:T(8,128)(2,1)S(1)}, bf16[384,256]{1,0:T(8,128)(2,1)S(1)}) custom-call(f32[768,256]{1,0:T(8,128)} %pad_maximum_fusion.trig, bf16[4608,256]{1,0:T(8,128)(2,1)} %wq.5, bf16[4608,128]{1,0:T(8,128)(2,1)} %wk.5, bf16[4608,128]{1,0:T(8,128)(2,1)} %wv.5, ...), custom_call_target="tpu_custom_call", output_to_operand_aliasing={{0}: (6, {}), {1}: (7, {})} | custom-call | flops 1 | bytes 1 | tf_op jit(solution)/shard_map/qkv/pallas_call | solution.py:38
  51.6 2.3 %collective-permute-start.10 = (bf16[384,256]{1,0:T(8,128)(2,1)S(1)}, bf16[384,256]{1,0:T(8,128)(2,1)S(1)}, u32[]{:S(2)}, u32[]{:S(2)}) collective-permute-start(bf16[384,256]{1,0:T(8,128)(2,1)S(1)} %get-tuple-element.54), channel_id=1, source_target_pairs={{0,1},{1,2},{2,3},{3,0},{4,5},{5,6},{6,7},{7,4},{8,9},{9,10},{10,1... | collective-permute-start | bytes 589832 | tf_op jit(solution)/shard_map/ppermute | solution.py:599
  53.8 1.9 %collective-permute-done.12.refs_0_ = bf16[32,4608]{1,0:T(8,128)(2,1)S(1)} collective-permute-done((bf16[32,4608]{1,0:T(8,128)(2,1)S(1)}, bf16[32,4608]{1,0:T(8,128)(2,1)S(1)}, u32[]{:S(2)}, u32[]{:S(2)}) %collective-permute-start.12) | collective-permute-done | bytes 294944 | tf_op jit(solution)/shard_map/ppermute | solution.py:581
  55.8 1.5 %collective-permute-start.13 = (bf16[32,4608]{1,0:T(8,128)(2,1)S(1)}, bf16[32,4608]{1,0:T(8,128)(2,1)S(1)}, u32[]{:S(2)}, u32[]{:S(2)}) collective-permute-start(bf16[32,4608]{1,0:T(8,128)(2,1)S(1)} %collective-permute-done.12.refs_0_), channel_id=1, source_target_pairs={{0,16},{16,0},{1,17},{17,1},{2,18},{18,2},{3,19},{19,3},{4,20},{20... | collective-permute-start | bytes 884744 | tf_op jit(solution)/shard_map/ppermute | solution.py:581
  57.3 3.1 %collective-permute-done.10 = bf16[384,256]{1,0:T(8,128)(2,1)S(1)} collective-permute-done((bf16[384,256]{1,0:T(8,128)(2,1)S(1)}, bf16[384,256]{1,0:T(8,128)(2,1)S(1)}, u32[]{:S(2)}, u32[]{:S(2)}) %collective-permute-start.10) | collective-permute-done | bytes 196640 | tf_op jit(solution)/shard_map/ppermute | solution.py:599
  61.5 3.7 %collective-permute-done.16.refs_1_ = bf16[48,4608]{1,0:T(8,128)(2,1)S(1)} collective-permute-done((bf16[48,4608]{1,0:T(8,128)(2,1)S(1)}, bf16[48,4608]{1,0:T(8,128)(2,1)S(1)}, u32[]{:S(2)}, u32[]{:S(2)}) %collective-permute-start.16) | collective-permute-done | bytes 442400 | tf_op jit(solution)/shard_map/ppermute | solution.py:581
  65.3 1.5 %collective-permute-start.18 = (bf16[48,4608]{1,0:T(8,128)(2,1)S(1)}, bf16[48,4608]{1,0:T(8,128)(2,1)S(1)}, u32[]{:S(2)}, u32[]{:S(2)}) collective-permute-start(bf16[48,4608]{1,0:T(8,128)(2,1)S(1)} %collective-permute-done.16.refs_1_), channel_id=1, source_target_pairs={{0,16},{16,0},{1,17},{17,1},{2,18},{18,2},{3,19},{19,3},{4,20},{20... | collective-permute-start | bytes 1327112 | tf_op jit(solution)/shard_map/ppermute | solution.py:581
  66.8 1.5 %collective-permute-done.11 = bf16[384,256]{1,0:T(8,128)(2,1)S(1)} collective-permute-done((bf16[384,256]{1,0:T(8,128)(2,1)S(1)}, bf16[384,256]{1,0:T(8,128)(2,1)S(1)}, u32[]{:S(2)}, u32[]{:S(2)}) %collective-permute-start.11) | collective-permute-done | bytes 196640 | tf_op jit(solution)/shard_map/ppermute | solution.py:599
  69.0 4.1 %attention.5 = (f32[3,8,256]{2,1,0:T(8,128)S(1)}, f32[3,144,256]{2,1,0:T(8,128)S(1)}, f32[3,8,256]{2,1,0:T(8,128)S(1)}, f32[3,144,256]{2,1,0:T(8,128)S(1)}) custom-call(s32[10]{0:T(128)S(1)} %pad_add_fusion.1.table, bf16[2,384,128]{2,1,0:T(8,128)(2,1)S(1)} %get-tuple-element.46.refs_0_, ...), custom_call_target="tpu_custom_call", output_to_operand_aliasing={{0}: (8, {}), {1}: (9, {})} | custom-call | flops 1 | bytes 1 | tf_op jit(solution)/shard_map/attention/pallas_call | solution.py:38
  73.1 1.2 %collective-permute-start.20 = (bf16[32,4608]{1,0:T(8,128)(2,1)S(1)}, bf16[32,4608]{1,0:T(8,128)(2,1)S(1)}, u32[]{:S(2)}, u32[]{:S(2)}) collective-permute-start(bf16[32,4608]{1,0:T(8,128)(2,1)S(1)} %copy-done.2), channel_id=1, source_target_pairs={{0,8},{4,12},{8,0},{12,4},{1,9},{5,13},{9,1},{13,5},{2,10},{6,14},... | collective-permute-start | bytes 884744 | tf_op jit(solution)/shard_map/ppermute | solution.py:581
  74.3 1.5 %collective-permute-start.19 = (bf16[32,4608]{1,0:T(8,128)(2,1)S(1)}, bf16[32,4608]{1,0:T(8,128)(2,1)S(1)}, u32[]{:S(2)}, u32[]{:S(2)}) collective-permute-start(bf16[32,4608]{1,0:T(8,128)(2,1)S(1)} %collective-permute-done.17.refs_2_), channel_id=1, source_target_pairs={{0,16},{16,0},{1,17},{17,1},{2,18},{18,2},{3,19},{19,3},{4,20},{20... | collective-permute-start | bytes 884744 | tf_op jit(solution)/shard_map/ppermute | solution.py:581
  75.8 3.1 %attention.6 = (bf16[384,256]{1,0:T(8,128)(2,1)S(1)}, f32[3,8,256]{2,1,0:T(8,128)S(1)}, f32[3,144,256]{2,1,0:T(8,128)S(1)}) custom-call(s32[10]{0:T(128)S(1)} %pad_add_fusion.1.table, bf16[2,384,128]{2,1,0:T(8,128)(2,1)S(1)} %get-tuple-element.53.refs_1_.refs_0_, bf16[1,384,256]{2,1,0:T(8,128)(2,1)S(1)} %bitcast.15, ...), custom_call_target="tpu_custom_call", output_to_operand_aliasing={{1}: (6, {}), {2}: (7, {})} | custom-call | flops 1 | bytes 1 | tf_op jit(solution)/shard_map/attention/pallas_call | solution.py:38
  79.4 3.1 %attention.7 = (bf16[384,256]{1,0:T(8,128)(2,1)S(1)}, f32[3,8,256]{2,1,0:T(8,128)S(1)}, f32[3,144,256]{2,1,0:T(8,128)S(1)}) custom-call(s32[10]{0:T(128)S(1)} %pad_add_fusion.1.table, bf16[2,384,128]{2,1,0:T(8,128)(2,1)S(1)} %get-tuple-element.46.refs_0_, bf16[1,384,256]{2,1,0:T(8,128)(2,1)S(1)} %bitcast.16, ...), custom_call_target="tpu_custom_call", output_to_operand_aliasing={{1}: (6, {}), {2}: (7, {})} | custom-call | flops 1 | bytes 1 | tf_op jit(solution)/shard_map/attention/pallas_call | solution.py:38
  82.6 3.3 %output_near.1.near = bf16[384,4608]{1,0:T(8,128)(2,1)S(1)} custom-call(bf16[384,256]{1,0:T(8,128)(2,1)S(1)} %get-tuple-element.63.left, bf16[256,4608]{1,0:T(8,128)(2,1)} %weights_hbm.1), custom_call_target="tpu_custom_call" | custom-call | flops 1 | bytes 1 | tf_op jit(solution)/shard_map/output_near/pallas_call | solution.py:38
  85.9 3.6 %output_send.1 = (bf16[192,4608]{1,0:T(8,128)(2,1)}, bf16[256,4608]{1,0:T(8,128)(2,1)S(1)}) custom-call(s32[10]{0:T(128)S(1)} %pad_add_fusion.1.table, bf16[384,256]{1,0:T(8,128)(2,1)S(1)} %collective-permute-done.15.left_hbm, bf16[384,4608]{1,0:T(8,128)(2,1)S(1)} %output_near.1.near, bf16[32,4608]{1,0:T(8,128)(2,1)S(1)} %collective-permute-done.12.refs_0_, ...), custom_call_target="tpu_custom_call" | custom-call | flops 1 | bytes 1 | tf_op jit(solution)/shard_map/output_send/pallas_call | solution.py:38
  89.5 1.7 %output_keep.1 = (f32[192,4608]{1,0:T(8,128)S(1)}, bf16[192,4608]{1,0:T(8,128)(2,1)S(1)}) custom-call(bf16[384,256]{1,0:T(8,128)(2,1)S(1)} %collective-permute-done.15.left_hbm, bf16[192,4608]{1,0:T(8,128)(2,1)} %hidden.5, bf16[384,4608]{1,0:T(8,128)(2,1)S(1)} %output_near.1.near, bf16[256,4608]{1,0:T(8,128)(2,1)S(1)} %get-tuple-element.70.weights), custom_call_target="tpu_custom_call" | custom-call | flops 1 | bytes 1 | tf_op jit(solution)/shard_map/output_keep/pallas_call | solution.py:38
  91.3 2.1 %collective-permute-done.21.received = bf16[192,4608]{1,0:T(8,128)(2,1)S(1)} collective-permute-done((bf16[192,4608]{1,0:T(8,128)(2,1)}, bf16[192,4608]{1,0:T(8,128)(2,1)S(1)}, u32[]{:S(2)}, u32[]{:S(2)}) %collective-permute-start.21) | collective-permute-done | bytes 1769504 | tf_op jit(solution)/shard_map/ppermute | solution.py:581
  93.4 2.6 %output_norm.1 = bf16[192,4608]{1,0:T(8,128)(2,1)} custom-call(bf16[192,4608]{1,0:T(8,128)(2,1)S(1)} %collective-permute-done.21.received, bf16[192,4608]{1,0:T(8,128)(2,1)S(1)} %get-tuple-element.71.hidden, f32[192,4608]{1,0:T(8,128)S(1)} %get-tuple-element.72.kept, f32[4608]{0:T(1024)} %gain.5), custom_call_target="tpu_custom_call" | custom-call | flops 1 | bytes 1 | tf_op jit(solution)/shard_map/output_norm/pallas_call | solution.py:38
  (48 shorter events, 7.8 us)
Async XLA Ops:
  2.3 5.7 %copy-start = (s32[8]{0:T(128)S(1)}, s32[8]{0:T(128)}, u32[]{:S(2)}) copy-start(s32[8]{0:T(128)} %param.15) | copy-start | bytes 100
  2.4 8.8 %collective-permute-start.2 = (bf16[96,4608]{1,0:T(8,128)(2,1)}, bf16[96,4608]{1,0:T(8,128)(2,1)S(1)}, u32[]{:S(2)}, u32[]{:S(2)}) collective-permute-start(bf16[96,4608]{1,0:T(8,128)(2,1)} %norm_rows.3.refs_0_), channel_id=1, source_target_pairs={{0,4},{4,0},{8,12},{12,8},{1,5},{5,1},{9,13},{13,9},{2,6},{6,2},{1... | collective-permute-start | bytes 2654216 | tf_op jit(solution)/shard_map/ppermute | solution.py:581
  2.9 36.9 %collective-permute-start.1 = (bf16[96,4608]{1,0:T(8,128)(2,1)}, bf16[96,4608]{1,0:T(8,128)(2,1)S(1)}, u32[]{:S(2)}, u32[]{:S(2)}) collective-permute-start(bf16[96,4608]{1,0:T(8,128)(2,1)} %norm_rows.3.refs_0_), channel_id=1, source_target_pairs={{0,8},{4,12},{8,0},{12,4},{1,9},{5,13},{9,1},{13,5},{2,10},{6,14},... | collective-permute-start | bytes 2654216 | tf_op jit(solution)/shard_map/ppermute | solution.py:581
  7.8 3.4 %collective-permute-start.3 = (bf16[96,4608]{1,0:T(8,128)(2,1)}, bf16[96,4608]{1,0:T(8,128)(2,1)S(1)}, u32[]{:S(2)}, u32[]{:S(2)}) collective-permute-start(bf16[96,4608]{1,0:T(8,128)(2,1)} %norm_rows.2.refs_1_), channel_id=1, source_target_pairs={{0,4},{4,0},{8,12},{12,8},{1,5},{5,1},{9,13},{13,9},{2,6},{6,2},{1... | collective-permute-start | bytes 2654216 | tf_op jit(solution)/shard_map/ppermute | solution.py:581
  16.0 9.0 %collective-permute-start.6 = (bf16[384,256]{1,0:T(8,128)(2,1)S(1)}, bf16[384,256]{1,0:T(8,128)(2,1)S(1)}, u32[]{:S(2)}, u32[]{:S(2)}) collective-permute-start(bf16[384,256]{1,0:T(8,128)(2,1)S(1)} %get-tuple-element.40), channel_id=1, source_target_pairs={{0,3},{1,0},{2,1},{3,2},{4,7},{5,4},{6,5},{7,6},{8,11},{9,8},{10,9... | collective-permute-start | bytes 589832 | tf_op jit(solution)/shard_map/ppermute | solution.py:588
  19.6 17.2 %collective-permute-start.5 = (bf16[384,256]{1,0:T(8,128)(2,1)S(1)}, bf16[384,256]{1,0:T(8,128)(2,1)S(1)}, u32[]{:S(2)}, u32[]{:S(2)}) collective-permute-start(bf16[384,256]{1,0:T(8,128)(2,1)S(1)} %get-tuple-element.40), channel_id=1, source_target_pairs={{0,2},{1,3},{2,0},{3,1},{4,6},{5,7},{6,4},{7,5},{8,10},{9,11},{10,... | collective-permute-start | bytes 589832 | tf_op jit(solution)/shard_map/ppermute | solution.py:588
  19.6 17.2 %collective-permute-start.4 = (bf16[384,256]{1,0:T(8,128)(2,1)S(1)}, bf16[384,256]{1,0:T(8,128)(2,1)S(1)}, u32[]{:S(2)}, u32[]{:S(2)}) collective-permute-start(bf16[384,256]{1,0:T(8,128)(2,1)S(1)} %get-tuple-element.40), channel_id=1, source_target_pairs={{0,1},{1,2},{2,3},{3,0},{4,5},{5,6},{6,7},{7,4},{8,9},{9,10},{10,1... | collective-permute-start | bytes 589832 | tf_op jit(solution)/shard_map/ppermute | solution.py:588
  20.6 25.1 %collective-permute-start = (bf16[96,4608]{1,0:T(8,128)(2,1)}, bf16[96,4608]{1,0:T(8,128)(2,1)S(1)}, u32[]{:S(2)}, u32[]{:S(2)}) collective-permute-start(bf16[96,4608]{1,0:T(8,128)(2,1)} %norm_rows.2.refs_1_), channel_id=1, source_target_pairs={{0,8},{4,12},{8,0},{12,4},{1,9},{5,13},{9,1},{13,5},{2,10},{6,14},... | collective-permute-start | bytes 2654216 | tf_op jit(solution)/shard_map/ppermute | solution.py:581
  39.9 1.9 %collective-permute-start.8 = (bf16[48,4608]{1,0:T(8,128)(2,1)S(1)}, bf16[48,4608]{1,0:T(8,128)(2,1)S(1)}, u32[]{:S(2)}, u32[]{:S(2)}) collective-permute-start(bf16[48,4608]{1,0:T(8,128)(2,1)S(1)} %get-tuple-element.75), channel_id=1, source_target_pairs={{0,4},{4,0},{8,12},{12,8},{1,5},{5,1},{9,13},{13,9},{2,6},{6,2},{1... | collective-permute-start | bytes 1327112 | tf_op jit(solution)/shard_map/ppermute | solution.py:581
  39.9 6.0 %copy-start.4 = (bf16[32,4608]{1,0:T(8,128)(2,1)S(1)}, bf16[32,4608]{1,0:T(8,128)(2,1)}, u32[]{:S(2)}) copy-start(bf16[32,4608]{1,0:T(8,128)(2,1)} %get-tuple-element.55) | copy-start | bytes 884740
  39.9 7.2 %copy-start.1 = (bf16[48,4608]{1,0:T(8,128)(2,1)S(1)}, bf16[48,4608]{1,0:T(8,128)(2,1)}, u32[]{:S(2)}) copy-start(bf16[48,4608]{1,0:T(8,128)(2,1)} %get-tuple-element.64) | copy-start | bytes 1327108
  40.0 2.4 %collective-permute-start.7 = (bf16[48,4608]{1,0:T(8,128)(2,1)S(1)}, bf16[48,4608]{1,0:T(8,128)(2,1)S(1)}, u32[]{:S(2)}, u32[]{:S(2)}) collective-permute-start(bf16[48,4608]{1,0:T(8,128)(2,1)S(1)} %get-tuple-element.76), channel_id=1, source_target_pairs={{0,4},{4,0},{8,12},{12,8},{1,5},{5,1},{9,13},{13,9},{2,6},{6,2},{1... | collective-permute-start | bytes 1327112 | tf_op jit(solution)/shard_map/ppermute | solution.py:581
  45.7 15.1 %copy-start.3 = (bf16[32,4608]{1,0:T(8,128)(2,1)S(1)}, bf16[32,4608]{1,0:T(8,128)(2,1)}, u32[]{:S(2)}) copy-start(bf16[32,4608]{1,0:T(8,128)(2,1)} %get-tuple-element.66) | copy-start | bytes 884740
  45.7 2.5 %collective-permute-start.9 = (bf16[96,4608]{1,0:T(8,128)(2,1)S(1)}, bf16[96,4608]{1,0:T(8,128)(2,1)S(1)}, u32[]{:S(2)}, u32[]{:S(2)}) collective-permute-start(bf16[96,4608]{1,0:T(8,128)(2,1)S(1)} %collective-permute-done.refs_0_), channel_id=1, source_target_pairs={{0,4},{4,0},{8,12},{12,8},{1,5},{5,1},{9,13},{13,9},{2,6},{6,2},{1... | collective-permute-start | bytes 2654216 | tf_op jit(solution)/shard_map/ppermute | solution.py:581
  46.0 9.8 %collective-permute-start.12 = (bf16[32,4608]{1,0:T(8,128)(2,1)S(1)}, bf16[32,4608]{1,0:T(8,128)(2,1)S(1)}, u32[]{:S(2)}, u32[]{:S(2)}) collective-permute-start(bf16[32,4608]{1,0:T(8,128)(2,1)S(1)} %copy-done.4), channel_id=1, source_target_pairs={{0,8},{4,12},{8,0},{12,4},{1,9},{5,13},{9,1},{13,5},{2,10},{6,14},... | collective-permute-start | bytes 884744 | tf_op jit(solution)/shard_map/ppermute | solution.py:581
  47.2 18.1 %collective-permute-start.16 = (bf16[48,4608]{1,0:T(8,128)(2,1)S(1)}, bf16[48,4608]{1,0:T(8,128)(2,1)S(1)}, u32[]{:S(2)}, u32[]{:S(2)}) collective-permute-start(bf16[48,4608]{1,0:T(8,128)(2,1)S(1)} %copy-done.1), channel_id=1, source_target_pairs={{0,8},{4,12},{8,0},{12,4},{1,9},{5,13},{9,1},{13,5},{2,10},{6,14},... | collective-permute-start | bytes 1327112 | tf_op jit(solution)/shard_map/ppermute | solution.py:581
  51.5 21.6 %copy-start.2 = (bf16[32,4608]{1,0:T(8,128)(2,1)S(1)}, bf16[32,4608]{1,0:T(8,128)(2,1)}, u32[]{:S(2)}) copy-start(bf16[32,4608]{1,0:T(8,128)(2,1)} %get-tuple-element.68) | copy-start | bytes 884740
  51.6 8.8 %collective-permute-start.10 = (bf16[384,256]{1,0:T(8,128)(2,1)S(1)}, bf16[384,256]{1,0:T(8,128)(2,1)S(1)}, u32[]{:S(2)}, u32[]{:S(2)}) collective-permute-start(bf16[384,256]{1,0:T(8,128)(2,1)S(1)} %get-tuple-element.54), channel_id=1, source_target_pairs={{0,1},{1,2},{2,3},{3,0},{4,5},{5,6},{6,7},{7,4},{8,9},{9,10},{10,1... | collective-permute-start | bytes 589832 | tf_op jit(solution)/shard_map/ppermute | solution.py:599
  55.8 11.0 %collective-permute-start.13 = (bf16[32,4608]{1,0:T(8,128)(2,1)S(1)}, bf16[32,4608]{1,0:T(8,128)(2,1)S(1)}, u32[]{:S(2)}, u32[]{:S(2)}) collective-permute-start(bf16[32,4608]{1,0:T(8,128)(2,1)S(1)} %collective-permute-done.12.refs_0_), channel_id=1, source_target_pairs={{0,16},{16,0},{1,17},{17,1},{2,18},{18,2},{3,19},{19,3},{4,20},{20... | collective-permute-start | bytes 884744 | tf_op jit(solution)/shard_map/ppermute | solution.py:581
  60.4 7.9 %collective-permute-start.11 = (bf16[384,256]{1,0:T(8,128)(2,1)S(1)}, bf16[384,256]{1,0:T(8,128)(2,1)S(1)}, u32[]{:S(2)}, u32[]{:S(2)}) collective-permute-start(bf16[384,256]{1,0:T(8,128)(2,1)S(1)} %collective-permute-done.10), channel_id=1, source_target_pairs={{0,1},{1,2},{2,3},{3,0},{4,5},{5,6},{6,7},{7,4},{8,9},{9,10},{10,1... | collective-permute-start | bytes 589832 | tf_op jit(solution)/shard_map/ppermute | solution.py:599
  60.8 13.5 %collective-permute-start.17 = (bf16[32,4608]{1,0:T(8,128)(2,1)S(1)}, bf16[32,4608]{1,0:T(8,128)(2,1)S(1)}, u32[]{:S(2)}, u32[]{:S(2)}) collective-permute-start(bf16[32,4608]{1,0:T(8,128)(2,1)S(1)} %copy-done.3), channel_id=1, source_target_pairs={{0,8},{4,12},{8,0},{12,4},{1,9},{5,13},{9,1},{13,5},{2,10},{6,14},... | collective-permute-start | bytes 884744 | tf_op jit(solution)/shard_map/ppermute | solution.py:581
  65.3 20.6 %collective-permute-start.18 = (bf16[48,4608]{1,0:T(8,128)(2,1)S(1)}, bf16[48,4608]{1,0:T(8,128)(2,1)S(1)}, u32[]{:S(2)}, u32[]{:S(2)}) collective-permute-start(bf16[48,4608]{1,0:T(8,128)(2,1)S(1)} %collective-permute-done.16.refs_1_), channel_id=1, source_target_pairs={{0,16},{16,0},{1,17},{17,1},{2,18},{18,2},{3,19},{19,3},{4,20},{20... | collective-permute-start | bytes 1327112 | tf_op jit(solution)/shard_map/ppermute | solution.py:581
  68.3 7.6 %collective-permute-start.14 = (bf16[384,256]{1,0:T(8,128)(2,1)S(1)}, bf16[384,256]{1,0:T(8,128)(2,1)S(1)}, u32[]{:S(2)}, u32[]{:S(2)}) collective-permute-start(bf16[384,256]{1,0:T(8,128)(2,1)S(1)} %collective-permute-done.11), channel_id=1, source_target_pairs={{0,1},{1,2},{2,3},{3,0},{4,5},{5,6},{6,7},{7,4},{8,9},{9,10},{10,1... | collective-permute-start | bytes 589832 | tf_op jit(solution)/shard_map/ppermute | solution.py:599
  73.1 12.7 %collective-permute-start.20 = (bf16[32,4608]{1,0:T(8,128)(2,1)S(1)}, bf16[32,4608]{1,0:T(8,128)(2,1)S(1)}, u32[]{:S(2)}, u32[]{:S(2)}) collective-permute-start(bf16[32,4608]{1,0:T(8,128)(2,1)S(1)} %copy-done.2), channel_id=1, source_target_pairs={{0,8},{4,12},{8,0},{12,4},{1,9},{5,13},{9,1},{13,5},{2,10},{6,14},... | collective-permute-start | bytes 884744 | tf_op jit(solution)/shard_map/ppermute | solution.py:581
  74.3 11.5 %collective-permute-start.19 = (bf16[32,4608]{1,0:T(8,128)(2,1)S(1)}, bf16[32,4608]{1,0:T(8,128)(2,1)S(1)}, u32[]{:S(2)}, u32[]{:S(2)}) collective-permute-start(bf16[32,4608]{1,0:T(8,128)(2,1)S(1)} %collective-permute-done.17.refs_2_), channel_id=1, source_target_pairs={{0,16},{16,0},{1,17},{17,1},{2,18},{18,2},{3,19},{19,3},{4,20},{20... | collective-permute-start | bytes 884744 | tf_op jit(solution)/shard_map/ppermute | solution.py:581
  79.0 6.9 %collective-permute-start.15 = (bf16[384,256]{1,0:T(8,128)(2,1)S(1)}, bf16[384,256]{1,0:T(8,128)(2,1)S(1)}, u32[]{:S(2)}, u32[]{:S(2)}) collective-permute-start(bf16[384,256]{1,0:T(8,128)(2,1)S(1)} %get-tuple-element.60), channel_id=1, source_target_pairs={{0,8},{4,12},{8,0},{12,4},{1,9},{5,13},{9,1},{13,5},{2,10},{6,14},... | collective-permute-start | bytes 589832 | tf_op jit(solution)/shard_map/ppermute | solution.py:581
  89.4 4.0 %collective-permute-start.21 = (bf16[192,4608]{1,0:T(8,128)(2,1)}, bf16[192,4608]{1,0:T(8,128)(2,1)S(1)}, u32[]{:S(2)}, u32[]{:S(2)}) collective-permute-start(bf16[192,4608]{1,0:T(8,128)(2,1)} %get-tuple-element.69), channel_id=1, source_target_pairs={{0,4},{4,0},{8,12},{12,8},{1,5},{5,1},{9,13},{13,9},{2,6},{6,2},{1... | collective-permute-start | bytes 5308424 | tf_op jit(solution)/shard_map/ppermute | solution.py:581

commit v9 on v8

--- a/solution.py
+++ b/solution.py
@@ -638,7 +638,7 @@
     q_near, kv_near = qkv([*own, *partner], places, block_rows, weights, trig, 0)
     near = along_line(kv_near)
     eighth = w_out.shape[0] // 8
-    sizes = [eighth, eighth * 3 // 2, eighth]
+    sizes = [eighth, eighth, eighth * 3 // 2]
     w_cut = cut(table, group_at, after(w_out, kv_near), sizes)
     q_near = after(q_near, *w_cut)
     (near_state,) = attention(
@@ -687,7 +687,7 @@
         [near_chunk, far_chunk],
         [near_state, None],
     )
-    w_far[2] = after(w_far[2], *far_state)
+    w_far[2] = after(w_far[2], *far_state, w_other[1], came(far)[-1])
     w_other.append(swap(w_far[2]))
     rest = [Step(0, 0, others)]
     (gone,) = attention(

time: 96.6 us -> 101 us (1.046); the launches traced: 96.1 us -> 102 us
  waiting for transfers between devices: 27.4 us -> 32.1 us
  Pallas kernels: 43.3 us -> 47.3 us
  starting transfers between devices: 21.8 us -> 18.7 us
    ppermute x3, waiting for transfers between devices: 4.55 us -> 9.09 us  [along_ring(): part = lax.ppermute(part, 'seq', [(i, (i + 1) % size) for i in range(size)])]
    pallas_call x14, Pallas kernels: 43.3 us -> 47.3 us  [call(): pl.pallas_call(kernel, in_specs=in_specs, out_specs=[spec for _, _, spec...]
    ppermute x3, starting transfers between devices: 3.48 us -> 0.27 us  [along_ring(): part = lax.ppermute(part, 'seq', [(i, (i + 1) % size) for i in range(size)])]
  transfers between devices with their start and end apart: 22 -> 22, of which waited for: 10 -> 12; matrix products, arithmetic and copies ran while one was open for 3% -> 3% of each run, Pallas kernels for 36% -> 38%
where the time goes in v9:
time: 101 us; the launch traced here: 102 us
  Pallas kernels  47.3 us (47%)
  waiting for transfers between devices  32.1 us (32%)
  starting transfers between devices  18.7 us (19%)
  other arithmetic  3.15 us (3%)
    pallas_call x14, Pallas kernels, call(): pl.pallas_call(kernel, in_specs=in_specs, out_specs=[spec for _, _, spec...  47.3 us
    ppermute x16, starting transfers between devices, flipped(): return lax.ppermute(array, axis, [(i, i ^ bit) for i in range(size)])  13.8 us
    ppermute x3, waiting for transfers between devices, along_line(): lax.ppermute(array, 'seq', [(i, (i + by) % size) for i in range(size)])  12.9 us
    ppermute x16, waiting for transfers between devices, flipped(): return lax.ppermute(array, axis, [(i, i ^ bit) for i in range(size)])  10.1 us
    ppermute x3, waiting for transfers between devices, along_ring(): part = lax.ppermute(part, 'seq', [(i, (i + 1) % size) for i in range(size)])  9.09 us
    ppermute x3, starting transfers between devices, along_line(): lax.ppermute(array, 'seq', [(i, (i + by) % size) for i in range(size)])  4.67 us
  transfers between devices with their start and end apart: 22, of which 12 were waited for; matrix products, arithmetic and copies ran while one was open for 3% of the time, Pallas kernels for 38%

profile of v9, /device:TPU:0, one launch (start us, length us, event | category | flops | bytes accessed | tf_op | source)
XLA Modules:
  0.0 101.9 jit_solution(2758127256903461339)
XLA Ops:
  0.0 2.3 %norm_rows.3.refs_0_ = bf16[96,4608]{1,0:T(8,128)(2,1)} custom-call(bf16[192,4608]{1,0:T(8,128)(2,1)} %hidden.5, f32[4608]{0:T(1024)} %gain.4), custom_call_target="tpu_custom_call" | custom-call | flops 1 | bytes 1 | tf_op jit(solution)/shard_map/norm_rows/pallas_call | solution.py:38
  2.9 2.6 %collective-permute-start.1 = (bf16[96,4608]{1,0:T(8,128)(2,1)}, bf16[96,4608]{1,0:T(8,128)(2,1)S(1)}, u32[]{:S(2)}, u32[]{:S(2)}) collective-permute-start(bf16[96,4608]{1,0:T(8,128)(2,1)} %norm_rows.3.refs_0_), channel_id=1, source_target_pairs={{0,8},{4,12},{8,0},{12,4},{1,9},{5,13},{9,1},{13,5},{2,10},{6,14},... | collective-permute-start | bytes 2654216 | tf_op jit(solution)/shard_map/ppermute | solution.py:581
  5.5 2.3 %norm_rows.2.refs_1_ = bf16[96,4608]{1,0:T(8,128)(2,1)} custom-call(bf16[192,4608]{1,0:T(8,128)(2,1)} %hidden.5, f32[4608]{0:T(1024)} %gain.4), custom_call_target="tpu_custom_call" | custom-call | flops 1 | bytes 1 | tf_op jit(solution)/shard_map/norm_rows/pallas_call | solution.py:38
  8.4 1.4 %multiply_cosine_fusion = (f32[768,64]{1,0:T(8,128)S(1)}, f32[768,64]{1,0:T(8,128)S(1)}, f32[768,64]{1,0:T(8,128)S(1)}) fusion(f32[768]{0:T(1024)S(1)} %add_convert_fusion, f32[64]{0:T(128)S(1)} %multiply_power_fusion), kind=kLoop, calls=%fused_computation.2 | loop fusion | flops 98304 | bytes 593152 | tf_op jit(solution)/shard_map/cos | solution.py:570
  9.9 1.3 %pad_maximum_fusion.trig = f32[768,256]{1,0:T(8,128)} fusion(f32[768,64]{1,0:T(8,128)S(1)} %get-tuple-element.79, f32[768,64]{1,0:T(8,128)S(1)} %get-tuple-element.78, f32[768,64]{1,0:T(8,128)S(1)} %get-tuple-element.77), kind=kLoop, calls=%fused_computation | loop fusion | flops 589824 | bytes 1376256 | tf_op jit(solution)/shard_map/concatenate | solution.py:571
  11.2 4.8 %qkv.3 = (bf16[2,384,128]{2,1,0:T(8,128)(2,1)S(1)}, bf16[384,256]{1,0:T(8,128)(2,1)S(1)}) custom-call(f32[768,256]{1,0:T(8,128)} %pad_maximum_fusion.trig, bf16[4608,256]{1,0:T(8,128)(2,1)} %wq.5, bf16[4608,128]{1,0:T(8,128)(2,1)} %wk.5, bf16[4608,128]{1,0:T(8,128)(2,1)} %wv.5, bf16[96,4608]{1,0:T(8,128)(2,1)} %norm_rows.3.refs_0_, ...), custom_call_target="tpu_custom_call" | custom-call | flops 1 | bytes 1 | tf_op jit(solution)/shard_map/qkv/pallas_call | solution.py:38
  16.0 3.7 %collective-permute-start.6 = (bf16[384,256]{1,0:T(8,128)(2,1)S(1)}, bf16[384,256]{1,0:T(8,128)(2,1)S(1)}, u32[]{:S(2)}, u32[]{:S(2)}) collective-permute-start(bf16[384,256]{1,0:T(8,128)(2,1)S(1)} %get-tuple-element.40), channel_id=1, source_target_pairs={{0,3},{1,0},{2,1},{3,2},{4,7},{5,4},{6,5},{7,6},{8,11},{9,8},{10,9... | collective-permute-start | bytes 589832 | tf_op jit(solution)/shard_map/ppermute | solution.py:588
  21.2 2.7 %cut_weights.1 = (bf16[32,4608]{1,0:T(8,128)(2,1)}, bf16[32,4608]{1,0:T(8,128)(2,1)}, bf16[48,4608]{1,0:T(8,128)(2,1)}, bf16[32,4608]{1,0:T(8,128)(2,1)}) custom-call(s32[10]{0:T(128)S(1)} %pad_add_fusion.1.table, bf16[256,4608]{1,0:T(8,128)(2,1)} %weights_hbm.1), custom_call_target="tpu_custom_call" | custom-call | flops 1 | bytes 1 | tf_op jit(solution)/shard_map/cut_weights/pallas_call | solution.py:38
  23.9 1.0 %collective-permute-done.6 = bf16[384,256]{1,0:T(8,128)(2,1)S(1)} collective-permute-done((bf16[384,256]{1,0:T(8,128)(2,1)S(1)}, bf16[384,256]{1,0:T(8,128)(2,1)S(1)}, u32[]{:S(2)}, u32[]{:S(2)}) %collective-permute-start.6) | collective-permute-done | bytes 196640 | tf_op jit(solution)/shard_map/ppermute | solution.py:588
  24.9 11.9 %collective-permute-done.5 = bf16[384,256]{1,0:T(8,128)(2,1)S(1)} collective-permute-done((bf16[384,256]{1,0:T(8,128)(2,1)S(1)}, bf16[384,256]{1,0:T(8,128)(2,1)S(1)}, u32[]{:S(2)}, u32[]{:S(2)}) %collective-permute-start.5) | collective-permute-done | bytes 196640 | tf_op jit(solution)/shard_map/ppermute | solution.py:588
  36.8 4.3 %attention.4 = (f32[3,8,256]{2,1,0:T(8,128)S(1)}, f32[3,144,256]{2,1,0:T(8,128)S(1)}) custom-call(s32[10]{0:T(128)S(1)} %pad_add_fusion.1.table, bf16[2,384,128]{2,1,0:T(8,128)(2,1)S(1)} %get-tuple-element.46.refs_0_, bf16[1,384,256]{2,1,0:T(8,128)(2,1)S(1)} %bitcast.17, bf16[1,384,256]{2,1,0:T(8,128)(2,1)S(1)} %bitcast.23, ...), custom_call_target="tpu_custom_call" | custom-call | flops 1 | bytes 1 | tf_op jit(solution)/shard_map/attention/pallas_call | solution.py:38
  41.8 1.3 %collective-permute-done.8.refs_2_ = bf16[48,4608]{1,0:T(8,128)(2,1)S(1)} collective-permute-done((bf16[48,4608]{1,0:T(8,128)(2,1)S(1)}, bf16[48,4608]{1,0:T(8,128)(2,1)S(1)}, u32[]{:S(2)}, u32[]{:S(2)}) %collective-permute-start.8) | collective-permute-done | bytes 442400 | tf_op jit(solution)/shard_map/ppermute | solution.py:581
  43.7 3.4 %qkv.4 = (bf16[2,384,128]{2,1,0:T(8,128)(2,1)S(1)}, bf16[384,256]{1,0:T(8,128)(2,1)S(1)}) custom-call(f32[768,256]{1,0:T(8,128)} %pad_maximum_fusion.trig, bf16[4608,256]{1,0:T(8,128)(2,1)} %wq.5, bf16[4608,128]{1,0:T(8,128)(2,1)} %wk.5, bf16[4608,128]{1,0:T(8,128)(2,1)} %wv.5, bf16[96,4608]{1,0:T(8,128)(2,1)S(1)} %collective-permute-done.1.refs_0_, ...), custom_call_target="tpu_custom_call" | custom-call | flops 1 | bytes 1 | tf_op jit(solution)/shard_map/qkv/pallas_call | solution.py:38
  47.8 1.5 %collective-permute-start.16 = (bf16[32,4608]{1,0:T(8,128)(2,1)S(1)}, bf16[32,4608]{1,0:T(8,128)(2,1)S(1)}, u32[]{:S(2)}, u32[]{:S(2)}) collective-permute-start(bf16[32,4608]{1,0:T(8,128)(2,1)S(1)} %copy-done.3), channel_id=1, source_target_pairs={{0,8},{4,12},{8,0},{12,4},{1,9},{5,13},{9,1},{13,5},{2,10},{6,14},... | collective-permute-start | bytes 884744 | tf_op jit(solution)/shard_map/ppermute | solution.py:581
  49.6 3.3 %qkv.5 = (bf16[2,384,128]{2,1,0:T(8,128)(2,1)S(1)}, bf16[384,256]{1,0:T(8,128)(2,1)S(1)}) custom-call(f32[768,256]{1,0:T(8,128)} %pad_maximum_fusion.trig, bf16[4608,256]{1,0:T(8,128)(2,1)} %wq.5, bf16[4608,128]{1,0:T(8,128)(2,1)} %wk.5, bf16[4608,128]{1,0:T(8,128)(2,1)} %wv.5, ...), custom_call_target="tpu_custom_call", output_to_operand_aliasing={{0}: (6, {}), {1}: (7, {})} | custom-call | flops 1 | bytes 1 | tf_op jit(solution)/shard_map/qkv/pallas_call | solution.py:38
  53.2 4.0 %collective-permute-done.12.refs_0_ = bf16[32,4608]{1,0:T(8,128)(2,1)S(1)} collective-permute-done((bf16[32,4608]{1,0:T(8,128)(2,1)S(1)}, bf16[32,4608]{1,0:T(8,128)(2,1)S(1)}, u32[]{:S(2)}, u32[]{:S(2)}) %collective-permute-start.12) | collective-permute-done | bytes 294944 | tf_op jit(solution)/shard_map/ppermute | solution.py:581
  57.1 1.5 %collective-permute-start.13 = (bf16[32,4608]{1,0:T(8,128)(2,1)S(1)}, bf16[32,4608]{1,0:T(8,128)(2,1)S(1)}, u32[]{:S(2)}, u32[]{:S(2)}) collective-permute-start(bf16[32,4608]{1,0:T(8,128)(2,1)S(1)} %collective-permute-done.12.refs_0_), channel_id=1, source_target_pairs={{0,16},{16,0},{1,17},{17,1},{2,18},{18,2},{3,19},{19,3},{4,20},{20... | collective-permute-start | bytes 884744 | tf_op jit(solution)/shard_map/ppermute | solution.py:581
  59.1 2.6 %collective-permute-done.10 = bf16[384,256]{1,0:T(8,128)(2,1)S(1)} collective-permute-done((bf16[384,256]{1,0:T(8,128)(2,1)S(1)}, bf16[384,256]{1,0:T(8,128)(2,1)S(1)}, u32[]{:S(2)}, u32[]{:S(2)}) %collective-permute-start.10) | collective-permute-done | bytes 196640 | tf_op jit(solution)/shard_map/ppermute | solution.py:599
  61.7 1.8 %collective-permute-done.16.refs_1_ = bf16[32,4608]{1,0:T(8,128)(2,1)S(1)} collective-permute-done((bf16[32,4608]{1,0:T(8,128)(2,1)S(1)}, bf16[32,4608]{1,0:T(8,128)(2,1)S(1)}, u32[]{:S(2)}, u32[]{:S(2)}) %collective-permute-start.16) | collective-permute-done | bytes 294944 | tf_op jit(solution)/shard_map/ppermute | solution.py:581
  63.5 1.5 %collective-permute-start.18 = (bf16[32,4608]{1,0:T(8,128)(2,1)S(1)}, bf16[32,4608]{1,0:T(8,128)(2,1)S(1)}, u32[]{:S(2)}, u32[]{:S(2)}) collective-permute-start(bf16[32,4608]{1,0:T(8,128)(2,1)S(1)} %collective-permute-done.16.refs_1_), channel_id=1, source_target_pairs={{0,16},{16,0},{1,17},{17,1},{2,18},{18,2},{3,19},{19,3},{4,20},{20... | collective-permute-start | bytes 884744 | tf_op jit(solution)/shard_map/ppermute | solution.py:581
  65.1 4.5 %collective-permute-done.11 = bf16[384,256]{1,0:T(8,128)(2,1)S(1)} collective-permute-done((bf16[384,256]{1,0:T(8,128)(2,1)S(1)}, bf16[384,256]{1,0:T(8,128)(2,1)S(1)}, u32[]{:S(2)}, u32[]{:S(2)}) %collective-permute-start.11) | collective-permute-done | bytes 196640 | tf_op jit(solution)/shard_map/ppermute | solution.py:599
  69.6 5.5 %attention.5 = (f32[3,8,256]{2,1,0:T(8,128)S(1)}, f32[3,144,256]{2,1,0:T(8,128)S(1)}, f32[3,8,256]{2,1,0:T(8,128)S(1)}, f32[3,144,256]{2,1,0:T(8,128)S(1)}) custom-call(s32[10]{0:T(128)S(1)} %pad_add_fusion.1.table, bf16[2,384,128]{2,1,0:T(8,128)(2,1)S(1)} %get-tuple-element.46.refs_0_, ...), custom_call_target="tpu_custom_call", output_to_operand_aliasing={{0}: (8, {}), {1}: (9, {})} | custom-call | flops 1 | bytes 1 | tf_op jit(solution)/shard_map/attention/pallas_call | solution.py:38
  75.1 2.0 %collective-permute-done.14 = bf16[384,256]{1,0:T(8,128)(2,1)S(1)} collective-permute-done((bf16[384,256]{1,0:T(8,128)(2,1)S(1)}, bf16[384,256]{1,0:T(8,128)(2,1)S(1)}, u32[]{:S(2)}, u32[]{:S(2)}) %collective-permute-start.14) | collective-permute-done | bytes 196640 | tf_op jit(solution)/shard_map/ppermute | solution.py:599
  77.1 1.5 %collective-permute-start.19 = (bf16[48,4608]{1,0:T(8,128)(2,1)S(1)}, bf16[48,4608]{1,0:T(8,128)(2,1)S(1)}, u32[]{:S(2)}, u32[]{:S(2)}) collective-permute-start(bf16[48,4608]{1,0:T(8,128)(2,1)S(1)} %collective-permute-done.17.refs_2_), channel_id=1, source_target_pairs={{0,16},{16,0},{1,17},{17,1},{2,18},{18,2},{3,19},{19,3},{4,20},{20... | collective-permute-start | bytes 1327112 | tf_op jit(solution)/shard_map/ppermute | solution.py:581
  79.1 3.8 %attention.6 = (bf16[384,256]{1,0:T(8,128)(2,1)S(1)}, f32[3,8,256]{2,1,0:T(8,128)S(1)}, f32[3,144,256]{2,1,0:T(8,128)S(1)}) custom-call(s32[10]{0:T(128)S(1)} %pad_add_fusion.1.table, bf16[2,384,128]{2,1,0:T(8,128)(2,1)S(1)} %get-tuple-element.53.refs_1_.refs_0_, bf16[1,384,256]{2,1,0:T(8,128)(2,1)S(1)} %bitcast.15, ...), custom_call_target="tpu_custom_call", output_to_operand_aliasing={{1}: (6, {}), {2}: (7, {})} | custom-call | flops 1 | bytes 1 | tf_op jit(solution)/shard_map/attention/pallas_call | solution.py:38
  82.9 1.6 %collective-permute-start.15 = (bf16[384,256]{1,0:T(8,128)(2,1)S(1)}, bf16[384,256]{1,0:T(8,128)(2,1)S(1)}, u32[]{:S(2)}, u32[]{:S(2)}) collective-permute-start(bf16[384,256]{1,0:T(8,128)(2,1)S(1)} %get-tuple-element.60), channel_id=1, source_target_pairs={{0,8},{4,12},{8,0},{12,4},{1,9},{5,13},{9,1},{13,5},{2,10},{6,14},... | collective-permute-start | bytes 589832 | tf_op jit(solution)/shard_map/ppermute | solution.py:581
  84.5 3.8 %attention.7 = (bf16[384,256]{1,0:T(8,128)(2,1)S(1)}, f32[3,8,256]{2,1,0:T(8,128)S(1)}, f32[3,144,256]{2,1,0:T(8,128)S(1)}) custom-call(s32[10]{0:T(128)S(1)} %pad_add_fusion.1.table, bf16[2,384,128]{2,1,0:T(8,128)(2,1)S(1)} %get-tuple-element.46.refs_0_, bf16[1,384,256]{2,1,0:T(8,128)(2,1)S(1)} %bitcast.16, ...), custom_call_target="tpu_custom_call", output_to_operand_aliasing={{1}: (6, {}), {2}: (7, {})} | custom-call | flops 1 | bytes 1 | tf_op jit(solution)/shard_map/attention/pallas_call | solution.py:38
  88.3 3.3 %output_near.1.near = bf16[384,4608]{1,0:T(8,128)(2,1)S(1)} custom-call(bf16[384,256]{1,0:T(8,128)(2,1)S(1)} %get-tuple-element.63.left, bf16[256,4608]{1,0:T(8,128)(2,1)} %weights_hbm.1), custom_call_target="tpu_custom_call" | custom-call | flops 1 | bytes 1 | tf_op jit(solution)/shard_map/output_near/pallas_call | solution.py:38
  91.6 3.6 %output_send.1 = (bf16[192,4608]{1,0:T(8,128)(2,1)}, bf16[256,4608]{1,0:T(8,128)(2,1)S(1)}) custom-call(s32[10]{0:T(128)S(1)} %pad_add_fusion.1.table, bf16[384,256]{1,0:T(8,128)(2,1)S(1)} %collective-permute-done.15.left_hbm, bf16[384,4608]{1,0:T(8,128)(2,1)S(1)} %output_near.1.near, bf16[32,4608]{1,0:T(8,128)(2,1)S(1)} %collective-permute-done.12.refs_0_, ...), custom_call_target="tpu_custom_call" | custom-call | flops 1 | bytes 1 | tf_op jit(solution)/shard_map/output_send/pallas_call | solution.py:38
  95.3 1.7 %output_keep.1 = (f32[192,4608]{1,0:T(8,128)S(1)}, bf16[192,4608]{1,0:T(8,128)(2,1)S(1)}) custom-call(bf16[384,256]{1,0:T(8,128)(2,1)S(1)} %collective-permute-done.15.left_hbm, bf16[192,4608]{1,0:T(8,128)(2,1)} %hidden.5, bf16[384,4608]{1,0:T(8,128)(2,1)S(1)} %output_near.1.near, bf16[256,4608]{1,0:T(8,128)(2,1)S(1)} %get-tuple-element.70.weights), custom_call_target="tpu_custom_call" | custom-call | flops 1 | bytes 1 | tf_op jit(solution)/shard_map/output_keep/pallas_call | solution.py:38
  97.0 2.1 %collective-permute-done.21.received = bf16[192,4608]{1,0:T(8,128)(2,1)S(1)} collective-permute-done((bf16[192,4608]{1,0:T(8,128)(2,1)}, bf16[192,4608]{1,0:T(8,128)(2,1)S(1)}, u32[]{:S(2)}, u32[]{:S(2)}) %collective-permute-start.21) | collective-permute-done | bytes 1769504 | tf_op jit(solution)/shard_map/ppermute | solution.py:581
  99.1 2.6 %output_norm.1 = bf16[192,4608]{1,0:T(8,128)(2,1)} custom-call(bf16[192,4608]{1,0:T(8,128)(2,1)S(1)} %collective-permute-done.21.received, bf16[192,4608]{1,0:T(8,128)(2,1)S(1)} %get-tuple-element.71.hidden, f32[192,4608]{1,0:T(8,128)S(1)} %get-tuple-element.72.kept, f32[4608]{0:T(1024)} %gain.5), custom_call_target="tpu_custom_call" | custom-call | flops 1 | bytes 1 | tf_op jit(solution)/shard_map/output_norm/pallas_call | solution.py:38
  (48 shorter events, 6.4 us)
Async XLA Ops:
  2.3 5.7 %copy-start = (s32[8]{0:T(128)S(1)}, s32[8]{0:T(128)}, u32[]{:S(2)}) copy-start(s32[8]{0:T(128)} %param.15) | copy-start | bytes 100
  2.4 8.8 %collective-permute-start.2 = (bf16[96,4608]{1,0:T(8,128)(2,1)}, bf16[96,4608]{1,0:T(8,128)(2,1)S(1)}, u32[]{:S(2)}, u32[]{:S(2)}) collective-permute-start(bf16[96,4608]{1,0:T(8,128)(2,1)} %norm_rows.3.refs_0_), channel_id=1, source_target_pairs={{0,4},{4,0},{8,12},{12,8},{1,5},{5,1},{9,13},{13,9},{2,6},{6,2},{1... | collective-permute-start | bytes 2654216 | tf_op jit(solution)/shard_map/ppermute | solution.py:581
  2.9 38.3 %collective-permute-start.1 = (bf16[96,4608]{1,0:T(8,128)(2,1)}, bf16[96,4608]{1,0:T(8,128)(2,1)S(1)}, u32[]{:S(2)}, u32[]{:S(2)}) collective-permute-start(bf16[96,4608]{1,0:T(8,128)(2,1)} %norm_rows.3.refs_0_), channel_id=1, source_target_pairs={{0,8},{4,12},{8,0},{12,4},{1,9},{5,13},{9,1},{13,5},{2,10},{6,14},... | collective-permute-start | bytes 2654216 | tf_op jit(solution)/shard_map/ppermute | solution.py:581
  7.8 3.4 %collective-permute-start.3 = (bf16[96,4608]{1,0:T(8,128)(2,1)}, bf16[96,4608]{1,0:T(8,128)(2,1)S(1)}, u32[]{:S(2)}, u32[]{:S(2)}) collective-permute-start(bf16[96,4608]{1,0:T(8,128)(2,1)} %norm_rows.2.refs_1_), channel_id=1, source_target_pairs={{0,4},{4,0},{8,12},{12,8},{1,5},{5,1},{9,13},{13,9},{2,6},{6,2},{1... | collective-permute-start | bytes 2654216 | tf_op jit(solution)/shard_map/ppermute | solution.py:581
  16.0 9.0 %collective-permute-start.6 = (bf16[384,256]{1,0:T(8,128)(2,1)S(1)}, bf16[384,256]{1,0:T(8,128)(2,1)S(1)}, u32[]{:S(2)}, u32[]{:S(2)}) collective-permute-start(bf16[384,256]{1,0:T(8,128)(2,1)S(1)} %get-tuple-element.40), channel_id=1, source_target_pairs={{0,3},{1,0},{2,1},{3,2},{4,7},{5,4},{6,5},{7,6},{8,11},{9,8},{10,9... | collective-permute-start | bytes 589832 | tf_op jit(solution)/shard_map/ppermute | solution.py:588
  19.6 17.2 %collective-permute-start.5 = (bf16[384,256]{1,0:T(8,128)(2,1)S(1)}, bf16[384,256]{1,0:T(8,128)(2,1)S(1)}, u32[]{:S(2)}, u32[]{:S(2)}) collective-permute-start(bf16[384,256]{1,0:T(8,128)(2,1)S(1)} %get-tuple-element.40), channel_id=1, source_target_pairs={{0,2},{1,3},{2,0},{3,1},{4,6},{5,7},{6,4},{7,5},{8,10},{9,11},{10,... | collective-permute-start | bytes 589832 | tf_op jit(solution)/shard_map/ppermute | solution.py:588
  19.6 17.2 %collective-permute-start.4 = (bf16[384,256]{1,0:T(8,128)(2,1)S(1)}, bf16[384,256]{1,0:T(8,128)(2,1)S(1)}, u32[]{:S(2)}, u32[]{:S(2)}) collective-permute-start(bf16[384,256]{1,0:T(8,128)(2,1)S(1)} %get-tuple-element.40), channel_id=1, source_target_pairs={{0,1},{1,2},{2,3},{3,0},{4,5},{5,6},{6,7},{7,4},{8,9},{9,10},{10,1... | collective-permute-start | bytes 589832 | tf_op jit(solution)/shard_map/ppermute | solution.py:588
  20.6 26.5 %collective-permute-start = (bf16[96,4608]{1,0:T(8,128)(2,1)}, bf16[96,4608]{1,0:T(8,128)(2,1)S(1)}, u32[]{:S(2)}, u32[]{:S(2)}) collective-permute-start(bf16[96,4608]{1,0:T(8,128)(2,1)} %norm_rows.2.refs_1_), channel_id=1, source_target_pairs={{0,8},{4,12},{8,0},{12,4},{1,9},{5,13},{9,1},{13,5},{2,10},{6,14},... | collective-permute-start | bytes 2654216 | tf_op jit(solution)/shard_map/ppermute | solution.py:581
  41.2 1.9 %collective-permute-start.8 = (bf16[48,4608]{1,0:T(8,128)(2,1)S(1)}, bf16[48,4608]{1,0:T(8,128)(2,1)S(1)}, u32[]{:S(2)}, u32[]{:S(2)}) collective-permute-start(bf16[48,4608]{1,0:T(8,128)(2,1)S(1)} %get-tuple-element.75), channel_id=1, source_target_pairs={{0,4},{4,0},{8,12},{12,8},{1,5},{5,1},{9,13},{13,9},{2,6},{6,2},{1... | collective-permute-start | bytes 1327112 | tf_op jit(solution)/shard_map/ppermute | solution.py:581
  41.3 6.0 %copy-start.4 = (bf16[32,4608]{1,0:T(8,128)(2,1)S(1)}, bf16[32,4608]{1,0:T(8,128)(2,1)}, u32[]{:S(2)}) copy-start(bf16[32,4608]{1,0:T(8,128)(2,1)} %get-tuple-element.55) | copy-start | bytes 884740
  41.3 6.5 %copy-start.3 = (bf16[32,4608]{1,0:T(8,128)(2,1)S(1)}, bf16[32,4608]{1,0:T(8,128)(2,1)}, u32[]{:S(2)}) copy-start(bf16[32,4608]{1,0:T(8,128)(2,1)} %get-tuple-element.64) | copy-start | bytes 884740
  41.3 2.4 %collective-permute-start.7 = (bf16[48,4608]{1,0:T(8,128)(2,1)S(1)}, bf16[48,4608]{1,0:T(8,128)(2,1)S(1)}, u32[]{:S(2)}, u32[]{:S(2)}) collective-permute-start(bf16[48,4608]{1,0:T(8,128)(2,1)S(1)} %get-tuple-element.76), channel_id=1, source_target_pairs={{0,4},{4,0},{8,12},{12,8},{1,5},{5,1},{9,13},{13,9},{2,6},{6,2},{1... | collective-permute-start | bytes 1327112 | tf_op jit(solution)/shard_map/ppermute | solution.py:581
  47.1 11.6 %copy-start.1 = (bf16[48,4608]{1,0:T(8,128)(2,1)S(1)}, bf16[48,4608]{1,0:T(8,128)(2,1)}, u32[]{:S(2)}) copy-start(bf16[48,4608]{1,0:T(8,128)(2,1)} %get-tuple-element.66) | copy-start | bytes 1327108
  47.1 2.5 %collective-permute-start.9 = (bf16[96,4608]{1,0:T(8,128)(2,1)S(1)}, bf16[96,4608]{1,0:T(8,128)(2,1)S(1)}, u32[]{:S(2)}, u32[]{:S(2)}) collective-permute-start(bf16[96,4608]{1,0:T(8,128)(2,1)S(1)} %collective-permute-done.refs_0_), channel_id=1, source_target_pairs={{0,4},{4,0},{8,12},{12,8},{1,5},{5,1},{9,13},{13,9},{2,6},{6,2},{1... | collective-permute-start | bytes 2654216 | tf_op jit(solution)/shard_map/ppermute | solution.py:581
  47.3 9.8 %collective-permute-start.12 = (bf16[32,4608]{1,0:T(8,128)(2,1)S(1)}, bf16[32,4608]{1,0:T(8,128)(2,1)S(1)}, u32[]{:S(2)}, u32[]{:S(2)}) collective-permute-start(bf16[32,4608]{1,0:T(8,128)(2,1)S(1)} %copy-done.4), channel_id=1, source_target_pairs={{0,8},{4,12},{8,0},{12,4},{1,9},{5,13},{9,1},{13,5},{2,10},{6,14},... | collective-permute-start | bytes 884744 | tf_op jit(solution)/shard_map/ppermute | solution.py:581
  47.8 15.6 %collective-permute-start.16 = (bf16[32,4608]{1,0:T(8,128)(2,1)S(1)}, bf16[32,4608]{1,0:T(8,128)(2,1)S(1)}, u32[]{:S(2)}, u32[]{:S(2)}) collective-permute-start(bf16[32,4608]{1,0:T(8,128)(2,1)S(1)} %copy-done.3), channel_id=1, source_target_pairs={{0,8},{4,12},{8,0},{12,4},{1,9},{5,13},{9,1},{13,5},{2,10},{6,14},... | collective-permute-start | bytes 884744 | tf_op jit(solution)/shard_map/ppermute | solution.py:581
  52.9 25.7 %copy-start.2 = (bf16[32,4608]{1,0:T(8,128)(2,1)S(1)}, bf16[32,4608]{1,0:T(8,128)(2,1)}, u32[]{:S(2)}) copy-start(bf16[32,4608]{1,0:T(8,128)(2,1)} %get-tuple-element.68) | copy-start | bytes 884740
  52.9 8.8 %collective-permute-start.10 = (bf16[384,256]{1,0:T(8,128)(2,1)S(1)}, bf16[384,256]{1,0:T(8,128)(2,1)S(1)}, u32[]{:S(2)}, u32[]{:S(2)}) collective-permute-start(bf16[384,256]{1,0:T(8,128)(2,1)S(1)} %get-tuple-element.54), channel_id=1, source_target_pairs={{0,1},{1,2},{2,3},{3,0},{4,5},{5,6},{6,7},{7,4},{8,9},{9,10},{10,1... | collective-permute-start | bytes 589832 | tf_op jit(solution)/shard_map/ppermute | solution.py:599
  57.1 7.9 %collective-permute-start.13 = (bf16[32,4608]{1,0:T(8,128)(2,1)S(1)}, bf16[32,4608]{1,0:T(8,128)(2,1)S(1)}, u32[]{:S(2)}, u32[]{:S(2)}) collective-permute-start(bf16[32,4608]{1,0:T(8,128)(2,1)S(1)} %collective-permute-done.12.refs_0_), channel_id=1, source_target_pairs={{0,16},{16,0},{1,17},{17,1},{2,18},{18,2},{3,19},{19,3},{4,20},{20... | collective-permute-start | bytes 884744 | tf_op jit(solution)/shard_map/ppermute | solution.py:581
  58.6 16.4 %collective-permute-start.17 = (bf16[48,4608]{1,0:T(8,128)(2,1)S(1)}, bf16[48,4608]{1,0:T(8,128)(2,1)S(1)}, u32[]{:S(2)}, u32[]{:S(2)}) collective-permute-start(bf16[48,4608]{1,0:T(8,128)(2,1)S(1)} %copy-done.1), channel_id=1, source_target_pairs={{0,8},{4,12},{8,0},{12,4},{1,9},{5,13},{9,1},{13,5},{2,10},{6,14},... | collective-permute-start | bytes 1327112 | tf_op jit(solution)/shard_map/ppermute | solution.py:581
  61.7 7.9 %collective-permute-start.11 = (bf16[384,256]{1,0:T(8,128)(2,1)S(1)}, bf16[384,256]{1,0:T(8,128)(2,1)S(1)}, u32[]{:S(2)}, u32[]{:S(2)}) collective-permute-start(bf16[384,256]{1,0:T(8,128)(2,1)S(1)} %collective-permute-done.10), channel_id=1, source_target_pairs={{0,1},{1,2},{2,3},{3,0},{4,5},{5,6},{6,7},{7,4},{8,9},{9,10},{10,1... | collective-permute-start | bytes 589832 | tf_op jit(solution)/shard_map/ppermute | solution.py:599
  63.5 11.6 %collective-permute-start.18 = (bf16[32,4608]{1,0:T(8,128)(2,1)S(1)}, bf16[32,4608]{1,0:T(8,128)(2,1)S(1)}, u32[]{:S(2)}, u32[]{:S(2)}) collective-permute-start(bf16[32,4608]{1,0:T(8,128)(2,1)S(1)} %collective-permute-done.16.refs_1_), channel_id=1, source_target_pairs={{0,16},{16,0},{1,17},{17,1},{2,18},{18,2},{3,19},{19,3},{4,20},{20... | collective-permute-start | bytes 884744 | tf_op jit(solution)/shard_map/ppermute | solution.py:581
  69.6 7.5 %collective-permute-start.14 = (bf16[384,256]{1,0:T(8,128)(2,1)S(1)}, bf16[384,256]{1,0:T(8,128)(2,1)S(1)}, u32[]{:S(2)}, u32[]{:S(2)}) collective-permute-start(bf16[384,256]{1,0:T(8,128)(2,1)S(1)} %collective-permute-done.11), channel_id=1, source_target_pairs={{0,1},{1,2},{2,3},{3,0},{4,5},{5,6},{6,7},{7,4},{8,9},{9,10},{10,1... | collective-permute-start | bytes 589832 | tf_op jit(solution)/shard_map/ppermute | solution.py:599
  77.1 14.5 %collective-permute-start.19 = (bf16[48,4608]{1,0:T(8,128)(2,1)S(1)}, bf16[48,4608]{1,0:T(8,128)(2,1)S(1)}, u32[]{:S(2)}, u32[]{:S(2)}) collective-permute-start(bf16[48,4608]{1,0:T(8,128)(2,1)S(1)} %collective-permute-done.17.refs_2_), channel_id=1, source_target_pairs={{0,16},{16,0},{1,17},{17,1},{2,18},{18,2},{3,19},{19,3},{4,20},{20... | collective-permute-start | bytes 1327112 | tf_op jit(solution)/shard_map/ppermute | solution.py:581
  78.6 13.0 %collective-permute-start.20 = (bf16[32,4608]{1,0:T(8,128)(2,1)S(1)}, bf16[32,4608]{1,0:T(8,128)(2,1)S(1)}, u32[]{:S(2)}, u32[]{:S(2)}) collective-permute-start(bf16[32,4608]{1,0:T(8,128)(2,1)S(1)} %copy-done.2), channel_id=1, source_target_pairs={{0,8},{4,12},{8,0},{12,4},{1,9},{5,13},{9,1},{13,5},{2,10},{6,14},... | collective-permute-start | bytes 884744 | tf_op jit(solution)/shard_map/ppermute | solution.py:581
  82.9 8.7 %collective-permute-start.15 = (bf16[384,256]{1,0:T(8,128)(2,1)S(1)}, bf16[384,256]{1,0:T(8,128)(2,1)S(1)}, u32[]{:S(2)}, u32[]{:S(2)}) collective-permute-start(bf16[384,256]{1,0:T(8,128)(2,1)S(1)} %get-tuple-element.60), channel_id=1, source_target_pairs={{0,8},{4,12},{8,0},{12,4},{1,9},{5,13},{9,1},{13,5},{2,10},{6,14},... | collective-permute-start | bytes 589832 | tf_op jit(solution)/shard_map/ppermute | solution.py:581
  95.2 4.0 %collective-permute-start.21 = (bf16[192,4608]{1,0:T(8,128)(2,1)}, bf16[192,4608]{1,0:T(8,128)(2,1)S(1)}, u32[]{:S(2)}, u32[]{:S(2)}) collective-permute-start(bf16[192,4608]{1,0:T(8,128)(2,1)} %get-tuple-element.69), channel_id=1, source_target_pairs={{0,4},{4,0},{8,12},{12,8},{1,5},{5,1},{9,13},{13,9},{2,6},{6,2},{1... | collective-permute-start | bytes 5308424 | tf_op jit(solution)/shard_map/ppermute | solution.py:581

commit v10 on v9

--- a/solution.py
+++ b/solution.py
@@ -403,82 +403,94 @@
     )
 
 
-def near_kernel(chunks, left, weights_hbm, out, weights, semaphores):
+def near_kernel(at, sizes, chunks, table, left, own_hbm, *refs):
+    pieces, (out, laid, weights, semaphores) = refs[:-4], refs[-4:]
     copies = Copies(semaphores)
     step = out.shape[1] // chunks
     lanes = [pl.ds(chunk * step, step) for chunk in range(chunks)]
-    waits = [copies.start(weights_hbm.at[:, at], weights.at[:, at]) for at in lanes]
-    for at, copy in zip(lanes, waits):
-        copy.wait()
-        out[:, at] = jnp.dot(
-            left[...], weights[:, at], preferred_element_type=jnp.float32
+    waits = [copies.start(own_hbm.at[:, span], weights.at[:, span]) for span in lanes]
+    half, put, late = laid.shape[0] // 2, 0, []
+    for index, size in enumerate(sizes):
+        for piece, side in ((index, table[at]), (len(sizes) + index, 1 - table[at])):
+            if piece < len(pieces):
+                row = pl.multiple_of(side * half + put, 16)
+                late.append(copies.start(pieces[piece], laid.at[pl.ds(row, size)]))
+        put += size
+    for span, copy in zip(lanes, waits):
+        copy.wait()
+        out[:, span] = jnp.dot(
+            left[...], weights[:, span], preferred_element_type=jnp.float32
         ).astype(jnp.bfloat16)
-
-
-def output_near(left, weights, chunks=6):
+    for copy in late:
+        copy.wait()
+
+
+def output_near(table, at, left, weights, sizes, pieces, chunks=6):
     rows, width = left.shape[0], weights.shape[1]
     return call(
-        functools.partial(near_kernel, chunks),
+        functools.partial(near_kernel, at, sizes, chunks),
         "output_near",
         8,
-        [VMEM, HBM],
-        [((rows, width), jnp.bfloat16, VMEM)],
-        [pltpu.VMEM(weights.shape, weights.dtype), pltpu.SemaphoreType.DMA((chunks,))],
+        [SMEM, VMEM, HBM] + [HBM] * len(pieces),
+        [((rows, width), jnp.bfloat16, VMEM), (weights.shape, weights.dtype, VMEM)],
+        [
+            pltpu.VMEM(weights.shape, weights.dtype),
+            pltpu.SemaphoreType.DMA((chunks + len(pieces),)),
+        ],
+        table,
         left,
         weights,
-    )[0]
-
-
-def send_kernel(at, splits, chunks, table, left_hbm, near, *refs):
-    pieces, refs = refs[: 2 * splits + 1], refs[2 * splits + 1 :]
+        *pieces,
+    )
+
+
+def send_kernel(at, sizes, chunks, table, left_hbm, near, last, both, held, *refs):
     out, weights, left, staged, semaphores = refs
     copies = Copies(semaphores)
     depth, width = weights.shape
-    half, step = depth // 2, width // chunks
-    first = copies.start(left_hbm, left)
-    waits, put = [], 0
-    for own, other in zip(pieces[:splits], pieces[splits:-1]):
-        for piece, side in ((own, table[at]), (other, 1 - table[at])):
-            row = pl.multiple_of(side * half + put, 16)
-            waits.append(copies.start(piece, weights.at[pl.ds(row, piece.shape[0])]))
-        put += own.shape[0]
+    half, step, put = depth // 2, width // chunks, sum(sizes)
+    waits = [copies.start(left_hbm, left)]
+    row = pl.multiple_of((1 - table[at]) * half + put - sizes[-1], 16)
+    waits.append(copies.start(last, weights.at[pl.ds(row, sizes[-1])]))
     for side in range(2):
-        source = pieces[-1].at[pl.ds(side * (half - put), half - put)]
+        source = both.at[pl.ds(side * (half - put), half - put)]
         waits.append(copies.start(source, weights.at[pl.ds(side * half + put, half - put)]))
     for copy in waits:
         copy.wait()
-    first.wait()
-    half = left.shape[0] // 2
+    begin = left.shape[0] // 2
     stores = []
     for chunk in range(chunks):
         span = pl.ds(chunk * step, step)
         staged[:, span] = (
-            near[half:, span].astype(jnp.float32)
-            + jnp.dot(left[half:, :], weights[:, span], preferred_element_type=jnp.float32)
+            near[begin:, span].astype(jnp.float32)
+            + jnp.dot(left[begin:, :], weights[:, span], preferred_element_type=jnp.float32)
         ).astype(jnp.bfloat16)
         stores.append(copies.start(staged.at[:, span], out.at[:, span]))
     for copy in stores:
         copy.wait()
 
 
-def output_send(table, at, left, near, pieces, chunks=6):
-    (rows, width), columns = near.shape, left.shape[1]
-    half, bf16 = (rows // 2, width), jnp.bfloat16
+def output_send(table, at, left, near, laid, sizes, last, both, chunks=6):
+    (rows, width), bf16 = near.shape, jnp.bfloat16
+    part = (rows // 2, width)
     return call(
-        functools.partial(send_kernel, at, len(pieces) // 2, chunks),
+        functools.partial(send_kernel, at, sizes, chunks),
         "output_send",
         8,
-        [SMEM, HBM, VMEM] + [HBM] * len(pieces),
-        [(half, bf16, HBM), ((columns, width), bf16, VMEM)],
+        [SMEM, HBM, VMEM, HBM, HBM, VMEM],
+        [(part, bf16, HBM), (laid.shape, bf16, VMEM)],
         [
             pltpu.VMEM(left.shape, bf16),
-            pltpu.VMEM(half, bf16),
-            pltpu.SemaphoreType.DMA((2 + len(pieces) + chunks,)),
+            pltpu.VMEM(part, bf16),
+            pltpu.SemaphoreType.DMA((4 + chunks,)),
         ],
         table,
         left,
         near,
-        *pieces,
+        last,
+        both,
+        laid,
+        aliases={5: 1},
     )
 
 
@@ -590,12 +602,14 @@
     return parts
 
 
-def along_ring(array, beside):
+def along_ring(array, second, last):
     size = lax.axis_size("seq")
     parts, part = [array[None]], array
     for step in range(1, size):
+        if step == 2:
+            part = after(part, second)
         if step == size - 1:
-            part = after(part, beside)
+            part = after(part, last)
         part = lax.ppermute(part, "seq", [(i, (i + 1) % size) for i in range(size)])
         parts.append(Came(part[None]))
     return parts
@@ -673,7 +687,7 @@
     w_far = [fetched(piece, away[1]) for piece in w_cut[:2]]
     w_far[0] = after(w_far[0], kv_far)
     w_other = [swap(w_far[0])]
-    far = along_ring(kv_far, w_other[0])
+    far = along_ring(kv_far, w_far[1], w_other[0])
     w_far[1] = after(w_far[1], came(far)[0])
     w_far += [fetched(piece, before) for piece, before in zip(w_cut[2:], w_far[:2])]
     w_other.append(swap(w_far[1]))
@@ -697,9 +711,12 @@
     (attended,) = attention(
         rest, table, [q_near], [near_chunk], [far], [far_chunk], [near_state], final=[[0]]
     )
-    near_sum = output_near(attended, w_out)
-    pieces = [Came(piece) for piece in w_far[:3] + w_other + w_far[3:]]
-    sent, w_laid = output_send(table, group_at, Came(gone), near_sum, pieces)
+    arrived = [Came(piece) for piece in w_far[:3] + w_other[:2]]
+    near_sum, w_laid = output_near(table, group_at, attended, w_out, sizes, arrived)
+    last, both = Came(w_other[2]), Came(w_far[3])
+    sent, w_laid = output_send(
+        table, group_at, Came(gone), near_sum, w_laid, sizes, last, both
+    )
     received = flipped(sent, "tp", 1)
     kept, held = output_keep(Came(gone), hidden, near_sum, w_laid)
     return output(Came(received), held, kept, post_gain)

time: 101 us -> 103 us (1.020); the launches traced: 102 us -> 102 us
  waiting for transfers between devices: 32.1 us -> 33.8 us
  Pallas kernels: 47.3 us -> 46 us
    ppermute x16, waiting for transfers between devices: 10.1 us -> 12.9 us  [flipped(): return lax.ppermute(array, axis, [(i, i ^ bit) for i in range(size)])]
    pallas_call x14, Pallas kernels: 47.3 us -> 46 us  [call(): pl.pallas_call(kernel, in_specs=in_specs, out_specs=[spec for _, _, spec...]
    ppermute x3, waiting for transfers between devices: 9.09 us -> 8 us  [along_ring(): part = lax.ppermute(part, 'seq', [(i, (i + 1) % size) for i in range(size)])]
  transfers between devices with their start and end apart: 22 -> 22, of which waited for: 12 -> 11; matrix products, arithmetic and copies ran while one was open for 3% -> 3% of each run, Pallas kernels for 38% -> 37%
where the time goes in v10:
time: 103 us; the launch traced here: 102 us
  Pallas kernels  46 us (45%)
  waiting for transfers between devices  33.8 us (33%)
  starting transfers between devices  18.5 us (18%)
  other arithmetic  3.16 us (3%)
    pallas_call x14, Pallas kernels, call(): pl.pallas_call(kernel, in_specs=in_specs, out_specs=[spec for _, _, spec...  46 us
    ppermute x16, starting transfers between devices, flipped(): return lax.ppermute(array, axis, [(i, i ^ bit) for i in range(size)])  13.8 us
    ppermute x3, waiting for transfers between devices, along_line(): lax.ppermute(array, 'seq', [(i, (i + by) % size) for i in range(size)])  12.9 us
    ppermute x16, waiting for transfers between devices, flipped(): return lax.ppermute(array, axis, [(i, i ^ bit) for i in range(size)])  12.9 us
    ppermute x3, waiting for transfers between devices, along_ring(): part = lax.ppermute(part, 'seq', [(i, (i + 1) % size) for i in range(size)])  8 us
    ppermute x3, starting transfers between devices, along_line(): lax.ppermute(array, 'seq', [(i, (i + by) % size) for i in range(size)])  4.67 us
  transfers between devices with their start and end apart: 22, of which 11 were waited for; matrix products, arithmetic and copies ran while one was open for 3% of the time, Pallas kernels for 37%

profile of v10, /device:TPU:0, one launch (start us, length us, event | category | flops | bytes accessed | tf_op | source)
XLA Modules:
  0.0 102.0 jit_solution(15878524073146384351)
XLA Ops:
  0.0 2.3 %norm_rows.3.refs_0_ = bf16[96,4608]{1,0:T(8,128)(2,1)} custom-call(bf16[192,4608]{1,0:T(8,128)(2,1)} %hidden.5, f32[4608]{0:T(1024)} %gain.4), custom_call_target="tpu_custom_call" | custom-call | flops 1 | bytes 1 | tf_op jit(solution)/shard_map/norm_rows/pallas_call | solution.py:38
  2.9 2.6 %collective-permute-start.1 = (bf16[96,4608]{1,0:T(8,128)(2,1)}, bf16[96,4608]{1,0:T(8,128)(2,1)S(1)}, u32[]{:S(2)}, u32[]{:S(2)}) collective-permute-start(bf16[96,4608]{1,0:T(8,128)(2,1)} %norm_rows.3.refs_0_), channel_id=1, source_target_pairs={{0,8},{4,12},{8,0},{12,4},{1,9},{5,13},{9,1},{13,5},{2,10},{6,14},... | collective-permute-start | bytes 2654216 | tf_op jit(solution)/shard_map/ppermute | solution.py:593
  5.5 2.3 %norm_rows.2.refs_1_ = bf16[96,4608]{1,0:T(8,128)(2,1)} custom-call(bf16[192,4608]{1,0:T(8,128)(2,1)} %hidden.5, f32[4608]{0:T(1024)} %gain.4), custom_call_target="tpu_custom_call" | custom-call | flops 1 | bytes 1 | tf_op jit(solution)/shard_map/norm_rows/pallas_call | solution.py:38
  8.5 1.4 %multiply_cosine_fusion = (f32[768,64]{1,0:T(8,128)S(1)}, f32[768,64]{1,0:T(8,128)S(1)}, f32[768,64]{1,0:T(8,128)S(1)}) fusion(f32[768]{0:T(1024)S(1)} %add_convert_fusion, f32[64]{0:T(128)S(1)} %multiply_power_fusion), kind=kLoop, calls=%fused_computation.2 | loop fusion | flops 98304 | bytes 593152 | tf_op jit(solution)/shard_map/cos | solution.py:582
  9.9 1.3 %pad_maximum_fusion.trig = f32[768,256]{1,0:T(8,128)} fusion(f32[768,64]{1,0:T(8,128)S(1)} %get-tuple-element.85, f32[768,64]{1,0:T(8,128)S(1)} %get-tuple-element.84, f32[768,64]{1,0:T(8,128)S(1)} %get-tuple-element.83), kind=kLoop, calls=%fused_computation | loop fusion | flops 589824 | bytes 1376256 | tf_op jit(solution)/shard_map/concatenate | solution.py:583
  11.2 4.8 %qkv.3 = (bf16[2,384,128]{2,1,0:T(8,128)(2,1)S(1)}, bf16[384,256]{1,0:T(8,128)(2,1)S(1)}) custom-call(f32[768,256]{1,0:T(8,128)} %pad_maximum_fusion.trig, bf16[4608,256]{1,0:T(8,128)(2,1)} %wq.5, bf16[4608,128]{1,0:T(8,128)(2,1)} %wk.5, bf16[4608,128]{1,0:T(8,128)(2,1)} %wv.5, bf16[96,4608]{1,0:T(8,128)(2,1)} %norm_rows.3.refs_0_, ...), custom_call_target="tpu_custom_call" | custom-call | flops 1 | bytes 1 | tf_op jit(solution)/shard_map/qkv/pallas_call | solution.py:38
  16.0 3.7 %collective-permute-start.6 = (bf16[384,256]{1,0:T(8,128)(2,1)S(1)}, bf16[384,256]{1,0:T(8,128)(2,1)S(1)}, u32[]{:S(2)}, u32[]{:S(2)}) collective-permute-start(bf16[384,256]{1,0:T(8,128)(2,1)S(1)} %get-tuple-element.43), channel_id=1, source_target_pairs={{0,3},{1,0},{2,1},{3,2},{4,7},{5,4},{6,5},{7,6},{8,11},{9,8},{10,9... | collective-permute-start | bytes 589832 | tf_op jit(solution)/shard_map/ppermute | solution.py:600
  19.6 1.0 collective-permute-start.4
  21.2 2.7 %cut_weights.1 = (bf16[32,4608]{1,0:T(8,128)(2,1)}, bf16[32,4608]{1,0:T(8,128)(2,1)}, bf16[48,4608]{1,0:T(8,128)(2,1)}, bf16[32,4608]{1,0:T(8,128)(2,1)}) custom-call(s32[10]{0:T(128)S(1)} %pad_add_fusion.1.table, bf16[256,4608]{1,0:T(8,128)(2,1)} %own_hbm.1), custom_call_target="tpu_custom_call" | custom-call | flops 1 | bytes 1 | tf_op jit(solution)/shard_map/cut_weights/pallas_call | solution.py:38
  23.9 1.0 %collective-permute-done.6 = bf16[384,256]{1,0:T(8,128)(2,1)S(1)} collective-permute-done((bf16[384,256]{1,0:T(8,128)(2,1)S(1)}, bf16[384,256]{1,0:T(8,128)(2,1)S(1)}, u32[]{:S(2)}, u32[]{:S(2)}) %collective-permute-start.6) | collective-permute-done | bytes 196640 | tf_op jit(solution)/shard_map/ppermute | solution.py:600
  25.0 11.9 %collective-permute-done.5 = bf16[384,256]{1,0:T(8,128)(2,1)S(1)} collective-permute-done((bf16[384,256]{1,0:T(8,128)(2,1)S(1)}, bf16[384,256]{1,0:T(8,128)(2,1)S(1)}, u32[]{:S(2)}, u32[]{:S(2)}) %collective-permute-start.5) | collective-permute-done | bytes 196640 | tf_op jit(solution)/shard_map/ppermute | solution.py:600
  36.8 4.3 %attention.4 = (f32[3,8,256]{2,1,0:T(8,128)S(1)}, f32[3,144,256]{2,1,0:T(8,128)S(1)}) custom-call(s32[10]{0:T(128)S(1)} %pad_add_fusion.1.table, bf16[2,384,128]{2,1,0:T(8,128)(2,1)S(1)} %get-tuple-element.49.refs_0_, bf16[1,384,256]{2,1,0:T(8,128)(2,1)S(1)} %bitcast.17, bf16[1,384,256]{2,1,0:T(8,128)(2,1)S(1)} %bitcast.23, ...), custom_call_target="tpu_custom_call" | custom-call | flops 1 | bytes 1 | tf_op jit(solution)/shard_map/attention/pallas_call | solution.py:38
  41.8 1.3 %collective-permute-done.8.refs_2_ = bf16[48,4608]{1,0:T(8,128)(2,1)S(1)} collective-permute-done((bf16[48,4608]{1,0:T(8,128)(2,1)S(1)}, bf16[48,4608]{1,0:T(8,128)(2,1)S(1)}, u32[]{:S(2)}, u32[]{:S(2)}) %collective-permute-start.8) | collective-permute-done | bytes 442400 | tf_op jit(solution)/shard_map/ppermute | solution.py:593
  43.7 3.4 %qkv.4 = (bf16[2,384,128]{2,1,0:T(8,128)(2,1)S(1)}, bf16[384,256]{1,0:T(8,128)(2,1)S(1)}) custom-call(f32[768,256]{1,0:T(8,128)} %pad_maximum_fusion.trig, bf16[4608,256]{1,0:T(8,128)(2,1)} %wq.5, bf16[4608,128]{1,0:T(8,128)(2,1)} %wk.5, bf16[4608,128]{1,0:T(8,128)(2,1)} %wv.5, bf16[96,4608]{1,0:T(8,128)(2,1)S(1)} %collective-permute-done.1.refs_0_, ...), custom_call_target="tpu_custom_call" | custom-call | flops 1 | bytes 1 | tf_op jit(solution)/shard_map/qkv/pallas_call | solution.py:38
  47.9 1.5 %collective-permute-start.11 = (bf16[32,4608]{1,0:T(8,128)(2,1)S(1)}, bf16[32,4608]{1,0:T(8,128)(2,1)S(1)}, u32[]{:S(2)}, u32[]{:S(2)}) collective-permute-start(bf16[32,4608]{1,0:T(8,128)(2,1)S(1)} %copy-done.3), channel_id=1, source_target_pairs={{0,8},{4,12},{8,0},{12,4},{1,9},{5,13},{9,1},{13,5},{2,10},{6,14},... | collective-permute-start | bytes 884744 | tf_op jit(solution)/shard_map/ppermute | solution.py:593
  49.6 3.3 %qkv.5 = (bf16[2,384,128]{2,1,0:T(8,128)(2,1)S(1)}, bf16[384,256]{1,0:T(8,128)(2,1)S(1)}) custom-call(f32[768,256]{1,0:T(8,128)} %pad_maximum_fusion.trig, bf16[4608,256]{1,0:T(8,128)(2,1)} %wq.5, bf16[4608,128]{1,0:T(8,128)(2,1)} %wk.5, bf16[4608,128]{1,0:T(8,128)(2,1)} %wv.5, ...), custom_call_target="tpu_custom_call", output_to_operand_aliasing={{0}: (6, {}), {1}: (7, {})} | custom-call | flops 1 | bytes 1 | tf_op jit(solution)/shard_map/qkv/pallas_call | solution.py:38
  53.0 4.2 %collective-permute-done.13.refs_0_ = bf16[32,4608]{1,0:T(8,128)(2,1)S(1)} collective-permute-done((bf16[32,4608]{1,0:T(8,128)(2,1)S(1)}, bf16[32,4608]{1,0:T(8,128)(2,1)S(1)}, u32[]{:S(2)}, u32[]{:S(2)}) %collective-permute-start.13) | collective-permute-done | bytes 294944 | tf_op jit(solution)/shard_map/ppermute | solution.py:593
  57.2 1.5 %collective-permute-start.14 = (bf16[32,4608]{1,0:T(8,128)(2,1)S(1)}, bf16[32,4608]{1,0:T(8,128)(2,1)S(1)}, u32[]{:S(2)}, u32[]{:S(2)}) collective-permute-start(bf16[32,4608]{1,0:T(8,128)(2,1)S(1)} %collective-permute-done.13.refs_0_), channel_id=1, source_target_pairs={{0,16},{16,0},{1,17},{17,1},{2,18},{18,2},{3,19},{19,3},{4,20},{20... | collective-permute-start | bytes 884744 | tf_op jit(solution)/shard_map/ppermute | solution.py:593
  59.2 4.3 %collective-permute-done.11.refs_1_ = bf16[32,4608]{1,0:T(8,128)(2,1)S(1)} collective-permute-done((bf16[32,4608]{1,0:T(8,128)(2,1)S(1)}, bf16[32,4608]{1,0:T(8,128)(2,1)S(1)}, u32[]{:S(2)}, u32[]{:S(2)}) %collective-permute-start.11) | collective-permute-done | bytes 294944 | tf_op jit(solution)/shard_map/ppermute | solution.py:593
  63.5 1.5 %collective-permute-start.18 = (bf16[32,4608]{1,0:T(8,128)(2,1)S(1)}, bf16[32,4608]{1,0:T(8,128)(2,1)S(1)}, u32[]{:S(2)}, u32[]{:S(2)}) collective-permute-start(bf16[32,4608]{1,0:T(8,128)(2,1)S(1)} %collective-permute-done.11.refs_1_), channel_id=1, source_target_pairs={{0,16},{16,0},{1,17},{17,1},{2,18},{18,2},{3,19},{19,3},{4,20},{20... | collective-permute-start | bytes 884744 | tf_op jit(solution)/shard_map/ppermute | solution.py:593
  65.1 6.0 %collective-permute-done.12 = bf16[384,256]{1,0:T(8,128)(2,1)S(1)} collective-permute-done((bf16[384,256]{1,0:T(8,128)(2,1)S(1)}, bf16[384,256]{1,0:T(8,128)(2,1)S(1)}, u32[]{:S(2)}, u32[]{:S(2)}) %collective-permute-start.12) | collective-permute-done | bytes 196640 | tf_op jit(solution)/shard_map/ppermute | solution.py:613
  71.1 5.5 %attention.5 = (f32[3,8,256]{2,1,0:T(8,128)S(1)}, f32[3,144,256]{2,1,0:T(8,128)S(1)}, f32[3,8,256]{2,1,0:T(8,128)S(1)}, f32[3,144,256]{2,1,0:T(8,128)S(1)}) custom-call(s32[10]{0:T(128)S(1)} %pad_add_fusion.1.table, bf16[2,384,128]{2,1,0:T(8,128)(2,1)S(1)} %get-tuple-element.49.refs_0_, ...), custom_call_target="tpu_custom_call", output_to_operand_aliasing={{0}: (8, {}), {1}: (9, {})} | custom-call | flops 1 | bytes 1 | tf_op jit(solution)/shard_map/attention/pallas_call | solution.py:38
  76.6 2.0 %collective-permute-done.15 = bf16[384,256]{1,0:T(8,128)(2,1)S(1)} collective-permute-done((bf16[384,256]{1,0:T(8,128)(2,1)S(1)}, bf16[384,256]{1,0:T(8,128)(2,1)S(1)}, u32[]{:S(2)}, u32[]{:S(2)}) %collective-permute-start.15) | collective-permute-done | bytes 196640 | tf_op jit(solution)/shard_map/ppermute | solution.py:613
  78.6 1.5 %collective-permute-start.19 = (bf16[48,4608]{1,0:T(8,128)(2,1)S(1)}, bf16[48,4608]{1,0:T(8,128)(2,1)S(1)}, u32[]{:S(2)}, u32[]{:S(2)}) collective-permute-start(bf16[48,4608]{1,0:T(8,128)(2,1)S(1)} %collective-permute-done.17.refs_2_), channel_id=1, source_target_pairs={{0,16},{16,0},{1,17},{17,1},{2,18},{18,2},{3,19},{19,3},{4,20},{20... | collective-permute-start | bytes 1327112 | tf_op jit(solution)/shard_map/ppermute | solution.py:593
  80.6 3.8 %attention.6 = (bf16[384,256]{1,0:T(8,128)(2,1)S(1)}, f32[3,8,256]{2,1,0:T(8,128)S(1)}, f32[3,144,256]{2,1,0:T(8,128)S(1)}) custom-call(s32[10]{0:T(128)S(1)} %pad_add_fusion.1.table, bf16[2,384,128]{2,1,0:T(8,128)(2,1)S(1)} %get-tuple-element.56.refs_1_.refs_0_, bf16[1,384,256]{2,1,0:T(8,128)(2,1)S(1)} %bitcast.15, ...), custom_call_target="tpu_custom_call", output_to_operand_aliasing={{1}: (6, {}), {2}: (7, {})} | custom-call | flops 1 | bytes 1 | tf_op jit(solution)/shard_map/attention/pallas_call | solution.py:38
  84.4 1.6 %collective-permute-start.16 = (bf16[384,256]{1,0:T(8,128)(2,1)S(1)}, bf16[384,256]{1,0:T(8,128)(2,1)S(1)}, u32[]{:S(2)}, u32[]{:S(2)}) collective-permute-start(bf16[384,256]{1,0:T(8,128)(2,1)S(1)} %get-tuple-element.65), channel_id=1, source_target_pairs={{0,8},{4,12},{8,0},{12,4},{1,9},{5,13},{9,1},{13,5},{2,10},{6,14},... | collective-permute-start | bytes 589832 | tf_op jit(solution)/shard_map/ppermute | solution.py:593
  86.0 2.4 %attention.7 = (bf16[384,256]{1,0:T(8,128)(2,1)S(1)}, f32[3,8,256]{2,1,0:T(8,128)S(1)}, f32[3,144,256]{2,1,0:T(8,128)S(1)}) custom-call(s32[10]{0:T(128)S(1)} %pad_add_fusion.1.table, bf16[2,384,128]{2,1,0:T(8,128)(2,1)S(1)} %get-tuple-element.49.refs_0_, bf16[1,384,256]{2,1,0:T(8,128)(2,1)S(1)} %bitcast.16, ...), custom_call_target="tpu_custom_call", output_to_operand_aliasing={{1}: (6, {}), {2}: (7, {})} | custom-call | flops 1 | bytes 1 | tf_op jit(solution)/shard_map/attention/pallas_call | solution.py:38
  88.4 3.8 %output_near.1 = (bf16[384,4608]{1,0:T(8,128)(2,1)S(1)}, bf16[256,4608]{1,0:T(8,128)(2,1)S(1)}) custom-call(s32[10]{0:T(128)S(1)} %pad_add_fusion.1.table, bf16[384,256]{1,0:T(8,128)(2,1)S(1)} %get-tuple-element.68.left, bf16[256,4608]{1,0:T(8,128)(2,1)} %own_hbm.1, bf16[32,4608]{1,0:T(8,128)(2,1)S(1)} %collective-permute-done.13.refs_0_, ...), custom_call_target="tpu_custom_call" | custom-call | flops 1 | bytes 1 | tf_op jit(solution)/shard_map/output_near/pallas_call | solution.py:38
  92.3 3.0 %output_send.1 = (bf16[192,4608]{1,0:T(8,128)(2,1)}, bf16[256,4608]{1,0:T(8,128)(2,1)S(1)}) custom-call(s32[10]{0:T(128)S(1)} %pad_add_fusion.1.table, bf16[384,256]{1,0:T(8,128)(2,1)S(1)} %collective-permute-done.16.left_hbm, bf16[384,4608]{1,0:T(8,128)(2,1)S(1)} %get-tuple-element.72.near, ...), custom_call_target="tpu_custom_call", output_to_operand_aliasing={{1}: (5, {})} | custom-call | flops 1 | bytes 1 | tf_op jit(solution)/shard_map/output_send/pallas_call | solution.py:38
  95.4 1.7 %output_keep.1 = (f32[192,4608]{1,0:T(8,128)S(1)}, bf16[192,4608]{1,0:T(8,128)(2,1)S(1)}) custom-call(bf16[384,256]{1,0:T(8,128)(2,1)S(1)} %collective-permute-done.16.left_hbm, bf16[192,4608]{1,0:T(8,128)(2,1)} %hidden.5, bf16[384,4608]{1,0:T(8,128)(2,1)S(1)} %get-tuple-element.72.near, bf16[256,4608]{1,0:T(8,128)(2,1)S(1)} %get-tuple-element.76.weights), custom_call_target="tpu_custom_call" | custom-call | flops 1 | bytes 1 | tf_op jit(solution)/shard_map/output_keep/pallas_call | solution.py:38
  97.2 2.1 %collective-permute-done.21.received = bf16[192,4608]{1,0:T(8,128)(2,1)S(1)} collective-permute-done((bf16[192,4608]{1,0:T(8,128)(2,1)}, bf16[192,4608]{1,0:T(8,128)(2,1)S(1)}, u32[]{:S(2)}, u32[]{:S(2)}) %collective-permute-start.21) | collective-permute-done | bytes 1769504 | tf_op jit(solution)/shard_map/ppermute | solution.py:593
  99.3 2.6 %output_norm.1 = bf16[192,4608]{1,0:T(8,128)(2,1)} custom-call(bf16[192,4608]{1,0:T(8,128)(2,1)S(1)} %collective-permute-done.21.received, bf16[192,4608]{1,0:T(8,128)(2,1)S(1)} %get-tuple-element.77.hidden, f32[192,4608]{1,0:T(8,128)S(1)} %get-tuple-element.78.kept, f32[4608]{0:T(1024)} %gain.5), custom_call_target="tpu_custom_call" | custom-call | flops 1 | bytes 1 | tf_op jit(solution)/shard_map/output_norm/pallas_call | solution.py:38
  (48 shorter events, 5.2 us)
Async XLA Ops:
  2.4 5.7 %copy-start = (s32[8]{0:T(128)S(1)}, s32[8]{0:T(128)}, u32[]{:S(2)}) copy-start(s32[8]{0:T(128)} %param.15) | copy-start | bytes 100
  2.4 8.8 %collective-permute-start.2 = (bf16[96,4608]{1,0:T(8,128)(2,1)}, bf16[96,4608]{1,0:T(8,128)(2,1)S(1)}, u32[]{:S(2)}, u32[]{:S(2)}) collective-permute-start(bf16[96,4608]{1,0:T(8,128)(2,1)} %norm_rows.3.refs_0_), channel_id=1, source_target_pairs={{0,4},{4,0},{8,12},{12,8},{1,5},{5,1},{9,13},{13,9},{2,6},{6,2},{1... | collective-permute-start | bytes 2654216 | tf_op jit(solution)/shard_map/ppermute | solution.py:593
  2.9 38.3 %collective-permute-start.1 = (bf16[96,4608]{1,0:T(8,128)(2,1)}, bf16[96,4608]{1,0:T(8,128)(2,1)S(1)}, u32[]{:S(2)}, u32[]{:S(2)}) collective-permute-start(bf16[96,4608]{1,0:T(8,128)(2,1)} %norm_rows.3.refs_0_), channel_id=1, source_target_pairs={{0,8},{4,12},{8,0},{12,4},{1,9},{5,13},{9,1},{13,5},{2,10},{6,14},... | collective-permute-start | bytes 2654216 | tf_op jit(solution)/shard_map/ppermute | solution.py:593
  7.8 3.4 %collective-permute-start.3 = (bf16[96,4608]{1,0:T(8,128)(2,1)}, bf16[96,4608]{1,0:T(8,128)(2,1)S(1)}, u32[]{:S(2)}, u32[]{:S(2)}) collective-permute-start(bf16[96,4608]{1,0:T(8,128)(2,1)} %norm_rows.2.refs_1_), channel_id=1, source_target_pairs={{0,4},{4,0},{8,12},{12,8},{1,5},{5,1},{9,13},{13,9},{2,6},{6,2},{1... | collective-permute-start | bytes 2654216 | tf_op jit(solution)/shard_map/ppermute | solution.py:593
  16.0 9.0 %collective-permute-start.6 = (bf16[384,256]{1,0:T(8,128)(2,1)S(1)}, bf16[384,256]{1,0:T(8,128)(2,1)S(1)}, u32[]{:S(2)}, u32[]{:S(2)}) collective-permute-start(bf16[384,256]{1,0:T(8,128)(2,1)S(1)} %get-tuple-element.43), channel_id=1, source_target_pairs={{0,3},{1,0},{2,1},{3,2},{4,7},{5,4},{6,5},{7,6},{8,11},{9,8},{10,9... | collective-permute-start | bytes 589832 | tf_op jit(solution)/shard_map/ppermute | solution.py:600
  19.6 17.2 %collective-permute-start.5 = (bf16[384,256]{1,0:T(8,128)(2,1)S(1)}, bf16[384,256]{1,0:T(8,128)(2,1)S(1)}, u32[]{:S(2)}, u32[]{:S(2)}) collective-permute-start(bf16[384,256]{1,0:T(8,128)(2,1)S(1)} %get-tuple-element.43), channel_id=1, source_target_pairs={{0,2},{1,3},{2,0},{3,1},{4,6},{5,7},{6,4},{7,5},{8,10},{9,11},{10,... | collective-permute-start | bytes 589832 | tf_op jit(solution)/shard_map/ppermute | solution.py:600
  19.6 17.2 %collective-permute-start.4 = (bf16[384,256]{1,0:T(8,128)(2,1)S(1)}, bf16[384,256]{1,0:T(8,128)(2,1)S(1)}, u32[]{:S(2)}, u32[]{:S(2)}) collective-permute-start(bf16[384,256]{1,0:T(8,128)(2,1)S(1)} %get-tuple-element.43), channel_id=1, source_target_pairs={{0,1},{1,2},{2,3},{3,0},{4,5},{5,6},{6,7},{7,4},{8,9},{9,10},{10,1... | collective-permute-start | bytes 589832 | tf_op jit(solution)/shard_map/ppermute | solution.py:600
  20.7 26.5 %collective-permute-start = (bf16[96,4608]{1,0:T(8,128)(2,1)}, bf16[96,4608]{1,0:T(8,128)(2,1)S(1)}, u32[]{:S(2)}, u32[]{:S(2)}) collective-permute-start(bf16[96,4608]{1,0:T(8,128)(2,1)} %norm_rows.2.refs_1_), channel_id=1, source_target_pairs={{0,8},{4,12},{8,0},{12,4},{1,9},{5,13},{9,1},{13,5},{2,10},{6,14},... | collective-permute-start | bytes 2654216 | tf_op jit(solution)/shard_map/ppermute | solution.py:593
  41.2 1.9 %collective-permute-start.8 = (bf16[48,4608]{1,0:T(8,128)(2,1)S(1)}, bf16[48,4608]{1,0:T(8,128)(2,1)S(1)}, u32[]{:S(2)}, u32[]{:S(2)}) collective-permute-start(bf16[48,4608]{1,0:T(8,128)(2,1)S(1)} %get-tuple-element.81), channel_id=1, source_target_pairs={{0,4},{4,0},{8,12},{12,8},{1,5},{5,1},{9,13},{13,9},{2,6},{6,2},{1... | collective-permute-start | bytes 1327112 | tf_op jit(solution)/shard_map/ppermute | solution.py:593
  41.3 6.0 %copy-start.4 = (bf16[32,4608]{1,0:T(8,128)(2,1)S(1)}, bf16[32,4608]{1,0:T(8,128)(2,1)}, u32[]{:S(2)}) copy-start(bf16[32,4608]{1,0:T(8,128)(2,1)} %get-tuple-element.60) | copy-start | bytes 884740
  41.3 6.5 %copy-start.3 = (bf16[32,4608]{1,0:T(8,128)(2,1)S(1)}, bf16[32,4608]{1,0:T(8,128)(2,1)}, u32[]{:S(2)}) copy-start(bf16[32,4608]{1,0:T(8,128)(2,1)} %get-tuple-element.58) | copy-start | bytes 884740
  41.3 2.4 %collective-permute-start.7 = (bf16[48,4608]{1,0:T(8,128)(2,1)S(1)}, bf16[48,4608]{1,0:T(8,128)(2,1)S(1)}, u32[]{:S(2)}, u32[]{:S(2)}) collective-permute-start(bf16[48,4608]{1,0:T(8,128)(2,1)S(1)} %get-tuple-element.82), channel_id=1, source_target_pairs={{0,4},{4,0},{8,12},{12,8},{1,5},{5,1},{9,13},{13,9},{2,6},{6,2},{1... | collective-permute-start | bytes 1327112 | tf_op jit(solution)/shard_map/ppermute | solution.py:593
  47.1 11.5 %copy-start.1 = (bf16[48,4608]{1,0:T(8,128)(2,1)S(1)}, bf16[48,4608]{1,0:T(8,128)(2,1)}, u32[]{:S(2)}) copy-start(bf16[48,4608]{1,0:T(8,128)(2,1)} %get-tuple-element.70) | copy-start | bytes 1327108
  47.1 2.5 %collective-permute-start.9 = (bf16[96,4608]{1,0:T(8,128)(2,1)S(1)}, bf16[96,4608]{1,0:T(8,128)(2,1)S(1)}, u32[]{:S(2)}, u32[]{:S(2)}) collective-permute-start(bf16[96,4608]{1,0:T(8,128)(2,1)S(1)} %collective-permute-done.refs_0_), channel_id=1, source_target_pairs={{0,4},{4,0},{8,12},{12,8},{1,5},{5,1},{9,13},{13,9},{2,6},{6,2},{1... | collective-permute-start | bytes 2654216 | tf_op jit(solution)/shard_map/ppermute | solution.py:593
  47.3 9.8 %collective-permute-start.13 = (bf16[32,4608]{1,0:T(8,128)(2,1)S(1)}, bf16[32,4608]{1,0:T(8,128)(2,1)S(1)}, u32[]{:S(2)}, u32[]{:S(2)}) collective-permute-start(bf16[32,4608]{1,0:T(8,128)(2,1)S(1)} %copy-done.4), channel_id=1, source_target_pairs={{0,8},{4,12},{8,0},{12,4},{1,9},{5,13},{9,1},{13,5},{2,10},{6,14},... | collective-permute-start | bytes 884744 | tf_op jit(solution)/shard_map/ppermute | solution.py:593
  47.9 15.6 %collective-permute-start.11 = (bf16[32,4608]{1,0:T(8,128)(2,1)S(1)}, bf16[32,4608]{1,0:T(8,128)(2,1)S(1)}, u32[]{:S(2)}, u32[]{:S(2)}) collective-permute-start(bf16[32,4608]{1,0:T(8,128)(2,1)S(1)} %copy-done.3), channel_id=1, source_target_pairs={{0,8},{4,12},{8,0},{12,4},{1,9},{5,13},{9,1},{13,5},{2,10},{6,14},... | collective-permute-start | bytes 884744 | tf_op jit(solution)/shard_map/ppermute | solution.py:593
  52.9 27.1 %copy-start.2 = (bf16[32,4608]{1,0:T(8,128)(2,1)S(1)}, bf16[32,4608]{1,0:T(8,128)(2,1)}, u32[]{:S(2)}) copy-start(bf16[32,4608]{1,0:T(8,128)(2,1)} %get-tuple-element.73) | copy-start | bytes 884740
  52.9 10.6 %collective-permute-start.10 = (bf16[384,256]{1,0:T(8,128)(2,1)S(1)}, bf16[384,256]{1,0:T(8,128)(2,1)S(1)}, u32[]{:S(2)}, u32[]{:S(2)}) collective-permute-start(bf16[384,256]{1,0:T(8,128)(2,1)S(1)} %get-tuple-element.57), channel_id=1, source_target_pairs={{0,1},{1,2},{2,3},{3,0},{4,5},{5,6},{6,7},{7,4},{8,9},{9,10},{10,1... | collective-permute-start | bytes 589832 | tf_op jit(solution)/shard_map/ppermute | solution.py:613
  57.2 7.9 %collective-permute-start.14 = (bf16[32,4608]{1,0:T(8,128)(2,1)S(1)}, bf16[32,4608]{1,0:T(8,128)(2,1)S(1)}, u32[]{:S(2)}, u32[]{:S(2)}) collective-permute-start(bf16[32,4608]{1,0:T(8,128)(2,1)S(1)} %collective-permute-done.13.refs_0_), channel_id=1, source_target_pairs={{0,16},{16,0},{1,17},{17,1},{2,18},{18,2},{3,19},{19,3},{4,20},{20... | collective-permute-start | bytes 884744 | tf_op jit(solution)/shard_map/ppermute | solution.py:593
  58.7 17.9 %collective-permute-start.17 = (bf16[48,4608]{1,0:T(8,128)(2,1)S(1)}, bf16[48,4608]{1,0:T(8,128)(2,1)S(1)}, u32[]{:S(2)}, u32[]{:S(2)}) collective-permute-start(bf16[48,4608]{1,0:T(8,128)(2,1)S(1)} %copy-done.1), channel_id=1, source_target_pairs={{0,8},{4,12},{8,0},{12,4},{1,9},{5,13},{9,1},{13,5},{2,10},{6,14},... | collective-permute-start | bytes 1327112 | tf_op jit(solution)/shard_map/ppermute | solution.py:593
  63.5 7.6 %collective-permute-start.12 = (bf16[384,256]{1,0:T(8,128)(2,1)S(1)}, bf16[384,256]{1,0:T(8,128)(2,1)S(1)}, u32[]{:S(2)}, u32[]{:S(2)}) collective-permute-start(bf16[384,256]{1,0:T(8,128)(2,1)S(1)} %collective-permute-done.10), channel_id=1, source_target_pairs={{0,1},{1,2},{2,3},{3,0},{4,5},{5,6},{6,7},{7,4},{8,9},{9,10},{10,1... | collective-permute-start | bytes 589832 | tf_op jit(solution)/shard_map/ppermute | solution.py:613
  63.5 13.1 %collective-permute-start.18 = (bf16[32,4608]{1,0:T(8,128)(2,1)S(1)}, bf16[32,4608]{1,0:T(8,128)(2,1)S(1)}, u32[]{:S(2)}, u32[]{:S(2)}) collective-permute-start(bf16[32,4608]{1,0:T(8,128)(2,1)S(1)} %collective-permute-done.11.refs_1_), channel_id=1, source_target_pairs={{0,16},{16,0},{1,17},{17,1},{2,18},{18,2},{3,19},{19,3},{4,20},{20... | collective-permute-start | bytes 884744 | tf_op jit(solution)/shard_map/ppermute | solution.py:593
  71.1 7.5 %collective-permute-start.15 = (bf16[384,256]{1,0:T(8,128)(2,1)S(1)}, bf16[384,256]{1,0:T(8,128)(2,1)S(1)}, u32[]{:S(2)}, u32[]{:S(2)}) collective-permute-start(bf16[384,256]{1,0:T(8,128)(2,1)S(1)} %collective-permute-done.12), channel_id=1, source_target_pairs={{0,1},{1,2},{2,3},{3,0},{4,5},{5,6},{6,7},{7,4},{8,9},{9,10},{10,1... | collective-permute-start | bytes 589832 | tf_op jit(solution)/shard_map/ppermute | solution.py:613
  78.6 13.7 %collective-permute-start.19 = (bf16[48,4608]{1,0:T(8,128)(2,1)S(1)}, bf16[48,4608]{1,0:T(8,128)(2,1)S(1)}, u32[]{:S(2)}, u32[]{:S(2)}) collective-permute-start(bf16[48,4608]{1,0:T(8,128)(2,1)S(1)} %collective-permute-done.17.refs_2_), channel_id=1, source_target_pairs={{0,16},{16,0},{1,17},{17,1},{2,18},{18,2},{3,19},{19,3},{4,20},{20... | collective-permute-start | bytes 1327112 | tf_op jit(solution)/shard_map/ppermute | solution.py:593
  80.1 12.2 %collective-permute-start.20 = (bf16[32,4608]{1,0:T(8,128)(2,1)S(1)}, bf16[32,4608]{1,0:T(8,128)(2,1)S(1)}, u32[]{:S(2)}, u32[]{:S(2)}) collective-permute-start(bf16[32,4608]{1,0:T(8,128)(2,1)S(1)} %copy-done.2), channel_id=1, source_target_pairs={{0,8},{4,12},{8,0},{12,4},{1,9},{5,13},{9,1},{13,5},{2,10},{6,14},... | collective-permute-start | bytes 884744 | tf_op jit(solution)/shard_map/ppermute | solution.py:593
  84.4 7.9 %collective-permute-start.16 = (bf16[384,256]{1,0:T(8,128)(2,1)S(1)}, bf16[384,256]{1,0:T(8,128)(2,1)S(1)}, u32[]{:S(2)}, u32[]{:S(2)}) collective-permute-start(bf16[384,256]{1,0:T(8,128)(2,1)S(1)} %get-tuple-element.65), channel_id=1, source_target_pairs={{0,8},{4,12},{8,0},{12,4},{1,9},{5,13},{9,1},{13,5},{2,10},{6,14},... | collective-permute-start | bytes 589832 | tf_op jit(solution)/shard_map/ppermute | solution.py:593
  95.3 4.0 %collective-permute-start.21 = (bf16[192,4608]{1,0:T(8,128)(2,1)}, bf16[192,4608]{1,0:T(8,128)(2,1)S(1)}, u32[]{:S(2)}, u32[]{:S(2)}) collective-permute-start(bf16[192,4608]{1,0:T(8,128)(2,1)} %get-tuple-element.75), channel_id=1, source_target_pairs={{0,4},{4,0},{8,12},{12,8},{1,5},{5,1},{9,13},{13,9},{2,6},{6,2},{1... | collective-permute-start | bytes 5308424 | tf_op jit(solution)/shard_map/ppermute | solution.py:593
